TPU v7x, 512 devices: a whole 4x4x16 slice. The times are simulated.
512 devices in a mesh: grp: 8 (over x, y_hi), slab: 64 (over z, y_lo, core).
Axes of the slice: x: 4, y: 4 (y_hi: 2, y_lo: 2; y = y_hi * 2 + y_lo), z: 16, core: 2. Of those that a mesh axis runs over, the one named last changes fastest.
Arguments:
- vectors: float32 [262144, 256], P(('grp', 'slab')), may hold values from -6 to 6
- diag_block: float32 [262144, 512], P(('grp', 'slab')), may hold values from -0.25 to 0.25
- slab_tiles: float32 [262144, 512], P(('grp', 'slab')), may hold values from -0.4375 to 0.4375
- slab_mask: int32 [2048, 4], P(('grp', 'slab')), may hold values from 0 to 1, as said below
- grp_tiles: float32 [262144, 512], P(('grp', 'slab')), may hold values from -0.4375 to 0.4375
- grp_mask: int32 [2048, 4], P(('grp', 'slab')), may hold values from 0 to 1, as said below
Outputs:
- filtered: float32 [262144, 256], P(('grp', 'slab'))
Inputs may be any that keep to these rules, and one draw needn't show every extreme that they name: `slab_mask`: in every slab's 4 x 4 block of tiles toward its slab partner at least one tile is stored. `grp_mask`: in every slab's 4 x 4 block of tiles toward its group partner at least one tile is stored.
All inputs are finite; a program needn't handle non-finite values.
Results may differ from a plain program's by a relative error of at most 0.00005.
Values sent between devices are 32-bit elements; how exact they have to be, the bound alone decides.
No kernel may reach another device: no remote copies, remote signals or barrier semaphores. Data moves between devices by JAX's collectives and lax.ppermute only.
A program may use at most 64 MiB of HBM per device.

v0:
```python
import jax
import jax.numpy as jnp
from jax import lax
from jax.sharding import PartitionSpec as P

CENTER = 0.5
HALF_SPAN = 5.0


def swapped(shard, axis, apart):
    return lax.ppermute(shard, axis, [(i, i ^ 1 << apart) for i in range(lax.axis_size(axis))])


def expand(mask, width):
    return jnp.repeat(jnp.repeat(mask.astype(jnp.float32), width, axis=0), width, axis=1)


def direct(block, vecs):
    return jnp.dot(block, vecs, precision=lax.Precision.HIGHEST, preferred_element_type=jnp.float32)


def transposed(block, vecs):
    return lax.dot_general(
        block,
        vecs,
        (((0,), (0,)), ((), ())),
        precision=lax.Precision.HIGHEST,
        preferred_element_type=jnp.float32,
    )


def body(vectors, diag_block, slab_tiles, slab_mask, grp_tiles, grp_mask):
    width = slab_tiles.shape[0] // slab_mask.shape[0]
    slab_bit = lax.axis_size("slab").bit_length() - 2
    grp_bit = lax.axis_size("grp").bit_length() - 2
    diag_sym = 0.5 * (diag_block + diag_block.T)
    slab_block = slab_tiles * expand(slab_mask, width)
    grp_block = grp_tiles * expand(grp_mask, width)

    def apply(vecs):
        slab_vecs = swapped(vecs, "slab", slab_bit)
        grp_vecs = swapped(vecs, "grp", grp_bit)
        total = direct(diag_sym, vecs)
        slab_part = swapped(transposed(slab_block, vecs), "slab", slab_bit)
        grp_part = swapped(transposed(grp_block, vecs), "grp", grp_bit)
        total = total + slab_part + grp_part
        total = total + direct(slab_block, slab_vecs)
        total = total + direct(grp_block, grp_vecs)
        return total

    first = (apply(vectors) - CENTER * vectors) / HALF_SPAN
    return 2.0 * (apply(first) - CENTER * first) / HALF_SPAN - vectors


def solution(mesh):
    in_specs = (
        P(("grp", "slab"), None),
        P(("grp", "slab"), None),
        P(("grp", "slab"), None),
        P(("grp", "slab"), None),
        P(("grp", "slab"), None),
        P(("grp", "slab"), None),
    )
    out_specs = P(("grp", "slab"), None)
    return jax.shard_map(body, mesh=mesh, in_specs=in_specs, out_specs=out_specs, check_vma=False)
```

profile of v0, /device:TPU:1, one launch (start us, length us, event | category | flops | bytes accessed | tf_op | source)
XLA Modules:
  0.0 212.9 jit_solution(8467062825458139504)
XLA Ops:
  0.0 5.6 %collective-permute-start.3 = (f32[512,256]{1,0:T(8,128)}, f32[512,256]{1,0:T(8,128)}, u32[]{:S(2)}, u32[]{:S(2)}) collective-permute-start(f32[512,256]{1,0:T(8,128)} %param.6), channel_id=1, source_target_pairs={{0,256},{64,320},{128,384},{192,448},{256,0},{320,64},{384,128},{4... | collective-permute-start | bytes 1572872 | tf_op jit(solution)/shard_map/ppermute | solution.py:11
  5.6 15.4 %collective-permute-start.2 = (f32[512,256]{1,0:T(8,128)}, f32[512,256]{1,0:T(8,128)}, u32[]{:S(2)}, u32[]{:S(2)}) collective-permute-start(f32[512,256]{1,0:T(8,128)} %param.6), channel_id=1, source_target_pairs={{0,32},{1,33},{2,34},{3,35},{4,36},{5,37},{6,38},{7,39},{8,40},{9,... | collective-permute-start | bytes 1572872 | tf_op jit(solution)/shard_map/ppermute | solution.py:11
  22.6 0.8 copy-done.2
  23.4 2.6 %fusion.21 = f32[512,256]{1,0:T(8,128)} fusion(f32[512,512]{1,0:T(8,128)S(1)} %bitcast_multiply_fusion, f32[512,256]{1,0:T(8,128)S(1)} %copy-done.2), kind=kOutput, calls=%fused_computation.25 | convolution fusion | flops 805306368 | bytes 2097152 | tf_op jit(solution)/shard_map/dot_general | solution.py:23
  26.1 2.3 %collective-permute-start.1 = (f32[512,256]{1,0:T(8,128)}, f32[512,256]{1,0:T(8,128)}, u32[]{:S(2)}, u32[]{:S(2)}) collective-permute-start(f32[512,256]{1,0:T(8,128)} %fusion.21), channel_id=1, source_target_pairs={{0,256},{64,320},{128,384},{192,448},{256,0},{320,64},{384,128},{4... | collective-permute-start | bytes 1572872 | tf_op jit(solution)/shard_map/ppermute | solution.py:11
  29.2 2.6 %fusion.20 = f32[512,256]{1,0:T(8,128)} fusion(f32[512,512]{1,0:T(8,128)S(1)} %bitcast_multiply_fusion.1, f32[512,256]{1,0:T(8,128)S(1)} %copy-done.2), kind=kOutput, calls=%fused_computation.24 | convolution fusion | flops 805306368 | bytes 2097152 | tf_op jit(solution)/shard_map/dot_general | solution.py:23
  31.8 1.9 collective-permute-start
  33.8 1.3 copy.7
  35.1 2.0 fusion.23
  37.1 2.1 %fusion.22 = f32[512,256]{1,0:T(8,128)S(1)} fusion(f32[512,512]{1,0:T(8,128)S(1)} %bitcast_multiply_fusion.1, f32[512,256]{1,0:T(8,128)} %collective-permute-done.2), kind=kOutput, calls=%fused_computation.26 | convolution fusion | flops 805306368 | bytes 2097152 | tf_op jit(solution)/shard_map/dot_general | solution.py:19
  39.3 2.8 %collective-permute-done.1 = f32[512,256]{1,0:T(8,128)} collective-permute-done((f32[512,256]{1,0:T(8,128)}, f32[512,256]{1,0:T(8,128)}, u32[]{:S(2)}, u32[]{:S(2)}) %collective-permute-start.1) | collective-permute-done | bytes 524320 | tf_op jit(solution)/shard_map/ppermute | solution.py:11
  42.1 35.7 %collective-permute-done = f32[512,256]{1,0:T(8,128)} collective-permute-done((f32[512,256]{1,0:T(8,128)}, f32[512,256]{1,0:T(8,128)}, u32[]{:S(2)}, u32[]{:S(2)}) %collective-permute-start) | collective-permute-done | bytes 524320 | tf_op jit(solution)/shard_map/ppermute | solution.py:11
  77.8 2.3 %broadcast_multiply_fusion = (f32[512,256]{1,0:T(8,128)S(1)}, f32[512,256]{1,0:T(8,128)S(1)}) fusion(f32[512,256]{1,0:T(8,128)S(1)} %copy-done.3, f32[512,256]{1,0:T(8,128)S(1)} %fusion.23, f32[512,256]{1,0:T(8,128)S(1)} %fusion.22, f32[512,256]{1,0:T(8,128)} %collective-permute-done.1, f32[512,256]{1,0:T(8,128)} %collective-permute-done, ...), kind=kOutput, calls=%fused_computation.16 | convolution fusion | flops 806748160 | bytes 5767168 | tf_op jit(solution)/shard_map/dot_general | solution.py:19
  80.1 41.7 %collective-permute-start.7 = (f32[512,256]{1,0:T(8,128)S(1)}, f32[512,256]{1,0:T(8,128)S(1)}, u32[]{:S(2)}, u32[]{:S(2)}) collective-permute-start(f32[512,256]{1,0:T(8,128)S(1)} %get-tuple-element.5), channel_id=1, source_target_pairs={{0,256},{64,320},{128,384},{192,448},{256,0},{320,64},{384,128},{4... | collective-permute-start | bytes 1572872 | tf_op jit(solution)/shard_map/ppermute | solution.py:11
  121.8 5.4 %collective-permute-start.6 = (f32[512,256]{1,0:T(8,128)S(1)}, f32[512,256]{1,0:T(8,128)S(1)}, u32[]{:S(2)}, u32[]{:S(2)}) collective-permute-start(f32[512,256]{1,0:T(8,128)S(1)} %get-tuple-element.5), channel_id=1, source_target_pairs={{0,32},{1,33},{2,34},{3,35},{4,36},{5,37},{6,38},{7,39},{8,40},{9,... | collective-permute-start | bytes 1572872 | tf_op jit(solution)/shard_map/ppermute | solution.py:11
  127.2 1.8 fusion.13
  129.0 2.1 collective-permute-start.5
  131.1 1.8 fusion.14
  133.0 8.6 %collective-permute-start.4 = (f32[512,256]{1,0:T(8,128)S(1)}, f32[512,256]{1,0:T(8,128)S(1)}, u32[]{:S(2)}, u32[]{:S(2)}) collective-permute-start(f32[512,256]{1,0:T(8,128)S(1)} %fusion.14), channel_id=1, source_target_pairs={{0,32},{1,33},{2,34},{3,35},{4,36},{5,37},{6,38},{7,39},{8,40},{9,... | collective-permute-start | bytes 1572872 | tf_op jit(solution)/shard_map/ppermute | solution.py:11
  141.6 1.0 fusion.25
  142.6 57.1 %collective-permute-done.6 = f32[512,256]{1,0:T(8,128)S(1)} collective-permute-done((f32[512,256]{1,0:T(8,128)S(1)}, f32[512,256]{1,0:T(8,128)S(1)}, u32[]{:S(2)}, u32[]{:S(2)}) %collective-permute-start.6) | collective-permute-done | bytes 524320 | tf_op jit(solution)/shard_map/ppermute | solution.py:11
  199.7 1.0 fusion.24
  200.7 10.2 %collective-permute-done.4 = f32[512,256]{1,0:T(8,128)S(1)} collective-permute-done((f32[512,256]{1,0:T(8,128)S(1)}, f32[512,256]{1,0:T(8,128)S(1)}, u32[]{:S(2)}, u32[]{:S(2)}) %collective-permute-start.4) | collective-permute-done | bytes 524320 | tf_op jit(solution)/shard_map/ppermute | solution.py:11
  210.9 2.0 fusion.6
  (25 shorter events, 2.4 us)
Async XLA Ops:
  0.0 22.4 %copy-start.4 = (f32[512,512]{1,0:T(8,128)S(1)}, f32[512,512]{1,0:T(8,128)}, u32[]{:S(2)}) copy-start(f32[512,512]{1,0:T(8,128)} %param.10) | copy-start | bytes 3145732
  0.0 35.1 %collective-permute-start.3 = (f32[512,256]{1,0:T(8,128)}, f32[512,256]{1,0:T(8,128)}, u32[]{:S(2)}, u32[]{:S(2)}) collective-permute-start(f32[512,256]{1,0:T(8,128)} %param.6), channel_id=1, source_target_pairs={{0,256},{64,320},{128,384},{192,448},{256,0},{320,64},{384,128},{4... | collective-permute-start | bytes 1572872 | tf_op jit(solution)/shard_map/ppermute | solution.py:11
  5.6 31.5 %collective-permute-start.2 = (f32[512,256]{1,0:T(8,128)}, f32[512,256]{1,0:T(8,128)}, u32[]{:S(2)}, u32[]{:S(2)}) collective-permute-start(f32[512,256]{1,0:T(8,128)} %param.6), channel_id=1, source_target_pairs={{0,32},{1,33},{2,34},{3,35},{4,36},{5,37},{6,38},{7,39},{8,40},{9,... | collective-permute-start | bytes 1572872 | tf_op jit(solution)/shard_map/ppermute | solution.py:11
  22.4 1.0 copy-start.2
  23.4 4.9 %copy-start.6 = (s32[4,4]{1,0:T(4,128)S(1)}, s32[4,4]{1,0:T(4,128)}, u32[]{:S(2)}) copy-start(s32[4,4]{1,0:T(4,128)} %param.9) | copy-start | bytes 196
  26.1 2.9 %copy-start.5 = (f32[512,512]{1,0:T(8,128)S(1)}, f32[512,512]{1,0:T(8,128)}, u32[]{:S(2)}) copy-start(f32[512,512]{1,0:T(8,128)} %param.8) | copy-start | bytes 3145732
  26.1 16.0 %collective-permute-start.1 = (f32[512,256]{1,0:T(8,128)}, f32[512,256]{1,0:T(8,128)}, u32[]{:S(2)}, u32[]{:S(2)}) collective-permute-start(f32[512,256]{1,0:T(8,128)} %fusion.21), channel_id=1, source_target_pairs={{0,256},{64,320},{128,384},{192,448},{256,0},{320,64},{384,128},{4... | collective-permute-start | bytes 1572872 | tf_op jit(solution)/shard_map/ppermute | solution.py:11
  29.2 4.6 %copy-start = (f32[512,512]{1,0:T(8,128)S(1)}, f32[512,512]{1,0:T(8,128)}, u32[]{:S(2)}) copy-start(f32[512,512]{1,0:T(8,128)} %param.7) | copy-start | bytes 3145732
  31.8 45.9 %collective-permute-start = (f32[512,256]{1,0:T(8,128)}, f32[512,256]{1,0:T(8,128)}, u32[]{:S(2)}, u32[]{:S(2)}) collective-permute-start(f32[512,256]{1,0:T(8,128)} %fusion.20), channel_id=1, source_target_pairs={{0,32},{1,33},{2,34},{3,35},{4,36},{5,37},{6,38},{7,39},{8,40},{9,... | collective-permute-start | bytes 1572872 | tf_op jit(solution)/shard_map/ppermute | solution.py:11
  37.1 40.6 %copy-start.1 = (f32[512,512]{0,1:T(8,128)S(1)}, f32[512,512]{0,1:T(8,128)}, u32[]{:S(2)}) copy-start(f32[512,512]{0,1:T(8,128)} %copy.7) | copy-start | bytes 3145732
  37.1 40.6 %copy-start.3 = (f32[512,256]{1,0:T(8,128)S(1)}, f32[512,256]{1,0:T(8,128)}, u32[]{:S(2)}) copy-start(f32[512,256]{1,0:T(8,128)} %param.6) | copy-start | bytes 1572868
  80.1 61.5 %collective-permute-start.7 = (f32[512,256]{1,0:T(8,128)S(1)}, f32[512,256]{1,0:T(8,128)S(1)}, u32[]{:S(2)}, u32[]{:S(2)}) collective-permute-start(f32[512,256]{1,0:T(8,128)S(1)} %get-tuple-element.5), channel_id=1, source_target_pairs={{0,256},{64,320},{128,384},{192,448},{256,0},{320,64},{384,128},{4... | collective-permute-start | bytes 1572872 | tf_op jit(solution)/shard_map/ppermute | solution.py:11
  121.8 77.9 %collective-permute-start.6 = (f32[512,256]{1,0:T(8,128)S(1)}, f32[512,256]{1,0:T(8,128)S(1)}, u32[]{:S(2)}, u32[]{:S(2)}) collective-permute-start(f32[512,256]{1,0:T(8,128)S(1)} %get-tuple-element.5), channel_id=1, source_target_pairs={{0,32},{1,33},{2,34},{3,35},{4,36},{5,37},{6,38},{7,39},{8,40},{9,... | collective-permute-start | bytes 1572872 | tf_op jit(solution)/shard_map/ppermute | solution.py:11
  129.0 71.7 %collective-permute-start.5 = (f32[512,256]{1,0:T(8,128)S(1)}, f32[512,256]{1,0:T(8,128)S(1)}, u32[]{:S(2)}, u32[]{:S(2)}) collective-permute-start(f32[512,256]{1,0:T(8,128)S(1)} %fusion.13), channel_id=1, source_target_pairs={{0,256},{64,320},{128,384},{192,448},{256,0},{320,64},{384,128},{4... | collective-permute-start | bytes 1572872 | tf_op jit(solution)/shard_map/ppermute | solution.py:11
  133.0 78.0 %collective-permute-start.4 = (f32[512,256]{1,0:T(8,128)S(1)}, f32[512,256]{1,0:T(8,128)S(1)}, u32[]{:S(2)}, u32[]{:S(2)}) collective-permute-start(f32[512,256]{1,0:T(8,128)S(1)} %fusion.14), channel_id=1, source_target_pairs={{0,32},{1,33},{2,34},{3,35},{4,36},{5,37},{6,38},{7,39},{8,40},{9,... | collective-permute-start | bytes 1572872 | tf_op jit(solution)/shard_map/ppermute | solution.py:11
where the time goes:
time: 213 us
  waiting for transfers between devices  106 us (50%)
  starting transfers between devices  83 us (39%)
  matrix products  19.3 us (9%)
  local copies, waits for them, and re-layouts  3.4 us (2%)
    ppermute x8, waiting for transfers between devices, swapped(): lax.ppermute(shard, axis, [(i, i ^ 1 << apart) for i in range(lax.axis_si...  106 us
    ppermute x8, starting transfers between devices, swapped(): lax.ppermute(shard, axis, [(i, i ^ 1 << apart) for i in range(lax.axis_si...  83 us
    dot_general x6, matrix products, direct(): jnp.dot(block, vecs, precision=lax.Precision.HIGHEST, preferred_element_t...  10.4 us
    dot_general x4, matrix products, transposed(): lax.dot_general(block, vecs, (((0,), (0,)), ((), ())), precision=lax.Prec...  8.88 us
  transfers between devices with their start and end apart: 8, of which 4 were waited for; matrix products, arithmetic and copies ran while one was open for 9% of the time, Pallas kernels for 0%

commit v1 on v0

v1 whole, which is shorter than its diff:
```python
import jax
import jax.numpy as jnp
from jax import lax
from jax.sharding import PartitionSpec as P

CENTER = 0.5
HALF_SPAN = 5.0


def expand(mask, width):
    return jnp.repeat(jnp.repeat(mask.astype(jnp.float32), width, axis=0), width, axis=1)


def direct(block, vecs):
    return jnp.dot(block, vecs, precision=lax.Precision.HIGH, preferred_element_type=jnp.float32)


def transposed(block, vecs):
    return lax.dot_general(
        block,
        vecs,
        (((0,), (0,)), ((), ())),
        precision=lax.Precision.HIGH,
        preferred_element_type=jnp.float32,
    )


def owns(slab, half):
    return (slab < half) == (slab % 2 == 0)


def body(vectors, diag_block, slab_tiles, slab_mask, grp_tiles, grp_mask):
    width = slab_tiles.shape[0] // slab_mask.shape[0]
    n_slab, n_grp = lax.axis_size("slab"), lax.axis_size("grp")
    half = n_slab // 2
    owner = owns(lax.axis_index("slab"), half)
    to_owner = [(i, i ^ half) for i in range(n_slab) if not owns(i, half)]
    from_owner = [(i, i ^ half) for i in range(n_slab) if owns(i, half)]
    grp_pairs = [(i, i ^ (n_grp // 2)) for i in range(n_grp)]

    slab_block = slab_tiles * expand(slab_mask, width)
    grp_block = grp_tiles * expand(grp_mask, width)

    vecs_in = lax.ppermute(vectors, "slab", to_owner)
    slab_in = lax.ppermute(slab_block, "slab", to_owner)
    vecs_grp = lax.ppermute(vectors, "grp", grp_pairs)
    grp_in = lax.ppermute(grp_block, "grp", grp_pairs)

    diag = 0.5 * (diag_block + diag_block.T) - CENTER * jnp.eye(diag_block.shape[0], dtype=jnp.float32)
    across = grp_block + grp_in.T
    base = direct(diag, vectors) + direct(across, vecs_grp)
    base_in = lax.ppermute(base, "slab", to_owner)

    pair = slab_block + slab_in.T
    back = transposed(pair, vectors)
    back_in = lax.ppermute(back, "slab", from_owner)
    first_own = (base + direct(pair, vecs_in)) / HALF_SPAN
    back2 = transposed(pair, first_own)
    back2_in = lax.ppermute(back2, "slab", from_owner)

    first = jnp.where(owner, first_own, (base + back_in) / HALF_SPAN)
    first_grp = lax.ppermute(first, "grp", grp_pairs)
    partner_first = (base_in + back) / HALF_SPAN
    cross = jnp.where(owner, direct(pair, partner_first), back2_in)
    total = direct(diag, first) + direct(across, first_grp) + cross
    return 2.0 * total / HALF_SPAN - vectors


def solution(mesh):
    spec = P(("grp", "slab"), None)
    return jax.shard_map(body, mesh=mesh, in_specs=(spec,) * 6, out_specs=spec, check_vma=False)
```

time: 213 us -> 169 us (0.79)
  the two profiles are of different devices: /device:TPU:1 before, /device:TPU:202 now
where the time goes in v1:
time: 169 us
  waiting for transfers between devices  125 us (74%)
  starting transfers between devices  19.4 us (11%)
  matrix products  14.4 us (9%)
  local copies, waits for them, and re-layouts  5.26 us (3%)
  other arithmetic  3.77 us (2%)
    ppermute x1, waiting for transfers between devices, body(): slab_in = lax.ppermute(slab_block, 'slab', to_owner)  87.9 us
    ppermute x1, waiting for transfers between devices, body(): vecs_in = lax.ppermute(vectors, 'slab', to_owner)  23.9 us
    ppermute x1, waiting for transfers between devices, body(): base_in = lax.ppermute(base, 'slab', to_owner)  13.5 us
    dot_general x6, matrix products, direct(): jnp.dot(block, vecs, precision=lax.Precision.HIGH, preferred_element_type...  10.8 us
    ppermute x1, starting transfers between devices, body(): grp_in = lax.ppermute(grp_block, 'grp', grp_pairs)  4.02 us
    ppermute x1, starting transfers between devices, body(): first_grp = lax.ppermute(first, 'grp', grp_pairs)  3.94 us
    dot_general x2, matrix products, transposed(): lax.dot_general(block, vecs, (((0,), (0,)), ((), ())), precision=lax.Prec...  3.6 us
  transfers between devices with their start and end apart: 8, of which 3 were waited for; matrix products, arithmetic and copies ran while one was open for 10% of the time, Pallas kernels for 0%

profile of v1, /device:TPU:202, one launch (start us, length us, event | category | flops | bytes accessed | tf_op | source)
XLA Modules:
  0.0 168.5 jit_solution(15176262351547181288)
XLA Ops:
  1.6 1.3 copy.9
  3.0 1.4 collective-permute-start.2
  5.3 1.3 copy.8
  6.6 4.0 %collective-permute-start = (f32[512,512]{0,1:T(8,128)}, f32[512,512]{0,1:T(8,128)}, u32[]{:S(2)}, u32[]{:S(2)}) collective-permute-start(f32[512,512]{0,1:T(8,128)} %copy.8), channel_id=1, source_target_pairs={{0,256},{64,320},{128,384},{192,448},{256,0},{320,64},{384,128},{4... | collective-permute-start | bytes 3145736 | tf_op jit(solution)/shard_map/ppermute | solution.py:47
  10.6 3.3 %collective-permute-start.1 = (f32[512,256]{1,0:T(8,128)}, f32[512,256]{1,0:T(8,128)}, u32[]{:S(2)}, u32[]{:S(2)}) collective-permute-start(f32[512,256]{1,0:T(8,128)} %param.6), channel_id=1, source_target_pairs={{0,256},{64,320},{128,384},{192,448},{256,0},{320,64},{384,128},{4... | collective-permute-start | bytes 1572872 | tf_op jit(solution)/shard_map/ppermute | solution.py:46
  14.0 1.3 collective-permute-start.3
  15.3 1.3 copy.7
  16.6 2.0 %fusion.11 = f32[512,256]{1,0:T(8,128)S(1)} fusion(f32[512,256]{1,0:T(8,128)} %param.6, f32[512,512]{1,0:T(8,128)S(1)} %copy-done, f32[512,512]{0,1:T(8,128)} %copy.7), kind=kOutput, calls=%fused_computation.21 | convolution fusion | flops 403963904 | bytes 3145728 | tf_op jit(solution)/shard_map/dot_general | solution.py:15
  18.6 87.9 %collective-permute-done.2 = f32[512,512]{0,1:T(8,128)} collective-permute-done((f32[512,512]{0,1:T(8,128)}, f32[512,512]{0,1:T(8,128)}, u32[]{:S(2)}, u32[]{:S(2)}) %collective-permute-start.2) | collective-permute-done | bytes 1048608 | tf_op jit(solution)/shard_map/ppermute | solution.py:45
  106.5 1.4 bitcast_add_fusion
  108.0 1.8 %fusion.18 = f32[512,256]{1,0:T(8,128)} fusion(f32[512,512]{1,0:T(8,128)S(1)} %bitcast_add_fusion, f32[512,256]{1,0:T(8,128)S(1)} %copy-done.3), kind=kOutput, calls=%fused_computation.27 | convolution fusion | flops 402653184 | bytes 2097152 | tf_op jit(solution)/shard_map/dot_general | solution.py:19
  109.8 2.1 %collective-permute-start.4 = (f32[512,256]{1,0:T(8,128)}, f32[512,256]{1,0:T(8,128)}, u32[]{:S(2)}, u32[]{:S(2)}) collective-permute-start(f32[512,256]{1,0:T(8,128)} %fusion.18), channel_id=1, source_target_pairs={{0,32},{2,34},{4,36},{6,38},{8,40},{10,42},{12,44},{14,46},{16,48}... | collective-permute-start | bytes 1572872 | tf_op jit(solution)/shard_map/ppermute | solution.py:56
  111.9 2.0 %convolution_add_fusion.2 = f32[512,256]{1,0:T(8,128)S(1)} fusion(f32[512,256]{1,0:T(8,128)S(1)} %fusion.11, f32[512,256]{1,0:T(8,128)} %collective-permute-done.1, f32[512,512]{1,0:T(8,128)S(1)} %bitcast_multiply_fusion.1, f32[512,512]{0,1:T(8,128)} %collective-permute-done), kind=kOutput, calls=%fused_computation.2 | convolution fusion | flops 403046400 | bytes 3670016 | tf_op jit(solution)/shard_map/dot_general | solution.py:15
  113.8 23.9 %collective-permute-done.3 = f32[512,256]{1,0:T(8,128)} collective-permute-done((f32[512,256]{1,0:T(8,128)}, f32[512,256]{1,0:T(8,128)}, u32[]{:S(2)}, u32[]{:S(2)}) %collective-permute-start.3) | collective-permute-done | bytes 524320 | tf_op jit(solution)/shard_map/ppermute | solution.py:44
  137.8 1.6 fusion
  139.4 1.8 %fusion.19 = f32[512,256]{1,0:T(8,128)} fusion(f32[512,512]{1,0:T(8,128)S(1)} %bitcast_add_fusion, f32[512,256]{1,0:T(8,128)S(1)} %fusion), kind=kOutput, calls=%fused_computation.28 | convolution fusion | flops 402653184 | bytes 2097152 | tf_op jit(solution)/shard_map/dot_general | solution.py:19
  141.2 2.1 %collective-permute-start.7 = (f32[512,256]{1,0:T(8,128)}, f32[512,256]{1,0:T(8,128)}, u32[]{:S(2)}, u32[]{:S(2)}) collective-permute-start(f32[512,256]{1,0:T(8,128)} %fusion.19), channel_id=1, source_target_pairs={{0,32},{2,34},{4,36},{6,38},{8,40},{10,42},{12,44},{14,46},{16,48}... | collective-permute-start | bytes 1572872 | tf_op jit(solution)/shard_map/ppermute | solution.py:59
  143.3 1.3 collective-permute-start.6
  144.6 1.1 multiply_select_fusion
  145.8 3.9 %collective-permute-start.5 = (f32[512,256]{1,0:T(8,128)S(1)}, f32[512,256]{1,0:T(8,128)S(1)}, u32[]{:S(2)}, u32[]{:S(2)}) collective-permute-start(f32[512,256]{1,0:T(8,128)S(1)} %multiply_select_fusion), channel_id=1, source_target_pairs={{0,256},{64,320},{128,384},{192,448},{256,0},{320,64},{384,128},{4... | collective-permute-start | bytes 1572872 | tf_op jit(solution)/shard_map/ppermute | solution.py:62
  149.7 13.5 %collective-permute-done.6 = f32[512,256]{1,0:T(8,128)} collective-permute-done((f32[512,256]{1,0:T(8,128)S(1)}, f32[512,256]{1,0:T(8,128)}, u32[]{:S(2)}, u32[]{:S(2)}) %collective-permute-start.6) | collective-permute-done | bytes 524320 | tf_op jit(solution)/shard_map/ppermute | solution.py:52
  163.2 1.8 %convolution_select_fusion = f32[512,256]{1,0:T(8,128)S(1)} fusion(f32[512,256]{1,0:T(8,128)} %collective-permute-done.7, f32[512,512]{1,0:T(8,128)S(1)} %bitcast_add_fusion, f32[512,256]{1,0:T(8,128)} %collective-permute-done.6, f32[512,256]{1,0:T(8,128)} %fusion.18, pred[]{:T(512)S(6)} %eq.13), kind=kOutput, calls=%fused_computation.5 | convolution fusion | flops 403046400 | bytes 3145729 | tf_op jit(solution)/shard_map/dot_general | solution.py:15
  165.1 2.0 %fusion.8 = f32[512,256]{1,0:T(8,128)S(1)} fusion(f32[512,256]{1,0:T(8,128)S(1)} %collective-permute-done.5, f32[512,512]{1,0:T(8,128)S(1)} %bitcast_multiply_fusion.1, f32[512,512]{0,1:T(8,128)} %collective-permute-done), kind=kOutput, calls=%fused_computation.19 | convolution fusion | flops 402915328 | bytes 3145728 | tf_op jit(solution)/shard_map/dot_general | solution.py:15
  167.1 1.4 fusion.3
  (29 shorter events, 2.5 us)
Async XLA Ops:
  0.0 1.4 copy-start.5
  1.6 2.8 %copy-start.7 = (s32[4,4]{1,0:T(4,128)S(1)}, s32[4,4]{1,0:T(4,128)}, u32[]{:S(2)}) copy-start(s32[4,4]{1,0:T(4,128)} %param.11) | copy-start | bytes 196
  3.0 2.1 %copy-start.6 = (f32[512,512]{1,0:T(8,128)S(1)}, f32[512,512]{1,0:T(8,128)}, u32[]{:S(2)}) copy-start(f32[512,512]{1,0:T(8,128)} %param.10) | copy-start | bytes 3145732
  3.0 103.6 %collective-permute-start.2 = (f32[512,512]{0,1:T(8,128)}, f32[512,512]{0,1:T(8,128)}, u32[]{:S(2)}, u32[]{:S(2)}) collective-permute-start(f32[512,512]{0,1:T(8,128)} %copy.9), channel_id=1, source_target_pairs={{1,33},{3,35},{5,37},{7,39},{9,41},{11,43},{13,45},{15,47},{17,49}... | collective-permute-start | bytes 3145736 | tf_op jit(solution)/shard_map/ppermute | solution.py:45
  5.3 10.0 %copy-start = (f32[512,512]{1,0:T(8,128)S(1)}, f32[512,512]{1,0:T(8,128)}, u32[]{:S(2)}) copy-start(f32[512,512]{1,0:T(8,128)} %param.7) | copy-start | bytes 3145732
  6.6 105.3 %collective-permute-start = (f32[512,512]{0,1:T(8,128)}, f32[512,512]{0,1:T(8,128)}, u32[]{:S(2)}, u32[]{:S(2)}) collective-permute-start(f32[512,512]{0,1:T(8,128)} %copy.8), channel_id=1, source_target_pairs={{0,256},{64,320},{128,384},{192,448},{256,0},{320,64},{384,128},{4... | collective-permute-start | bytes 3145736 | tf_op jit(solution)/shard_map/ppermute | solution.py:47
  10.6 101.2 %collective-permute-start.1 = (f32[512,256]{1,0:T(8,128)}, f32[512,256]{1,0:T(8,128)}, u32[]{:S(2)}, u32[]{:S(2)}) collective-permute-start(f32[512,256]{1,0:T(8,128)} %param.6), channel_id=1, source_target_pairs={{0,256},{64,320},{128,384},{192,448},{256,0},{320,64},{384,128},{4... | collective-permute-start | bytes 1572872 | tf_op jit(solution)/shard_map/ppermute | solution.py:46
  14.0 123.8 %collective-permute-start.3 = (f32[512,256]{1,0:T(8,128)}, f32[512,256]{1,0:T(8,128)}, u32[]{:S(2)}, u32[]{:S(2)}) collective-permute-start(f32[512,256]{1,0:T(8,128)} %param.6), channel_id=1, source_target_pairs={{1,33},{3,35},{5,37},{7,39},{9,41},{11,43},{13,45},{15,47},{17,49}... | collective-permute-start | bytes 1572872 | tf_op jit(solution)/shard_map/ppermute | solution.py:44
  18.6 89.4 %copy-start.3 = (f32[512,256]{1,0:T(8,128)S(1)}, f32[512,256]{1,0:T(8,128)}, u32[]{:S(2)}) copy-start(f32[512,256]{1,0:T(8,128)} %param.6) | copy-start | bytes 1572868
  109.8 34.8 %collective-permute-start.4 = (f32[512,256]{1,0:T(8,128)}, f32[512,256]{1,0:T(8,128)}, u32[]{:S(2)}, u32[]{:S(2)}) collective-permute-start(f32[512,256]{1,0:T(8,128)} %fusion.18), channel_id=1, source_target_pairs={{0,32},{2,34},{4,36},{6,38},{8,40},{10,42},{12,44},{14,46},{16,48}... | collective-permute-start | bytes 1572872 | tf_op jit(solution)/shard_map/ppermute | solution.py:56
  141.2 8.5 %collective-permute-start.7 = (f32[512,256]{1,0:T(8,128)}, f32[512,256]{1,0:T(8,128)}, u32[]{:S(2)}, u32[]{:S(2)}) collective-permute-start(f32[512,256]{1,0:T(8,128)} %fusion.19), channel_id=1, source_target_pairs={{0,32},{2,34},{4,36},{6,38},{8,40},{10,42},{12,44},{14,46},{16,48}... | collective-permute-start | bytes 1572872 | tf_op jit(solution)/shard_map/ppermute | solution.py:59
  143.3 19.9 %collective-permute-start.6 = (f32[512,256]{1,0:T(8,128)S(1)}, f32[512,256]{1,0:T(8,128)}, u32[]{:S(2)}, u32[]{:S(2)}) collective-permute-start(f32[512,256]{1,0:T(8,128)S(1)} %convolution_add_fusion.2), channel_id=1, source_target_pairs={{1,33},{3,35},{5,37},{7,39},{9,41},{11,43},{13,45},{15,47},{17,49}... | collective-permute-start | bytes 1572872 | tf_op jit(solution)/shard_map/ppermute | solution.py:52
  145.8 19.3 %collective-permute-start.5 = (f32[512,256]{1,0:T(8,128)S(1)}, f32[512,256]{1,0:T(8,128)S(1)}, u32[]{:S(2)}, u32[]{:S(2)}) collective-permute-start(f32[512,256]{1,0:T(8,128)S(1)} %multiply_select_fusion), channel_id=1, source_target_pairs={{0,256},{64,320},{128,384},{192,448},{256,0},{320,64},{384,128},{4... | collective-permute-start | bytes 1572872 | tf_op jit(solution)/shard_map/ppermute | solution.py:62
  165.0 2.0 %copy-start.1 = (f32[512,512]{1,0:T(8,128)S(1)}, f32[512,512]{1,0:T(8,128)}, u32[]{:S(2)}) copy-start(f32[512,512]{1,0:T(8,128)} %param.7) | copy-start | bytes 3145732
  165.1 2.0 %copy-start.2 = (f32[512,512]{0,1:T(8,128)S(1)}, f32[512,512]{0,1:T(8,128)}, u32[]{:S(2)}) copy-start(f32[512,512]{0,1:T(8,128)} %copy.7) | copy-start | bytes 3145732
  165.1 2.0 %copy-start.4 = (f32[512,256]{1,0:T(8,128)S(1)}, f32[512,256]{1,0:T(8,128)}, u32[]{:S(2)}) copy-start(f32[512,256]{1,0:T(8,128)} %param.6) | copy-start | bytes 1572868

commit v2 on v1

v2 whole, which is shorter than its diff:
```python
import functools

import jax
import jax.numpy as jnp
from jax import lax
from jax.experimental import pallas as pl
from jax.experimental.pallas import tpu as pltpu
from jax.sharding import PartitionSpec as P

CENTER = 0.5
HALF_SPAN = 5.0
FIXED = 6
COST = 1000
GRP_CUTS = 2
BACK_CUTS = 1


def split(x):
    high = x.astype(jnp.bfloat16)
    return high, (x - high.astype(jnp.float32)).astype(jnp.bfloat16)


def product(a, b):
    dot = functools.partial(jnp.dot, preferred_element_type=jnp.float32)
    return dot(a[0], b[0]) + (dot(a[0], b[1]) + dot(a[1], b[0]))


def owns(slab, half):
    return (slab < half) == (slab % 2 == 0)


def pack_kernel(tile, slab_mask, grp_mask, slab_ref, grp_ref, fixed_ref, extra_ref, grp_out):
    n = slab_ref.shape[0] // tile
    fixed_ref[...] = jnp.zeros_like(fixed_ref)
    extra_ref[...] = jnp.zeros_like(extra_ref)
    slot = jnp.int32(0)
    for i in range(n):
        for j in range(n):
            at = (slice(i * tile, (i + 1) * tile), slice(j * tile, (j + 1) * tile))
            grp_out[at] = grp_ref[at] * grp_mask[i, j].astype(jnp.float32)
            stored = slab_mask[i, j] > 0

            @pl.when(jnp.logical_and(stored, slot < FIXED))
            def _():
                fixed_ref[slot] = slab_ref[at]

            @pl.when(jnp.logical_and(stored, slot >= FIXED))
            def _():
                extra_ref[slot - FIXED] = slab_ref[at]

            slot = slot + stored.astype(jnp.int32)


def pair_kernel(tile, own_mask, in_mask, own_ref, fixed_ref, extra_ref, vec_ref, out_ref, back_ref):
    n = own_ref.shape[0] // tile
    slot = jnp.int32(0)
    for i in range(n):
        for j in range(n):
            at = (slice(i * tile, (i + 1) * tile), slice(j * tile, (j + 1) * tile))
            out_ref[at] = own_ref[at] * own_mask[i, j].astype(jnp.float32)
    for i in range(n):
        for j in range(n):
            to = (slice(j * tile, (j + 1) * tile), slice(i * tile, (i + 1) * tile))
            stored = in_mask[i, j] > 0

            @pl.when(jnp.logical_and(stored, slot < FIXED))
            def _():
                out_ref[to] += fixed_ref[slot].T

            @pl.when(jnp.logical_and(stored, slot >= FIXED))
            def _():
                out_ref[to] += extra_ref[slot - FIXED].T

            slot = slot + stored.astype(jnp.int32)
    back_ref[...] = product(split(out_ref[...].T), split(vec_ref[...]))


def base_kernel(vec_ref, diag_ref, grp_ref, grp_in_ref, vec_grp_ref, base_ref, sym_ref, across_ref):
    raw = diag_ref[...]
    row = lax.broadcasted_iota(jnp.int32, raw.shape, 0)
    col = lax.broadcasted_iota(jnp.int32, raw.shape, 1)
    sym = 0.5 * (raw + raw.T) - jnp.where(row == col, jnp.float32(CENTER), jnp.float32(0))
    across = grp_ref[...] + grp_in_ref[...].T
    sym_ref[...] = sym
    across_ref[...] = across
    base_ref[...] = product(split(sym), split(vec_ref[...])) + product(split(across), split(vec_grp_ref[...]))


def first_kernel(base_ref, pair_ref, vec_in_ref, first_ref, back_ref):
    pair = pair_ref[...]
    first = (base_ref[...] + product(split(pair), split(vec_in_ref[...]))) / HALF_SPAN
    first_ref[...] = first
    back_ref[...] = product(split(pair.T), split(first))


def near_kernel(sym_ref, across_ref, first_ref, *refs):
    *first_grp_refs, near_ref = refs
    first_grp = jnp.concatenate([ref[...] for ref in first_grp_refs], axis=0)
    near_ref[...] = product(split(sym_ref[...]), split(first_ref[...])) + product(
        split(across_ref[...]), split(first_grp)
    )


def far_kernel(pair_ref, base_in_ref, back_ref, far_ref):
    first = (base_in_ref[...] + back_ref[...]) / HALF_SPAN
    far_ref[...] = product(split(pair_ref[...]), split(first))


def local_call(kernel, ins, out_shape):
    spaces = [pl.BlockSpec(memory_space=pltpu.SMEM if x.dtype == jnp.int32 else pltpu.VMEM) for x in ins]
    many = isinstance(out_shape, tuple)
    vmem = pl.BlockSpec(memory_space=pltpu.VMEM)
    return pl.pallas_call(
        kernel,
        out_shape=out_shape,
        in_specs=spaces,
        out_specs=(vmem,) * len(out_shape) if many else vmem,
        compiler_params=pltpu.CompilerParams(vmem_limit_bytes=24 * 1024 * 1024),
        cost_estimate=pl.CostEstimate(flops=COST, bytes_accessed=COST, transcendentals=0),
    )(*ins)


def body(vectors, diag_block, slab_tiles, slab_mask, grp_tiles, grp_mask):
    rows, n_tile = slab_tiles.shape[0], slab_mask.shape[0]
    tile = rows // n_tile
    slots = n_tile * n_tile
    n_slab, n_grp = lax.axis_size("slab"), lax.axis_size("grp")
    half = n_slab // 2
    owner = owns(lax.axis_index("slab"), half)
    to_owner = [(i, i ^ half) for i in range(n_slab) if not owns(i, half)]
    from_owner = [(i, i ^ half) for i in range(n_slab) if owns(i, half)]
    grp_pairs = [(i, i ^ (n_grp // 2)) for i in range(n_grp)]
    f32 = jnp.float32
    square = jax.ShapeDtypeStruct((rows, rows), f32)
    block = jax.ShapeDtypeStruct(vectors.shape, f32)

    vecs_grp = lax.ppermute(vectors, "grp", grp_pairs)
    vecs_in = lax.ppermute(vectors, "slab", to_owner)
    mask_in = lax.ppermute(slab_mask, "slab", to_owner)

    fixed, extra, grp_block = local_call(
        functools.partial(pack_kernel, tile),
        (slab_mask, grp_mask, slab_tiles, grp_tiles),
        (
            jax.ShapeDtypeStruct((FIXED, tile, tile), f32),
            jax.ShapeDtypeStruct((slots - FIXED, tile, tile), f32),
            square,
        ),
    )
    grp_in = lax.ppermute(grp_block, "grp", grp_pairs)
    fixed_in = lax.ppermute(fixed, "slab", to_owner)

    sizes = (0, 1, 2, 3, 4, 6, slots - FIXED)

    def send(k):
        def branch(tiles):
            if k == 0:
                return jnp.zeros_like(tiles)
            got = lax.ppermute(tiles[:k], "slab", to_owner)
            return jnp.concatenate([got, jnp.zeros((tiles.shape[0] - k, tile, tile), f32)], axis=0)

        return branch

    over = jnp.sum(jnp.where(owner, mask_in, slab_mask)) - FIXED
    which = sum((over > k).astype(jnp.int32) for k in sizes[:-1])
    extra_in = lax.switch(which, [send(k) for k in sizes], extra)

    base, sym, across = local_call(
        base_kernel, (vectors, diag_block, grp_block, grp_in, vecs_grp), (block, square, square)
    )
    base_in = lax.ppermute(base, "slab", to_owner)

    base, fixed_in, extra_in = lax.optimization_barrier((base, fixed_in, extra_in))
    pair, back = local_call(
        functools.partial(pair_kernel, tile),
        (slab_mask, mask_in, slab_tiles, fixed_in, extra_in, vectors),
        (square, block),
    )
    back_in = jnp.concatenate(
        [lax.ppermute(x, "slab", from_owner) for x in jnp.split(back, BACK_CUTS, axis=0)], axis=0
    )
    first_own, back2 = local_call(first_kernel, (base, pair, vecs_in), (block, block))
    back2_in = lax.ppermute(back2, "slab", from_owner)

    first = jnp.where(owner, first_own, (base + back_in) / HALF_SPAN)
    first_grp = [lax.ppermute(x, "grp", grp_pairs) for x in jnp.split(first, GRP_CUTS, axis=0)]
    far = local_call(far_kernel, (pair, base_in, back), block)
    near = local_call(near_kernel, (sym, across, first, *first_grp), block)
    total = near + jnp.where(owner, far, back2_in)
    return 2.0 * total / HALF_SPAN - vectors


def solution(mesh):
    spec = P(("grp", "slab"), None)
    return jax.shard_map(body, mesh=mesh, in_specs=(spec,) * 6, out_specs=spec, check_vma=False)
```

time: 169 us -> 165 us (0.976)
  the two profiles are of different devices: /device:TPU:202 before, /device:TPU:218 now
where the time goes in v2:
time: 165 us; the launch traced here: 164 us
  waiting for transfers between devices  81.7 us (50%)
  starting transfers between devices  64.8 us (39%)
  Pallas kernels  10.7 us (6%)
  local copies, waits for them, and re-layouts  4.66 us (3%)
  other arithmetic  1.69 us (1%)
    ppermute x1, waiting for transfers between devices, body(): mask_in = lax.ppermute(slab_mask, 'slab', to_owner)  45.2 us
    ppermute x2, starting transfers between devices, body(): lax.ppermute(x, 'grp', grp_pairs)  37.1 us
    ppermute x1, waiting for transfers between devices, body(): lax.ppermute(x, 'slab', from_owner)  29.3 us
    ppermute x1, starting transfers between devices, body(): back2_in = lax.ppermute(back2, 'slab', from_owner)  13.3 us
    pallas_call x6, Pallas kernels, local_call(): pl.pallas_call(kernel, out_shape=out_shape, in_specs=spaces, out_specs=(v...  10.7 us
    ppermute x2, waiting for transfers between devices, body(): lax.ppermute(x, 'grp', grp_pairs)  7.2 us
    ppermute x1, starting transfers between devices, body(): grp_in = lax.ppermute(grp_block, 'grp', grp_pairs)  3.99 us
    unnamed x12, local copies, waits for them, and re-layouts  3.72 us
  transfers between devices with their start and end apart: 10, of which 4 were waited for; matrix products, arithmetic and copies ran while one was open for 1% of the time, Pallas kernels for 5%

profile of v2, /device:TPU:218, one launch (start us, length us, event | category | flops | bytes accessed | tf_op | source)
XLA Modules:
  0.0 164.4 jit_solution(12652018922002865567)
XLA Ops:
  0.0 1.3 copy-done.1
  1.3 1.2 copy-done.3
  3.2 2.0 %shard_map.64 = (f32[6,128,128]{2,1,0:T(8,128)}, f32[10,128,128]{2,1,0:T(8,128)}, f32[512,512]{1,0:T(8,128)S(1)}) custom-call(s32[4,4]{1,0:T(4,128)} %own_mask.1, s32[4,4]{1,0:T(4,128)S(1)} %copy-done.5, f32[512,512]{1,0:T(8,128)S(1)} %copy-done.1, f32[512,512]{1,0:T(8,128)S(1)} %copy-done.3), custom_call_target="tpu_custom_call" | custom-call | flops 1000 | bytes 1000 | tf_op jit(solution)/shard_map/pallas_call | solution.py:113
  5.2 4.0 %collective-permute-start.6 = (f32[512,512]{1,0:T(8,128)S(1)}, f32[512,512]{1,0:T(8,128)}, u32[]{:S(2)}, u32[]{:S(2)}) collective-permute-start(f32[512,512]{1,0:T(8,128)S(1)} %get-tuple-element.32.grp_ref), channel_id=1, source_target_pairs={{0,256},{64,320},{128,384},{192,448},{256,0},{320,64},{384,128},{4... | collective-permute-start | bytes 3145736 | tf_op jit(solution)/shard_map/ppermute | solution.py:150
  9.2 3.3 %collective-permute-start.7 = (f32[512,256]{1,0:T(8,128)S(1)}, f32[512,256]{1,0:T(8,128)}, u32[]{:S(2)}, u32[]{:S(2)}) collective-permute-start(f32[512,256]{1,0:T(8,128)S(1)} %copy-done), channel_id=1, source_target_pairs={{0,256},{64,320},{128,384},{192,448},{256,0},{320,64},{384,128},{4... | collective-permute-start | bytes 1572872 | tf_op jit(solution)/shard_map/ppermute | solution.py:137
  12.6 1.3 collective-permute-start.8
  13.9 1.3 collective-permute-start.9
  15.2 1.3 collective-permute-start.10
  16.5 45.2 %collective-permute-done.9.in_mask = s32[4,4]{1,0:T(4,128)S(1)} collective-permute-done((s32[4,4]{1,0:T(4,128)}, s32[4,4]{1,0:T(4,128)S(1)}, u32[]{:S(2)}, u32[]{:S(2)}) %collective-permute-start.9) | collective-permute-done | bytes 96 | tf_op jit(solution)/shard_map/ppermute | solution.py:139
  63.0 0.9 conditional.1
  63.1 0.9 broadcast.11
  64.5 2.7 %shard_map.65 = (f32[512,256]{1,0:T(8,128)S(1)}, f32[512,512]{1,0:T(8,128)S(1)}, f32[512,512]{1,0:T(8,128)S(1)}) custom-call(f32[512,256]{1,0:T(8,128)S(1)} %copy-done, f32[512,512]{1,0:T(8,128)S(1)} %copy-done.4, f32[512,512]{1,0:T(8,128)S(1)} %get-tuple-element.32.grp_ref, f32[512,512]{1,0:T(8,128)} %collective-permute-done.6.grp_in_ref, ...), custom_call_target="tpu_custom_call" | custom-call | flops 1000 | bytes 1000 | tf_op jit(solution)/shard_map/pallas_call | solution.py:113
  67.2 2.5 %shard_map.66 = (f32[512,512]{1,0:T(8,128)S(1)}, f32[512,256]{1,0:T(8,128)S(1)}) custom-call(s32[4,4]{1,0:T(4,128)} %own_mask.1, s32[4,4]{1,0:T(4,128)S(1)} %collective-permute-done.9.in_mask, f32[512,512]{1,0:T(8,128)S(1)} %copy-done.2, f32[6,128,128]{2,1,0:T(8,128)S(1)} %collective-permute-done.8.fixed_ref, f32[10,128,128]{2,1,0:T(8,128)} %get-tuple-element.47.extra_ref, ...), custom_call_target="tpu_custom_call" | custom-call | flops 1000 | bytes 1000 | tf_op jit(solution)/shard_map/pallas_call | solution.py:113
  69.7 1.8 %collective-permute-start.11 = (f32[512,256]{1,0:T(8,128)S(1)}, f32[512,256]{1,0:T(8,128)S(1)}, u32[]{:S(2)}, u32[]{:S(2)}) collective-permute-start(f32[512,256]{1,0:T(8,128)S(1)} %get-tuple-element.43.back_ref), channel_id=1, source_target_pairs={{0,32},{2,34},{4,36},{6,38},{8,40},{10,42},{12,44},{14,46},{16,48}... | collective-permute-start | bytes 1572872 | tf_op jit(solution)/shard_map/ppermute | solution.py:180
  71.5 1.3 collective-permute-start.14
  72.8 1.8 %shard_map.67 = (f32[512,256]{1,0:T(8,128)S(1)}, f32[512,256]{1,0:T(8,128)S(1)}) custom-call(f32[512,256]{1,0:T(8,128)S(1)} %get-tuple-element.38.base_ref, f32[512,512]{1,0:T(8,128)S(1)} %get-tuple-element.41.pair_ref, f32[512,256]{1,0:T(8,128)S(1)} %collective-permute-done.10.vec_in_ref), custom_call_target="tpu_custom_call" | custom-call | flops 1000 | bytes 1000 | tf_op jit(solution)/shard_map/pallas_call | solution.py:113
  74.7 13.3 %collective-permute-start.15 = (f32[512,256]{1,0:T(8,128)S(1)}, f32[512,256]{1,0:T(8,128)S(1)}, u32[]{:S(2)}, u32[]{:S(2)}) collective-permute-start(f32[512,256]{1,0:T(8,128)S(1)} %get-tuple-element.44), channel_id=1, source_target_pairs={{0,32},{2,34},{4,36},{6,38},{8,40},{10,42},{12,44},{14,46},{16,48}... | collective-permute-start | bytes 1572872 | tf_op jit(solution)/shard_map/ppermute | solution.py:183
  88.0 29.3 %collective-permute-done.11 = f32[512,256]{1,0:T(8,128)S(1)} collective-permute-done((f32[512,256]{1,0:T(8,128)S(1)}, f32[512,256]{1,0:T(8,128)S(1)}, u32[]{:S(2)}, u32[]{:S(2)}) %collective-permute-start.11) | collective-permute-done | bytes 524320 | tf_op jit(solution)/shard_map/ppermute | solution.py:180
  117.4 35.2 %collective-permute-start.12 = (f32[256,256]{1,0:T(8,128)S(1)}, f32[256,256]{1,0:T(8,128)S(1)}, u32[]{:S(2)}, u32[]{:S(2)}) collective-permute-start(f32[256,256]{1,0:T(8,128)S(1)} %get-tuple-element.46), channel_id=1, source_target_pairs={{0,256},{64,320},{128,384},{192,448},{256,0},{320,64},{384,128},{4... | collective-permute-start | bytes 786440 | tf_op jit(solution)/shard_map/ppermute | solution.py:186
  152.6 1.9 %collective-permute-start.13 = (f32[256,256]{1,0:T(8,128)S(1)}, f32[256,256]{1,0:T(8,128)S(1)}, u32[]{:S(2)}, u32[]{:S(2)}) collective-permute-start(f32[256,256]{1,0:T(8,128)S(1)} %get-tuple-element.45), channel_id=1, source_target_pairs={{0,256},{64,320},{128,384},{192,448},{256,0},{320,64},{384,128},{4... | collective-permute-start | bytes 786440 | tf_op jit(solution)/shard_map/ppermute | solution.py:186
  155.2 1.8 %collective-permute-done.12.refs_0_ = f32[256,256]{1,0:T(8,128)S(1)} collective-permute-done((f32[256,256]{1,0:T(8,128)S(1)}, f32[256,256]{1,0:T(8,128)S(1)}, u32[]{:S(2)}, u32[]{:S(2)}) %collective-permute-start.12) | collective-permute-done | bytes 262176 | tf_op jit(solution)/shard_map/ppermute | solution.py:186
  156.9 5.4 %collective-permute-done.13.refs_1_ = f32[256,256]{1,0:T(8,128)S(1)} collective-permute-done((f32[256,256]{1,0:T(8,128)S(1)}, f32[256,256]{1,0:T(8,128)S(1)}, u32[]{:S(2)}, u32[]{:S(2)}) %collective-permute-start.13) | collective-permute-done | bytes 262176 | tf_op jit(solution)/shard_map/ppermute | solution.py:186
  162.4 1.0 shard_map.68
  163.4 0.9 multiply_subtract_fusion
  (20 shorter events, 2.6 us)
Async XLA Ops:
  0.0 9.2 %copy-start = (f32[512,256]{1,0:T(8,128)S(1)}, f32[512,256]{1,0:T(8,128)}, u32[]{:S(2)}) copy-start(f32[512,256]{1,0:T(8,128)} %vec_ref.3) | copy-start | bytes 1572868
  0.0 1.3 copy-start.1
  1.3 1.2 copy-start.3
  2.5 0.7 copy-start.5
  5.2 58.7 %collective-permute-start.6 = (f32[512,512]{1,0:T(8,128)S(1)}, f32[512,512]{1,0:T(8,128)}, u32[]{:S(2)}, u32[]{:S(2)}) collective-permute-start(f32[512,512]{1,0:T(8,128)S(1)} %get-tuple-element.32.grp_ref), channel_id=1, source_target_pairs={{0,256},{64,320},{128,384},{192,448},{256,0},{320,64},{384,128},{4... | collective-permute-start | bytes 3145736 | tf_op jit(solution)/shard_map/ppermute | solution.py:150
  9.2 54.7 %collective-permute-start.7 = (f32[512,256]{1,0:T(8,128)S(1)}, f32[512,256]{1,0:T(8,128)}, u32[]{:S(2)}, u32[]{:S(2)}) collective-permute-start(f32[512,256]{1,0:T(8,128)S(1)} %copy-done), channel_id=1, source_target_pairs={{0,256},{64,320},{128,384},{192,448},{256,0},{320,64},{384,128},{4... | collective-permute-start | bytes 1572872 | tf_op jit(solution)/shard_map/ppermute | solution.py:137
  12.6 54.6 %collective-permute-start.8 = (f32[6,128,128]{2,1,0:T(8,128)}, f32[6,128,128]{2,1,0:T(8,128)S(1)}, u32[]{:S(2)}, u32[]{:S(2)}) collective-permute-start(f32[6,128,128]{2,1,0:T(8,128)} %get-tuple-element.36), channel_id=1, source_target_pairs={{1,33},{3,35},{5,37},{7,39},{9,41},{11,43},{13,45},{15,47},{17,49}... | collective-permute-start | bytes 1179656 | tf_op jit(solution)/shard_map/ppermute | solution.py:151
  13.9 47.8 %collective-permute-start.9 = (s32[4,4]{1,0:T(4,128)}, s32[4,4]{1,0:T(4,128)S(1)}, u32[]{:S(2)}, u32[]{:S(2)}) collective-permute-start(s32[4,4]{1,0:T(4,128)} %own_mask.1), channel_id=1, source_target_pairs={{1,33},{3,35},{5,37},{7,39},{9,41},{11,43},{13,45},{15,47},{17,49}... | collective-permute-start | bytes 200 | tf_op jit(solution)/shard_map/ppermute | solution.py:139
  15.2 57.6 %collective-permute-start.10 = (f32[512,256]{1,0:T(8,128)S(1)}, f32[512,256]{1,0:T(8,128)S(1)}, u32[]{:S(2)}, u32[]{:S(2)}) collective-permute-start(f32[512,256]{1,0:T(8,128)S(1)} %copy-done), channel_id=1, source_target_pairs={{1,33},{3,35},{5,37},{7,39},{9,41},{11,43},{13,45},{15,47},{17,49}... | collective-permute-start | bytes 1572872 | tf_op jit(solution)/shard_map/ppermute | solution.py:138
  63.0 1.5 copy-start.4
  64.0 3.2 %copy-start.2 = (f32[512,512]{1,0:T(8,128)S(1)}, f32[512,512]{1,0:T(8,128)}, u32[]{:S(2)}) copy-start(f32[512,512]{1,0:T(8,128)} %own_ref.1) | copy-start | bytes 3145732
  69.7 47.6 %collective-permute-start.11 = (f32[512,256]{1,0:T(8,128)S(1)}, f32[512,256]{1,0:T(8,128)S(1)}, u32[]{:S(2)}, u32[]{:S(2)}) collective-permute-start(f32[512,256]{1,0:T(8,128)S(1)} %get-tuple-element.43.back_ref), channel_id=1, source_target_pairs={{0,32},{2,34},{4,36},{6,38},{8,40},{10,42},{12,44},{14,46},{16,48}... | collective-permute-start | bytes 1572872 | tf_op jit(solution)/shard_map/ppermute | solution.py:180
  71.5 83.0 %collective-permute-start.14 = (f32[512,256]{1,0:T(8,128)S(1)}, f32[512,256]{1,0:T(8,128)S(1)}, u32[]{:S(2)}, u32[]{:S(2)}) collective-permute-start(f32[512,256]{1,0:T(8,128)S(1)} %get-tuple-element.38.base_ref), channel_id=1, source_target_pairs={{1,33},{3,35},{5,37},{7,39},{9,41},{11,43},{13,45},{15,47},{17,49}... | collective-permute-start | bytes 1572872 | tf_op jit(solution)/shard_map/ppermute | solution.py:171
  74.7 88.7 %collective-permute-start.15 = (f32[512,256]{1,0:T(8,128)S(1)}, f32[512,256]{1,0:T(8,128)S(1)}, u32[]{:S(2)}, u32[]{:S(2)}) collective-permute-start(f32[512,256]{1,0:T(8,128)S(1)} %get-tuple-element.44), channel_id=1, source_target_pairs={{0,32},{2,34},{4,36},{6,38},{8,40},{10,42},{12,44},{14,46},{16,48}... | collective-permute-start | bytes 1572872 | tf_op jit(solution)/shard_map/ppermute | solution.py:183
  117.4 39.5 %collective-permute-start.12 = (f32[256,256]{1,0:T(8,128)S(1)}, f32[256,256]{1,0:T(8,128)S(1)}, u32[]{:S(2)}, u32[]{:S(2)}) collective-permute-start(f32[256,256]{1,0:T(8,128)S(1)} %get-tuple-element.46), channel_id=1, source_target_pairs={{0,256},{64,320},{128,384},{192,448},{256,0},{320,64},{384,128},{4... | collective-permute-start | bytes 786440 | tf_op jit(solution)/shard_map/ppermute | solution.py:186
  152.6 9.8 %collective-permute-start.13 = (f32[256,256]{1,0:T(8,128)S(1)}, f32[256,256]{1,0:T(8,128)S(1)}, u32[]{:S(2)}, u32[]{:S(2)}) collective-permute-start(f32[256,256]{1,0:T(8,128)S(1)} %get-tuple-element.45), channel_id=1, source_target_pairs={{0,256},{64,320},{128,384},{192,448},{256,0},{320,64},{384,128},{4... | collective-permute-start | bytes 786440 | tf_op jit(solution)/shard_map/ppermute | solution.py:186

commit v3 on v2

--- a/solution.py
+++ b/solution.py
@@ -9,7 +9,9 @@
 
 CENTER = 0.5
 HALF_SPAN = 5.0
-FIXED = 6
+PIECE = 2
+PIECES = 3
+FIXED = PIECE * PIECES
 COST = 1000
 GRP_CUTS = 2
 BACK_CUTS = 1
@@ -29,29 +31,30 @@
     return (slab < half) == (slab % 2 == 0)
 
 
-def pack_kernel(tile, slab_mask, grp_mask, slab_ref, grp_ref, fixed_ref, extra_ref, grp_out):
+def pack_kernel(tile, slab_mask, grp_mask, slab_ref, grp_ref, *out_refs):
+    *slot_refs, grp_out = out_refs
     n = slab_ref.shape[0] // tile
-    fixed_ref[...] = jnp.zeros_like(fixed_ref)
-    extra_ref[...] = jnp.zeros_like(extra_ref)
+    for ref in slot_refs:
+        ref[...] = jnp.zeros_like(ref)
     slot = jnp.int32(0)
     for i in range(n):
         for j in range(n):
             at = (slice(i * tile, (i + 1) * tile), slice(j * tile, (j + 1) * tile))
             grp_out[at] = grp_ref[at] * grp_mask[i, j].astype(jnp.float32)
-            stored = slab_mask[i, j] > 0
+            stored, first = slab_mask[i, j] > 0, 0
+            for ref in slot_refs:
+                inside = jnp.logical_and(slot >= first, slot < first + ref.shape[0])
 
-            @pl.when(jnp.logical_and(stored, slot < FIXED))
-            def _():
-                fixed_ref[slot] = slab_ref[at]
+                @pl.when(jnp.logical_and(stored, inside))
+                def _():
+                    ref[slot - first] = slab_ref[at]
 
-            @pl.when(jnp.logical_and(stored, slot >= FIXED))
-            def _():
-                extra_ref[slot - FIXED] = slab_ref[at]
-
+                first += ref.shape[0]
             slot = slot + stored.astype(jnp.int32)
 
 
-def pair_kernel(tile, own_mask, in_mask, own_ref, fixed_ref, extra_ref, vec_ref, out_ref, back_ref):
+def pair_kernel(tile, own_mask, in_mask, own_ref, vec_ref, *refs):
+    *slot_refs, out_ref, back_ref = refs
     n = own_ref.shape[0] // tile
     slot = jnp.int32(0)
     for i in range(n):
@@ -61,16 +64,15 @@
     for i in range(n):
         for j in range(n):
             to = (slice(j * tile, (j + 1) * tile), slice(i * tile, (i + 1) * tile))
-            stored = in_mask[i, j] > 0
+            stored, first = in_mask[i, j] > 0, 0
+            for ref in slot_refs:
+                inside = jnp.logical_and(slot >= first, slot < first + ref.shape[0])
 
-            @pl.when(jnp.logical_and(stored, slot < FIXED))
-            def _():
-                out_ref[to] += fixed_ref[slot].T
+                @pl.when(jnp.logical_and(stored, inside))
+                def _():
+                    out_ref[to] += ref[slot - first].T
 
-            @pl.when(jnp.logical_and(stored, slot >= FIXED))
-            def _():
-                out_ref[to] += extra_ref[slot - FIXED].T
-
+                first += ref.shape[0]
             slot = slot + stored.astype(jnp.int32)
     back_ref[...] = product(split(out_ref[...].T), split(vec_ref[...]))
 
@@ -138,19 +140,19 @@
     vecs_in = lax.ppermute(vectors, "slab", to_owner)
     mask_in = lax.ppermute(slab_mask, "slab", to_owner)
 
-    fixed, extra, grp_block = local_call(
+    *fixed, extra, grp_block = local_call(
         functools.partial(pack_kernel, tile),
         (slab_mask, grp_mask, slab_tiles, grp_tiles),
         (
-            jax.ShapeDtypeStruct((FIXED, tile, tile), f32),
+            *[jax.ShapeDtypeStruct((PIECE, tile, tile), f32)] * PIECES,
             jax.ShapeDtypeStruct((slots - FIXED, tile, tile), f32),
             square,
         ),
     )
     grp_in = lax.ppermute(grp_block, "grp", grp_pairs)
-    fixed_in = lax.ppermute(fixed, "slab", to_owner)
+    fixed_in = [lax.ppermute(x, "slab", to_owner) for x in fixed]
 
-    sizes = (0, 1, 2, 3, 4, 6, slots - FIXED)
+    sizes = (0, 1, 2, 3, 4, 5, 6, 8, slots - FIXED)
 
     def send(k):
         def branch(tiles):
@@ -173,7 +175,7 @@
     base, fixed_in, extra_in = lax.optimization_barrier((base, fixed_in, extra_in))
     pair, back = local_call(
         functools.partial(pair_kernel, tile),
-        (slab_mask, mask_in, slab_tiles, fixed_in, extra_in, vectors),
+        (slab_mask, mask_in, slab_tiles, vectors, *fixed_in, extra_in),
         (square, block),
     )
     back_in = jnp.concatenate(

time: 165 us -> 169 us (1.024)
  the two profiles are of different devices: /device:TPU:218 before, /device:TPU:121 now
where the time goes in v3:
time: 169 us; the launch traced here: 168 us
  waiting for transfers between devices  79.6 us (47%)
  starting transfers between devices  69.6 us (41%)
  Pallas kernels  10.5 us (6%)
  local copies, waits for them, and re-layouts  5.18 us (3%)
  other arithmetic  2.35 us (1%)
    ppermute x1, waiting for transfers between devices, body(): vecs_in = lax.ppermute(vectors, 'slab', to_owner)  41.5 us
    ppermute x3, waiting for transfers between devices, body(): fixed_in = [lax.ppermute(x, 'slab', to_owner) for x in fixed]  19.7 us
    ppermute x3, starting transfers between devices, body(): fixed_in = [lax.ppermute(x, 'slab', to_owner) for x in fixed]  15.2 us
    ppermute x1, starting transfers between devices, body(): base_in = lax.ppermute(base, 'slab', to_owner)  14 us
    ppermute x1, starting transfers between devices, body(): mask_in = lax.ppermute(slab_mask, 'slab', to_owner)  12.7 us
    pallas_call x6, Pallas kernels, local_call(): pl.pallas_call(kernel, out_shape=out_shape, in_specs=spaces, out_specs=(v...  10.5 us
    ppermute x1, starting transfers between devices, branch(): got = lax.ppermute(tiles[:k], 'slab', to_owner)  10.1 us
    ppermute x1, waiting for transfers between devices, branch(): got = lax.ppermute(tiles[:k], 'slab', to_owner)  9.6 us
  transfers between devices with their start and end apart: 13, of which 6 were waited for; matrix products, arithmetic and copies ran while one was open for 2% of the time, Pallas kernels for 5%

profile of v3, /device:TPU:121, one launch (start us, length us, event | category | flops | bytes accessed | tf_op | source)
XLA Modules:
  0.0 168.1 jit_solution(7328394739324769731)
XLA Ops:
  3.2 2.1 %shard_map.64 = (f32[2,128,128]{2,1,0:T(8,128)}, f32[2,128,128]{2,1,0:T(8,128)}, f32[2,128,128]{2,1,0:T(8,128)S(1)}, f32[10,128,128]{2,1,0:T(8,128)}, f32[512,512]{1,0:T(8,128)S(1)}) custom-call(s32[4,4]{1,0:T(4,128)} %own_mask.1, s32[4,4]{1,0:T(4,128)S(1)} %copy-done.5, f32[512,512]{1,0:T(8,128)S(1)} %copy-done.1, f32[512,512]{1,0:T(8,128)S(1)} %copy-done.3), custom_call_target="tpu_custom_call" | custom-call | flops 1000 | bytes 1000 | tf_op jit(solution)/shard_map/pallas_call | solution.py:115
  5.3 4.6 %collective-permute-start.8 = (f32[512,512]{1,0:T(8,128)S(1)}, f32[512,512]{1,0:T(8,128)}, u32[]{:S(2)}, u32[]{:S(2)}) collective-permute-start(f32[512,512]{1,0:T(8,128)S(1)} %get-tuple-element.40.grp_ref), channel_id=1, source_target_pairs={{0,256},{64,320},{128,384},{192,448},{256,0},{320,64},{384,128},{4... | collective-permute-start | bytes 3145736 | tf_op jit(solution)/shard_map/ppermute | solution.py:152
  10.0 2.2 %collective-permute-start.9 = (f32[512,256]{1,0:T(8,128)S(1)}, f32[512,256]{1,0:T(8,128)S(1)}, u32[]{:S(2)}, u32[]{:S(2)}) collective-permute-start(f32[512,256]{1,0:T(8,128)S(1)} %copy-done), channel_id=1, source_target_pairs={{0,256},{64,320},{128,384},{192,448},{256,0},{320,64},{384,128},{4... | collective-permute-start | bytes 1572872 | tf_op jit(solution)/shard_map/ppermute | solution.py:139
  12.1 12.7 %collective-permute-start.13 = (s32[4,4]{1,0:T(4,128)}, s32[4,4]{1,0:T(4,128)S(1)}, u32[]{:S(2)}, u32[]{:S(2)}) collective-permute-start(s32[4,4]{1,0:T(4,128)} %own_mask.1), channel_id=1, source_target_pairs={{1,33},{3,35},{5,37},{7,39},{9,41},{11,43},{13,45},{15,47},{17,49}... | collective-permute-start | bytes 200 | tf_op jit(solution)/shard_map/ppermute | solution.py:141
  24.9 1.3 collective-permute-start.10
  26.2 1.3 collective-permute-start.11
  27.5 1.3 select_reduce_fusion
  29.4 21.7 %conditional.1 = (f32[10,128,128]{2,1,0:T(8,128)}) conditional(s32[]{:T(128)} %clamp.3, () %tuple.33, f32[10,128,128]{2,1,0:T(8,128)} %get-tuple-element.47, f32[10,128,128]{2,1,0:T(8,128)} %get-tuple-element.47, f32[10,128,128]{2,1,0:T(8,128)} %get-tuple-element.47, f32[10,128,128]{2,1,0:T(8,128)} %get-tuple-element.47, ...), branch_computations={%region_1.2_spmd, %region_2.3_spmd, %region_3.4_spmd, %region_4.5_... | conditional | bytes 4325428 | solution.py:168
  30.5 10.1 %collective-permute-start.3 = (f32[4,128,128]{2,1,0:T(8,128)S(1)}, f32[4,128,128]{2,1,0:T(8,128)S(1)}, u32[]{:S(2)}, u32[]{:S(2)}) collective-permute-start(f32[4,128,128]{2,1,0:T(8,128)S(1)} %slice.17), channel_id=1, source_target_pairs={{1,33},{3,35},{5,37},{7,39},{9,41},{11,43},{13,45},{15,47},{17,49}... | collective-permute-start | bytes 786440 | tf_op jit(solution)/shard_map/cond/branch_4_fun/ppermute | solution.py:161
  40.7 9.6 %collective-permute-done.3 = f32[4,128,128]{2,1,0:T(8,128)S(1)} collective-permute-done((f32[4,128,128]{2,1,0:T(8,128)S(1)}, f32[4,128,128]{2,1,0:T(8,128)S(1)}, u32[]{:S(2)}, u32[]{:S(2)}) %collective-permute-start.3) | collective-permute-done | bytes 262176 | tf_op jit(solution)/shard_map/cond/branch_4_fun/ppermute | solution.py:161
  51.2 12.7 %collective-permute-start.12 = (f32[2,128,128]{2,1,0:T(8,128)S(1)}, f32[2,128,128]{2,1,0:T(8,128)S(1)}, u32[]{:S(2)}, u32[]{:S(2)}) collective-permute-start(f32[2,128,128]{2,1,0:T(8,128)S(1)} %get-tuple-element.46), channel_id=1, source_target_pairs={{1,33},{3,35},{5,37},{7,39},{9,41},{11,43},{13,45},{15,47},{17,49}... | collective-permute-start | bytes 393224 | tf_op jit(solution)/shard_map/ppermute | solution.py:153
  63.8 1.3 collective-permute-start.14
  65.2 2.6 %shard_map.65 = (f32[512,256]{1,0:T(8,128)S(1)}, f32[512,512]{1,0:T(8,128)S(1)}, f32[512,512]{1,0:T(8,128)S(1)}) custom-call(f32[512,256]{1,0:T(8,128)S(1)} %copy-done, f32[512,512]{1,0:T(8,128)S(1)} %copy-done.4, f32[512,512]{1,0:T(8,128)S(1)} %get-tuple-element.40.grp_ref, f32[512,512]{1,0:T(8,128)} %collective-permute-done.8.grp_in_ref, ...), custom_call_target="tpu_custom_call" | custom-call | flops 1000 | bytes 1000 | tf_op jit(solution)/shard_map/pallas_call | solution.py:115
  67.8 19.7 %collective-permute-done.12.refs_2_ = f32[2,128,128]{2,1,0:T(8,128)S(1)} collective-permute-done((f32[2,128,128]{2,1,0:T(8,128)S(1)}, f32[2,128,128]{2,1,0:T(8,128)S(1)}, u32[]{:S(2)}, u32[]{:S(2)}) %collective-permute-start.12) | collective-permute-done | bytes 131104 | tf_op jit(solution)/shard_map/ppermute | solution.py:153
  87.4 2.3 %shard_map.66 = (f32[512,512]{1,0:T(8,128)S(1)}, f32[512,256]{1,0:T(8,128)S(1)}) custom-call(s32[4,4]{1,0:T(4,128)} %own_mask.1, s32[4,4]{1,0:T(4,128)S(1)} %collective-permute-done.13.in_mask, f32[512,512]{1,0:T(8,128)S(1)} %copy-done.2, f32[512,256]{1,0:T(8,128)S(1)} %copy-done, f32[2,128,128]{2,1,0:T(8,128)S(1)} %collective-permute-done.10.refs_0_, ...), custom_call_target="tpu_custom_call" | custom-call | flops 1000 | bytes 1000 | tf_op jit(solution)/shard_map/pallas_call | solution.py:115
  89.8 1.3 collective-permute-start.15
  91.1 14.0 %collective-permute-start.18 = (f32[512,256]{1,0:T(8,128)S(1)}, f32[512,256]{1,0:T(8,128)S(1)}, u32[]{:S(2)}, u32[]{:S(2)}) collective-permute-start(f32[512,256]{1,0:T(8,128)S(1)} %get-tuple-element.48.base_ref), channel_id=1, source_target_pairs={{1,33},{3,35},{5,37},{7,39},{9,41},{11,43},{13,45},{15,47},{17,49}... | collective-permute-start | bytes 1572872 | tf_op jit(solution)/shard_map/ppermute | solution.py:173
  105.0 41.5 %collective-permute-done.14.vec_in_ref = f32[512,256]{1,0:T(8,128)S(1)} collective-permute-done((f32[512,256]{1,0:T(8,128)S(1)}, f32[512,256]{1,0:T(8,128)S(1)}, u32[]{:S(2)}, u32[]{:S(2)}) %collective-permute-start.14) | collective-permute-done | bytes 524320 | tf_op jit(solution)/shard_map/ppermute | solution.py:140
  146.6 1.8 %shard_map.67 = (f32[512,256]{1,0:T(8,128)S(1)}, f32[512,256]{1,0:T(8,128)S(1)}) custom-call(f32[512,256]{1,0:T(8,128)S(1)} %get-tuple-element.48.base_ref, f32[512,512]{1,0:T(8,128)S(1)} %get-tuple-element.53.pair_ref, f32[512,256]{1,0:T(8,128)S(1)} %collective-permute-done.14.vec_in_ref), custom_call_target="tpu_custom_call" | custom-call | flops 1000 | bytes 1000 | tf_op jit(solution)/shard_map/pallas_call | solution.py:115
  148.4 1.3 collective-permute-start.19
  149.9 1.9 %collective-permute-start.16 = (f32[256,256]{1,0:T(8,128)S(1)}, f32[256,256]{1,0:T(8,128)S(1)}, u32[]{:S(2)}, u32[]{:S(2)}) collective-permute-start(f32[256,256]{1,0:T(8,128)S(1)} %get-tuple-element.58), channel_id=1, source_target_pairs={{0,256},{64,320},{128,384},{192,448},{256,0},{320,64},{384,128},{4... | collective-permute-start | bytes 786440 | tf_op jit(solution)/shard_map/ppermute | solution.py:188
  151.8 4.9 %collective-permute-start.17 = (f32[256,256]{1,0:T(8,128)S(1)}, f32[256,256]{1,0:T(8,128)S(1)}, u32[]{:S(2)}, u32[]{:S(2)}) collective-permute-start(f32[256,256]{1,0:T(8,128)S(1)} %get-tuple-element.57), channel_id=1, source_target_pairs={{0,256},{64,320},{128,384},{192,448},{256,0},{320,64},{384,128},{4... | collective-permute-start | bytes 786440 | tf_op jit(solution)/shard_map/ppermute | solution.py:188
  158.5 2.8 %collective-permute-done.17.refs_1_ = f32[256,256]{1,0:T(8,128)S(1)} collective-permute-done((f32[256,256]{1,0:T(8,128)S(1)}, f32[256,256]{1,0:T(8,128)S(1)}, u32[]{:S(2)}, u32[]{:S(2)}) %collective-permute-start.17) | collective-permute-done | bytes 262176 | tf_op jit(solution)/shard_map/ppermute | solution.py:188
  162.3 4.9 %collective-permute-done.19 = f32[512,256]{1,0:T(8,128)S(1)} collective-permute-done((f32[512,256]{1,0:T(8,128)S(1)}, f32[512,256]{1,0:T(8,128)S(1)}, u32[]{:S(2)}, u32[]{:S(2)}) %collective-permute-start.19) | collective-permute-done | bytes 524320 | tf_op jit(solution)/shard_map/ppermute | solution.py:185
  (27 shorter events, 9.0 us)
Async XLA Ops:
  0.0 10.0 %copy-start = (f32[512,256]{1,0:T(8,128)S(1)}, f32[512,256]{1,0:T(8,128)}, u32[]{:S(2)}) copy-start(f32[512,256]{1,0:T(8,128)} %vec_ref.3) | copy-start | bytes 1572868
  0.0 1.3 copy-start.1
  1.3 1.2 copy-start.3
  2.5 0.7 copy-start.5
  5.3 59.8 %collective-permute-start.8 = (f32[512,512]{1,0:T(8,128)S(1)}, f32[512,512]{1,0:T(8,128)}, u32[]{:S(2)}, u32[]{:S(2)}) collective-permute-start(f32[512,512]{1,0:T(8,128)S(1)} %get-tuple-element.40.grp_ref), channel_id=1, source_target_pairs={{0,256},{64,320},{128,384},{192,448},{256,0},{320,64},{384,128},{4... | collective-permute-start | bytes 3145736 | tf_op jit(solution)/shard_map/ppermute | solution.py:152
  10.0 53.9 %collective-permute-start.9 = (f32[512,256]{1,0:T(8,128)S(1)}, f32[512,256]{1,0:T(8,128)S(1)}, u32[]{:S(2)}, u32[]{:S(2)}) collective-permute-start(f32[512,256]{1,0:T(8,128)S(1)} %copy-done), channel_id=1, source_target_pairs={{0,256},{64,320},{128,384},{192,448},{256,0},{320,64},{384,128},{4... | collective-permute-start | bytes 1572872 | tf_op jit(solution)/shard_map/ppermute | solution.py:139
  12.1 15.4 %collective-permute-start.13 = (s32[4,4]{1,0:T(4,128)}, s32[4,4]{1,0:T(4,128)S(1)}, u32[]{:S(2)}, u32[]{:S(2)}) collective-permute-start(s32[4,4]{1,0:T(4,128)} %own_mask.1), channel_id=1, source_target_pairs={{1,33},{3,35},{5,37},{7,39},{9,41},{11,43},{13,45},{15,47},{17,49}... | collective-permute-start | bytes 200 | tf_op jit(solution)/shard_map/ppermute | solution.py:141
  24.9 42.9 %collective-permute-start.10 = (f32[2,128,128]{2,1,0:T(8,128)}, f32[2,128,128]{2,1,0:T(8,128)S(1)}, u32[]{:S(2)}, u32[]{:S(2)}) collective-permute-start(f32[2,128,128]{2,1,0:T(8,128)} %get-tuple-element.44), channel_id=1, source_target_pairs={{1,33},{3,35},{5,37},{7,39},{9,41},{11,43},{13,45},{15,47},{17,49}... | collective-permute-start | bytes 393224 | tf_op jit(solution)/shard_map/ppermute | solution.py:153
  26.2 41.6 %collective-permute-start.11 = (f32[2,128,128]{2,1,0:T(8,128)}, f32[2,128,128]{2,1,0:T(8,128)S(1)}, u32[]{:S(2)}, u32[]{:S(2)}) collective-permute-start(f32[2,128,128]{2,1,0:T(8,128)} %get-tuple-element.45), channel_id=1, source_target_pairs={{1,33},{3,35},{5,37},{7,39},{9,41},{11,43},{13,45},{15,47},{17,49}... | collective-permute-start | bytes 393224 | tf_op jit(solution)/shard_map/ppermute | solution.py:153
  29.4 35.8 %copy-start.4 = (f32[512,512]{1,0:T(8,128)S(1)}, f32[512,512]{1,0:T(8,128)}, u32[]{:S(2)}) copy-start(f32[512,512]{1,0:T(8,128)} %diag_ref.1) | copy-start | bytes 3145732
  30.5 19.8 %collective-permute-start.3 = (f32[4,128,128]{2,1,0:T(8,128)S(1)}, f32[4,128,128]{2,1,0:T(8,128)S(1)}, u32[]{:S(2)}, u32[]{:S(2)}) collective-permute-start(f32[4,128,128]{2,1,0:T(8,128)S(1)} %slice.17), channel_id=1, source_target_pairs={{1,33},{3,35},{5,37},{7,39},{9,41},{11,43},{13,45},{15,47},{17,49}... | collective-permute-start | bytes 786440 | tf_op jit(solution)/shard_map/cond/branch_4_fun/ppermute | solution.py:161
  51.2 36.3 %copy-start.2 = (f32[512,512]{1,0:T(8,128)S(1)}, f32[512,512]{1,0:T(8,128)}, u32[]{:S(2)}) copy-start(f32[512,512]{1,0:T(8,128)} %own_ref.1) | copy-start | bytes 3145732
  51.2 36.3 %collective-permute-start.12 = (f32[2,128,128]{2,1,0:T(8,128)S(1)}, f32[2,128,128]{2,1,0:T(8,128)S(1)}, u32[]{:S(2)}, u32[]{:S(2)}) collective-permute-start(f32[2,128,128]{2,1,0:T(8,128)S(1)} %get-tuple-element.46), channel_id=1, source_target_pairs={{1,33},{3,35},{5,37},{7,39},{9,41},{11,43},{13,45},{15,47},{17,49}... | collective-permute-start | bytes 393224 | tf_op jit(solution)/shard_map/ppermute | solution.py:153
  63.8 82.8 %collective-permute-start.14 = (f32[512,256]{1,0:T(8,128)S(1)}, f32[512,256]{1,0:T(8,128)S(1)}, u32[]{:S(2)}, u32[]{:S(2)}) collective-permute-start(f32[512,256]{1,0:T(8,128)S(1)} %copy-done), channel_id=1, source_target_pairs={{1,33},{3,35},{5,37},{7,39},{9,41},{11,43},{13,45},{15,47},{17,49}... | collective-permute-start | bytes 1572872 | tf_op jit(solution)/shard_map/ppermute | solution.py:140
  89.8 60.0 %collective-permute-start.15 = (f32[512,256]{1,0:T(8,128)S(1)}, f32[512,256]{1,0:T(8,128)S(1)}, u32[]{:S(2)}, u32[]{:S(2)}) collective-permute-start(f32[512,256]{1,0:T(8,128)S(1)} %get-tuple-element.55.back_ref), channel_id=1, source_target_pairs={{0,32},{2,34},{4,36},{6,38},{8,40},{10,42},{12,44},{14,46},{16,48}... | collective-permute-start | bytes 1572872 | tf_op jit(solution)/shard_map/ppermute | solution.py:182
  91.1 65.6 %collective-permute-start.18 = (f32[512,256]{1,0:T(8,128)S(1)}, f32[512,256]{1,0:T(8,128)S(1)}, u32[]{:S(2)}, u32[]{:S(2)}) collective-permute-start(f32[512,256]{1,0:T(8,128)S(1)} %get-tuple-element.48.base_ref), channel_id=1, source_target_pairs={{1,33},{3,35},{5,37},{7,39},{9,41},{11,43},{13,45},{15,47},{17,49}... | collective-permute-start | bytes 1572872 | tf_op jit(solution)/shard_map/ppermute | solution.py:173
  148.4 18.8 %collective-permute-start.19 = (f32[512,256]{1,0:T(8,128)S(1)}, f32[512,256]{1,0:T(8,128)S(1)}, u32[]{:S(2)}, u32[]{:S(2)}) collective-permute-start(f32[512,256]{1,0:T(8,128)S(1)} %get-tuple-element.56), channel_id=1, source_target_pairs={{0,32},{2,34},{4,36},{6,38},{8,40},{10,42},{12,44},{14,46},{16,48}... | collective-permute-start | bytes 1572872 | tf_op jit(solution)/shard_map/ppermute | solution.py:185
  149.9 8.6 %collective-permute-start.16 = (f32[256,256]{1,0:T(8,128)S(1)}, f32[256,256]{1,0:T(8,128)S(1)}, u32[]{:S(2)}, u32[]{:S(2)}) collective-permute-start(f32[256,256]{1,0:T(8,128)S(1)} %get-tuple-element.58), channel_id=1, source_target_pairs={{0,256},{64,320},{128,384},{192,448},{256,0},{320,64},{384,128},{4... | collective-permute-start | bytes 786440 | tf_op jit(solution)/shard_map/ppermute | solution.py:188
  151.8 9.5 %collective-permute-start.17 = (f32[256,256]{1,0:T(8,128)S(1)}, f32[256,256]{1,0:T(8,128)S(1)}, u32[]{:S(2)}, u32[]{:S(2)}) collective-permute-start(f32[256,256]{1,0:T(8,128)S(1)} %get-tuple-element.57), channel_id=1, source_target_pairs={{0,256},{64,320},{128,384},{192,448},{256,0},{320,64},{384,128},{4... | collective-permute-start | bytes 786440 | tf_op jit(solution)/shard_map/ppermute | solution.py:188

commit v4 on v3

--- a/solution.py
+++ b/solution.py
@@ -9,8 +9,8 @@
 
 CENTER = 0.5
 HALF_SPAN = 5.0
-PIECE = 2
-PIECES = 3
+PIECE = 6
+PIECES = 1
 FIXED = PIECE * PIECES
 COST = 1000
 GRP_CUTS = 2
@@ -77,7 +77,10 @@
     back_ref[...] = product(split(out_ref[...].T), split(vec_ref[...]))
 
 
-def base_kernel(vec_ref, diag_ref, grp_ref, grp_in_ref, vec_grp_ref, base_ref, sym_ref, across_ref):
+def base_kernel(
+    vec_ref, diag_ref, grp_ref, grp_in_ref, vec_grp_ref, vec_in_ref, base_ref, sym_ref, across_ref, high_ref, low_ref
+):
+    high_ref[...], low_ref[...] = split(vec_in_ref[...])
     raw = diag_ref[...]
     row = lax.broadcasted_iota(jnp.int32, raw.shape, 0)
     col = lax.broadcasted_iota(jnp.int32, raw.shape, 1)
@@ -88,11 +91,12 @@
     base_ref[...] = product(split(sym), split(vec_ref[...])) + product(split(across), split(vec_grp_ref[...]))
 
 
-def first_kernel(base_ref, pair_ref, vec_in_ref, first_ref, back_ref):
-    pair = pair_ref[...]
-    first = (base_ref[...] + product(split(pair), split(vec_in_ref[...]))) / HALF_SPAN
+def first_kernel(base_ref, pair_ref, high_ref, low_ref, base_in_ref, back_ref, first_ref, back2_ref, far_ref):
+    pair = split(pair_ref[...])
+    first = (base_ref[...] + product(pair, (high_ref[...], low_ref[...]))) / HALF_SPAN
     first_ref[...] = first
-    back_ref[...] = product(split(pair.T), split(first))
+    back2_ref[...] = product(split(pair_ref[...].T), split(first))
+    far_ref[...] = product(pair, split((base_in_ref[...] + back_ref[...]) / HALF_SPAN))
 
 
 def near_kernel(sym_ref, across_ref, first_ref, *refs):
@@ -101,11 +105,6 @@
     near_ref[...] = product(split(sym_ref[...]), split(first_ref[...])) + product(
         split(across_ref[...]), split(first_grp)
     )
-
-
-def far_kernel(pair_ref, base_in_ref, back_ref, far_ref):
-    first = (base_in_ref[...] + back_ref[...]) / HALF_SPAN
-    far_ref[...] = product(split(pair_ref[...]), split(first))
 
 
 def local_call(kernel, ins, out_shape):
@@ -152,7 +151,15 @@
     grp_in = lax.ppermute(grp_block, "grp", grp_pairs)
     fixed_in = [lax.ppermute(x, "slab", to_owner) for x in fixed]
 
-    sizes = (0, 1, 2, 3, 4, 5, 6, 8, slots - FIXED)
+    half_block = jax.ShapeDtypeStruct(vectors.shape, jnp.bfloat16)
+    base, sym, across, high, low = local_call(
+        base_kernel,
+        (vectors, diag_block, grp_block, grp_in, vecs_grp, vecs_in),
+        (block, square, square, half_block, half_block),
+    )
+    base_in = lax.ppermute(base, "slab", to_owner)
+
+    sizes = (0, 1, 2, 3, 4, 6, slots - FIXED)
 
     def send(k):
         def branch(tiles):
@@ -163,30 +170,24 @@
 
         return branch
 
+    extra, mask_in, base = lax.optimization_barrier((extra, mask_in, base))
     over = jnp.sum(jnp.where(owner, mask_in, slab_mask)) - FIXED
     which = sum((over > k).astype(jnp.int32) for k in sizes[:-1])
     extra_in = lax.switch(which, [send(k) for k in sizes], extra)
 
-    base, sym, across = local_call(
-        base_kernel, (vectors, diag_block, grp_block, grp_in, vecs_grp), (block, square, square)
-    )
-    base_in = lax.ppermute(base, "slab", to_owner)
-
-    base, fixed_in, extra_in = lax.optimization_barrier((base, fixed_in, extra_in))
     pair, back = local_call(
         functools.partial(pair_kernel, tile),
         (slab_mask, mask_in, slab_tiles, vectors, *fixed_in, extra_in),
         (square, block),
     )
-    back_in = jnp.concatenate(
-        [lax.ppermute(x, "slab", from_owner) for x in jnp.split(back, BACK_CUTS, axis=0)], axis=0
+    back_in = lax.ppermute(back, "slab", from_owner)
+    first_own, back2, far = local_call(
+        first_kernel, (base, pair, high, low, base_in, back), (block, block, block)
     )
-    first_own, back2 = local_call(first_kernel, (base, pair, vecs_in), (block, block))
     back2_in = lax.ppermute(back2, "slab", from_owner)
 
     first = jnp.where(owner, first_own, (base + back_in) / HALF_SPAN)
     first_grp = [lax.ppermute(x, "grp", grp_pairs) for x in jnp.split(first, GRP_CUTS, axis=0)]
-    far = local_call(far_kernel, (pair, base_in, back), block)
     near = local_call(near_kernel, (sym, across, first, *first_grp), block)
     total = near + jnp.where(owner, far, back2_in)
     return 2.0 * total / HALF_SPAN - vectors

time: 169 us -> 183 us (1.083)
  the two profiles are of different devices: /device:TPU:121 before, /device:TPU:4 now
where the time goes in v4:
time: 183 us
  starting transfers between devices  89.8 us (49%)
  waiting for transfers between devices  65.4 us (36%)
  local copies, waits for them, and re-layouts  14.5 us (8%)
  Pallas kernels  10.4 us (6%)
    ppermute x2, starting transfers between devices, body(): lax.ppermute(x, 'grp', grp_pairs)  56.8 us
    ppermute x1, waiting for transfers between devices, body(): back_in = lax.ppermute(back, 'slab', from_owner)  31.4 us
    ppermute x1, waiting for transfers between devices, body(): vecs_grp = lax.ppermute(vectors, 'grp', grp_pairs)  24.9 us
    ppermute x1, starting transfers between devices, body(): back_in = lax.ppermute(back, 'slab', from_owner)  16.9 us
    unnamed x36, local copies, waits for them, and re-layouts  13.5 us
    pallas_call x5, Pallas kernels, local_call(): pl.pallas_call(kernel, out_shape=out_shape, in_specs=spaces, out_specs=(v...  10.4 us
    ppermute x2, waiting for transfers between devices, body(): lax.ppermute(x, 'grp', grp_pairs)  7.84 us
    ppermute x1, starting transfers between devices, body(): grp_in = lax.ppermute(grp_block, 'grp', grp_pairs)  7.76 us
  transfers between devices with their start and end apart: 10, of which 5 were waited for; matrix products, arithmetic and copies ran while one was open for 1% of the time, Pallas kernels for 5%

profile of v4, /device:TPU:4, one launch (start us, length us, event | category | flops | bytes accessed | tf_op | source)
XLA Modules:
  0.0 182.6 jit_solution(16984972051241580800)
XLA Ops:
  0.0 1.3 copy-done.1
  1.3 1.2 copy-done.5
  3.2 2.0 %shard_map.64 = (f32[6,128,128]{2,1,0:T(8,128)}, f32[10,128,128]{2,1,0:T(8,128)}, f32[512,512]{1,0:T(8,128)S(1)}) custom-call(s32[4,4]{1,0:T(4,128)} %own_mask.1, s32[4,4]{1,0:T(4,128)S(1)} %copy-done.17, f32[512,512]{1,0:T(8,128)S(1)} %copy-done.1, f32[512,512]{1,0:T(8,128)S(1)} %copy-done.5), custom_call_target="tpu_custom_call" | custom-call | flops 1000 | bytes 1000 | tf_op jit(solution)/shard_map/pallas_call | solution.py:114
  5.2 7.8 %collective-permute-start.6 = (f32[512,512]{1,0:T(8,128)S(1)}, f32[512,512]{1,0:T(8,128)S(1)}, u32[]{:S(2)}, u32[]{:S(2)}) collective-permute-start(f32[512,512]{1,0:T(8,128)S(1)} %get-tuple-element.35.grp_ref), channel_id=1, source_target_pairs={{0,256},{64,320},{128,384},{192,448},{256,0},{320,64},{384,128},{4... | collective-permute-start | bytes 3145736 | tf_op jit(solution)/shard_map/ppermute | solution.py:151
  13.9 1.9 %collective-permute-start.7 = (f32[512,256]{1,0:T(8,128)S(1)}, f32[512,256]{1,0:T(8,128)S(1)}, u32[]{:S(2)}, u32[]{:S(2)}) collective-permute-start(f32[512,256]{1,0:T(8,128)S(1)} %copy-done), channel_id=1, source_target_pairs={{0,256},{64,320},{128,384},{192,448},{256,0},{320,64},{384,128},{4... | collective-permute-start | bytes 1572872 | tf_op jit(solution)/shard_map/ppermute | solution.py:138
  15.9 1.3 collective-permute-start.8
  17.2 1.3 collective-permute-start.10
  18.5 1.3 collective-permute-start.9
  19.8 24.9 %collective-permute-done.7.vec_grp_ref = f32[512,256]{1,0:T(8,128)S(1)} collective-permute-done((f32[512,256]{1,0:T(8,128)S(1)}, f32[512,256]{1,0:T(8,128)S(1)}, u32[]{:S(2)}, u32[]{:S(2)}) %collective-permute-start.7) | collective-permute-done | bytes 524320 | tf_op jit(solution)/shard_map/ppermute | solution.py:138
  46.5 1.2 copy-done.6
  47.7 1.2 copy-done.8
  48.9 1.2 copy-done.10
  51.2 2.4 %shard_map.65 = (f32[512,256]{1,0:T(8,128)S(1)}, f32[512,512]{1,0:T(8,128)S(1)}, f32[512,512]{1,0:T(8,128)S(1)}, bf16[512,256]{1,0:T(8,128)(2,1)S(1)}, bf16[512,256]{1,0:T(8,128)(2,1)S(1)}) custom-call(f32[512,256]{1,0:T(8,128)S(1)} %copy-done, f32[512,512]{1,0:T(8,128)S(1)} %copy-done.6, f32[512,512]{1,0:T(8,128)S(1)} %copy-done.8, ...), custom_call_target="tpu_custom_call" | custom-call | flops 1000 | bytes 1000 | tf_op jit(solution)/shard_map/pallas_call | solution.py:114
  57.2 1.3 collective-permute-start.11
  60.0 2.5 %shard_map.66 = (f32[512,512]{1,0:T(8,128)S(1)}, f32[512,256]{1,0:T(8,128)S(1)}) custom-call(s32[4,4]{1,0:T(4,128)} %own_mask.1, s32[4,4]{1,0:T(4,128)S(1)} %collective-permute-done.9.in_mask, f32[512,512]{1,0:T(8,128)S(1)} %copy-done.2, f32[512,256]{1,0:T(8,128)S(1)} %copy-done, f32[6,128,128]{2,1,0:T(8,128)S(1)} %collective-permute-done.10.refs_0_, ...), custom_call_target="tpu_custom_call" | custom-call | flops 1000 | bytes 1000 | tf_op jit(solution)/shard_map/pallas_call | solution.py:114
  62.5 16.9 %collective-permute-start.12 = (f32[512,256]{1,0:T(8,128)S(1)}, f32[512,256]{1,0:T(8,128)S(1)}, u32[]{:S(2)}, u32[]{:S(2)}) collective-permute-start(f32[512,256]{1,0:T(8,128)S(1)} %get-tuple-element.47.back_ref), channel_id=1, source_target_pairs={{0,32},{2,34},{4,36},{6,38},{8,40},{10,42},{12,44},{14,46},{16,48}... | collective-permute-start | bytes 1572872 | tf_op jit(solution)/shard_map/ppermute | solution.py:183
  79.4 1.3 collective-permute-done.11.base_in_ref
  80.6 2.5 %shard_map.67 = (f32[512,256]{1,0:T(8,128)S(1)}, f32[512,256]{1,0:T(8,128)S(1)}, f32[512,256]{1,0:T(8,128)S(1)}) custom-call(f32[512,256]{1,0:T(8,128)S(1)} %get-tuple-element.40.base_ref, f32[512,512]{1,0:T(8,128)S(1)} %get-tuple-element.44.pair_ref, bf16[512,256]{1,0:T(8,128)(2,1)S(1)} %copy-done.14, bf16[512,256]{1,0:T(8,128)(2,1)S(1)} %copy-done.16, ...), custom_call_target="tpu_custom_call" | custom-call | flops 1000 | bytes 1000 | tf_op jit(solution)/shard_map/pallas_call | solution.py:114
  83.2 1.3 collective-permute-start.15
  84.5 31.4 %collective-permute-done.12 = f32[512,256]{1,0:T(8,128)S(1)} collective-permute-done((f32[512,256]{1,0:T(8,128)S(1)}, f32[512,256]{1,0:T(8,128)S(1)}, u32[]{:S(2)}, u32[]{:S(2)}) %collective-permute-start.12) | collective-permute-done | bytes 524320 | tf_op jit(solution)/shard_map/ppermute | solution.py:183
  116.0 54.8 %collective-permute-start.13 = (f32[256,256]{1,0:T(8,128)S(1)}, f32[256,256]{1,0:T(8,128)S(1)}, u32[]{:S(2)}, u32[]{:S(2)}) collective-permute-start(f32[256,256]{1,0:T(8,128)S(1)} %get-tuple-element.52), channel_id=1, source_target_pairs={{0,256},{64,320},{128,384},{192,448},{256,0},{320,64},{384,128},{4... | collective-permute-start | bytes 786440 | tf_op jit(solution)/shard_map/ppermute | solution.py:190
  170.9 1.9 %collective-permute-start.14 = (f32[256,256]{1,0:T(8,128)S(1)}, f32[256,256]{1,0:T(8,128)S(1)}, u32[]{:S(2)}, u32[]{:S(2)}) collective-permute-start(f32[256,256]{1,0:T(8,128)S(1)} %get-tuple-element.51), channel_id=1, source_target_pairs={{0,256},{64,320},{128,384},{192,448},{256,0},{320,64},{384,128},{4... | collective-permute-start | bytes 786440 | tf_op jit(solution)/shard_map/ppermute | solution.py:190
  172.8 2.4 %collective-permute-done.13.refs_0_ = f32[256,256]{1,0:T(8,128)S(1)} collective-permute-done((f32[256,256]{1,0:T(8,128)S(1)}, f32[256,256]{1,0:T(8,128)S(1)}, u32[]{:S(2)}, u32[]{:S(2)}) %collective-permute-start.13) | collective-permute-done | bytes 262176 | tf_op jit(solution)/shard_map/ppermute | solution.py:190
  175.2 5.4 %collective-permute-done.14.refs_1_ = f32[256,256]{1,0:T(8,128)S(1)} collective-permute-done((f32[256,256]{1,0:T(8,128)S(1)}, f32[256,256]{1,0:T(8,128)S(1)}, u32[]{:S(2)}, u32[]{:S(2)}) %collective-permute-start.14) | collective-permute-done | bytes 262176 | tf_op jit(solution)/shard_map/ppermute | solution.py:190
  (43 shorter events, 11.9 us)
Async XLA Ops:
  0.0 13.9 %copy-start = (f32[512,256]{1,0:T(8,128)S(1)}, f32[512,256]{1,0:T(8,128)}, u32[]{:S(2)}) copy-start(f32[512,256]{1,0:T(8,128)} %vec_ref.3) | copy-start | bytes 1572868
  0.0 1.3 copy-start.1
  1.3 1.2 copy-start.5
  5.2 40.3 %collective-permute-start.6 = (f32[512,512]{1,0:T(8,128)S(1)}, f32[512,512]{1,0:T(8,128)S(1)}, u32[]{:S(2)}, u32[]{:S(2)}) collective-permute-start(f32[512,512]{1,0:T(8,128)S(1)} %get-tuple-element.35.grp_ref), channel_id=1, source_target_pairs={{0,256},{64,320},{128,384},{192,448},{256,0},{320,64},{384,128},{4... | collective-permute-start | bytes 3145736 | tf_op jit(solution)/shard_map/ppermute | solution.py:151
  13.0 1.0 copy-start.7
  13.9 30.8 %collective-permute-start.7 = (f32[512,256]{1,0:T(8,128)S(1)}, f32[512,256]{1,0:T(8,128)S(1)}, u32[]{:S(2)}, u32[]{:S(2)}) collective-permute-start(f32[512,256]{1,0:T(8,128)S(1)} %copy-done), channel_id=1, source_target_pairs={{0,256},{64,320},{128,384},{192,448},{256,0},{320,64},{384,128},{4... | collective-permute-start | bytes 1572872 | tf_op jit(solution)/shard_map/ppermute | solution.py:138
  15.9 29.6 %collective-permute-start.8 = (f32[512,256]{1,0:T(8,128)S(1)}, f32[512,256]{1,0:T(8,128)}, u32[]{:S(2)}, u32[]{:S(2)}) collective-permute-start(f32[512,256]{1,0:T(8,128)S(1)} %copy-done), channel_id=1, source_target_pairs={{1,33},{3,35},{5,37},{7,39},{9,41},{11,43},{13,45},{15,47},{17,49}... | collective-permute-start | bytes 1572872 | tf_op jit(solution)/shard_map/ppermute | solution.py:139
  17.2 42.3 %collective-permute-start.10 = (f32[6,128,128]{2,1,0:T(8,128)}, f32[6,128,128]{2,1,0:T(8,128)S(1)}, u32[]{:S(2)}, u32[]{:S(2)}) collective-permute-start(f32[6,128,128]{2,1,0:T(8,128)} %get-tuple-element.42), channel_id=1, source_target_pairs={{1,33},{3,35},{5,37},{7,39},{9,41},{11,43},{13,45},{15,47},{17,49}... | collective-permute-start | bytes 1179656 | tf_op jit(solution)/shard_map/ppermute | solution.py:152
  18.5 37.5 %collective-permute-start.9 = (s32[4,4]{1,0:T(4,128)}, s32[4,4]{1,0:T(4,128)S(1)}, u32[]{:S(2)}, u32[]{:S(2)}) collective-permute-start(s32[4,4]{1,0:T(4,128)} %own_mask.1), channel_id=1, source_target_pairs={{1,33},{3,35},{5,37},{7,39},{9,41},{11,43},{13,45},{15,47},{17,49}... | collective-permute-start | bytes 200 | tf_op jit(solution)/shard_map/ppermute | solution.py:140
  45.5 1.0 copy-start.9
  46.5 1.2 copy-start.6
  47.7 1.2 copy-start.8
  48.9 1.2 copy-start.10
  50.1 1.0 copy-start.12
  53.6 1.0 copy-start.3
  57.2 23.4 %collective-permute-start.11 = (f32[512,256]{1,0:T(8,128)S(1)}, f32[512,256]{1,0:T(8,128)}, u32[]{:S(2)}, u32[]{:S(2)}) collective-permute-start(f32[512,256]{1,0:T(8,128)S(1)} %get-tuple-element.40.base_ref), channel_id=1, source_target_pairs={{1,33},{3,35},{5,37},{7,39},{9,41},{11,43},{13,45},{15,47},{17,49}... | collective-permute-start | bytes 1572872 | tf_op jit(solution)/shard_map/ppermute | solution.py:160
  58.5 1.5 copy-start.2
  59.4 21.2 %copy-start.14 = (bf16[512,256]{1,0:T(8,128)(2,1)S(1)}, bf16[512,256]{1,0:T(8,128)(2,1)}, u32[]{:S(2)}) copy-start(bf16[512,256]{1,0:T(8,128)(2,1)} %copy-done.13) | copy-start | bytes 786436
  59.5 21.2 %copy-start.16 = (bf16[512,256]{1,0:T(8,128)(2,1)S(1)}, bf16[512,256]{1,0:T(8,128)(2,1)}, u32[]{:S(2)}) copy-start(bf16[512,256]{1,0:T(8,128)(2,1)} %copy-done.15) | copy-start | bytes 786436
  62.5 53.4 %collective-permute-start.12 = (f32[512,256]{1,0:T(8,128)S(1)}, f32[512,256]{1,0:T(8,128)S(1)}, u32[]{:S(2)}, u32[]{:S(2)}) collective-permute-start(f32[512,256]{1,0:T(8,128)S(1)} %get-tuple-element.47.back_ref), channel_id=1, source_target_pairs={{0,32},{2,34},{4,36},{6,38},{8,40},{10,42},{12,44},{14,46},{16,48}... | collective-permute-start | bytes 1572872 | tf_op jit(solution)/shard_map/ppermute | solution.py:183
  83.2 98.5 %collective-permute-start.15 = (f32[512,256]{1,0:T(8,128)S(1)}, f32[512,256]{1,0:T(8,128)S(1)}, u32[]{:S(2)}, u32[]{:S(2)}) collective-permute-start(f32[512,256]{1,0:T(8,128)S(1)} %get-tuple-element.50), channel_id=1, source_target_pairs={{0,32},{2,34},{4,36},{6,38},{8,40},{10,42},{12,44},{14,46},{16,48}... | collective-permute-start | bytes 1572872 | tf_op jit(solution)/shard_map/ppermute | solution.py:187
  116.0 64.7 %copy-start.4 = (f32[512,512]{1,0:T(8,128)S(1)}, f32[512,512]{1,0:T(8,128)}, u32[]{:S(2)}) copy-start(f32[512,512]{1,0:T(8,128)} %copy-done.3) | copy-start | bytes 3145732
  116.0 59.2 %collective-permute-start.13 = (f32[256,256]{1,0:T(8,128)S(1)}, f32[256,256]{1,0:T(8,128)S(1)}, u32[]{:S(2)}, u32[]{:S(2)}) collective-permute-start(f32[256,256]{1,0:T(8,128)S(1)} %get-tuple-element.52), channel_id=1, source_target_pairs={{0,256},{64,320},{128,384},{192,448},{256,0},{320,64},{384,128},{4... | collective-permute-start | bytes 786440 | tf_op jit(solution)/shard_map/ppermute | solution.py:190
  170.9 9.8 %collective-permute-start.14 = (f32[256,256]{1,0:T(8,128)S(1)}, f32[256,256]{1,0:T(8,128)S(1)}, u32[]{:S(2)}, u32[]{:S(2)}) collective-permute-start(f32[256,256]{1,0:T(8,128)S(1)} %get-tuple-element.51), channel_id=1, source_target_pairs={{0,256},{64,320},{128,384},{192,448},{256,0},{320,64},{384,128},{4... | collective-permute-start | bytes 786440 | tf_op jit(solution)/shard_map/ppermute | solution.py:190
  (4 other events, 2.9 us)

commit v5 on v2

--- a/solution.py
+++ b/solution.py
@@ -9,10 +9,9 @@
 
 CENTER = 0.5
 HALF_SPAN = 5.0
-FIXED = 6
+FIXED = 12
 COST = 1000
-GRP_CUTS = 2
-BACK_CUTS = 1
+GRP_CUTS = 1
 
 
 def split(x):
@@ -29,35 +28,49 @@
     return (slab < half) == (slab % 2 == 0)
 
 
-def pack_kernel(tile, slab_mask, grp_mask, slab_ref, grp_ref, fixed_ref, extra_ref, grp_out):
+def pack_kernel(tile, slab_mask, slab_ref, bulk_ref, extra_ref):
     n = slab_ref.shape[0] // tile
-    fixed_ref[...] = jnp.zeros_like(fixed_ref)
+    bulk_ref[...] = jnp.zeros_like(bulk_ref)
     extra_ref[...] = jnp.zeros_like(extra_ref)
+    tail = (bulk_ref.shape[0] - FIXED * tile, tile)
+    row, col = lax.broadcasted_iota(jnp.int32, tail, 0), lax.broadcasted_iota(jnp.int32, tail, 1)
+    mask = jnp.zeros(tail, jnp.float32)
     slot = jnp.int32(0)
     for i in range(n):
         for j in range(n):
             at = (slice(i * tile, (i + 1) * tile), slice(j * tile, (j + 1) * tile))
-            grp_out[at] = grp_ref[at] * grp_mask[i, j].astype(jnp.float32)
             stored = slab_mask[i, j] > 0
+            mask = jnp.where(jnp.logical_and(row == i, col == j), slab_mask[i, j].astype(jnp.float32), mask)
 
             @pl.when(jnp.logical_and(stored, slot < FIXED))
             def _():
-                fixed_ref[slot] = slab_ref[at]
+                bulk_ref[pl.ds(pl.multiple_of(slot * tile, tile), tile), :] = slab_ref[at]
 
             @pl.when(jnp.logical_and(stored, slot >= FIXED))
             def _():
                 extra_ref[slot - FIXED] = slab_ref[at]
 
             slot = slot + stored.astype(jnp.int32)
-
-
-def pair_kernel(tile, own_mask, in_mask, own_ref, fixed_ref, extra_ref, vec_ref, out_ref, back_ref):
+    bulk_ref[FIXED * tile :, :] = mask
+
+
+def masked_kernel(tile, mask, tiles_ref, *out_refs):
+    n = tiles_ref.shape[0] // tile
+    for i in range(n):
+        out_ref = out_refs[i * len(out_refs) // n]
+        top = i * tile % out_ref.shape[0]
+        for j in range(n):
+            cols = slice(j * tile, (j + 1) * tile)
+            out_ref[top : top + tile, cols] = tiles_ref[i * tile : (i + 1) * tile, cols] * mask[i, j].astype(jnp.float32)
+
+
+def pair_kernel(tile, own_mask, in_mask, own_ref, bulk_ref, extra_ref, vec_ref, out_ref, back_ref):
     n = own_ref.shape[0] // tile
-    slot = jnp.int32(0)
     for i in range(n):
         for j in range(n):
             at = (slice(i * tile, (i + 1) * tile), slice(j * tile, (j + 1) * tile))
             out_ref[at] = own_ref[at] * own_mask[i, j].astype(jnp.float32)
+    slot = jnp.int32(0)
     for i in range(n):
         for j in range(n):
             to = (slice(j * tile, (j + 1) * tile), slice(i * tile, (i + 1) * tile))
@@ -65,7 +78,7 @@
 
             @pl.when(jnp.logical_and(stored, slot < FIXED))
             def _():
-                out_ref[to] += fixed_ref[slot].T
+                out_ref[to] += bulk_ref[pl.ds(pl.multiple_of(slot * tile, tile), tile), :].T
 
             @pl.when(jnp.logical_and(stored, slot >= FIXED))
             def _():
@@ -75,12 +88,15 @@
     back_ref[...] = product(split(out_ref[...].T), split(vec_ref[...]))
 
 
-def base_kernel(vec_ref, diag_ref, grp_ref, grp_in_ref, vec_grp_ref, base_ref, sym_ref, across_ref):
+def base_kernel(vec_ref, diag_ref, vec_grp_ref, *refs):
+    *grp_refs, base_ref, sym_ref, across_ref = refs
+    half = len(grp_refs) // 2
+    grp, grp_in = (jnp.concatenate([ref[...] for ref in part], axis=0) for part in (grp_refs[:half], grp_refs[half:]))
     raw = diag_ref[...]
     row = lax.broadcasted_iota(jnp.int32, raw.shape, 0)
     col = lax.broadcasted_iota(jnp.int32, raw.shape, 1)
     sym = 0.5 * (raw + raw.T) - jnp.where(row == col, jnp.float32(CENTER), jnp.float32(0))
-    across = grp_ref[...] + grp_in_ref[...].T
+    across = grp + grp_in.T
     sym_ref[...] = sym
     across_ref[...] = across
     base_ref[...] = product(split(sym), split(vec_ref[...])) + product(split(across), split(vec_grp_ref[...]))
@@ -136,28 +152,37 @@
 
     vecs_grp = lax.ppermute(vectors, "grp", grp_pairs)
     vecs_in = lax.ppermute(vectors, "slab", to_owner)
-    mask_in = lax.ppermute(slab_mask, "slab", to_owner)
-
-    fixed, extra, grp_block = local_call(
+
+    bulk, extra = local_call(
         functools.partial(pack_kernel, tile),
-        (slab_mask, grp_mask, slab_tiles, grp_tiles),
+        (slab_mask, slab_tiles),
         (
-            jax.ShapeDtypeStruct((FIXED, tile, tile), f32),
+            jax.ShapeDtypeStruct((FIXED * tile + 8, tile), f32),
             jax.ShapeDtypeStruct((slots - FIXED, tile, tile), f32),
-            square,
         ),
     )
-    grp_in = lax.ppermute(grp_block, "grp", grp_pairs)
-    fixed_in = lax.ppermute(fixed, "slab", to_owner)
-
-    sizes = (0, 1, 2, 3, 4, 6, slots - FIXED)
+    bulk_in = lax.ppermute(bulk, "slab", to_owner)
+    grp_blocks = local_call(
+        functools.partial(masked_kernel, tile),
+        (grp_mask, grp_tiles),
+        (jax.ShapeDtypeStruct((rows // GRP_CUTS, rows), f32),) * GRP_CUTS,
+    )
+    grp_in = [lax.ppermute(x, "grp", grp_pairs) for x in grp_blocks]
+
+    base, sym, across = local_call(
+        base_kernel, (vectors, diag_block, vecs_grp, *grp_blocks, *grp_in), (block, square, square)
+    )
+    base_in = lax.ppermute(base, "slab", to_owner)
+
+    base, bulk_in = lax.optimization_barrier((base, bulk_in))
+    mask_in = bulk_in[FIXED * tile : FIXED * tile + n_tile, :n_tile].astype(jnp.int32)
+    sizes = (0, slots - FIXED)
 
     def send(k):
         def branch(tiles):
             if k == 0:
                 return jnp.zeros_like(tiles)
-            got = lax.ppermute(tiles[:k], "slab", to_owner)
-            return jnp.concatenate([got, jnp.zeros((tiles.shape[0] - k, tile, tile), f32)], axis=0)
+            return lax.ppermute(tiles, "slab", to_owner)
 
         return branch
 
@@ -165,26 +190,19 @@
     which = sum((over > k).astype(jnp.int32) for k in sizes[:-1])
     extra_in = lax.switch(which, [send(k) for k in sizes], extra)
 
-    base, sym, across = local_call(
-        base_kernel, (vectors, diag_block, grp_block, grp_in, vecs_grp), (block, square, square)
-    )
-    base_in = lax.ppermute(base, "slab", to_owner)
-
-    base, fixed_in, extra_in = lax.optimization_barrier((base, fixed_in, extra_in))
     pair, back = local_call(
         functools.partial(pair_kernel, tile),
-        (slab_mask, mask_in, slab_tiles, fixed_in, extra_in, vectors),
+        (slab_mask, mask_in, slab_tiles, bulk_in, extra_in, vectors),
         (square, block),
     )
-    back_in = jnp.concatenate(
-        [lax.ppermute(x, "slab", from_owner) for x in jnp.split(back, BACK_CUTS, axis=0)], axis=0
-    )
+    back_in = lax.ppermute(back, "slab", from_owner)
     first_own, back2 = local_call(first_kernel, (base, pair, vecs_in), (block, block))
     back2_in = lax.ppermute(back2, "slab", from_owner)
 
+    far = local_call(far_kernel, (pair, base_in, back), block)
+    far, back_in = lax.optimization_barrier((far, back_in))
     first = jnp.where(owner, first_own, (base + back_in) / HALF_SPAN)
-    first_grp = [lax.ppermute(x, "grp", grp_pairs) for x in jnp.split(first, GRP_CUTS, axis=0)]
-    far = local_call(far_kernel, (pair, base_in, back), block)
+    first_grp = [lax.ppermute(x, "grp", grp_pairs) for x in jnp.split(first, 2, axis=0)]
     near = local_call(near_kernel, (sym, across, first, *first_grp), block)
     total = near + jnp.where(owner, far, back2_in)
     return 2.0 * total / HALF_SPAN - vectors

time: 165 us -> 167 us (1.012)
  the two profiles are of different devices: /device:TPU:218 before, /device:TPU:208 now
where the time goes in v5:
time: 167 us; the launch traced here: 166 us
  waiting for transfers between devices  109 us (65%)
  starting transfers between devices  32.7 us (20%)
  Pallas kernels  12.3 us (7%)
  local copies, waits for them, and re-layouts  7.84 us (5%)
  other arithmetic  3.04 us (2%)
    ppermute x1, waiting for transfers between devices, body(): base_in = lax.ppermute(base, 'slab', to_owner)  48.3 us
    ppermute x1, waiting for transfers between devices, body(): vecs_grp = lax.ppermute(vectors, 'grp', grp_pairs)  27.8 us
    ppermute x1, waiting for transfers between devices, body(): bulk_in = lax.ppermute(bulk, 'slab', to_owner)  24 us
    ppermute x1, starting transfers between devices, body(): back_in = lax.ppermute(back, 'slab', from_owner)  12.6 us
    pallas_call x7, Pallas kernels, local_call(): pl.pallas_call(kernel, out_shape=out_shape, in_specs=spaces, out_specs=(v...  12.3 us
    ppermute x2, waiting for transfers between devices, body(): lax.ppermute(x, 'grp', grp_pairs)  9.32 us
    ppermute x2, starting transfers between devices, body(): lax.ppermute(x, 'grp', grp_pairs)  7.48 us
    unnamed x24, local copies, waits for them, and re-layouts  7.07 us
  transfers between devices with their start and end apart: 9, of which 5 were waited for; matrix products, arithmetic and copies ran while one was open for 2% of the time, Pallas kernels for 7%

profile of v5, /device:TPU:208, one launch (start us, length us, event | category | flops | bytes accessed | tf_op | source)
XLA Modules:
  0.0 166.3 jit_solution(7472132753530029822)
XLA Ops:
  0.0 1.3 copy-done.6
  2.7 5.1 %collective-permute-start.2 = (f32[512,512]{1,0:T(8,128)S(1)}, f32[512,512]{1,0:T(8,128)}, u32[]{:S(2)}, u32[]{:S(2)}) collective-permute-start(f32[512,512]{1,0:T(8,128)S(1)} %shard_map.64.refs_0_), channel_id=1, source_target_pairs={{0,256},{64,320},{128,384},{192,448},{256,0},{320,64},{384,128},{4... | collective-permute-start | bytes 3145736 | tf_op jit(solution)/shard_map/ppermute | solution.py:170
  7.8 1.7 %shard_map.66 = (f32[1544,128]{1,0:T(8,128)}, f32[4,128,128]{2,1,0:T(8,128)S(1)}) custom-call(s32[4,4]{1,0:T(4,128)S(1)} %copy-done.10, f32[512,512]{1,0:T(8,128)S(1)} %copy-done.1), custom_call_target="tpu_custom_call" | custom-call | flops 1000 | bytes 1000 | tf_op jit(solution)/shard_map/pallas_call | solution.py:129
  9.5 1.3 collective-permute-start.3
  10.8 2.4 %collective-permute-start.1 = (f32[512,256]{1,0:T(8,128)S(1)}, f32[512,256]{1,0:T(8,128)S(1)}, u32[]{:S(2)}, u32[]{:S(2)}) collective-permute-start(f32[512,256]{1,0:T(8,128)S(1)} %copy-done), channel_id=1, source_target_pairs={{0,256},{64,320},{128,384},{192,448},{256,0},{320,64},{384,128},{4... | collective-permute-start | bytes 1572872 | tf_op jit(solution)/shard_map/ppermute | solution.py:153
  13.2 1.3 collective-permute-start.4
  14.5 27.8 %collective-permute-done.1.vec_grp_ref = f32[512,256]{1,0:T(8,128)S(1)} collective-permute-done((f32[512,256]{1,0:T(8,128)S(1)}, f32[512,256]{1,0:T(8,128)S(1)}, u32[]{:S(2)}, u32[]{:S(2)}) %collective-permute-start.1) | collective-permute-done | bytes 524320 | tf_op jit(solution)/shard_map/ppermute | solution.py:153
  43.1 1.2 copy-done.7
  44.4 1.0 copy-done.9
  45.4 2.5 %shard_map.65 = (f32[512,256]{1,0:T(8,128)S(1)}, f32[512,512]{1,0:T(8,128)S(1)}, f32[512,512]{1,0:T(8,128)S(1)}) custom-call(f32[512,256]{1,0:T(8,128)S(1)} %copy-done, f32[512,512]{1,0:T(8,128)S(1)} %copy-done.7, f32[512,256]{1,0:T(8,128)S(1)} %copy-done.9, f32[512,512]{1,0:T(8,128)S(1)} %shard_map.64.refs_0_, f32[512,512]{1,0:T(8,128)} %collective-permute-done.2.refs_1_), custom_call_target="tpu_custom_call" | custom-call | flops 1000 | bytes 1000 | tf_op jit(solution)/shard_map/pallas_call | solution.py:129
  47.9 1.0 copy-done.2
  48.9 1.0 copy-done.4
  49.9 24.0 %collective-permute-done.3.bulk_ref = f32[1544,128]{1,0:T(8,128)} collective-permute-done((f32[1544,128]{1,0:T(8,128)}, f32[1544,128]{1,0:T(8,128)}, u32[]{:S(2)}, u32[]{:S(2)}) %collective-permute-start.3) | collective-permute-done | bytes 790560 | tf_op jit(solution)/shard_map/ppermute | solution.py:164
  74.7 1.3 select_reduce_fusion
  77.4 1.3 collective-permute-start.5
  78.7 2.9 %shard_map.67 = (f32[512,512]{1,0:T(8,128)S(1)}, f32[512,256]{1,0:T(8,128)S(1)}) custom-call(s32[4,4]{1,0:T(4,128)S(1)} %copy-done.10, s32[4,4]{1,0:T(4,128)S(1)} %slice_convert_fusion.in_mask, f32[512,512]{1,0:T(8,128)S(1)} %copy-done.1, f32[1544,128]{1,0:T(8,128)} %collective-permute-done.3.bulk_ref, f32[4,128,128]{2,1,0:T(8,128)} %get-tuple-element.37.extra_ref, ...), custom_call_target="tpu_custom_call" | custom-call | flops 1000 | bytes 1000 | tf_op jit(solution)/shard_map/pallas_call | solution.py:129
  81.6 12.6 %collective-permute-start.6 = (f32[512,256]{1,0:T(8,128)S(1)}, f32[512,256]{1,0:T(8,128)S(1)}, u32[]{:S(2)}, u32[]{:S(2)}) collective-permute-start(f32[512,256]{1,0:T(8,128)S(1)} %get-tuple-element.31.back_ref), channel_id=1, source_target_pairs={{0,32},{2,34},{4,36},{6,38},{8,40},{10,42},{12,44},{14,46},{16,48}... | collective-permute-start | bytes 1572872 | tf_op jit(solution)/shard_map/ppermute | solution.py:198
  94.2 2.9 %shard_map.68 = (f32[512,256]{1,0:T(8,128)S(1)}, f32[512,256]{1,0:T(8,128)S(1)}) custom-call(f32[512,256]{1,0:T(8,128)S(1)} %get-tuple-element.26.base_ref, f32[512,512]{1,0:T(8,128)S(1)} %get-tuple-element.29.pair_ref, f32[512,256]{1,0:T(8,128)} %collective-permute-done.4.vec_in_ref), custom_call_target="tpu_custom_call" | custom-call | flops 1000 | bytes 1000 | tf_op jit(solution)/shard_map/pallas_call | solution.py:129
  97.1 1.3 collective-permute-start.9
  98.4 48.3 %collective-permute-done.5.base_in_ref = f32[512,256]{1,0:T(8,128)S(1)} collective-permute-done((f32[512,256]{1,0:T(8,128)S(1)}, f32[512,256]{1,0:T(8,128)S(1)}, u32[]{:S(2)}, u32[]{:S(2)}) %collective-permute-start.5) | collective-permute-done | bytes 524320 | tf_op jit(solution)/shard_map/ppermute | solution.py:175
  147.5 2.5 %collective-permute-start.7 = (f32[256,256]{1,0:T(8,128)S(1)}, f32[256,256]{1,0:T(8,128)S(1)}, u32[]{:S(2)}, u32[]{:S(2)}) collective-permute-start(f32[256,256]{1,0:T(8,128)S(1)} %get-tuple-element.36), channel_id=1, source_target_pairs={{0,256},{64,320},{128,384},{192,448},{256,0},{320,64},{384,128},{4... | collective-permute-start | bytes 786440 | tf_op jit(solution)/shard_map/ppermute | solution.py:205
  150.0 5.0 %collective-permute-start.8 = (f32[256,256]{1,0:T(8,128)S(1)}, f32[256,256]{1,0:T(8,128)S(1)}, u32[]{:S(2)}, u32[]{:S(2)}) collective-permute-start(f32[256,256]{1,0:T(8,128)S(1)} %get-tuple-element.35), channel_id=1, source_target_pairs={{0,256},{64,320},{128,384},{192,448},{256,0},{320,64},{384,128},{4... | collective-permute-start | bytes 786440 | tf_op jit(solution)/shard_map/ppermute | solution.py:205
  155.0 5.3 %collective-permute-done.7.refs_0_ = f32[256,256]{1,0:T(8,128)S(1)} collective-permute-done((f32[256,256]{1,0:T(8,128)S(1)}, f32[256,256]{1,0:T(8,128)S(1)}, u32[]{:S(2)}, u32[]{:S(2)}) %collective-permute-start.7) | collective-permute-done | bytes 262176 | tf_op jit(solution)/shard_map/ppermute | solution.py:205
  160.3 4.0 %collective-permute-done.8.refs_1_ = f32[256,256]{1,0:T(8,128)S(1)} collective-permute-done((f32[256,256]{1,0:T(8,128)S(1)}, f32[256,256]{1,0:T(8,128)S(1)}, u32[]{:S(2)}, u32[]{:S(2)}) %collective-permute-start.8) | collective-permute-done | bytes 262176 | tf_op jit(solution)/shard_map/ppermute | solution.py:205
  (32 shorter events, 7.0 us)
Async XLA Ops:
  0.0 7.8 %copy-start.1 = (f32[512,512]{1,0:T(8,128)S(1)}, f32[512,512]{1,0:T(8,128)}, u32[]{:S(2)}) copy-start(f32[512,512]{1,0:T(8,128)} %own_ref.1) | copy-start | bytes 3145732
  0.0 1.3 copy-start.6
  1.3 0.7 copy-start.11
  2.0 5.8 %copy-start.10 = (s32[4,4]{1,0:T(4,128)S(1)}, s32[4,4]{1,0:T(4,128)}, u32[]{:S(2)}) copy-start(s32[4,4]{1,0:T(4,128)} %own_mask.1) | copy-start | bytes 196
  2.7 8.1 %copy-start = (f32[512,256]{1,0:T(8,128)S(1)}, f32[512,256]{1,0:T(8,128)}, u32[]{:S(2)}) copy-start(f32[512,256]{1,0:T(8,128)} %vec_ref.3) | copy-start | bytes 1572868
  2.7 40.5 %collective-permute-start.2 = (f32[512,512]{1,0:T(8,128)S(1)}, f32[512,512]{1,0:T(8,128)}, u32[]{:S(2)}, u32[]{:S(2)}) collective-permute-start(f32[512,512]{1,0:T(8,128)S(1)} %shard_map.64.refs_0_), channel_id=1, source_target_pairs={{0,256},{64,320},{128,384},{192,448},{256,0},{320,64},{384,128},{4... | collective-permute-start | bytes 3145736 | tf_op jit(solution)/shard_map/ppermute | solution.py:170
  9.5 64.5 %collective-permute-start.3 = (f32[1544,128]{1,0:T(8,128)}, f32[1544,128]{1,0:T(8,128)}, u32[]{:S(2)}, u32[]{:S(2)}) collective-permute-start(f32[1544,128]{1,0:T(8,128)} %get-tuple-element.25), channel_id=1, source_target_pairs={{1,33},{3,35},{5,37},{7,39},{9,41},{11,43},{13,45},{15,47},{17,49}... | collective-permute-start | bytes 2371592 | tf_op jit(solution)/shard_map/ppermute | solution.py:164
  10.8 31.6 %collective-permute-start.1 = (f32[512,256]{1,0:T(8,128)S(1)}, f32[512,256]{1,0:T(8,128)S(1)}, u32[]{:S(2)}, u32[]{:S(2)}) collective-permute-start(f32[512,256]{1,0:T(8,128)S(1)} %copy-done), channel_id=1, source_target_pairs={{0,256},{64,320},{128,384},{192,448},{256,0},{320,64},{384,128},{4... | collective-permute-start | bytes 1572872 | tf_op jit(solution)/shard_map/ppermute | solution.py:153
  13.2 81.0 %collective-permute-start.4 = (f32[512,256]{1,0:T(8,128)S(1)}, f32[512,256]{1,0:T(8,128)}, u32[]{:S(2)}, u32[]{:S(2)}) collective-permute-start(f32[512,256]{1,0:T(8,128)S(1)} %copy-done), channel_id=1, source_target_pairs={{1,33},{3,35},{5,37},{7,39},{9,41},{11,43},{13,45},{15,47},{17,49}... | collective-permute-start | bytes 1572872 | tf_op jit(solution)/shard_map/ppermute | solution.py:154
  42.4 0.8 copy-start.8
  43.1 1.2 copy-start.7
  44.4 1.0 copy-start.9
  47.9 1.0 copy-start.2
  48.9 1.0 copy-start.4
  77.4 69.3 %collective-permute-start.5 = (f32[512,256]{1,0:T(8,128)S(1)}, f32[512,256]{1,0:T(8,128)S(1)}, u32[]{:S(2)}, u32[]{:S(2)}) collective-permute-start(f32[512,256]{1,0:T(8,128)S(1)} %get-tuple-element.26.base_ref), channel_id=1, source_target_pairs={{1,33},{3,35},{5,37},{7,39},{9,41},{11,43},{13,45},{15,47},{17,49}... | collective-permute-start | bytes 1572872 | tf_op jit(solution)/shard_map/ppermute | solution.py:175
  81.6 65.7 %collective-permute-start.6 = (f32[512,256]{1,0:T(8,128)S(1)}, f32[512,256]{1,0:T(8,128)S(1)}, u32[]{:S(2)}, u32[]{:S(2)}) collective-permute-start(f32[512,256]{1,0:T(8,128)S(1)} %get-tuple-element.31.back_ref), channel_id=1, source_target_pairs={{0,32},{2,34},{4,36},{6,38},{8,40},{10,42},{12,44},{14,46},{16,48}... | collective-permute-start | bytes 1572872 | tf_op jit(solution)/shard_map/ppermute | solution.py:198
  97.1 68.2 %collective-permute-start.9 = (f32[512,256]{1,0:T(8,128)S(1)}, f32[512,256]{1,0:T(8,128)S(1)}, u32[]{:S(2)}, u32[]{:S(2)}) collective-permute-start(f32[512,256]{1,0:T(8,128)S(1)} %get-tuple-element.34), channel_id=1, source_target_pairs={{0,32},{2,34},{4,36},{6,38},{8,40},{10,42},{12,44},{14,46},{16,48}... | collective-permute-start | bytes 1572872 | tf_op jit(solution)/shard_map/ppermute | solution.py:200
  147.3 17.0 %copy-start.5 = (f32[512,512]{1,0:T(8,128)S(1)}, f32[512,512]{1,0:T(8,128)}, u32[]{:S(2)}) copy-start(f32[512,512]{1,0:T(8,128)} %copy-done.4) | copy-start | bytes 3145732
  147.5 16.9 %copy-start.3 = (f32[512,512]{1,0:T(8,128)S(1)}, f32[512,512]{1,0:T(8,128)}, u32[]{:S(2)}) copy-start(f32[512,512]{1,0:T(8,128)} %copy-done.2) | copy-start | bytes 3145732
  147.5 12.8 %collective-permute-start.7 = (f32[256,256]{1,0:T(8,128)S(1)}, f32[256,256]{1,0:T(8,128)S(1)}, u32[]{:S(2)}, u32[]{:S(2)}) collective-permute-start(f32[256,256]{1,0:T(8,128)S(1)} %get-tuple-element.36), channel_id=1, source_target_pairs={{0,256},{64,320},{128,384},{192,448},{256,0},{320,64},{384,128},{4... | collective-permute-start | bytes 786440 | tf_op jit(solution)/shard_map/ppermute | solution.py:205
  150.0 14.3 %collective-permute-start.8 = (f32[256,256]{1,0:T(8,128)S(1)}, f32[256,256]{1,0:T(8,128)S(1)}, u32[]{:S(2)}, u32[]{:S(2)}) collective-permute-start(f32[256,256]{1,0:T(8,128)S(1)} %get-tuple-element.35), channel_id=1, source_target_pairs={{0,256},{64,320},{128,384},{192,448},{256,0},{320,64},{384,128},{4... | collective-permute-start | bytes 786440 | tf_op jit(solution)/shard_map/ppermute | solution.py:205

commit v6 on v5

--- a/solution.py
+++ b/solution.py
@@ -11,7 +11,7 @@
 HALF_SPAN = 5.0
 FIXED = 12
 COST = 1000
-GRP_CUTS = 1
+GRP_CUTS = 2
 
 
 def split(x):
@@ -200,7 +200,6 @@
     back2_in = lax.ppermute(back2, "slab", from_owner)
 
     far = local_call(far_kernel, (pair, base_in, back), block)
-    far, back_in = lax.optimization_barrier((far, back_in))
     first = jnp.where(owner, first_own, (base + back_in) / HALF_SPAN)
     first_grp = [lax.ppermute(x, "grp", grp_pairs) for x in jnp.split(first, 2, axis=0)]
     near = local_call(near_kernel, (sym, across, first, *first_grp), block)

time: 167 us -> 160 us (0.958)
  the two profiles are of different devices: /device:TPU:208 before, /device:TPU:57 now
where the time goes in v6:
time: 160 us; the launch traced here: 159 us
  waiting for transfers between devices  79.7 us (50%)
  starting transfers between devices  52 us (32%)
  local copies, waits for them, and re-layouts  11.7 us (7%)
  Pallas kernels  11.5 us (7%)
  other arithmetic  3.05 us (2%)
    ppermute x1, waiting for transfers between devices, body(): back_in = lax.ppermute(back, 'slab', from_owner)  56.2 us
    ppermute x1, starting transfers between devices, body(): bulk_in = lax.ppermute(bulk, 'slab', to_owner)  15.5 us
    ppermute x1, starting transfers between devices, body(): base_in = lax.ppermute(base, 'slab', to_owner)  13.5 us
    pallas_call x7, Pallas kernels, local_call(): pl.pallas_call(kernel, out_shape=out_shape, in_specs=spaces, out_specs=(v...  11.5 us
    unnamed x32, local copies, waits for them, and re-layouts  10.9 us
    ppermute x2, waiting for transfers between devices, body(): grp_in = [lax.ppermute(x, 'grp', grp_pairs) for x in grp_blocks]  10.3 us
    ppermute x2, starting transfers between devices, body(): lax.ppermute(x, 'grp', grp_pairs)  6.92 us
    ppermute x2, starting transfers between devices, body(): grp_in = [lax.ppermute(x, 'grp', grp_pairs) for x in grp_blocks]  6.78 us
  transfers between devices with their start and end apart: 10, of which 6 were waited for; matrix products, arithmetic and copies ran while one was open for 2% of the time, Pallas kernels for 6%

profile of v6, /device:TPU:57, one launch (start us, length us, event | category | flops | bytes accessed | tf_op | source)
XLA Modules:
  0.0 158.8 jit_solution(10903819314093347225)
XLA Ops:
  0.0 1.3 copy-done.1
  2.0 1.7 %shard_map.66 = (f32[1544,128]{1,0:T(8,128)}, f32[4,128,128]{2,1,0:T(8,128)S(1)}) custom-call(s32[4,4]{1,0:T(4,128)S(1)} %copy-done.13, f32[512,512]{1,0:T(8,128)S(1)} %copy-done.1), custom_call_target="tpu_custom_call" | custom-call | flops 1000 | bytes 1000 | tf_op jit(solution)/shard_map/pallas_call | solution.py:129
  3.7 15.5 %collective-permute-start.4 = (f32[1544,128]{1,0:T(8,128)}, f32[1544,128]{1,0:T(8,128)}, u32[]{:S(2)}, u32[]{:S(2)}) collective-permute-start(f32[1544,128]{1,0:T(8,128)} %get-tuple-element.27), channel_id=1, source_target_pairs={{1,33},{3,35},{5,37},{7,39},{9,41},{11,43},{13,45},{15,47},{17,49}... | collective-permute-start | bytes 2371592 | tf_op jit(solution)/shard_map/ppermute | solution.py:164
  19.2 4.6 %collective-permute-start.1 = (f32[512,256]{1,0:T(8,128)S(1)}, f32[512,256]{1,0:T(8,128)S(1)}, u32[]{:S(2)}, u32[]{:S(2)}) collective-permute-start(f32[512,256]{1,0:T(8,128)S(1)} %copy-done), channel_id=1, source_target_pairs={{0,256},{64,320},{128,384},{192,448},{256,0},{320,64},{384,128},{4... | collective-permute-start | bytes 1572872 | tf_op jit(solution)/shard_map/ppermute | solution.py:153
  23.8 1.2 copy-done.5
  25.7 2.2 %collective-permute-start.2 = (f32[256,512]{1,0:T(8,128)S(1)}, f32[256,512]{1,0:T(8,128)}, u32[]{:S(2)}, u32[]{:S(2)}) collective-permute-start(f32[256,512]{1,0:T(8,128)S(1)} %get-tuple-element.22.refs_0_), channel_id=1, source_target_pairs={{0,256},{64,320},{128,384},{192,448},{256,0},{320,64},{384,128},{4... | collective-permute-start | bytes 1572872 | tf_op jit(solution)/shard_map/ppermute | solution.py:170
  28.7 4.6 %collective-permute-start.3 = (f32[256,512]{1,0:T(8,128)S(1)}, f32[256,512]{1,0:T(8,128)}, u32[]{:S(2)}, u32[]{:S(2)}) collective-permute-start(f32[256,512]{1,0:T(8,128)S(1)} %get-tuple-element.23.refs_1_), channel_id=1, source_target_pairs={{0,256},{64,320},{128,384},{192,448},{256,0},{320,64},{384,128},{4... | collective-permute-start | bytes 1572872 | tf_op jit(solution)/shard_map/ppermute | solution.py:170
  34.1 2.1 %collective-permute-start.5 = (f32[512,256]{1,0:T(8,128)S(1)}, f32[512,256]{1,0:T(8,128)}, u32[]{:S(2)}, u32[]{:S(2)}) collective-permute-start(f32[512,256]{1,0:T(8,128)S(1)} %copy-done), channel_id=1, source_target_pairs={{1,33},{3,35},{5,37},{7,39},{9,41},{11,43},{13,45},{15,47},{17,49}... | collective-permute-start | bytes 1572872 | tf_op jit(solution)/shard_map/ppermute | solution.py:154
  37.0 4.7 %collective-permute-done.2.refs_2_ = f32[256,512]{1,0:T(8,128)} collective-permute-done((f32[256,512]{1,0:T(8,128)S(1)}, f32[256,512]{1,0:T(8,128)}, u32[]{:S(2)}, u32[]{:S(2)}) %collective-permute-start.2) | collective-permute-done | bytes 524320 | tf_op jit(solution)/shard_map/ppermute | solution.py:170
  41.7 5.6 %collective-permute-done.3.refs_3_ = f32[256,512]{1,0:T(8,128)} collective-permute-done((f32[256,512]{1,0:T(8,128)S(1)}, f32[256,512]{1,0:T(8,128)}, u32[]{:S(2)}, u32[]{:S(2)}) %collective-permute-start.3) | collective-permute-done | bytes 524320 | tf_op jit(solution)/shard_map/ppermute | solution.py:170
  47.3 1.2 copy-done.6
  51.6 2.5 %shard_map.65 = (f32[512,256]{1,0:T(8,128)S(1)}, f32[512,512]{1,0:T(8,128)S(1)}, f32[512,512]{1,0:T(8,128)S(1)}) custom-call(f32[512,256]{1,0:T(8,128)S(1)} %copy-done, f32[512,512]{1,0:T(8,128)S(1)} %copy-done.6, f32[512,256]{1,0:T(8,128)S(1)} %copy-done.8, f32[256,512]{1,0:T(8,128)S(1)} %copy-done.10, f32[256,512]{1,0:T(8,128)S(1)} %copy-done.12, ...), custom_call_target="tpu_custom_call" | custom-call | flops 1000 | bytes 1000 | tf_op jit(solution)/shard_map/pallas_call | solution.py:129
  55.1 6.4 %collective-permute-done.4.bulk_ref = f32[1544,128]{1,0:T(8,128)} collective-permute-done((f32[1544,128]{1,0:T(8,128)}, f32[1544,128]{1,0:T(8,128)}, u32[]{:S(2)}, u32[]{:S(2)}) %collective-permute-start.4) | collective-permute-done | bytes 790560 | tf_op jit(solution)/shard_map/ppermute | solution.py:164
  62.3 1.3 select_reduce_fusion
  65.0 2.2 %shard_map.67 = (f32[512,512]{1,0:T(8,128)S(1)}, f32[512,256]{1,0:T(8,128)S(1)}) custom-call(s32[4,4]{1,0:T(4,128)S(1)} %copy-done.14, s32[4,4]{1,0:T(4,128)S(1)} %slice_convert_fusion.in_mask, f32[512,512]{1,0:T(8,128)S(1)} %copy-done.2, f32[1544,128]{1,0:T(8,128)} %collective-permute-done.4.bulk_ref, f32[4,128,128]{2,1,0:T(8,128)} %get-tuple-element.37.extra_ref, ...), custom_call_target="tpu_custom_call" | custom-call | flops 1000 | bytes 1000 | tf_op jit(solution)/shard_map/pallas_call | solution.py:129
  67.2 1.3 collective-permute-start.6
  68.5 13.5 %collective-permute-start.9 = (f32[512,256]{1,0:T(8,128)S(1)}, f32[512,256]{1,0:T(8,128)S(1)}, u32[]{:S(2)}, u32[]{:S(2)}) collective-permute-start(f32[512,256]{1,0:T(8,128)S(1)} %get-tuple-element.28.base_ref), channel_id=1, source_target_pairs={{1,33},{3,35},{5,37},{7,39},{9,41},{11,43},{13,45},{15,47},{17,49}... | collective-permute-start | bytes 1572872 | tf_op jit(solution)/shard_map/ppermute | solution.py:175
  82.0 2.9 %shard_map.68 = (f32[512,256]{1,0:T(8,128)S(1)}, f32[512,256]{1,0:T(8,128)S(1)}) custom-call(f32[512,256]{1,0:T(8,128)S(1)} %get-tuple-element.28.base_ref, f32[512,512]{1,0:T(8,128)S(1)} %get-tuple-element.31.pair_ref, f32[512,256]{1,0:T(8,128)} %collective-permute-done.5.vec_in_ref), custom_call_target="tpu_custom_call" | custom-call | flops 1000 | bytes 1000 | tf_op jit(solution)/shard_map/pallas_call | solution.py:129
  84.9 1.3 collective-permute-start.10
  86.2 56.2 %collective-permute-done.6 = f32[512,256]{1,0:T(8,128)S(1)} collective-permute-done((f32[512,256]{1,0:T(8,128)S(1)}, f32[512,256]{1,0:T(8,128)S(1)}, u32[]{:S(2)}, u32[]{:S(2)}) %collective-permute-start.6) | collective-permute-done | bytes 524320 | tf_op jit(solution)/shard_map/ppermute | solution.py:198
  142.6 4.8 %collective-permute-start.7 = (f32[256,256]{1,0:T(8,128)S(1)}, f32[256,256]{1,0:T(8,128)S(1)}, u32[]{:S(2)}, u32[]{:S(2)}) collective-permute-start(f32[256,256]{1,0:T(8,128)S(1)} %get-tuple-element.36), channel_id=1, source_target_pairs={{0,256},{64,320},{128,384},{192,448},{256,0},{320,64},{384,128},{4... | collective-permute-start | bytes 786440 | tf_op jit(solution)/shard_map/ppermute | solution.py:204
  147.4 2.1 %collective-permute-start.8 = (f32[256,256]{1,0:T(8,128)S(1)}, f32[256,256]{1,0:T(8,128)S(1)}, u32[]{:S(2)}, u32[]{:S(2)}) collective-permute-start(f32[256,256]{1,0:T(8,128)S(1)} %get-tuple-element.35), channel_id=1, source_target_pairs={{0,256},{64,320},{128,384},{192,448},{256,0},{320,64},{384,128},{4... | collective-permute-start | bytes 786440 | tf_op jit(solution)/shard_map/ppermute | solution.py:204
  150.2 3.9 %collective-permute-done.7.refs_0_ = f32[256,256]{1,0:T(8,128)S(1)} collective-permute-done((f32[256,256]{1,0:T(8,128)S(1)}, f32[256,256]{1,0:T(8,128)S(1)}, u32[]{:S(2)}, u32[]{:S(2)}) %collective-permute-start.7) | collective-permute-done | bytes 262176 | tf_op jit(solution)/shard_map/ppermute | solution.py:204
  154.0 2.8 %collective-permute-done.8.refs_1_ = f32[256,256]{1,0:T(8,128)S(1)} collective-permute-done((f32[256,256]{1,0:T(8,128)S(1)}, f32[256,256]{1,0:T(8,128)S(1)}, u32[]{:S(2)}, u32[]{:S(2)}) %collective-permute-start.8) | collective-permute-done | bytes 262176 | tf_op jit(solution)/shard_map/ppermute | solution.py:204
  (42 shorter events, 12.7 us)
Async XLA Ops:
  0.0 19.2 %copy-start = (f32[512,256]{1,0:T(8,128)S(1)}, f32[512,256]{1,0:T(8,128)}, u32[]{:S(2)}) copy-start(f32[512,256]{1,0:T(8,128)} %vec_ref.3) | copy-start | bytes 1572868
  0.0 1.3 copy-start.1
  2.0 21.8 %copy-start.15 = (s32[4,4]{1,0:T(4,128)S(1)}, s32[4,4]{1,0:T(4,128)}, u32[]{:S(2)}) copy-start(s32[4,4]{1,0:T(4,128)} %mask.1) | copy-start | bytes 196
  3.7 57.9 %collective-permute-start.4 = (f32[1544,128]{1,0:T(8,128)}, f32[1544,128]{1,0:T(8,128)}, u32[]{:S(2)}, u32[]{:S(2)}) collective-permute-start(f32[1544,128]{1,0:T(8,128)} %get-tuple-element.27), channel_id=1, source_target_pairs={{1,33},{3,35},{5,37},{7,39},{9,41},{11,43},{13,45},{15,47},{17,49}... | collective-permute-start | bytes 2371592 | tf_op jit(solution)/shard_map/ppermute | solution.py:164
  19.2 17.0 %collective-permute-start.1 = (f32[512,256]{1,0:T(8,128)S(1)}, f32[512,256]{1,0:T(8,128)S(1)}, u32[]{:S(2)}, u32[]{:S(2)}) collective-permute-start(f32[512,256]{1,0:T(8,128)S(1)} %copy-done), channel_id=1, source_target_pairs={{0,256},{64,320},{128,384},{192,448},{256,0},{320,64},{384,128},{4... | collective-permute-start | bytes 1572872 | tf_op jit(solution)/shard_map/ppermute | solution.py:153
  23.8 1.2 copy-start.5
  25.7 16.0 %collective-permute-start.2 = (f32[256,512]{1,0:T(8,128)S(1)}, f32[256,512]{1,0:T(8,128)}, u32[]{:S(2)}, u32[]{:S(2)}) collective-permute-start(f32[256,512]{1,0:T(8,128)S(1)} %get-tuple-element.22.refs_0_), channel_id=1, source_target_pairs={{0,256},{64,320},{128,384},{192,448},{256,0},{320,64},{384,128},{4... | collective-permute-start | bytes 1572872 | tf_op jit(solution)/shard_map/ppermute | solution.py:170
  27.9 0.8 copy-start.9
  28.7 18.6 %collective-permute-start.3 = (f32[256,512]{1,0:T(8,128)S(1)}, f32[256,512]{1,0:T(8,128)}, u32[]{:S(2)}, u32[]{:S(2)}) collective-permute-start(f32[256,512]{1,0:T(8,128)S(1)} %get-tuple-element.23.refs_1_), channel_id=1, source_target_pairs={{0,256},{64,320},{128,384},{192,448},{256,0},{320,64},{384,128},{4... | collective-permute-start | bytes 1572872 | tf_op jit(solution)/shard_map/ppermute | solution.py:170
  33.3 0.8 copy-start.11
  34.1 47.9 %collective-permute-start.5 = (f32[512,256]{1,0:T(8,128)S(1)}, f32[512,256]{1,0:T(8,128)}, u32[]{:S(2)}, u32[]{:S(2)}) collective-permute-start(f32[512,256]{1,0:T(8,128)S(1)} %copy-done), channel_id=1, source_target_pairs={{1,33},{3,35},{5,37},{7,39},{9,41},{11,43},{13,45},{15,47},{17,49}... | collective-permute-start | bytes 1572872 | tf_op jit(solution)/shard_map/ppermute | solution.py:154
  36.2 28.8 %copy-start.2 = (f32[512,512]{1,0:T(8,128)S(1)}, f32[512,512]{1,0:T(8,128)}, u32[]{:S(2)}) copy-start(f32[512,512]{1,0:T(8,128)} %own_ref.1) | copy-start | bytes 3145732
  36.2 0.8 copy-start.7
  47.3 1.2 copy-start.6
  48.5 1.0 copy-start.8
  49.5 1.0 copy-start.10
  50.6 1.0 copy-start.12
  54.1 1.0 copy-start.3
  67.2 75.3 %collective-permute-start.6 = (f32[512,256]{1,0:T(8,128)S(1)}, f32[512,256]{1,0:T(8,128)S(1)}, u32[]{:S(2)}, u32[]{:S(2)}) collective-permute-start(f32[512,256]{1,0:T(8,128)S(1)} %get-tuple-element.33.back_ref), channel_id=1, source_target_pairs={{0,32},{2,34},{4,36},{6,38},{8,40},{10,42},{12,44},{14,46},{16,48}... | collective-permute-start | bytes 1572872 | tf_op jit(solution)/shard_map/ppermute | solution.py:198
  68.5 81.1 %collective-permute-start.9 = (f32[512,256]{1,0:T(8,128)S(1)}, f32[512,256]{1,0:T(8,128)S(1)}, u32[]{:S(2)}, u32[]{:S(2)}) collective-permute-start(f32[512,256]{1,0:T(8,128)S(1)} %get-tuple-element.28.base_ref), channel_id=1, source_target_pairs={{1,33},{3,35},{5,37},{7,39},{9,41},{11,43},{13,45},{15,47},{17,49}... | collective-permute-start | bytes 1572872 | tf_op jit(solution)/shard_map/ppermute | solution.py:175
  84.9 72.9 %collective-permute-start.10 = (f32[512,256]{1,0:T(8,128)S(1)}, f32[512,256]{1,0:T(8,128)S(1)}, u32[]{:S(2)}, u32[]{:S(2)}) collective-permute-start(f32[512,256]{1,0:T(8,128)S(1)} %get-tuple-element.34), channel_id=1, source_target_pairs={{0,32},{2,34},{4,36},{6,38},{8,40},{10,42},{12,44},{14,46},{16,48}... | collective-permute-start | bytes 1572872 | tf_op jit(solution)/shard_map/ppermute | solution.py:200
  142.6 11.4 %collective-permute-start.7 = (f32[256,256]{1,0:T(8,128)S(1)}, f32[256,256]{1,0:T(8,128)S(1)}, u32[]{:S(2)}, u32[]{:S(2)}) collective-permute-start(f32[256,256]{1,0:T(8,128)S(1)} %get-tuple-element.36), channel_id=1, source_target_pairs={{0,256},{64,320},{128,384},{192,448},{256,0},{320,64},{384,128},{4... | collective-permute-start | bytes 786440 | tf_op jit(solution)/shard_map/ppermute | solution.py:204
  147.4 9.4 %copy-start.4 = (f32[512,512]{1,0:T(8,128)S(1)}, f32[512,512]{1,0:T(8,128)}, u32[]{:S(2)}) copy-start(f32[512,512]{1,0:T(8,128)} %copy-done.3) | copy-start | bytes 3145732
  147.4 9.4 %collective-permute-start.8 = (f32[256,256]{1,0:T(8,128)S(1)}, f32[256,256]{1,0:T(8,128)S(1)}, u32[]{:S(2)}, u32[]{:S(2)}) collective-permute-start(f32[256,256]{1,0:T(8,128)S(1)} %get-tuple-element.35), channel_id=1, source_target_pairs={{0,256},{64,320},{128,384},{192,448},{256,0},{320,64},{384,128},{4... | collective-permute-start | bytes 786440 | tf_op jit(solution)/shard_map/ppermute | solution.py:204
  (2 other events, 1.4 us)

commit v7 on v6

--- a/solution.py
+++ b/solution.py
@@ -9,7 +9,7 @@
 
 CENTER = 0.5
 HALF_SPAN = 5.0
-FIXED = 12
+SIZES = (4, 5, 6, 7, 8, 9, 10, 12, 16)
 COST = 1000
 GRP_CUTS = 2
 
@@ -28,30 +28,19 @@
     return (slab < half) == (slab % 2 == 0)
 
 
-def pack_kernel(tile, slab_mask, slab_ref, bulk_ref, extra_ref):
+def pack_kernel(tile, slab_mask, slab_ref, out_ref):
     n = slab_ref.shape[0] // tile
-    bulk_ref[...] = jnp.zeros_like(bulk_ref)
-    extra_ref[...] = jnp.zeros_like(extra_ref)
-    tail = (bulk_ref.shape[0] - FIXED * tile, tile)
-    row, col = lax.broadcasted_iota(jnp.int32, tail, 0), lax.broadcasted_iota(jnp.int32, tail, 1)
-    mask = jnp.zeros(tail, jnp.float32)
+    out_ref[...] = jnp.zeros_like(out_ref)
     slot = jnp.int32(0)
     for i in range(n):
         for j in range(n):
-            at = (slice(i * tile, (i + 1) * tile), slice(j * tile, (j + 1) * tile))
             stored = slab_mask[i, j] > 0
-            mask = jnp.where(jnp.logical_and(row == i, col == j), slab_mask[i, j].astype(jnp.float32), mask)
 
-            @pl.when(jnp.logical_and(stored, slot < FIXED))
+            @pl.when(stored)
             def _():
-                bulk_ref[pl.ds(pl.multiple_of(slot * tile, tile), tile), :] = slab_ref[at]
-
-            @pl.when(jnp.logical_and(stored, slot >= FIXED))
-            def _():
-                extra_ref[slot - FIXED] = slab_ref[at]
+                out_ref[slot] = slab_ref[i * tile : (i + 1) * tile, j * tile : (j + 1) * tile]
 
             slot = slot + stored.astype(jnp.int32)
-    bulk_ref[FIXED * tile :, :] = mask
 
 
 def masked_kernel(tile, mask, tiles_ref, *out_refs):
@@ -64,25 +53,21 @@
             out_ref[top : top + tile, cols] = tiles_ref[i * tile : (i + 1) * tile, cols] * mask[i, j].astype(jnp.float32)
 
 
-def pair_kernel(tile, own_mask, in_mask, own_ref, bulk_ref, extra_ref, vec_ref, out_ref, back_ref):
+def pair_kernel(tile, own_mask, in_mask, own_ref, slots_ref, vec_ref, out_ref, back_ref):
     n = own_ref.shape[0] // tile
+    slot = jnp.int32(0)
     for i in range(n):
         for j in range(n):
             at = (slice(i * tile, (i + 1) * tile), slice(j * tile, (j + 1) * tile))
             out_ref[at] = own_ref[at] * own_mask[i, j].astype(jnp.float32)
-    slot = jnp.int32(0)
     for i in range(n):
         for j in range(n):
             to = (slice(j * tile, (j + 1) * tile), slice(i * tile, (i + 1) * tile))
             stored = in_mask[i, j] > 0
 
-            @pl.when(jnp.logical_and(stored, slot < FIXED))
+            @pl.when(stored)
             def _():
-                out_ref[to] += bulk_ref[pl.ds(pl.multiple_of(slot * tile, tile), tile), :].T
-
-            @pl.when(jnp.logical_and(stored, slot >= FIXED))
-            def _():
-                out_ref[to] += extra_ref[slot - FIXED].T
+                out_ref[to] += slots_ref[slot].T
 
             slot = slot + stored.astype(jnp.int32)
     back_ref[...] = product(split(out_ref[...].T), split(vec_ref[...]))
@@ -150,18 +135,16 @@
     square = jax.ShapeDtypeStruct((rows, rows), f32)
     block = jax.ShapeDtypeStruct(vectors.shape, f32)
 
-    vecs_grp = lax.ppermute(vectors, "grp", grp_pairs)
+    mask_in = lax.ppermute(slab_mask, "slab", to_owner)
     vecs_in = lax.ppermute(vectors, "slab", to_owner)
-
-    bulk, extra = local_call(
+    packed = local_call(
         functools.partial(pack_kernel, tile),
         (slab_mask, slab_tiles),
-        (
-            jax.ShapeDtypeStruct((FIXED * tile + 8, tile), f32),
-            jax.ShapeDtypeStruct((slots - FIXED, tile, tile), f32),
-        ),
+        jax.ShapeDtypeStruct((slots, tile, tile), f32),
     )
-    bulk_in = lax.ppermute(bulk, "slab", to_owner)
+    later = vectors
+    vecs_grp = lax.ppermute(later, "grp", grp_pairs)
+
     grp_blocks = local_call(
         functools.partial(masked_kernel, tile),
         (grp_mask, grp_tiles),
@@ -174,27 +157,18 @@
     )
     base_in = lax.ppermute(base, "slab", to_owner)
 
-    base, bulk_in = lax.optimization_barrier((base, bulk_in))
-    mask_in = bulk_in[FIXED * tile : FIXED * tile + n_tile, :n_tile].astype(jnp.int32)
-    sizes = (0, slots - FIXED)
-
     def send(k):
-        def branch(tiles):
-            if k == 0:
-                return jnp.zeros_like(tiles)
-            return lax.ppermute(tiles, "slab", to_owner)
+        def branch(tiles, own_mask, in_mask, own, vecs):
+            got = lax.ppermute(tiles[:k], "slab", to_owner)
+            return local_call(
+                functools.partial(pair_kernel, tile), (own_mask, in_mask, own, got, vecs), (square, block)
+            )
 
         return branch
 
-    over = jnp.sum(jnp.where(owner, mask_in, slab_mask)) - FIXED
-    which = sum((over > k).astype(jnp.int32) for k in sizes[:-1])
-    extra_in = lax.switch(which, [send(k) for k in sizes], extra)
-
-    pair, back = local_call(
-        functools.partial(pair_kernel, tile),
-        (slab_mask, mask_in, slab_tiles, bulk_in, extra_in, vectors),
-        (square, block),
-    )
+    count = jnp.sum(jnp.where(owner, mask_in, slab_mask))
+    which = sum((count > k).astype(jnp.int32) for k in SIZES[:-1])
+    pair, back = lax.switch(which, [send(k) for k in SIZES], packed, slab_mask, mask_in, slab_tiles, vectors)
     back_in = lax.ppermute(back, "slab", from_owner)
     first_own, back2 = local_call(first_kernel, (base, pair, vecs_in), (block, block))
     back2_in = lax.ppermute(back2, "slab", from_owner)

time: 160 us -> 167 us (1.044)
  the two profiles are of different devices: /device:TPU:57 before, /device:TPU:33 now
where the time goes in v7:
time: 167 us; the launch traced here: 166 us
  starting transfers between devices  80.1 us (48%)
  waiting for transfers between devices  63.4 us (38%)
  Pallas kernels  11.5 us (7%)
  between operations  5.44 us (3%)
  local copies, waits for them, and re-layouts  4.17 us (2%)
    ppermute x1, waiting for transfers between devices, branch(): got = lax.ppermute(tiles[:k], 'slab', to_owner)  37.4 us
    ppermute x2, starting transfers between devices, body(): lax.ppermute(x, 'grp', grp_pairs)  20.5 us
    ppermute x1, starting transfers between devices, branch(): got = lax.ppermute(tiles[:k], 'slab', to_owner)  16.1 us
    ppermute x1, waiting for transfers between devices, body(): back_in = lax.ppermute(back, 'slab', from_owner)  15.5 us
    ppermute x1, starting transfers between devices, body(): vecs_in = lax.ppermute(vectors, 'slab', to_owner)  14.6 us
    ppermute x1, starting transfers between devices, body(): base_in = lax.ppermute(base, 'slab', to_owner)  13.5 us
    pallas_call x7, Pallas kernels, local_call(): pl.pallas_call(kernel, out_shape=out_shape, in_specs=spaces, out_specs=(v...  11.5 us
    ppermute x2, starting transfers between devices, body(): grp_in = [lax.ppermute(x, 'grp', grp_pairs) for x in grp_blocks]  6.79 us
  transfers between devices with their start and end apart: 11, of which 5 were waited for; matrix products, arithmetic and copies ran while one was open for 1% of the time, Pallas kernels for 7%

profile of v7, /device:TPU:33, one launch (start us, length us, event | category | flops | bytes accessed | tf_op | source)
XLA Modules:
  0.0 166.4 jit_solution(14084485781798678911)
XLA Ops:
  0.0 4.6 %collective-permute-start.9 = (f32[512,256]{1,0:T(8,128)}, f32[512,256]{1,0:T(8,128)S(1)}, u32[]{:S(2)}, u32[]{:S(2)}) collective-permute-start(f32[512,256]{1,0:T(8,128)} %vec_ref.1), channel_id=1, source_target_pairs={{0,256},{64,320},{128,384},{192,448},{256,0},{320,64},{384,128},{4... | collective-permute-start | bytes 1572872 | tf_op jit(solution)/shard_map/ppermute | solution.py:146
  4.7 14.6 %collective-permute-start.13 = (f32[512,256]{1,0:T(8,128)}, f32[512,256]{1,0:T(8,128)S(1)}, u32[]{:S(2)}, u32[]{:S(2)}) collective-permute-start(f32[512,256]{1,0:T(8,128)} %vec_ref.1), channel_id=1, source_target_pairs={{1,33},{3,35},{5,37},{7,39},{9,41},{11,43},{13,45},{15,47},{17,49}... | collective-permute-start | bytes 1572872 | tf_op jit(solution)/shard_map/ppermute | solution.py:139
  19.2 1.3 collective-permute-start.12
  20.5 1.2 copy-done
  23.1 2.1 %collective-permute-start.10 = (f32[256,512]{1,0:T(8,128)S(1)}, f32[256,512]{1,0:T(8,128)}, u32[]{:S(2)}, u32[]{:S(2)}) collective-permute-start(f32[256,512]{1,0:T(8,128)S(1)} %get-tuple-element.149.refs_0_), channel_id=1, source_target_pairs={{0,256},{64,320},{128,384},{192,448},{256,0},{320,64},{384,128},{4... | collective-permute-start | bytes 1572872 | tf_op jit(solution)/shard_map/ppermute | solution.py:153
  25.3 4.7 %collective-permute-start.11 = (f32[256,512]{1,0:T(8,128)S(1)}, f32[256,512]{1,0:T(8,128)}, u32[]{:S(2)}, u32[]{:S(2)}) collective-permute-start(f32[256,512]{1,0:T(8,128)S(1)} %get-tuple-element.150.refs_1_), channel_id=1, source_target_pairs={{0,256},{64,320},{128,384},{192,448},{256,0},{320,64},{384,128},{4... | collective-permute-start | bytes 1572872 | tf_op jit(solution)/shard_map/ppermute | solution.py:153
  30.6 1.8 %shard_map.66 = f32[16,128,128]{2,1,0:T(8,128)} custom-call(s32[4,4]{1,0:T(4,128)S(1)} %copy-done.15, f32[512,512]{1,0:T(8,128)S(1)} %copy-done.3), custom_call_target="tpu_custom_call" | custom-call | flops 1000 | bytes 1000 | tf_op jit(solution)/shard_map/pallas_call | solution.py:114
  32.4 3.8 %collective-permute-done.12 = s32[4,4]{1,0:T(4,128)S(1)} collective-permute-done((s32[4,4]{1,0:T(4,128)}, s32[4,4]{1,0:T(4,128)S(1)}, u32[]{:S(2)}, u32[]{:S(2)}) %collective-permute-start.12) | collective-permute-done | bytes 96 | tf_op jit(solution)/shard_map/ppermute | solution.py:138
  42.1 57.7 %conditional.1 = ((f32[512,512]{1,0:T(8,128)}, f32[512,256]{1,0:T(8,128)})) conditional(s32[]{:T(128)} %clamp.3, (f32[16,128,128]{2,1,0:T(8,128)}, s32[4,4]{1,0:T(4,128)S(1)}, s32[4,4]{1,0:T(4,128)S(1)}, f32[512,512]{1,0:T(8,128)}, f32[512,256]{1,0:T(8,128)}) %tuple.52, (f32[16,128,128]{2,1,0:T(8,128)}, ...), branch_computations={%region_1.2_spmd, %region_2.3_spmd, %region_3.4_spmd, %region_4.5_... | conditional | flops 1000 | bytes 11011152 | solution.py:171
  42.1 1.2 slice.19
  43.3 16.1 %collective-permute-start.3 = (f32[7,128,128]{2,1,0:T(8,128)S(1)}, f32[7,128,128]{2,1,0:T(8,128)S(1)}, u32[]{:S(2)}, u32[]{:S(2)}) collective-permute-start(f32[7,128,128]{2,1,0:T(8,128)S(1)} %slice.19), channel_id=1, source_target_pairs={{1,33},{3,35},{5,37},{7,39},{9,41},{11,43},{13,45},{15,47},{17,49}... | collective-permute-start | bytes 1376264 | tf_op jit(solution)/shard_map/cond/branch_3_fun/ppermute | solution.py:162
  59.4 37.4 %collective-permute-done.3.slots_ref = f32[7,128,128]{2,1,0:T(8,128)S(1)} collective-permute-done((f32[7,128,128]{2,1,0:T(8,128)S(1)}, f32[7,128,128]{2,1,0:T(8,128)S(1)}, u32[]{:S(2)}, u32[]{:S(2)}) %collective-permute-start.3) | collective-permute-done | bytes 458784 | tf_op jit(solution)/shard_map/cond/branch_3_fun/ppermute | solution.py:162
  96.8 3.0 %branch_3_fun.1 = (f32[512,512]{1,0:T(8,128)}, f32[512,256]{1,0:T(8,128)}) custom-call(s32[4,4]{1,0:T(4,128)S(1)} %get-tuple-element.110.own_mask, s32[4,4]{1,0:T(4,128)S(1)} %get-tuple-element.111.in_mask, f32[512,512]{1,0:T(8,128)} %get-tuple-element.112.own_ref, f32[7,128,128]{2,1,0:T(8,128)S(1)} %collective-permute-done.3.slots_ref, ...), custom_call_target="tpu_custom_call" | custom-call | flops 1000 | bytes 1000 | tf_op jit(solution)/shard_map/cond/branch_3_fun/pallas_call | solution.py:114
  99.8 1.4 collective-permute-start.14
  101.2 2.6 %shard_map.65 = (f32[512,256]{1,0:T(8,128)S(1)}, f32[512,512]{1,0:T(8,128)S(1)}, f32[512,512]{1,0:T(8,128)S(1)}) custom-call(f32[512,256]{1,0:T(8,128)} %vec_ref.1, f32[512,512]{1,0:T(8,128)S(1)} %copy-done.1, f32[512,256]{1,0:T(8,128)S(1)} %collective-permute-done.9.vec_grp_ref, f32[256,512]{1,0:T(8,128)S(1)} %get-tuple-element.149.refs_0_, ...), custom_call_target="tpu_custom_call" | custom-call | flops 1000 | bytes 1000 | tf_op jit(solution)/shard_map/pallas_call | solution.py:114
  103.9 13.5 %collective-permute-start.17 = (f32[512,256]{1,0:T(8,128)S(1)}, f32[512,256]{1,0:T(8,128)S(1)}, u32[]{:S(2)}, u32[]{:S(2)}) collective-permute-start(f32[512,256]{1,0:T(8,128)S(1)} %get-tuple-element.153.base_ref), channel_id=1, source_target_pairs={{1,33},{3,35},{5,37},{7,39},{9,41},{11,43},{13,45},{15,47},{17,49}... | collective-permute-start | bytes 1572872 | tf_op jit(solution)/shard_map/ppermute | solution.py:158
  117.4 1.8 %shard_map.67 = (f32[512,256]{1,0:T(8,128)S(1)}, f32[512,256]{1,0:T(8,128)S(1)}) custom-call(f32[512,256]{1,0:T(8,128)S(1)} %get-tuple-element.153.base_ref, f32[512,512]{1,0:T(8,128)S(1)} %copy-done.13, f32[512,256]{1,0:T(8,128)S(1)} %collective-permute-done.13.vec_in_ref), custom_call_target="tpu_custom_call" | custom-call | flops 1000 | bytes 1000 | tf_op jit(solution)/shard_map/pallas_call | solution.py:114
  119.3 1.3 collective-permute-start.18
  120.6 15.5 %collective-permute-done.14 = f32[512,256]{1,0:T(8,128)S(1)} collective-permute-done((f32[512,256]{1,0:T(8,128)}, f32[512,256]{1,0:T(8,128)S(1)}, u32[]{:S(2)}, u32[]{:S(2)}) %collective-permute-start.14) | collective-permute-done | bytes 524320 | tf_op jit(solution)/shard_map/ppermute | solution.py:172
  136.2 18.6 %collective-permute-start.15 = (f32[256,256]{1,0:T(8,128)S(1)}, f32[256,256]{1,0:T(8,128)S(1)}, u32[]{:S(2)}, u32[]{:S(2)}) collective-permute-start(f32[256,256]{1,0:T(8,128)S(1)} %get-tuple-element.159), channel_id=1, source_target_pairs={{0,256},{64,320},{128,384},{192,448},{256,0},{320,64},{384,128},{4... | collective-permute-start | bytes 786440 | tf_op jit(solution)/shard_map/ppermute | solution.py:178
  154.8 1.9 %collective-permute-start.16 = (f32[256,256]{1,0:T(8,128)S(1)}, f32[256,256]{1,0:T(8,128)S(1)}, u32[]{:S(2)}, u32[]{:S(2)}) collective-permute-start(f32[256,256]{1,0:T(8,128)S(1)} %get-tuple-element.158), channel_id=1, source_target_pairs={{0,256},{64,320},{128,384},{192,448},{256,0},{320,64},{384,128},{4... | collective-permute-start | bytes 786440 | tf_op jit(solution)/shard_map/ppermute | solution.py:178
  156.7 1.8 %collective-permute-done.15.refs_0_ = f32[256,256]{1,0:T(8,128)S(1)} collective-permute-done((f32[256,256]{1,0:T(8,128)S(1)}, f32[256,256]{1,0:T(8,128)S(1)}, u32[]{:S(2)}, u32[]{:S(2)}) %collective-permute-start.15) | collective-permute-done | bytes 262176 | tf_op jit(solution)/shard_map/ppermute | solution.py:178
  158.5 4.9 %collective-permute-done.16.refs_1_ = f32[256,256]{1,0:T(8,128)S(1)} collective-permute-done((f32[256,256]{1,0:T(8,128)S(1)}, f32[256,256]{1,0:T(8,128)S(1)}, u32[]{:S(2)}, u32[]{:S(2)}) %collective-permute-start.16) | collective-permute-done | bytes 262176 | tf_op jit(solution)/shard_map/ppermute | solution.py:178
  163.4 1.0 shard_map.68
  (29 shorter events, 4.8 us)
Async XLA Ops:
  0.0 101.2 %collective-permute-start.9 = (f32[512,256]{1,0:T(8,128)}, f32[512,256]{1,0:T(8,128)S(1)}, u32[]{:S(2)}, u32[]{:S(2)}) collective-permute-start(f32[512,256]{1,0:T(8,128)} %vec_ref.1), channel_id=1, source_target_pairs={{0,256},{64,320},{128,384},{192,448},{256,0},{320,64},{384,128},{4... | collective-permute-start | bytes 1572872 | tf_op jit(solution)/shard_map/ppermute | solution.py:146
  4.7 112.8 %collective-permute-start.13 = (f32[512,256]{1,0:T(8,128)}, f32[512,256]{1,0:T(8,128)S(1)}, u32[]{:S(2)}, u32[]{:S(2)}) collective-permute-start(f32[512,256]{1,0:T(8,128)} %vec_ref.1), channel_id=1, source_target_pairs={{1,33},{3,35},{5,37},{7,39},{9,41},{11,43},{13,45},{15,47},{17,49}... | collective-permute-start | bytes 1572872 | tf_op jit(solution)/shard_map/ppermute | solution.py:139
  19.2 17.0 %collective-permute-start.12 = (s32[4,4]{1,0:T(4,128)}, s32[4,4]{1,0:T(4,128)S(1)}, u32[]{:S(2)}, u32[]{:S(2)}) collective-permute-start(s32[4,4]{1,0:T(4,128)} %slab_mask.1), channel_id=1, source_target_pairs={{1,33},{3,35},{5,37},{7,39},{9,41},{11,43},{13,45},{15,47},{17,49}... | collective-permute-start | bytes 200 | tf_op jit(solution)/shard_map/ppermute | solution.py:138
  20.5 1.2 copy-start
  21.8 0.7 copy-start.2
  22.4 7.5 %copy-start.3 = (f32[512,512]{1,0:T(8,128)S(1)}, f32[512,512]{1,0:T(8,128)}, u32[]{:S(2)}) copy-start(f32[512,512]{1,0:T(8,128)} %slab_ref.1) | copy-start | bytes 3145732
  23.1 78.1 %collective-permute-start.10 = (f32[256,512]{1,0:T(8,128)S(1)}, f32[256,512]{1,0:T(8,128)}, u32[]{:S(2)}, u32[]{:S(2)}) collective-permute-start(f32[256,512]{1,0:T(8,128)S(1)} %get-tuple-element.149.refs_0_), channel_id=1, source_target_pairs={{0,256},{64,320},{128,384},{192,448},{256,0},{320,64},{384,128},{4... | collective-permute-start | bytes 1572872 | tf_op jit(solution)/shard_map/ppermute | solution.py:153
  25.3 76.0 %collective-permute-start.11 = (f32[256,512]{1,0:T(8,128)S(1)}, f32[256,512]{1,0:T(8,128)}, u32[]{:S(2)}, u32[]{:S(2)}) collective-permute-start(f32[256,512]{1,0:T(8,128)S(1)} %get-tuple-element.150.refs_1_), channel_id=1, source_target_pairs={{0,256},{64,320},{128,384},{192,448},{256,0},{320,64},{384,128},{4... | collective-permute-start | bytes 1572872 | tf_op jit(solution)/shard_map/ppermute | solution.py:153
  29.9 0.7 copy-start.15
  42.1 59.2 %copy-start.1 = (f32[512,512]{1,0:T(8,128)S(1)}, f32[512,512]{1,0:T(8,128)}, u32[]{:S(2)}) copy-start(f32[512,512]{1,0:T(8,128)} %diag_ref.1) | copy-start | bytes 3145732
  42.1 54.7 %copy-start.11 = (f32[512,256]{1,0:T(8,128)S(1)}, f32[512,256]{1,0:T(8,128)}, u32[]{:S(2)}) copy-start(f32[512,256]{1,0:T(8,128)} %get-tuple-element.114.vec_ref) | copy-start | bytes 1572868 | tf_op jit(solution)/shard_map/cond
  43.3 53.5 %collective-permute-start.3 = (f32[7,128,128]{2,1,0:T(8,128)S(1)}, f32[7,128,128]{2,1,0:T(8,128)S(1)}, u32[]{:S(2)}, u32[]{:S(2)}) collective-permute-start(f32[7,128,128]{2,1,0:T(8,128)S(1)} %slice.19), channel_id=1, source_target_pairs={{1,33},{3,35},{5,37},{7,39},{9,41},{11,43},{13,45},{15,47},{17,49}... | collective-permute-start | bytes 1376264 | tf_op jit(solution)/shard_map/cond/branch_3_fun/ppermute | solution.py:162
  99.8 17.7 %copy-start.13 = (f32[512,512]{1,0:T(8,128)S(1)}, f32[512,512]{1,0:T(8,128)}, u32[]{:S(2)}) copy-start(f32[512,512]{1,0:T(8,128)} %get-tuple-element.154.pair_ref) | copy-start | bytes 3145732
  99.8 36.3 %collective-permute-start.14 = (f32[512,256]{1,0:T(8,128)}, f32[512,256]{1,0:T(8,128)S(1)}, u32[]{:S(2)}, u32[]{:S(2)}) collective-permute-start(f32[512,256]{1,0:T(8,128)} %get-tuple-element.156.back_ref), channel_id=1, source_target_pairs={{0,32},{2,34},{4,36},{6,38},{8,40},{10,42},{12,44},{14,46},{16,48}... | collective-permute-start | bytes 1572872 | tf_op jit(solution)/shard_map/ppermute | solution.py:172
  103.9 60.5 %collective-permute-start.17 = (f32[512,256]{1,0:T(8,128)S(1)}, f32[512,256]{1,0:T(8,128)S(1)}, u32[]{:S(2)}, u32[]{:S(2)}) collective-permute-start(f32[512,256]{1,0:T(8,128)S(1)} %get-tuple-element.153.base_ref), channel_id=1, source_target_pairs={{1,33},{3,35},{5,37},{7,39},{9,41},{11,43},{13,45},{15,47},{17,49}... | collective-permute-start | bytes 1572872 | tf_op jit(solution)/shard_map/ppermute | solution.py:158
  119.3 45.8 %collective-permute-start.18 = (f32[512,256]{1,0:T(8,128)S(1)}, f32[512,256]{1,0:T(8,128)S(1)}, u32[]{:S(2)}, u32[]{:S(2)}) collective-permute-start(f32[512,256]{1,0:T(8,128)S(1)} %get-tuple-element.157), channel_id=1, source_target_pairs={{0,32},{2,34},{4,36},{6,38},{8,40},{10,42},{12,44},{14,46},{16,48}... | collective-permute-start | bytes 1572872 | tf_op jit(solution)/shard_map/ppermute | solution.py:174
  136.2 22.3 %collective-permute-start.15 = (f32[256,256]{1,0:T(8,128)S(1)}, f32[256,256]{1,0:T(8,128)S(1)}, u32[]{:S(2)}, u32[]{:S(2)}) collective-permute-start(f32[256,256]{1,0:T(8,128)S(1)} %get-tuple-element.159), channel_id=1, source_target_pairs={{0,256},{64,320},{128,384},{192,448},{256,0},{320,64},{384,128},{4... | collective-permute-start | bytes 786440 | tf_op jit(solution)/shard_map/ppermute | solution.py:178
  154.8 8.6 %collective-permute-start.16 = (f32[256,256]{1,0:T(8,128)S(1)}, f32[256,256]{1,0:T(8,128)S(1)}, u32[]{:S(2)}, u32[]{:S(2)}) collective-permute-start(f32[256,256]{1,0:T(8,128)S(1)} %get-tuple-element.158), channel_id=1, source_target_pairs={{0,256},{64,320},{128,384},{192,448},{256,0},{320,64},{384,128},{4... | collective-permute-start | bytes 786440 | tf_op jit(solution)/shard_map/ppermute | solution.py:178
  163.4 1.0 copy-start.14
  164.4 1.1 copy-start.8

commit v8 on v6

--- a/solution.py
+++ b/solution.py
@@ -197,6 +197,7 @@
     )
     back_in = lax.ppermute(back, "slab", from_owner)
     first_own, back2 = local_call(first_kernel, (base, pair, vecs_in), (block, block))
+    back2, back_in = lax.optimization_barrier((back2, back_in))
     back2_in = lax.ppermute(back2, "slab", from_owner)
 
     far = local_call(far_kernel, (pair, base_in, back), block)

time: 160 us -> 155 us (0.969)
  the two profiles are of different devices: /device:TPU:57 before, /device:TPU:49 now
where the time goes in v8:
time: 155 us; the launch traced here: 154 us
  waiting for transfers between devices  75.2 us (49%)
  starting transfers between devices  51.9 us (33%)
  local copies, waits for them, and re-layouts  11.7 us (8%)
  Pallas kernels  11.5 us (7%)
  other arithmetic  3.05 us (2%)
    ppermute x1, waiting for transfers between devices, body(): back_in = lax.ppermute(back, 'slab', from_owner)  46.4 us
    ppermute x1, starting transfers between devices, body(): bulk_in = lax.ppermute(bulk, 'slab', to_owner)  15.4 us
    ppermute x1, starting transfers between devices, body(): base_in = lax.ppermute(base, 'slab', to_owner)  13.5 us
    pallas_call x7, Pallas kernels, local_call(): pl.pallas_call(kernel, out_shape=out_shape, in_specs=spaces, out_specs=(v...  11.5 us
    unnamed x32, local copies, waits for them, and re-layouts  10.9 us
    ppermute x2, waiting for transfers between devices, body(): grp_in = [lax.ppermute(x, 'grp', grp_pairs) for x in grp_blocks]  10.3 us
    ppermute x1, waiting for transfers between devices, body(): back2_in = lax.ppermute(back2, 'slab', from_owner)  8.02 us
    ppermute x2, starting transfers between devices, body(): lax.ppermute(x, 'grp', grp_pairs)  6.92 us
  transfers between devices with their start and end apart: 10, of which 7 were waited for; matrix products, arithmetic and copies ran while one was open for 2% of the time, Pallas kernels for 6%

profile of v8, /device:TPU:49, one launch (start us, length us, event | category | flops | bytes accessed | tf_op | source)
XLA Modules:
  0.0 154.2 jit_solution(2740251050355577711)
XLA Ops:
  0.0 1.3 copy-done.1
  2.0 1.7 %shard_map.66 = (f32[1544,128]{1,0:T(8,128)}, f32[4,128,128]{2,1,0:T(8,128)S(1)}) custom-call(s32[4,4]{1,0:T(4,128)S(1)} %copy-done.13, f32[512,512]{1,0:T(8,128)S(1)} %copy-done.1), custom_call_target="tpu_custom_call" | custom-call | flops 1000 | bytes 1000 | tf_op jit(solution)/shard_map/pallas_call | solution.py:129
  3.7 15.4 %collective-permute-start.4 = (f32[1544,128]{1,0:T(8,128)}, f32[1544,128]{1,0:T(8,128)}, u32[]{:S(2)}, u32[]{:S(2)}) collective-permute-start(f32[1544,128]{1,0:T(8,128)} %get-tuple-element.29), channel_id=1, source_target_pairs={{1,33},{3,35},{5,37},{7,39},{9,41},{11,43},{13,45},{15,47},{17,49}... | collective-permute-start | bytes 2371592 | tf_op jit(solution)/shard_map/ppermute | solution.py:164
  19.1 4.7 %collective-permute-start.1 = (f32[512,256]{1,0:T(8,128)S(1)}, f32[512,256]{1,0:T(8,128)S(1)}, u32[]{:S(2)}, u32[]{:S(2)}) collective-permute-start(f32[512,256]{1,0:T(8,128)S(1)} %copy-done), channel_id=1, source_target_pairs={{0,256},{64,320},{128,384},{192,448},{256,0},{320,64},{384,128},{4... | collective-permute-start | bytes 1572872 | tf_op jit(solution)/shard_map/ppermute | solution.py:153
  23.8 1.2 copy-done.5
  25.7 2.1 %collective-permute-start.2 = (f32[256,512]{1,0:T(8,128)S(1)}, f32[256,512]{1,0:T(8,128)}, u32[]{:S(2)}, u32[]{:S(2)}) collective-permute-start(f32[256,512]{1,0:T(8,128)S(1)} %get-tuple-element.24.refs_0_), channel_id=1, source_target_pairs={{0,256},{64,320},{128,384},{192,448},{256,0},{320,64},{384,128},{4... | collective-permute-start | bytes 1572872 | tf_op jit(solution)/shard_map/ppermute | solution.py:170
  28.6 4.7 %collective-permute-start.3 = (f32[256,512]{1,0:T(8,128)S(1)}, f32[256,512]{1,0:T(8,128)}, u32[]{:S(2)}, u32[]{:S(2)}) collective-permute-start(f32[256,512]{1,0:T(8,128)S(1)} %get-tuple-element.25.refs_1_), channel_id=1, source_target_pairs={{0,256},{64,320},{128,384},{192,448},{256,0},{320,64},{384,128},{4... | collective-permute-start | bytes 1572872 | tf_op jit(solution)/shard_map/ppermute | solution.py:170
  34.1 2.1 %collective-permute-start.5 = (f32[512,256]{1,0:T(8,128)S(1)}, f32[512,256]{1,0:T(8,128)}, u32[]{:S(2)}, u32[]{:S(2)}) collective-permute-start(f32[512,256]{1,0:T(8,128)S(1)} %copy-done), channel_id=1, source_target_pairs={{1,33},{3,35},{5,37},{7,39},{9,41},{11,43},{13,45},{15,47},{17,49}... | collective-permute-start | bytes 1572872 | tf_op jit(solution)/shard_map/ppermute | solution.py:154
  37.0 4.7 %collective-permute-done.2.refs_2_ = f32[256,512]{1,0:T(8,128)} collective-permute-done((f32[256,512]{1,0:T(8,128)S(1)}, f32[256,512]{1,0:T(8,128)}, u32[]{:S(2)}, u32[]{:S(2)}) %collective-permute-start.2) | collective-permute-done | bytes 524320 | tf_op jit(solution)/shard_map/ppermute | solution.py:170
  41.6 5.6 %collective-permute-done.3.refs_3_ = f32[256,512]{1,0:T(8,128)} collective-permute-done((f32[256,512]{1,0:T(8,128)S(1)}, f32[256,512]{1,0:T(8,128)}, u32[]{:S(2)}, u32[]{:S(2)}) %collective-permute-start.3) | collective-permute-done | bytes 524320 | tf_op jit(solution)/shard_map/ppermute | solution.py:170
  47.3 1.2 copy-done.6
  51.6 2.5 %shard_map.65 = (f32[512,256]{1,0:T(8,128)S(1)}, f32[512,512]{1,0:T(8,128)S(1)}, f32[512,512]{1,0:T(8,128)S(1)}) custom-call(f32[512,256]{1,0:T(8,128)S(1)} %copy-done, f32[512,512]{1,0:T(8,128)S(1)} %copy-done.6, f32[512,256]{1,0:T(8,128)S(1)} %copy-done.8, f32[256,512]{1,0:T(8,128)S(1)} %copy-done.10, f32[256,512]{1,0:T(8,128)S(1)} %copy-done.12, ...), custom_call_target="tpu_custom_call" | custom-call | flops 1000 | bytes 1000 | tf_op jit(solution)/shard_map/pallas_call | solution.py:129
  55.1 6.6 %collective-permute-done.4.bulk_ref = f32[1544,128]{1,0:T(8,128)} collective-permute-done((f32[1544,128]{1,0:T(8,128)}, f32[1544,128]{1,0:T(8,128)}, u32[]{:S(2)}, u32[]{:S(2)}) %collective-permute-start.4) | collective-permute-done | bytes 790560 | tf_op jit(solution)/shard_map/ppermute | solution.py:164
  62.4 1.3 select_reduce_fusion
  65.1 2.2 %shard_map.67 = (f32[512,512]{1,0:T(8,128)S(1)}, f32[512,256]{1,0:T(8,128)S(1)}) custom-call(s32[4,4]{1,0:T(4,128)S(1)} %copy-done.14, s32[4,4]{1,0:T(4,128)S(1)} %slice_convert_fusion.in_mask, f32[512,512]{1,0:T(8,128)S(1)} %copy-done.2, f32[1544,128]{1,0:T(8,128)} %collective-permute-done.4.bulk_ref, f32[4,128,128]{2,1,0:T(8,128)} %get-tuple-element.41.extra_ref, ...), custom_call_target="tpu_custom_call" | custom-call | flops 1000 | bytes 1000 | tf_op jit(solution)/shard_map/pallas_call | solution.py:129
  67.3 1.3 collective-permute-start.6
  68.6 13.5 %collective-permute-start.9 = (f32[512,256]{1,0:T(8,128)S(1)}, f32[512,256]{1,0:T(8,128)S(1)}, u32[]{:S(2)}, u32[]{:S(2)}) collective-permute-start(f32[512,256]{1,0:T(8,128)S(1)} %get-tuple-element.30.base_ref), channel_id=1, source_target_pairs={{1,33},{3,35},{5,37},{7,39},{9,41},{11,43},{13,45},{15,47},{17,49}... | collective-permute-start | bytes 1572872 | tf_op jit(solution)/shard_map/ppermute | solution.py:175
  82.1 2.9 %shard_map.68 = (f32[512,256]{1,0:T(8,128)S(1)}, f32[512,256]{1,0:T(8,128)S(1)}) custom-call(f32[512,256]{1,0:T(8,128)S(1)} %get-tuple-element.30.base_ref, f32[512,512]{1,0:T(8,128)S(1)} %get-tuple-element.33.pair_ref, f32[512,256]{1,0:T(8,128)} %collective-permute-done.5.vec_in_ref), custom_call_target="tpu_custom_call" | custom-call | flops 1000 | bytes 1000 | tf_op jit(solution)/shard_map/pallas_call | solution.py:129
  85.0 46.4 %collective-permute-done.6 = f32[512,256]{1,0:T(8,128)S(1)} collective-permute-done((f32[512,256]{1,0:T(8,128)S(1)}, f32[512,256]{1,0:T(8,128)S(1)}, u32[]{:S(2)}, u32[]{:S(2)}) %collective-permute-start.6) | collective-permute-done | bytes 524320 | tf_op jit(solution)/shard_map/ppermute | solution.py:198
  131.4 1.3 collective-permute-start.10
  132.9 1.9 %collective-permute-start.7 = (f32[256,256]{1,0:T(8,128)S(1)}, f32[256,256]{1,0:T(8,128)S(1)}, u32[]{:S(2)}, u32[]{:S(2)}) collective-permute-start(f32[256,256]{1,0:T(8,128)S(1)} %get-tuple-element.40), channel_id=1, source_target_pairs={{0,256},{64,320},{128,384},{192,448},{256,0},{320,64},{384,128},{4... | collective-permute-start | bytes 786440 | tf_op jit(solution)/shard_map/ppermute | solution.py:205
  134.8 5.0 %collective-permute-start.8 = (f32[256,256]{1,0:T(8,128)S(1)}, f32[256,256]{1,0:T(8,128)S(1)}, u32[]{:S(2)}, u32[]{:S(2)}) collective-permute-start(f32[256,256]{1,0:T(8,128)S(1)} %get-tuple-element.39), channel_id=1, source_target_pairs={{0,256},{64,320},{128,384},{192,448},{256,0},{320,64},{384,128},{4... | collective-permute-start | bytes 786440 | tf_op jit(solution)/shard_map/ppermute | solution.py:205
  141.5 2.8 %collective-permute-done.8.refs_1_ = f32[256,256]{1,0:T(8,128)S(1)} collective-permute-done((f32[256,256]{1,0:T(8,128)S(1)}, f32[256,256]{1,0:T(8,128)S(1)}, u32[]{:S(2)}, u32[]{:S(2)}) %collective-permute-start.8) | collective-permute-done | bytes 262176 | tf_op jit(solution)/shard_map/ppermute | solution.py:205
  145.3 8.0 %collective-permute-done.10 = f32[512,256]{1,0:T(8,128)S(1)} collective-permute-done((f32[512,256]{1,0:T(8,128)S(1)}, f32[512,256]{1,0:T(8,128)S(1)}, u32[]{:S(2)}, u32[]{:S(2)}) %collective-permute-start.10) | collective-permute-done | bytes 524320 | tf_op jit(solution)/shard_map/ppermute | solution.py:201
  (42 shorter events, 13.7 us)
Async XLA Ops:
  0.0 19.1 %copy-start = (f32[512,256]{1,0:T(8,128)S(1)}, f32[512,256]{1,0:T(8,128)}, u32[]{:S(2)}) copy-start(f32[512,256]{1,0:T(8,128)} %vec_ref.3) | copy-start | bytes 1572868
  0.0 1.3 copy-start.1
  2.0 21.8 %copy-start.15 = (s32[4,4]{1,0:T(4,128)S(1)}, s32[4,4]{1,0:T(4,128)}, u32[]{:S(2)}) copy-start(s32[4,4]{1,0:T(4,128)} %mask.1) | copy-start | bytes 196
  3.7 58.0 %collective-permute-start.4 = (f32[1544,128]{1,0:T(8,128)}, f32[1544,128]{1,0:T(8,128)}, u32[]{:S(2)}, u32[]{:S(2)}) collective-permute-start(f32[1544,128]{1,0:T(8,128)} %get-tuple-element.29), channel_id=1, source_target_pairs={{1,33},{3,35},{5,37},{7,39},{9,41},{11,43},{13,45},{15,47},{17,49}... | collective-permute-start | bytes 2371592 | tf_op jit(solution)/shard_map/ppermute | solution.py:164
  19.1 17.0 %collective-permute-start.1 = (f32[512,256]{1,0:T(8,128)S(1)}, f32[512,256]{1,0:T(8,128)S(1)}, u32[]{:S(2)}, u32[]{:S(2)}) collective-permute-start(f32[512,256]{1,0:T(8,128)S(1)} %copy-done), channel_id=1, source_target_pairs={{0,256},{64,320},{128,384},{192,448},{256,0},{320,64},{384,128},{4... | collective-permute-start | bytes 1572872 | tf_op jit(solution)/shard_map/ppermute | solution.py:153
  23.8 1.2 copy-start.5
  25.7 15.9 %collective-permute-start.2 = (f32[256,512]{1,0:T(8,128)S(1)}, f32[256,512]{1,0:T(8,128)}, u32[]{:S(2)}, u32[]{:S(2)}) collective-permute-start(f32[256,512]{1,0:T(8,128)S(1)} %get-tuple-element.24.refs_0_), channel_id=1, source_target_pairs={{0,256},{64,320},{128,384},{192,448},{256,0},{320,64},{384,128},{4... | collective-permute-start | bytes 1572872 | tf_op jit(solution)/shard_map/ppermute | solution.py:170
  27.8 0.8 copy-start.9
  28.6 18.6 %collective-permute-start.3 = (f32[256,512]{1,0:T(8,128)S(1)}, f32[256,512]{1,0:T(8,128)}, u32[]{:S(2)}, u32[]{:S(2)}) collective-permute-start(f32[256,512]{1,0:T(8,128)S(1)} %get-tuple-element.25.refs_1_), channel_id=1, source_target_pairs={{0,256},{64,320},{128,384},{192,448},{256,0},{320,64},{384,128},{4... | collective-permute-start | bytes 1572872 | tf_op jit(solution)/shard_map/ppermute | solution.py:170
  33.3 0.8 copy-start.11
  34.1 48.0 %collective-permute-start.5 = (f32[512,256]{1,0:T(8,128)S(1)}, f32[512,256]{1,0:T(8,128)}, u32[]{:S(2)}, u32[]{:S(2)}) collective-permute-start(f32[512,256]{1,0:T(8,128)S(1)} %copy-done), channel_id=1, source_target_pairs={{1,33},{3,35},{5,37},{7,39},{9,41},{11,43},{13,45},{15,47},{17,49}... | collective-permute-start | bytes 1572872 | tf_op jit(solution)/shard_map/ppermute | solution.py:154
  36.2 28.9 %copy-start.2 = (f32[512,512]{1,0:T(8,128)S(1)}, f32[512,512]{1,0:T(8,128)}, u32[]{:S(2)}) copy-start(f32[512,512]{1,0:T(8,128)} %own_ref.1) | copy-start | bytes 3145732
  36.2 0.8 copy-start.7
  47.3 1.2 copy-start.6
  48.5 1.0 copy-start.8
  49.5 1.0 copy-start.10
  50.6 1.0 copy-start.12
  54.1 1.0 copy-start.3
  67.3 64.1 %collective-permute-start.6 = (f32[512,256]{1,0:T(8,128)S(1)}, f32[512,256]{1,0:T(8,128)S(1)}, u32[]{:S(2)}, u32[]{:S(2)}) collective-permute-start(f32[512,256]{1,0:T(8,128)S(1)} %get-tuple-element.36.back_ref), channel_id=1, source_target_pairs={{0,32},{2,34},{4,36},{6,38},{8,40},{10,42},{12,44},{14,46},{16,48}... | collective-permute-start | bytes 1572872 | tf_op jit(solution)/shard_map/ppermute | solution.py:198
  68.6 71.2 %collective-permute-start.9 = (f32[512,256]{1,0:T(8,128)S(1)}, f32[512,256]{1,0:T(8,128)S(1)}, u32[]{:S(2)}, u32[]{:S(2)}) collective-permute-start(f32[512,256]{1,0:T(8,128)S(1)} %get-tuple-element.30.base_ref), channel_id=1, source_target_pairs={{1,33},{3,35},{5,37},{7,39},{9,41},{11,43},{13,45},{15,47},{17,49}... | collective-permute-start | bytes 1572872 | tf_op jit(solution)/shard_map/ppermute | solution.py:175
  131.4 21.9 %collective-permute-start.10 = (f32[512,256]{1,0:T(8,128)S(1)}, f32[512,256]{1,0:T(8,128)S(1)}, u32[]{:S(2)}, u32[]{:S(2)}) collective-permute-start(f32[512,256]{1,0:T(8,128)S(1)} %get-tuple-element.38), channel_id=1, source_target_pairs={{0,32},{2,34},{4,36},{6,38},{8,40},{10,42},{12,44},{14,46},{16,48}... | collective-permute-start | bytes 1572872 | tf_op jit(solution)/shard_map/ppermute | solution.py:201
  132.9 8.6 %collective-permute-start.7 = (f32[256,256]{1,0:T(8,128)S(1)}, f32[256,256]{1,0:T(8,128)S(1)}, u32[]{:S(2)}, u32[]{:S(2)}) collective-permute-start(f32[256,256]{1,0:T(8,128)S(1)} %get-tuple-element.40), channel_id=1, source_target_pairs={{0,256},{64,320},{128,384},{192,448},{256,0},{320,64},{384,128},{4... | collective-permute-start | bytes 786440 | tf_op jit(solution)/shard_map/ppermute | solution.py:205
  134.8 9.5 %copy-start.4 = (f32[512,512]{1,0:T(8,128)S(1)}, f32[512,512]{1,0:T(8,128)}, u32[]{:S(2)}) copy-start(f32[512,512]{1,0:T(8,128)} %copy-done.3) | copy-start | bytes 3145732
  134.8 9.5 %collective-permute-start.8 = (f32[256,256]{1,0:T(8,128)S(1)}, f32[256,256]{1,0:T(8,128)S(1)}, u32[]{:S(2)}, u32[]{:S(2)}) collective-permute-start(f32[256,256]{1,0:T(8,128)S(1)} %get-tuple-element.39), channel_id=1, source_target_pairs={{0,256},{64,320},{128,384},{192,448},{256,0},{320,64},{384,128},{4... | collective-permute-start | bytes 786440 | tf_op jit(solution)/shard_map/ppermute | solution.py:205
  (2 other events, 1.4 us)

commit v9 on v6

--- a/solution.py
+++ b/solution.py
@@ -12,6 +12,7 @@
 FIXED = 12
 COST = 1000
 GRP_CUTS = 2
+CUTS = 2
 
 
 def split(x):
@@ -64,7 +65,7 @@
             out_ref[top : top + tile, cols] = tiles_ref[i * tile : (i + 1) * tile, cols] * mask[i, j].astype(jnp.float32)
 
 
-def pair_kernel(tile, own_mask, in_mask, own_ref, bulk_ref, extra_ref, vec_ref, out_ref, back_ref):
+def pair_kernel(tile, own_mask, in_mask, own_ref, bulk_ref, extra_ref, vec_ref, out_ref, *back_refs):
     n = own_ref.shape[0] // tile
     for i in range(n):
         for j in range(n):
@@ -85,7 +86,10 @@
                 out_ref[to] += extra_ref[slot - FIXED].T
 
             slot = slot + stored.astype(jnp.int32)
-    back_ref[...] = product(split(out_ref[...].T), split(vec_ref[...]))
+    back, top = product(split(out_ref[...].T), split(vec_ref[...])), 0
+    for ref in back_refs:
+        ref[...] = back[top : top + ref.shape[0]]
+        top += ref.shape[0]
 
 
 def base_kernel(vec_ref, diag_ref, vec_grp_ref, *refs):
@@ -109,16 +113,24 @@
     back_ref[...] = product(split(pair.T), split(first))
 
 
-def near_kernel(sym_ref, across_ref, first_ref, *refs):
-    *first_grp_refs, near_ref = refs
-    first_grp = jnp.concatenate([ref[...] for ref in first_grp_refs], axis=0)
-    near_ref[...] = product(split(sym_ref[...]), split(first_ref[...])) + product(
-        split(across_ref[...]), split(first_grp)
-    )
-
-
-def far_kernel(pair_ref, base_in_ref, back_ref, far_ref):
-    first = (base_in_ref[...] + back_ref[...]) / HALF_SPAN
+def step_kernel(top, owner, own_ref, base_ref, back_ref, out_ref):
+    rows = slice(top, top + out_ref.shape[0])
+    stepped = (base_ref[rows] + back_ref[...]) / HALF_SPAN
+    out_ref[...] = jnp.where(owner[0, 0] > 0, own_ref[rows], stepped)
+
+
+def near_kernel(sym_ref, across_ref, *refs):
+    *first_refs, near_ref = refs
+    half = len(first_refs) // 2
+    first, first_grp = (
+        jnp.concatenate([ref[...] for ref in part], axis=0) for part in (first_refs[:half], first_refs[half:])
+    )
+    near_ref[...] = product(split(sym_ref[...]), split(first)) + product(split(across_ref[...]), split(first_grp))
+
+
+def far_kernel(pair_ref, base_in_ref, *refs):
+    *back_refs, far_ref = refs
+    first = (base_in_ref[...] + jnp.concatenate([ref[...] for ref in back_refs], axis=0)) / HALF_SPAN
     far_ref[...] = product(split(pair_ref[...]), split(first))
 
 
@@ -190,19 +202,27 @@
     which = sum((over > k).astype(jnp.int32) for k in sizes[:-1])
     extra_in = lax.switch(which, [send(k) for k in sizes], extra)
 
-    pair, back = local_call(
+    half_block = jax.ShapeDtypeStruct((rows // CUTS, vectors.shape[1]), f32)
+    pair, *back = local_call(
         functools.partial(pair_kernel, tile),
         (slab_mask, mask_in, slab_tiles, bulk_in, extra_in, vectors),
-        (square, block),
-    )
-    back_in = lax.ppermute(back, "slab", from_owner)
+        (square,) + (half_block,) * CUTS,
+    )
+    back_in = [lax.ppermute(x, "slab", from_owner) for x in back]
     first_own, back2 = local_call(first_kernel, (base, pair, vecs_in), (block, block))
+    back2, back_in[0] = lax.optimization_barrier((back2, back_in[0]))
     back2_in = lax.ppermute(back2, "slab", from_owner)
 
-    far = local_call(far_kernel, (pair, base_in, back), block)
-    first = jnp.where(owner, first_own, (base + back_in) / HALF_SPAN)
-    first_grp = [lax.ppermute(x, "grp", grp_pairs) for x in jnp.split(first, 2, axis=0)]
-    near = local_call(near_kernel, (sym, across, first, *first_grp), block)
+    far = local_call(far_kernel, (pair, base_in, *back), block)
+    role = owner.astype(jnp.int32).reshape(1, 1)
+    first = [
+        local_call(
+            functools.partial(step_kernel, at * half_block.shape[0]), (role, first_own, base, got), half_block
+        )
+        for at, got in enumerate(back_in)
+    ]
+    first_grp = [lax.ppermute(x, "grp", grp_pairs) for x in first]
+    near = local_call(near_kernel, (sym, across, *first, *first_grp), block)
     total = near + jnp.where(owner, far, back2_in)
     return 2.0 * total / HALF_SPAN - vectors
 

time: 160 us -> 164 us (1.025)
  the two profiles are of different devices: /device:TPU:57 before, /device:TPU:40 now
where the time goes in v9:
time: 164 us; the launch traced here: 163 us
  waiting for transfers between devices  79.9 us (49%)
  starting transfers between devices  53.9 us (33%)
  Pallas kernels  16.4 us (10%)
  local copies, waits for them, and re-layouts  9.33 us (6%)
  other arithmetic  2.95 us (2%)
    ppermute x2, waiting for transfers between devices, body(): back_in = [lax.ppermute(x, 'slab', from_owner) for x in back]  40.1 us
    ppermute x1, waiting for transfers between devices, body(): bulk_in = lax.ppermute(bulk, 'slab', to_owner)  18.8 us
    pallas_call x9, Pallas kernels, local_call(): pl.pallas_call(kernel, out_shape=out_shape, in_specs=spaces, out_specs=(v...  16.4 us
    ppermute x2, starting transfers between devices, body(): back_in = [lax.ppermute(x, 'slab', from_owner) for x in back]  16.3 us
    ppermute x2, waiting for transfers between devices, body(): grp_in = [lax.ppermute(x, 'grp', grp_pairs) for x in grp_blocks]  15.2 us
    ppermute x1, starting transfers between devices, body(): back2_in = lax.ppermute(back2, 'slab', from_owner)  13.9 us
    unnamed x32, local copies, waits for them, and re-layouts  8.63 us
    ppermute x2, starting transfers between devices, body(): first_grp = [lax.ppermute(x, 'grp', grp_pairs) for x in first]  7.48 us
  transfers between devices with their start and end apart: 11, of which 6 were waited for; matrix products, arithmetic and copies ran while one was open for 2% of the time, Pallas kernels for 9%

profile of v9, /device:TPU:40, one launch (start us, length us, event | category | flops | bytes accessed | tf_op | source)
XLA Modules:
  0.0 163.3 jit_solution(5213880738975890188)
XLA Ops:
  0.0 1.3 copy-done.1
  2.0 1.7 %shard_map.66 = (f32[1544,128]{1,0:T(8,128)}, f32[4,128,128]{2,1,0:T(8,128)S(1)}) custom-call(s32[4,4]{1,0:T(4,128)S(1)} %copy-done.13, f32[512,512]{1,0:T(8,128)S(1)} %copy-done.1), custom_call_target="tpu_custom_call" | custom-call | flops 1000 | bytes 1000 | tf_op jit(solution)/shard_map/pallas_call | solution.py:141
  3.7 1.3 collective-permute-start.4
  5.0 4.9 %collective-permute-start.1 = (f32[512,256]{1,0:T(8,128)S(1)}, f32[512,256]{1,0:T(8,128)S(1)}, u32[]{:S(2)}, u32[]{:S(2)}) collective-permute-start(f32[512,256]{1,0:T(8,128)S(1)} %copy-done), channel_id=1, source_target_pairs={{0,256},{64,320},{128,384},{192,448},{256,0},{320,64},{384,128},{4... | collective-permute-start | bytes 1572872 | tf_op jit(solution)/shard_map/ppermute | solution.py:165
  11.2 1.7 %shard_map.64 = (f32[256,512]{1,0:T(8,128)}, f32[256,512]{1,0:T(8,128)}) custom-call(s32[4,4]{1,0:T(4,128)S(1)} %copy-done.15, f32[512,512]{1,0:T(8,128)S(1)} %copy-done.7), custom_call_target="tpu_custom_call" | custom-call | flops 1000 | bytes 1000 | tf_op jit(solution)/shard_map/pallas_call | solution.py:141
  12.8 2.4 %collective-permute-start.2 = (f32[256,512]{1,0:T(8,128)}, f32[256,512]{1,0:T(8,128)}, u32[]{:S(2)}, u32[]{:S(2)}) collective-permute-start(f32[256,512]{1,0:T(8,128)} %get-tuple-element.25.refs_0_), channel_id=1, source_target_pairs={{0,256},{64,320},{128,384},{192,448},{256,0},{320,64},{384,128},{4... | collective-permute-start | bytes 1572872 | tf_op jit(solution)/shard_map/ppermute | solution.py:182
  15.2 4.9 %collective-permute-start.3 = (f32[256,512]{1,0:T(8,128)}, f32[256,512]{1,0:T(8,128)}, u32[]{:S(2)}, u32[]{:S(2)}) collective-permute-start(f32[256,512]{1,0:T(8,128)} %get-tuple-element.26.refs_1_), channel_id=1, source_target_pairs={{0,256},{64,320},{128,384},{192,448},{256,0},{320,64},{384,128},{4... | collective-permute-start | bytes 1572872 | tf_op jit(solution)/shard_map/ppermute | solution.py:182
  20.2 1.3 collective-permute-start.5
  22.3 4.0 %collective-permute-done.2.refs_2_ = f32[256,512]{1,0:T(8,128)} collective-permute-done((f32[256,512]{1,0:T(8,128)}, f32[256,512]{1,0:T(8,128)}, u32[]{:S(2)}, u32[]{:S(2)}) %collective-permute-start.2) | collective-permute-done | bytes 524320 | tf_op jit(solution)/shard_map/ppermute | solution.py:182
  26.3 11.2 %collective-permute-done.3.refs_3_ = f32[256,512]{1,0:T(8,128)} collective-permute-done((f32[256,512]{1,0:T(8,128)}, f32[256,512]{1,0:T(8,128)}, u32[]{:S(2)}, u32[]{:S(2)}) %collective-permute-start.3) | collective-permute-done | bytes 524320 | tf_op jit(solution)/shard_map/ppermute | solution.py:182
  38.6 2.8 %shard_map.65 = (f32[512,256]{1,0:T(8,128)S(1)}, f32[512,512]{1,0:T(8,128)S(1)}, f32[512,512]{1,0:T(8,128)S(1)}) custom-call(f32[512,256]{1,0:T(8,128)S(1)} %copy-done, f32[512,512]{1,0:T(8,128)S(1)} %copy-done.8, f32[512,256]{1,0:T(8,128)S(1)} %copy-done.10, f32[256,512]{1,0:T(8,128)} %get-tuple-element.25.refs_0_, f32[256,512]{1,0:T(8,128)} %get-tuple-element.26.refs_1_, ...), custom_call_target="tpu_custom_call" | custom-call | flops 1000 | bytes 1000 | tf_op jit(solution)/shard_map/pallas_call | solution.py:141
  43.3 18.8 %collective-permute-done.4.bulk_ref = f32[1544,128]{1,0:T(8,128)} collective-permute-done((f32[1544,128]{1,0:T(8,128)}, f32[1544,128]{1,0:T(8,128)}, u32[]{:S(2)}, u32[]{:S(2)}) %collective-permute-start.4) | collective-permute-done | bytes 790560 | tf_op jit(solution)/shard_map/ppermute | solution.py:176
  62.1 1.3 select_reduce_fusion
  65.5 3.7 %shard_map.67 = (f32[512,512]{1,0:T(8,128)S(1)}, f32[256,256]{1,0:T(8,128)S(1)}, f32[256,256]{1,0:T(8,128)}) custom-call(s32[4,4]{1,0:T(4,128)S(1)} %copy-done.14, s32[4,4]{1,0:T(4,128)S(1)} %slice_convert_fusion.in_mask, f32[512,512]{1,0:T(8,128)S(1)} %copy-done.2, f32[1544,128]{1,0:T(8,128)} %collective-permute-done.4.bulk_ref, ...), custom_call_target="tpu_custom_call" | custom-call | flops 1000 | bytes 1000 | tf_op jit(solution)/shard_map/pallas_call | solution.py:141
  69.2 2.3 %collective-permute-start.6 = (f32[256,256]{1,0:T(8,128)S(1)}, f32[256,256]{1,0:T(8,128)S(1)}, u32[]{:S(2)}, u32[]{:S(2)}) collective-permute-start(f32[256,256]{1,0:T(8,128)S(1)} %get-tuple-element.37.refs_0_), channel_id=1, source_target_pairs={{0,32},{2,34},{4,36},{6,38},{8,40},{10,42},{12,44},{14,46},{16,48}... | collective-permute-start | bytes 786440 | tf_op jit(solution)/shard_map/ppermute | solution.py:211
  71.5 1.3 collective-permute-start.10
  72.8 14.1 %collective-permute-start.7 = (f32[256,256]{1,0:T(8,128)}, f32[256,256]{1,0:T(8,128)S(1)}, u32[]{:S(2)}, u32[]{:S(2)}) collective-permute-start(f32[256,256]{1,0:T(8,128)} %get-tuple-element.39.refs_1_), channel_id=1, source_target_pairs={{0,32},{2,34},{4,36},{6,38},{8,40},{10,42},{12,44},{14,46},{16,48}... | collective-permute-start | bytes 786440 | tf_op jit(solution)/shard_map/ppermute | solution.py:211
  86.9 3.7 %shard_map.68 = (f32[512,256]{1,0:T(8,128)S(1)}, f32[512,256]{1,0:T(8,128)}) custom-call(f32[512,256]{1,0:T(8,128)S(1)} %get-tuple-element.31.base_ref, f32[512,512]{1,0:T(8,128)S(1)} %get-tuple-element.34.pair_ref, f32[512,256]{1,0:T(8,128)} %collective-permute-done.5.vec_in_ref), custom_call_target="tpu_custom_call" | custom-call | flops 1000 | bytes 1000 | tf_op jit(solution)/shard_map/pallas_call | solution.py:141
  90.6 40.1 %collective-permute-done.6.back_ref = f32[256,256]{1,0:T(8,128)S(1)} collective-permute-done((f32[256,256]{1,0:T(8,128)S(1)}, f32[256,256]{1,0:T(8,128)S(1)}, u32[]{:S(2)}, u32[]{:S(2)}) %collective-permute-start.6) | collective-permute-done | bytes 262176 | tf_op jit(solution)/shard_map/ppermute | solution.py:211
  131.4 13.9 %collective-permute-start.11 = (f32[512,256]{1,0:T(8,128)}, f32[512,256]{1,0:T(8,128)}, u32[]{:S(2)}, u32[]{:S(2)}) collective-permute-start(f32[512,256]{1,0:T(8,128)} %get-tuple-element.40), channel_id=1, source_target_pairs={{0,32},{2,34},{4,36},{6,38},{8,40},{10,42},{12,44},{14,46},{16,48}... | collective-permute-start | bytes 1572872 | tf_op jit(solution)/shard_map/ppermute | solution.py:214
  146.3 5.1 %collective-permute-start.8 = (f32[256,256]{1,0:T(8,128)S(1)}, f32[256,256]{1,0:T(8,128)S(1)}, u32[]{:S(2)}, u32[]{:S(2)}) collective-permute-start(f32[256,256]{1,0:T(8,128)S(1)} %shard_map.69.refs_0_), channel_id=1, source_target_pairs={{0,256},{64,320},{128,384},{192,448},{256,0},{320,64},{384,128},{4... | collective-permute-start | bytes 786440 | tf_op jit(solution)/shard_map/ppermute | solution.py:224
  151.5 2.4 %collective-permute-start.9 = (f32[256,256]{1,0:T(8,128)S(1)}, f32[256,256]{1,0:T(8,128)S(1)}, u32[]{:S(2)}, u32[]{:S(2)}) collective-permute-start(f32[256,256]{1,0:T(8,128)S(1)} %shard_map.70.refs_1_), channel_id=1, source_target_pairs={{0,256},{64,320},{128,384},{192,448},{256,0},{320,64},{384,128},{4... | collective-permute-start | bytes 786440 | tf_op jit(solution)/shard_map/ppermute | solution.py:224
  153.9 1.7 %shard_map.72 = f32[512,256]{1,0:T(8,128)S(1)} custom-call(f32[512,512]{1,0:T(8,128)S(1)} %get-tuple-element.34.pair_ref, f32[512,256]{1,0:T(8,128)} %collective-permute-done.10.base_in_ref, f32[256,256]{1,0:T(8,128)S(1)} %get-tuple-element.37.refs_0_, f32[256,256]{1,0:T(8,128)} %get-tuple-element.39.refs_1_), custom_call_target="tpu_custom_call" | custom-call | flops 1000 | bytes 1000 | tf_op jit(solution)/shard_map/pallas_call | solution.py:141
  156.3 5.1 %collective-permute-done.9.refs_3_ = f32[256,256]{1,0:T(8,128)S(1)} collective-permute-done((f32[256,256]{1,0:T(8,128)S(1)}, f32[256,256]{1,0:T(8,128)S(1)}, u32[]{:S(2)}, u32[]{:S(2)}) %collective-permute-start.9) | collective-permute-done | bytes 262176 | tf_op jit(solution)/shard_map/ppermute | solution.py:224
  (44 shorter events, 12.1 us)
Async XLA Ops:
  0.0 5.0 %copy-start = (f32[512,256]{1,0:T(8,128)S(1)}, f32[512,256]{1,0:T(8,128)}, u32[]{:S(2)}) copy-start(f32[512,256]{1,0:T(8,128)} %vec_ref.3) | copy-start | bytes 1572868
  0.0 1.3 copy-start.1
  2.0 7.9 %copy-start.15 = (s32[4,4]{1,0:T(4,128)S(1)}, s32[4,4]{1,0:T(4,128)}, u32[]{:S(2)}) copy-start(s32[4,4]{1,0:T(4,128)} %mask.1) | copy-start | bytes 196
  3.7 58.5 %collective-permute-start.4 = (f32[1544,128]{1,0:T(8,128)}, f32[1544,128]{1,0:T(8,128)}, u32[]{:S(2)}, u32[]{:S(2)}) collective-permute-start(f32[1544,128]{1,0:T(8,128)} %get-tuple-element.30), channel_id=1, source_target_pairs={{1,33},{3,35},{5,37},{7,39},{9,41},{11,43},{13,45},{15,47},{17,49}... | collective-permute-start | bytes 2371592 | tf_op jit(solution)/shard_map/ppermute | solution.py:176
  5.0 16.5 %collective-permute-start.1 = (f32[512,256]{1,0:T(8,128)S(1)}, f32[512,256]{1,0:T(8,128)S(1)}, u32[]{:S(2)}, u32[]{:S(2)}) collective-permute-start(f32[512,256]{1,0:T(8,128)S(1)} %copy-done), channel_id=1, source_target_pairs={{0,256},{64,320},{128,384},{192,448},{256,0},{320,64},{384,128},{4... | collective-permute-start | bytes 1572872 | tf_op jit(solution)/shard_map/ppermute | solution.py:165
  9.9 1.2 copy-start.7
  11.2 26.4 %copy-start.8 = (f32[512,512]{1,0:T(8,128)S(1)}, f32[512,512]{1,0:T(8,128)}, u32[]{:S(2)}) copy-start(f32[512,512]{1,0:T(8,128)} %diag_ref.1) | copy-start | bytes 3145732
  12.8 13.5 %collective-permute-start.2 = (f32[256,512]{1,0:T(8,128)}, f32[256,512]{1,0:T(8,128)}, u32[]{:S(2)}, u32[]{:S(2)}) collective-permute-start(f32[256,512]{1,0:T(8,128)} %get-tuple-element.25.refs_0_), channel_id=1, source_target_pairs={{0,256},{64,320},{128,384},{192,448},{256,0},{320,64},{384,128},{4... | collective-permute-start | bytes 1572872 | tf_op jit(solution)/shard_map/ppermute | solution.py:182
  15.2 22.3 %collective-permute-start.3 = (f32[256,512]{1,0:T(8,128)}, f32[256,512]{1,0:T(8,128)}, u32[]{:S(2)}, u32[]{:S(2)}) collective-permute-start(f32[256,512]{1,0:T(8,128)} %get-tuple-element.26.refs_1_), channel_id=1, source_target_pairs={{0,256},{64,320},{128,384},{192,448},{256,0},{320,64},{384,128},{4... | collective-permute-start | bytes 1572872 | tf_op jit(solution)/shard_map/ppermute | solution.py:182
  20.2 66.7 %collective-permute-start.5 = (f32[512,256]{1,0:T(8,128)S(1)}, f32[512,256]{1,0:T(8,128)}, u32[]{:S(2)}, u32[]{:S(2)}) collective-permute-start(f32[512,256]{1,0:T(8,128)S(1)} %copy-done), channel_id=1, source_target_pairs={{1,33},{3,35},{5,37},{7,39},{9,41},{11,43},{13,45},{15,47},{17,49}... | collective-permute-start | bytes 1572872 | tf_op jit(solution)/shard_map/ppermute | solution.py:166
  21.5 44.0 %copy-start.2 = (f32[512,512]{1,0:T(8,128)S(1)}, f32[512,512]{1,0:T(8,128)}, u32[]{:S(2)}) copy-start(f32[512,512]{1,0:T(8,128)} %own_ref.1) | copy-start | bytes 3145732
  37.5 1.0 copy-start.10
  38.6 23.6 %copy-start.14 = (s32[4,4]{1,0:T(4,128)S(1)}, s32[4,4]{1,0:T(4,128)}, u32[]{:S(2)}) copy-start(s32[4,4]{1,0:T(4,128)} %own_mask.1) | copy-start | bytes 196
  41.4 1.0 copy-start.3
  42.4 1.0 copy-start.5
  69.2 61.5 %collective-permute-start.6 = (f32[256,256]{1,0:T(8,128)S(1)}, f32[256,256]{1,0:T(8,128)S(1)}, u32[]{:S(2)}, u32[]{:S(2)}) collective-permute-start(f32[256,256]{1,0:T(8,128)S(1)} %get-tuple-element.37.refs_0_), channel_id=1, source_target_pairs={{0,32},{2,34},{4,36},{6,38},{8,40},{10,42},{12,44},{14,46},{16,48}... | collective-permute-start | bytes 786440 | tf_op jit(solution)/shard_map/ppermute | solution.py:211
  71.5 82.4 %collective-permute-start.10 = (f32[512,256]{1,0:T(8,128)S(1)}, f32[512,256]{1,0:T(8,128)}, u32[]{:S(2)}, u32[]{:S(2)}) collective-permute-start(f32[512,256]{1,0:T(8,128)S(1)} %get-tuple-element.31.base_ref), channel_id=1, source_target_pairs={{1,33},{3,35},{5,37},{7,39},{9,41},{11,43},{13,45},{15,47},{17,49}... | collective-permute-start | bytes 1572872 | tf_op jit(solution)/shard_map/ppermute | solution.py:187
  72.8 78.6 %collective-permute-start.7 = (f32[256,256]{1,0:T(8,128)}, f32[256,256]{1,0:T(8,128)S(1)}, u32[]{:S(2)}, u32[]{:S(2)}) collective-permute-start(f32[256,256]{1,0:T(8,128)} %get-tuple-element.39.refs_1_), channel_id=1, source_target_pairs={{0,32},{2,34},{4,36},{6,38},{8,40},{10,42},{12,44},{14,46},{16,48}... | collective-permute-start | bytes 786440 | tf_op jit(solution)/shard_map/ppermute | solution.py:211
  131.4 31.0 %collective-permute-start.11 = (f32[512,256]{1,0:T(8,128)}, f32[512,256]{1,0:T(8,128)}, u32[]{:S(2)}, u32[]{:S(2)}) collective-permute-start(f32[512,256]{1,0:T(8,128)} %get-tuple-element.40), channel_id=1, source_target_pairs={{0,32},{2,34},{4,36},{6,38},{8,40},{10,42},{12,44},{14,46},{16,48}... | collective-permute-start | bytes 1572872 | tf_op jit(solution)/shard_map/ppermute | solution.py:214
  145.3 0.9 copy-start.12
  146.3 10.0 %collective-permute-start.8 = (f32[256,256]{1,0:T(8,128)S(1)}, f32[256,256]{1,0:T(8,128)S(1)}, u32[]{:S(2)}, u32[]{:S(2)}) collective-permute-start(f32[256,256]{1,0:T(8,128)S(1)} %shard_map.69.refs_0_), channel_id=1, source_target_pairs={{0,256},{64,320},{128,384},{192,448},{256,0},{320,64},{384,128},{4... | collective-permute-start | bytes 786440 | tf_op jit(solution)/shard_map/ppermute | solution.py:224
  151.5 9.9 %copy-start.4 = (f32[512,512]{1,0:T(8,128)S(1)}, f32[512,512]{1,0:T(8,128)}, u32[]{:S(2)}) copy-start(f32[512,512]{1,0:T(8,128)} %copy-done.3) | copy-start | bytes 3145732
  151.5 9.9 %copy-start.6 = (f32[512,512]{1,0:T(8,128)S(1)}, f32[512,512]{1,0:T(8,128)}, u32[]{:S(2)}) copy-start(f32[512,512]{1,0:T(8,128)} %copy-done.5) | copy-start | bytes 3145732
  151.5 9.9 %collective-permute-start.9 = (f32[256,256]{1,0:T(8,128)S(1)}, f32[256,256]{1,0:T(8,128)S(1)}, u32[]{:S(2)}, u32[]{:S(2)}) collective-permute-start(f32[256,256]{1,0:T(8,128)S(1)} %shard_map.70.refs_1_), channel_id=1, source_target_pairs={{0,256},{64,320},{128,384},{192,448},{256,0},{320,64},{384,128},{4... | collective-permute-start | bytes 786440 | tf_op jit(solution)/shard_map/ppermute | solution.py:224
  (3 other events, 2.2 us)

commit v10 on v6

--- a/solution.py
+++ b/solution.py
@@ -102,11 +102,12 @@
     base_ref[...] = product(split(sym), split(vec_ref[...])) + product(split(across), split(vec_grp_ref[...]))
 
 
-def first_kernel(base_ref, pair_ref, vec_in_ref, first_ref, back_ref):
-    pair = pair_ref[...]
-    first = (base_ref[...] + product(split(pair), split(vec_in_ref[...]))) / HALF_SPAN
+def first_kernel(base_ref, pair_ref, vec_in_ref, base_in_ref, back_ref, first_ref, back2_ref, far_ref):
+    pair = split(pair_ref[...])
+    first = (base_ref[...] + product(pair, split(vec_in_ref[...]))) / HALF_SPAN
     first_ref[...] = first
-    back_ref[...] = product(split(pair.T), split(first))
+    back2_ref[...] = product(split(pair_ref[...].T), split(first))
+    far_ref[...] = product(pair, split((base_in_ref[...] + back_ref[...]) / HALF_SPAN))
 
 
 def near_kernel(sym_ref, across_ref, first_ref, *refs):
@@ -115,11 +116,6 @@
     near_ref[...] = product(split(sym_ref[...]), split(first_ref[...])) + product(
         split(across_ref[...]), split(first_grp)
     )
-
-
-def far_kernel(pair_ref, base_in_ref, back_ref, far_ref):
-    first = (base_in_ref[...] + back_ref[...]) / HALF_SPAN
-    far_ref[...] = product(split(pair_ref[...]), split(first))
 
 
 def local_call(kernel, ins, out_shape):
@@ -196,10 +192,9 @@
         (square, block),
     )
     back_in = lax.ppermute(back, "slab", from_owner)
-    first_own, back2 = local_call(first_kernel, (base, pair, vecs_in), (block, block))
+    first_own, back2, far = local_call(first_kernel, (base, pair, vecs_in, base_in, back), (block,) * 3)
     back2_in = lax.ppermute(back2, "slab", from_owner)
 
-    far = local_call(far_kernel, (pair, base_in, back), block)
     first = jnp.where(owner, first_own, (base + back_in) / HALF_SPAN)
     first_grp = [lax.ppermute(x, "grp", grp_pairs) for x in jnp.split(first, 2, axis=0)]
     near = local_call(near_kernel, (sym, across, first, *first_grp), block)

time: 160 us -> 158 us (0.988)
  the two profiles are of different devices: /device:TPU:57 before, /device:TPU:120 now
where the time goes in v10:
time: 158 us
  waiting for transfers between devices  83.8 us (53%)
  starting transfers between devices  46.6 us (29%)
  local copies, waits for them, and re-layouts  11.7 us (7%)
  Pallas kernels  11.6 us (7%)
  other arithmetic  3.04 us (2%)
    ppermute x1, waiting for transfers between devices, body(): base_in = lax.ppermute(base, 'slab', to_owner)  61.7 us
    ppermute x1, starting transfers between devices, body(): back_in = lax.ppermute(back, 'slab', from_owner)  20.6 us
    ppermute x2, waiting for transfers between devices, body(): grp_in = [lax.ppermute(x, 'grp', grp_pairs) for x in grp_blocks]  14 us
    pallas_call x6, Pallas kernels, local_call(): pl.pallas_call(kernel, out_shape=out_shape, in_specs=spaces, out_specs=(v...  11.6 us
    unnamed x32, local copies, waits for them, and re-layouts  10.9 us
    ppermute x2, starting transfers between devices, body(): lax.ppermute(x, 'grp', grp_pairs)  8.44 us
    ppermute x2, waiting for transfers between devices, body(): lax.ppermute(x, 'grp', grp_pairs)  8.02 us
    ppermute x2, starting transfers between devices, body(): grp_in = [lax.ppermute(x, 'grp', grp_pairs) for x in grp_blocks]  7.34 us
  transfers between devices with their start and end apart: 10, of which 5 were waited for; matrix products, arithmetic and copies ran while one was open for 2% of the time, Pallas kernels for 6%

profile of v10, /device:TPU:120, one launch (start us, length us, event | category | flops | bytes accessed | tf_op | source)
XLA Modules:
  0.0 157.7 jit_solution(13044195999927442726)
XLA Ops:
  0.0 1.3 copy-done.1
  2.0 1.7 %shard_map.66 = (f32[1544,128]{1,0:T(8,128)}, f32[4,128,128]{2,1,0:T(8,128)S(1)}) custom-call(s32[4,4]{1,0:T(4,128)S(1)} %copy-done.13, f32[512,512]{1,0:T(8,128)S(1)} %copy-done.1), custom_call_target="tpu_custom_call" | custom-call | flops 1000 | bytes 1000 | tf_op jit(solution)/shard_map/pallas_call | solution.py:125
  3.7 1.3 collective-permute-start.4
  5.0 4.9 %collective-permute-start.1 = (f32[512,256]{1,0:T(8,128)S(1)}, f32[512,256]{1,0:T(8,128)S(1)}, u32[]{:S(2)}, u32[]{:S(2)}) collective-permute-start(f32[512,256]{1,0:T(8,128)S(1)} %copy-done), channel_id=1, source_target_pairs={{0,256},{64,320},{128,384},{192,448},{256,0},{320,64},{384,128},{4... | collective-permute-start | bytes 1572872 | tf_op jit(solution)/shard_map/ppermute | solution.py:149
  10.0 1.2 copy-done.5
  11.8 2.4 %collective-permute-start.2 = (f32[256,512]{1,0:T(8,128)S(1)}, f32[256,512]{1,0:T(8,128)}, u32[]{:S(2)}, u32[]{:S(2)}) collective-permute-start(f32[256,512]{1,0:T(8,128)S(1)} %get-tuple-element.23.refs_0_), channel_id=1, source_target_pairs={{0,256},{64,320},{128,384},{192,448},{256,0},{320,64},{384,128},{4... | collective-permute-start | bytes 1572872 | tf_op jit(solution)/shard_map/ppermute | solution.py:166
  15.1 4.9 %collective-permute-start.3 = (f32[256,512]{1,0:T(8,128)S(1)}, f32[256,512]{1,0:T(8,128)}, u32[]{:S(2)}, u32[]{:S(2)}) collective-permute-start(f32[256,512]{1,0:T(8,128)S(1)} %get-tuple-element.24.refs_1_), channel_id=1, source_target_pairs={{0,256},{64,320},{128,384},{192,448},{256,0},{320,64},{384,128},{4... | collective-permute-start | bytes 1572872 | tf_op jit(solution)/shard_map/ppermute | solution.py:166
  20.8 1.3 collective-permute-start.5
  22.9 2.8 %collective-permute-done.2.refs_2_ = f32[256,512]{1,0:T(8,128)} collective-permute-done((f32[256,512]{1,0:T(8,128)S(1)}, f32[256,512]{1,0:T(8,128)}, u32[]{:S(2)}, u32[]{:S(2)}) %collective-permute-start.2) | collective-permute-done | bytes 524320 | tf_op jit(solution)/shard_map/ppermute | solution.py:166
  25.7 11.2 %collective-permute-done.3.refs_3_ = f32[256,512]{1,0:T(8,128)} collective-permute-done((f32[256,512]{1,0:T(8,128)S(1)}, f32[256,512]{1,0:T(8,128)}, u32[]{:S(2)}, u32[]{:S(2)}) %collective-permute-start.3) | collective-permute-done | bytes 524320 | tf_op jit(solution)/shard_map/ppermute | solution.py:166
  37.0 1.2 copy-done.6
  38.2 1.0 copy-done.8
  41.3 2.5 %shard_map.65 = (f32[512,256]{1,0:T(8,128)S(1)}, f32[512,512]{1,0:T(8,128)S(1)}, f32[512,512]{1,0:T(8,128)S(1)}) custom-call(f32[512,256]{1,0:T(8,128)S(1)} %copy-done, f32[512,512]{1,0:T(8,128)S(1)} %copy-done.6, f32[512,256]{1,0:T(8,128)S(1)} %copy-done.8, f32[256,512]{1,0:T(8,128)S(1)} %copy-done.10, f32[256,512]{1,0:T(8,128)S(1)} %copy-done.12, ...), custom_call_target="tpu_custom_call" | custom-call | flops 1000 | bytes 1000 | tf_op jit(solution)/shard_map/pallas_call | solution.py:125
  44.8 1.4 collective-permute-start.6
  46.9 1.3 select_reduce_fusion
  49.6 3.1 %shard_map.67 = (f32[512,512]{1,0:T(8,128)S(1)}, f32[512,256]{1,0:T(8,128)S(1)}) custom-call(s32[4,4]{1,0:T(4,128)S(1)} %copy-done.14, s32[4,4]{1,0:T(4,128)S(1)} %slice_convert_fusion.in_mask, f32[512,512]{1,0:T(8,128)S(1)} %copy-done.2, f32[1544,128]{1,0:T(8,128)} %collective-permute-done.4.bulk_ref, f32[4,128,128]{2,1,0:T(8,128)} %get-tuple-element.39.extra_ref, ...), custom_call_target="tpu_custom_call" | custom-call | flops 1000 | bytes 1000 | tf_op jit(solution)/shard_map/pallas_call | solution.py:125
  52.7 20.6 %collective-permute-start.7 = (f32[512,256]{1,0:T(8,128)S(1)}, f32[512,256]{1,0:T(8,128)S(1)}, u32[]{:S(2)}, u32[]{:S(2)}) collective-permute-start(f32[512,256]{1,0:T(8,128)S(1)} %get-tuple-element.33.back_ref), channel_id=1, source_target_pairs={{0,32},{2,34},{4,36},{6,38},{8,40},{10,42},{12,44},{14,46},{16,48}... | collective-permute-start | bytes 1572872 | tf_op jit(solution)/shard_map/ppermute | solution.py:194
  73.4 61.7 %collective-permute-done.6.base_in_ref = f32[512,256]{1,0:T(8,128)} collective-permute-done((f32[512,256]{1,0:T(8,128)S(1)}, f32[512,256]{1,0:T(8,128)}, u32[]{:S(2)}, u32[]{:S(2)}) %collective-permute-start.6) | collective-permute-done | bytes 524320 | tf_op jit(solution)/shard_map/ppermute | solution.py:171
  135.1 2.7 %shard_map.68 = (f32[512,256]{1,0:T(8,128)S(1)}, f32[512,256]{1,0:T(8,128)S(1)}, f32[512,256]{1,0:T(8,128)S(1)}) custom-call(f32[512,256]{1,0:T(8,128)S(1)} %get-tuple-element.29.base_ref, f32[512,512]{1,0:T(8,128)S(1)} %get-tuple-element.32.pair_ref, f32[512,256]{1,0:T(8,128)} %collective-permute-done.5.vec_in_ref, ...), custom_call_target="tpu_custom_call" | custom-call | flops 1000 | bytes 1000 | tf_op jit(solution)/shard_map/pallas_call | solution.py:125
  137.8 1.3 collective-permute-start.10
  139.3 6.5 %collective-permute-start.9 = (f32[256,256]{1,0:T(8,128)S(1)}, f32[256,256]{1,0:T(8,128)S(1)}, u32[]{:S(2)}, u32[]{:S(2)}) collective-permute-start(f32[256,256]{1,0:T(8,128)S(1)} %get-tuple-element.37), channel_id=1, source_target_pairs={{0,256},{64,320},{128,384},{192,448},{256,0},{320,64},{384,128},{4... | collective-permute-start | bytes 786440 | tf_op jit(solution)/shard_map/ppermute | solution.py:199
  145.8 1.9 %collective-permute-start.8 = (f32[256,256]{1,0:T(8,128)S(1)}, f32[256,256]{1,0:T(8,128)S(1)}, u32[]{:S(2)}, u32[]{:S(2)}) collective-permute-start(f32[256,256]{1,0:T(8,128)S(1)} %get-tuple-element.38), channel_id=1, source_target_pairs={{0,256},{64,320},{128,384},{192,448},{256,0},{320,64},{384,128},{4... | collective-permute-start | bytes 786440 | tf_op jit(solution)/shard_map/ppermute | solution.py:199
  147.7 5.0 %collective-permute-done.9.refs_1_ = f32[256,256]{1,0:T(8,128)S(1)} collective-permute-done((f32[256,256]{1,0:T(8,128)S(1)}, f32[256,256]{1,0:T(8,128)S(1)}, u32[]{:S(2)}, u32[]{:S(2)}) %collective-permute-start.9) | collective-permute-done | bytes 262176 | tf_op jit(solution)/shard_map/ppermute | solution.py:199
  152.8 3.0 %collective-permute-done.8.refs_0_ = f32[256,256]{1,0:T(8,128)S(1)} collective-permute-done((f32[256,256]{1,0:T(8,128)S(1)}, f32[256,256]{1,0:T(8,128)S(1)}, u32[]{:S(2)}, u32[]{:S(2)}) %collective-permute-start.8) | collective-permute-done | bytes 262176 | tf_op jit(solution)/shard_map/ppermute | solution.py:199
  (41 shorter events, 11.0 us)
Async XLA Ops:
  0.0 5.0 %copy-start = (f32[512,256]{1,0:T(8,128)S(1)}, f32[512,256]{1,0:T(8,128)}, u32[]{:S(2)}) copy-start(f32[512,256]{1,0:T(8,128)} %vec_ref.3) | copy-start | bytes 1572868
  0.0 1.3 copy-start.1
  2.0 8.0 %copy-start.15 = (s32[4,4]{1,0:T(4,128)S(1)}, s32[4,4]{1,0:T(4,128)}, u32[]{:S(2)}) copy-start(s32[4,4]{1,0:T(4,128)} %mask.1) | copy-start | bytes 196
  3.7 42.5 %collective-permute-start.4 = (f32[1544,128]{1,0:T(8,128)}, f32[1544,128]{1,0:T(8,128)}, u32[]{:S(2)}, u32[]{:S(2)}) collective-permute-start(f32[1544,128]{1,0:T(8,128)} %get-tuple-element.28), channel_id=1, source_target_pairs={{1,33},{3,35},{5,37},{7,39},{9,41},{11,43},{13,45},{15,47},{17,49}... | collective-permute-start | bytes 2371592 | tf_op jit(solution)/shard_map/ppermute | solution.py:160
  5.0 17.1 %collective-permute-start.1 = (f32[512,256]{1,0:T(8,128)S(1)}, f32[512,256]{1,0:T(8,128)S(1)}, u32[]{:S(2)}, u32[]{:S(2)}) collective-permute-start(f32[512,256]{1,0:T(8,128)S(1)} %copy-done), channel_id=1, source_target_pairs={{0,256},{64,320},{128,384},{192,448},{256,0},{320,64},{384,128},{4... | collective-permute-start | bytes 1572872 | tf_op jit(solution)/shard_map/ppermute | solution.py:149
  9.9 1.2 copy-start.5
  11.8 13.9 %collective-permute-start.2 = (f32[256,512]{1,0:T(8,128)S(1)}, f32[256,512]{1,0:T(8,128)}, u32[]{:S(2)}, u32[]{:S(2)}) collective-permute-start(f32[256,512]{1,0:T(8,128)S(1)} %get-tuple-element.23.refs_0_), channel_id=1, source_target_pairs={{0,256},{64,320},{128,384},{192,448},{256,0},{320,64},{384,128},{4... | collective-permute-start | bytes 1572872 | tf_op jit(solution)/shard_map/ppermute | solution.py:166
  14.3 0.8 copy-start.9
  15.1 21.9 %collective-permute-start.3 = (f32[256,512]{1,0:T(8,128)S(1)}, f32[256,512]{1,0:T(8,128)}, u32[]{:S(2)}, u32[]{:S(2)}) collective-permute-start(f32[256,512]{1,0:T(8,128)S(1)} %get-tuple-element.24.refs_1_), channel_id=1, source_target_pairs={{0,256},{64,320},{128,384},{192,448},{256,0},{320,64},{384,128},{4... | collective-permute-start | bytes 1572872 | tf_op jit(solution)/shard_map/ppermute | solution.py:166
  20.0 0.8 copy-start.11
  20.8 52.6 %collective-permute-start.5 = (f32[512,256]{1,0:T(8,128)S(1)}, f32[512,256]{1,0:T(8,128)}, u32[]{:S(2)}, u32[]{:S(2)}) collective-permute-start(f32[512,256]{1,0:T(8,128)S(1)} %copy-done), channel_id=1, source_target_pairs={{1,33},{3,35},{5,37},{7,39},{9,41},{11,43},{13,45},{15,47},{17,49}... | collective-permute-start | bytes 1572872 | tf_op jit(solution)/shard_map/ppermute | solution.py:150
  22.1 27.5 %copy-start.2 = (f32[512,512]{1,0:T(8,128)S(1)}, f32[512,512]{1,0:T(8,128)}, u32[]{:S(2)}) copy-start(f32[512,512]{1,0:T(8,128)} %own_ref.1) | copy-start | bytes 3145732
  37.0 1.2 copy-start.6
  38.2 1.0 copy-start.8
  39.2 1.0 copy-start.10
  40.3 1.0 copy-start.12
  43.8 1.0 copy-start.3
  44.8 2.1 %copy-start.14 = (s32[4,4]{1,0:T(4,128)S(1)}, s32[4,4]{1,0:T(4,128)}, u32[]{:S(2)}) copy-start(s32[4,4]{1,0:T(4,128)} %own_mask.1) | copy-start | bytes 196
  44.8 90.3 %collective-permute-start.6 = (f32[512,256]{1,0:T(8,128)S(1)}, f32[512,256]{1,0:T(8,128)}, u32[]{:S(2)}, u32[]{:S(2)}) collective-permute-start(f32[512,256]{1,0:T(8,128)S(1)} %get-tuple-element.29.base_ref), channel_id=1, source_target_pairs={{1,33},{3,35},{5,37},{7,39},{9,41},{11,43},{13,45},{15,47},{17,49}... | collective-permute-start | bytes 1572872 | tf_op jit(solution)/shard_map/ppermute | solution.py:171
  52.7 86.4 %collective-permute-start.7 = (f32[512,256]{1,0:T(8,128)S(1)}, f32[512,256]{1,0:T(8,128)S(1)}, u32[]{:S(2)}, u32[]{:S(2)}) collective-permute-start(f32[512,256]{1,0:T(8,128)S(1)} %get-tuple-element.33.back_ref), channel_id=1, source_target_pairs={{0,32},{2,34},{4,36},{6,38},{8,40},{10,42},{12,44},{14,46},{16,48}... | collective-permute-start | bytes 1572872 | tf_op jit(solution)/shard_map/ppermute | solution.py:194
  137.8 19.0 %collective-permute-start.10 = (f32[512,256]{1,0:T(8,128)S(1)}, f32[512,256]{1,0:T(8,128)S(1)}, u32[]{:S(2)}, u32[]{:S(2)}) collective-permute-start(f32[512,256]{1,0:T(8,128)S(1)} %get-tuple-element.36), channel_id=1, source_target_pairs={{0,32},{2,34},{4,36},{6,38},{8,40},{10,42},{12,44},{14,46},{16,48}... | collective-permute-start | bytes 1572872 | tf_op jit(solution)/shard_map/ppermute | solution.py:196
  139.2 16.5 %copy-start.4 = (f32[512,512]{1,0:T(8,128)S(1)}, f32[512,512]{1,0:T(8,128)}, u32[]{:S(2)}) copy-start(f32[512,512]{1,0:T(8,128)} %copy-done.3) | copy-start | bytes 3145732
  139.3 13.5 %collective-permute-start.9 = (f32[256,256]{1,0:T(8,128)S(1)}, f32[256,256]{1,0:T(8,128)S(1)}, u32[]{:S(2)}, u32[]{:S(2)}) collective-permute-start(f32[256,256]{1,0:T(8,128)S(1)} %get-tuple-element.37), channel_id=1, source_target_pairs={{0,256},{64,320},{128,384},{192,448},{256,0},{320,64},{384,128},{4... | collective-permute-start | bytes 786440 | tf_op jit(solution)/shard_map/ppermute | solution.py:199
  145.8 10.0 %collective-permute-start.8 = (f32[256,256]{1,0:T(8,128)S(1)}, f32[256,256]{1,0:T(8,128)S(1)}, u32[]{:S(2)}, u32[]{:S(2)}) collective-permute-start(f32[256,256]{1,0:T(8,128)S(1)} %get-tuple-element.38), channel_id=1, source_target_pairs={{0,256},{64,320},{128,384},{192,448},{256,0},{320,64},{384,128},{4... | collective-permute-start | bytes 786440 | tf_op jit(solution)/shard_map/ppermute | solution.py:199
  (2 other events, 1.5 us)

commit v11 on v8

--- a/solution.py
+++ b/solution.py
@@ -9,7 +9,7 @@
 
 CENTER = 0.5
 HALF_SPAN = 5.0
-FIXED = 12
+FIXED = 8
 COST = 1000
 GRP_CUTS = 2
 
@@ -32,15 +32,11 @@
     n = slab_ref.shape[0] // tile
     bulk_ref[...] = jnp.zeros_like(bulk_ref)
     extra_ref[...] = jnp.zeros_like(extra_ref)
-    tail = (bulk_ref.shape[0] - FIXED * tile, tile)
-    row, col = lax.broadcasted_iota(jnp.int32, tail, 0), lax.broadcasted_iota(jnp.int32, tail, 1)
-    mask = jnp.zeros(tail, jnp.float32)
     slot = jnp.int32(0)
     for i in range(n):
         for j in range(n):
             at = (slice(i * tile, (i + 1) * tile), slice(j * tile, (j + 1) * tile))
             stored = slab_mask[i, j] > 0
-            mask = jnp.where(jnp.logical_and(row == i, col == j), slab_mask[i, j].astype(jnp.float32), mask)
 
             @pl.when(jnp.logical_and(stored, slot < FIXED))
             def _():
@@ -51,7 +47,6 @@
                 extra_ref[slot - FIXED] = slab_ref[at]
 
             slot = slot + stored.astype(jnp.int32)
-    bulk_ref[FIXED * tile :, :] = mask
 
 
 def masked_kernel(tile, mask, tiles_ref, *out_refs):
@@ -150,45 +145,45 @@
     square = jax.ShapeDtypeStruct((rows, rows), f32)
     block = jax.ShapeDtypeStruct(vectors.shape, f32)
 
-    vecs_grp = lax.ppermute(vectors, "grp", grp_pairs)
-    vecs_in = lax.ppermute(vectors, "slab", to_owner)
-
+    mask_in = lax.ppermute(slab_mask, "slab", to_owner)
     bulk, extra = local_call(
         functools.partial(pack_kernel, tile),
         (slab_mask, slab_tiles),
         (
-            jax.ShapeDtypeStruct((FIXED * tile + 8, tile), f32),
+            jax.ShapeDtypeStruct((FIXED * tile, tile), f32),
             jax.ShapeDtypeStruct((slots - FIXED, tile, tile), f32),
         ),
     )
     bulk_in = lax.ppermute(bulk, "slab", to_owner)
-    grp_blocks = local_call(
-        functools.partial(masked_kernel, tile),
-        (grp_mask, grp_tiles),
-        (jax.ShapeDtypeStruct((rows // GRP_CUTS, rows), f32),) * GRP_CUTS,
-    )
-    grp_in = [lax.ppermute(x, "grp", grp_pairs) for x in grp_blocks]
-
-    base, sym, across = local_call(
-        base_kernel, (vectors, diag_block, vecs_grp, *grp_blocks, *grp_in), (block, square, square)
-    )
-    base_in = lax.ppermute(base, "slab", to_owner)
-
-    base, bulk_in = lax.optimization_barrier((base, bulk_in))
-    mask_in = bulk_in[FIXED * tile : FIXED * tile + n_tile, :n_tile].astype(jnp.int32)
-    sizes = (0, slots - FIXED)
+    sizes = (0, 2, 4, slots - FIXED)
 
     def send(k):
         def branch(tiles):
             if k == 0:
                 return jnp.zeros_like(tiles)
-            return lax.ppermute(tiles, "slab", to_owner)
+            got = lax.ppermute(tiles[:k], "slab", to_owner)
+            return jnp.concatenate([got, jnp.zeros((tiles.shape[0] - k, tile, tile), f32)]) if k < len(tiles) else got
 
         return branch
 
     over = jnp.sum(jnp.where(owner, mask_in, slab_mask)) - FIXED
     which = sum((over > k).astype(jnp.int32) for k in sizes[:-1])
     extra_in = lax.switch(which, [send(k) for k in sizes], extra)
+
+    extra_in, later, later_mask = lax.optimization_barrier((extra_in, vectors, grp_mask))
+    vecs_in = lax.ppermute(later, "slab", to_owner)
+    vecs_grp = lax.ppermute(later, "grp", grp_pairs)
+    grp_blocks = local_call(
+        functools.partial(masked_kernel, tile),
+        (later_mask, grp_tiles),
+        (jax.ShapeDtypeStruct((rows // GRP_CUTS, rows), f32),) * GRP_CUTS,
+    )
+    grp_in = [lax.ppermute(x, "grp", grp_pairs) for x in grp_blocks]
+
+    base, sym, across = local_call(
+        base_kernel, (vectors, diag_block, vecs_grp, *grp_blocks, *grp_in), (block, square, square)
+    )
+    base_in = lax.ppermute(base, "slab", to_owner)
 
     pair, back = local_call(
         functools.partial(pair_kernel, tile),

time: 155 us -> 171 us (1.10)
  the two profiles are of different devices: /device:TPU:49 before, /device:TPU:59 now
where the time goes in v11:
time: 171 us; the launch traced here: 170 us
  waiting for transfers between devices  84.6 us (49%)
  starting transfers between devices  69.8 us (41%)
  Pallas kernels  9.32 us (5%)
  local copies, waits for them, and re-layouts  3.19 us (2%)
  other arithmetic  2.37 us (1%)
    ppermute x1, waiting for transfers between devices, body(): vecs_in = lax.ppermute(later, 'slab', to_owner)  46 us
    ppermute x1, waiting for transfers between devices, body(): mask_in = lax.ppermute(slab_mask, 'slab', to_owner)  20.5 us
    ppermute x1, starting transfers between devices, body(): bulk_in = lax.ppermute(bulk, 'slab', to_owner)  14.5 us
    ppermute x1, starting transfers between devices, body(): vecs_in = lax.ppermute(later, 'slab', to_owner)  12.6 us
    ppermute x1, starting transfers between devices, branch(): got = lax.ppermute(tiles[:k], 'slab', to_owner)  11.9 us
    ppermute x1, starting transfers between devices, body(): base_in = lax.ppermute(base, 'slab', to_owner)  11.3 us
    pallas_call x7, Pallas kernels, local_call(): pl.pallas_call(kernel, out_shape=out_shape, in_specs=spaces, out_specs=(v...  9.32 us
    ppermute x1, waiting for transfers between devices, body(): back2_in = lax.ppermute(back2, 'slab', from_owner)  7.83 us
  transfers between devices with their start and end apart: 12, of which 8 were waited for; matrix products, arithmetic and copies ran while one was open for 2% of the time, Pallas kernels for 4%

profile of v11, /device:TPU:59, one launch (start us, length us, event | category | flops | bytes accessed | tf_op | source)
XLA Modules:
  0.0 170.2 jit_solution(1485431633690540937)
XLA Ops:
  1.2 1.8 %shard_map.64 = (f32[1024,128]{1,0:T(8,128)S(1)}, f32[8,128,128]{2,1,0:T(8,128)}) custom-call(s32[4,4]{1,0:T(4,128)} %own_mask.1, f32[512,512]{1,0:T(8,128)S(1)} %copy-done.1), custom_call_target="tpu_custom_call" | custom-call | flops 1000 | bytes 1000 | tf_op jit(solution)/shard_map/pallas_call | solution.py:124
  3.0 14.5 %collective-permute-start.7 = (f32[1024,128]{1,0:T(8,128)S(1)}, f32[1024,128]{1,0:T(8,128)S(1)}, u32[]{:S(2)}, u32[]{:S(2)}) collective-permute-start(f32[1024,128]{1,0:T(8,128)S(1)} %get-tuple-element.37), channel_id=1, source_target_pairs={{1,33},{3,35},{5,37},{7,39},{9,41},{11,43},{13,45},{15,47},{17,49}... | collective-permute-start | bytes 1572872 | tf_op jit(solution)/shard_map/ppermute | solution.py:157
  17.5 1.3 collective-permute-start.3
  18.9 20.5 %collective-permute-done.3.in_mask = s32[4,4]{1,0:T(4,128)S(1)} collective-permute-done((s32[4,4]{1,0:T(4,128)}, s32[4,4]{1,0:T(4,128)S(1)}, u32[]{:S(2)}, u32[]{:S(2)}) %collective-permute-start.3) | collective-permute-done | bytes 96 | tf_op jit(solution)/shard_map/ppermute | solution.py:148
  39.3 1.3 select_reduce_fusion
  41.3 15.7 %conditional.1 = (f32[8,128,128]{2,1,0:T(8,128)}) conditional(s32[]{:T(128)} %clamp.3, () %tuple.19, f32[8,128,128]{2,1,0:T(8,128)} %get-tuple-element.29, f32[8,128,128]{2,1,0:T(8,128)} %get-tuple-element.29, f32[8,128,128]{2,1,0:T(8,128)} %get-tuple-element.29), branch_computations={%region_1.2_spmd, %region_2.3_spmd, %region_3.4_spmd, %region_4.5_... | conditional | bytes 2359348 | solution.py:171
  42.4 11.9 %collective-permute-start = (f32[2,128,128]{2,1,0:T(8,128)S(1)}, f32[2,128,128]{2,1,0:T(8,128)S(1)}, u32[]{:S(2)}, u32[]{:S(2)}) collective-permute-start(f32[2,128,128]{2,1,0:T(8,128)S(1)} %slice.4), channel_id=1, source_target_pairs={{1,33},{3,35},{5,37},{7,39},{9,41},{11,43},{13,45},{15,47},{17,49}... | collective-permute-start | bytes 393224 | tf_op jit(solution)/shard_map/cond/branch_1_fun/ppermute | solution.py:164
  54.3 1.9 %collective-permute-done = f32[2,128,128]{2,1,0:T(8,128)S(1)} collective-permute-done((f32[2,128,128]{2,1,0:T(8,128)S(1)}, f32[2,128,128]{2,1,0:T(8,128)S(1)}, u32[]{:S(2)}, u32[]{:S(2)}) %collective-permute-start) | collective-permute-done | bytes 131104 | tf_op jit(solution)/shard_map/cond/branch_1_fun/ppermute | solution.py:164
  57.7 1.9 %collective-permute-start.5 = (f32[256,512]{1,0:T(8,128)S(1)}, f32[256,512]{1,0:T(8,128)S(1)}, u32[]{:S(2)}, u32[]{:S(2)}) collective-permute-start(f32[256,512]{1,0:T(8,128)S(1)} %get-tuple-element.32.refs_0_), channel_id=1, source_target_pairs={{0,256},{64,320},{128,384},{192,448},{256,0},{320,64},{384,128},{4... | collective-permute-start | bytes 1572872 | tf_op jit(solution)/shard_map/ppermute | solution.py:181
  59.7 5.0 %collective-permute-start.6 = (f32[256,512]{1,0:T(8,128)S(1)}, f32[256,512]{1,0:T(8,128)S(1)}, u32[]{:S(2)}, u32[]{:S(2)}) collective-permute-start(f32[256,512]{1,0:T(8,128)S(1)} %get-tuple-element.33.refs_1_), channel_id=1, source_target_pairs={{0,256},{64,320},{128,384},{192,448},{256,0},{320,64},{384,128},{4... | collective-permute-start | bytes 1572872 | tf_op jit(solution)/shard_map/ppermute | solution.py:181
  64.7 1.9 %collective-permute-start.4 = (f32[512,256]{1,0:T(8,128)S(1)}, f32[512,256]{1,0:T(8,128)S(1)}, u32[]{:S(2)}, u32[]{:S(2)}) collective-permute-start(f32[512,256]{1,0:T(8,128)S(1)} %copy-done), channel_id=1, source_target_pairs={{0,256},{64,320},{128,384},{192,448},{256,0},{320,64},{384,128},{4... | collective-permute-start | bytes 1572872 | tf_op jit(solution)/shard_map/ppermute | solution.py:175
  66.6 12.6 %collective-permute-start.8 = (f32[512,256]{1,0:T(8,128)S(1)}, f32[512,256]{1,0:T(8,128)S(1)}, u32[]{:S(2)}, u32[]{:S(2)}) collective-permute-start(f32[512,256]{1,0:T(8,128)S(1)} %copy-done), channel_id=1, source_target_pairs={{1,33},{3,35},{5,37},{7,39},{9,41},{11,43},{13,45},{15,47},{17,49}... | collective-permute-start | bytes 1572872 | tf_op jit(solution)/shard_map/ppermute | solution.py:174
  79.3 2.1 %shard_map.67 = (f32[512,512]{1,0:T(8,128)S(1)}, f32[512,256]{1,0:T(8,128)S(1)}) custom-call(s32[4,4]{1,0:T(4,128)} %own_mask.1, s32[4,4]{1,0:T(4,128)S(1)} %collective-permute-done.3.in_mask, f32[512,512]{1,0:T(8,128)S(1)} %copy-done.2, f32[1024,128]{1,0:T(8,128)S(1)} %collective-permute-done.7.bulk_ref, f32[8,128,128]{2,1,0:T(8,128)} %get-tuple-element.47.extra_ref, ...), custom_call_target="tpu_custom_call" | custom-call | flops 1000 | bytes 1000 | tf_op jit(solution)/shard_map/pallas_call | solution.py:124
  81.4 1.3 collective-permute-start.9
  82.7 1.5 collective-permute-done.4.vec_grp_ref
  84.2 1.3 shard_map.66
  85.5 11.3 %collective-permute-start.12 = (f32[512,256]{1,0:T(8,128)S(1)}, f32[512,256]{1,0:T(8,128)S(1)}, u32[]{:S(2)}, u32[]{:S(2)}) collective-permute-start(f32[512,256]{1,0:T(8,128)S(1)} %get-tuple-element.36.base_ref), channel_id=1, source_target_pairs={{1,33},{3,35},{5,37},{7,39},{9,41},{11,43},{13,45},{15,47},{17,49}... | collective-permute-start | bytes 1572872 | tf_op jit(solution)/shard_map/ppermute | solution.py:186
  96.8 46.0 %collective-permute-done.8.vec_in_ref = f32[512,256]{1,0:T(8,128)S(1)} collective-permute-done((f32[512,256]{1,0:T(8,128)S(1)}, f32[512,256]{1,0:T(8,128)S(1)}, u32[]{:S(2)}, u32[]{:S(2)}) %collective-permute-start.8) | collective-permute-done | bytes 524320 | tf_op jit(solution)/shard_map/ppermute | solution.py:174
  142.7 1.8 %shard_map.68 = (f32[512,256]{1,0:T(8,128)S(1)}, f32[512,256]{1,0:T(8,128)S(1)}) custom-call(f32[512,256]{1,0:T(8,128)S(1)} %get-tuple-element.36.base_ref, f32[512,512]{1,0:T(8,128)S(1)} %get-tuple-element.39.pair_ref, f32[512,256]{1,0:T(8,128)S(1)} %collective-permute-done.8.vec_in_ref), custom_call_target="tpu_custom_call" | custom-call | flops 1000 | bytes 1000 | tf_op jit(solution)/shard_map/pallas_call | solution.py:124
  144.6 2.9 %collective-permute-done.9 = f32[512,256]{1,0:T(8,128)S(1)} collective-permute-done((f32[512,256]{1,0:T(8,128)S(1)}, f32[512,256]{1,0:T(8,128)S(1)}, u32[]{:S(2)}, u32[]{:S(2)}) %collective-permute-start.9) | collective-permute-done | bytes 524320 | tf_op jit(solution)/shard_map/ppermute | solution.py:193
  149.0 1.9 %collective-permute-start.10 = (f32[256,256]{1,0:T(8,128)S(1)}, f32[256,256]{1,0:T(8,128)S(1)}, u32[]{:S(2)}, u32[]{:S(2)}) collective-permute-start(f32[256,256]{1,0:T(8,128)S(1)} %get-tuple-element.46), channel_id=1, source_target_pairs={{0,256},{64,320},{128,384},{192,448},{256,0},{320,64},{384,128},{4... | collective-permute-start | bytes 786440 | tf_op jit(solution)/shard_map/ppermute | solution.py:200
  150.9 4.9 %collective-permute-start.11 = (f32[256,256]{1,0:T(8,128)S(1)}, f32[256,256]{1,0:T(8,128)S(1)}, u32[]{:S(2)}, u32[]{:S(2)}) collective-permute-start(f32[256,256]{1,0:T(8,128)S(1)} %get-tuple-element.45), channel_id=1, source_target_pairs={{0,256},{64,320},{128,384},{192,448},{256,0},{320,64},{384,128},{4... | collective-permute-start | bytes 786440 | tf_op jit(solution)/shard_map/ppermute | solution.py:200
  157.6 2.8 %collective-permute-done.11.refs_1_ = f32[256,256]{1,0:T(8,128)S(1)} collective-permute-done((f32[256,256]{1,0:T(8,128)S(1)}, f32[256,256]{1,0:T(8,128)S(1)}, u32[]{:S(2)}, u32[]{:S(2)}) %collective-permute-start.11) | collective-permute-done | bytes 262176 | tf_op jit(solution)/shard_map/ppermute | solution.py:200
  161.4 7.8 %collective-permute-done.13 = f32[512,256]{1,0:T(8,128)S(1)} collective-permute-done((f32[512,256]{1,0:T(8,128)S(1)}, f32[512,256]{1,0:T(8,128)S(1)}, u32[]{:S(2)}, u32[]{:S(2)}) %collective-permute-start.13) | collective-permute-done | bytes 524320 | tf_op jit(solution)/shard_map/ppermute | solution.py:196
  (26 shorter events, 9.0 us)
Async XLA Ops:
  0.0 1.2 copy-start.1
  3.0 76.3 %collective-permute-start.7 = (f32[1024,128]{1,0:T(8,128)S(1)}, f32[1024,128]{1,0:T(8,128)S(1)}, u32[]{:S(2)}, u32[]{:S(2)}) collective-permute-start(f32[1024,128]{1,0:T(8,128)S(1)} %get-tuple-element.37), channel_id=1, source_target_pairs={{1,33},{3,35},{5,37},{7,39},{9,41},{11,43},{13,45},{15,47},{17,49}... | collective-permute-start | bytes 1572872 | tf_op jit(solution)/shard_map/ppermute | solution.py:157
  17.5 21.8 %collective-permute-start.3 = (s32[4,4]{1,0:T(4,128)}, s32[4,4]{1,0:T(4,128)S(1)}, u32[]{:S(2)}, u32[]{:S(2)}) collective-permute-start(s32[4,4]{1,0:T(4,128)} %own_mask.1), channel_id=1, source_target_pairs={{1,33},{3,35},{5,37},{7,39},{9,41},{11,43},{13,45},{15,47},{17,49}... | collective-permute-start | bytes 200 | tf_op jit(solution)/shard_map/ppermute | solution.py:148
  41.3 15.8 %copy-start.3 = (f32[512,512]{1,0:T(8,128)S(1)}, f32[512,512]{1,0:T(8,128)}, u32[]{:S(2)}) copy-start(f32[512,512]{1,0:T(8,128)} %tiles_ref.1) | copy-start | bytes 3145732
  41.3 15.7 %copy-start.5 = (s32[4,4]{1,0:T(4,128)S(1)}, s32[4,4]{1,0:T(4,128)}, u32[]{:S(2)}) copy-start(s32[4,4]{1,0:T(4,128)} %mask) | copy-start | bytes 196
  41.3 37.9 %copy-start.2 = (f32[512,512]{1,0:T(8,128)S(1)}, f32[512,512]{1,0:T(8,128)}, u32[]{:S(2)}) copy-start(f32[512,512]{1,0:T(8,128)} %own_ref.1) | copy-start | bytes 3145732
  42.4 13.8 %collective-permute-start = (f32[2,128,128]{2,1,0:T(8,128)S(1)}, f32[2,128,128]{2,1,0:T(8,128)S(1)}, u32[]{:S(2)}, u32[]{:S(2)}) collective-permute-start(f32[2,128,128]{2,1,0:T(8,128)S(1)} %slice.4), channel_id=1, source_target_pairs={{1,33},{3,35},{5,37},{7,39},{9,41},{11,43},{13,45},{15,47},{17,49}... | collective-permute-start | bytes 393224 | tf_op jit(solution)/shard_map/cond/branch_1_fun/ppermute | solution.py:164
  57.1 7.6 %copy-start = (f32[512,256]{1,0:T(8,128)S(1)}, f32[512,256]{1,0:T(8,128)}, u32[]{:S(2)}) copy-start(f32[512,256]{1,0:T(8,128)} %vec_ref.3) | copy-start | bytes 1572868
  57.7 24.9 %collective-permute-start.5 = (f32[256,512]{1,0:T(8,128)S(1)}, f32[256,512]{1,0:T(8,128)S(1)}, u32[]{:S(2)}, u32[]{:S(2)}) collective-permute-start(f32[256,512]{1,0:T(8,128)S(1)} %get-tuple-element.32.refs_0_), channel_id=1, source_target_pairs={{0,256},{64,320},{128,384},{192,448},{256,0},{320,64},{384,128},{4... | collective-permute-start | bytes 1572872 | tf_op jit(solution)/shard_map/ppermute | solution.py:181
  59.7 24.5 %copy-start.4 = (f32[512,512]{1,0:T(8,128)S(1)}, f32[512,512]{1,0:T(8,128)}, u32[]{:S(2)}) copy-start(f32[512,512]{1,0:T(8,128)} %diag_ref.1) | copy-start | bytes 3145732
  59.7 23.0 %collective-permute-start.6 = (f32[256,512]{1,0:T(8,128)S(1)}, f32[256,512]{1,0:T(8,128)S(1)}, u32[]{:S(2)}, u32[]{:S(2)}) collective-permute-start(f32[256,512]{1,0:T(8,128)S(1)} %get-tuple-element.33.refs_1_), channel_id=1, source_target_pairs={{0,256},{64,320},{128,384},{192,448},{256,0},{320,64},{384,128},{4... | collective-permute-start | bytes 1572872 | tf_op jit(solution)/shard_map/ppermute | solution.py:181
  64.7 19.5 %collective-permute-start.4 = (f32[512,256]{1,0:T(8,128)S(1)}, f32[512,256]{1,0:T(8,128)S(1)}, u32[]{:S(2)}, u32[]{:S(2)}) collective-permute-start(f32[512,256]{1,0:T(8,128)S(1)} %copy-done), channel_id=1, source_target_pairs={{0,256},{64,320},{128,384},{192,448},{256,0},{320,64},{384,128},{4... | collective-permute-start | bytes 1572872 | tf_op jit(solution)/shard_map/ppermute | solution.py:175
  66.6 76.1 %collective-permute-start.8 = (f32[512,256]{1,0:T(8,128)S(1)}, f32[512,256]{1,0:T(8,128)S(1)}, u32[]{:S(2)}, u32[]{:S(2)}) collective-permute-start(f32[512,256]{1,0:T(8,128)S(1)} %copy-done), channel_id=1, source_target_pairs={{1,33},{3,35},{5,37},{7,39},{9,41},{11,43},{13,45},{15,47},{17,49}... | collective-permute-start | bytes 1572872 | tf_op jit(solution)/shard_map/ppermute | solution.py:174
  81.4 66.2 %collective-permute-start.9 = (f32[512,256]{1,0:T(8,128)S(1)}, f32[512,256]{1,0:T(8,128)S(1)}, u32[]{:S(2)}, u32[]{:S(2)}) collective-permute-start(f32[512,256]{1,0:T(8,128)S(1)} %get-tuple-element.42.back_ref), channel_id=1, source_target_pairs={{0,32},{2,34},{4,36},{6,38},{8,40},{10,42},{12,44},{14,46},{16,48}... | collective-permute-start | bytes 1572872 | tf_op jit(solution)/shard_map/ppermute | solution.py:193
  85.5 70.3 %collective-permute-start.12 = (f32[512,256]{1,0:T(8,128)S(1)}, f32[512,256]{1,0:T(8,128)S(1)}, u32[]{:S(2)}, u32[]{:S(2)}) collective-permute-start(f32[512,256]{1,0:T(8,128)S(1)} %get-tuple-element.36.base_ref), channel_id=1, source_target_pairs={{1,33},{3,35},{5,37},{7,39},{9,41},{11,43},{13,45},{15,47},{17,49}... | collective-permute-start | bytes 1572872 | tf_op jit(solution)/shard_map/ppermute | solution.py:186
  147.5 21.7 %collective-permute-start.13 = (f32[512,256]{1,0:T(8,128)S(1)}, f32[512,256]{1,0:T(8,128)S(1)}, u32[]{:S(2)}, u32[]{:S(2)}) collective-permute-start(f32[512,256]{1,0:T(8,128)S(1)} %get-tuple-element.44), channel_id=1, source_target_pairs={{0,32},{2,34},{4,36},{6,38},{8,40},{10,42},{12,44},{14,46},{16,48}... | collective-permute-start | bytes 1572872 | tf_op jit(solution)/shard_map/ppermute | solution.py:196
  149.0 8.6 %collective-permute-start.10 = (f32[256,256]{1,0:T(8,128)S(1)}, f32[256,256]{1,0:T(8,128)S(1)}, u32[]{:S(2)}, u32[]{:S(2)}) collective-permute-start(f32[256,256]{1,0:T(8,128)S(1)} %get-tuple-element.46), channel_id=1, source_target_pairs={{0,256},{64,320},{128,384},{192,448},{256,0},{320,64},{384,128},{4... | collective-permute-start | bytes 786440 | tf_op jit(solution)/shard_map/ppermute | solution.py:200
  150.9 9.5 %collective-permute-start.11 = (f32[256,256]{1,0:T(8,128)S(1)}, f32[256,256]{1,0:T(8,128)S(1)}, u32[]{:S(2)}, u32[]{:S(2)}) collective-permute-start(f32[256,256]{1,0:T(8,128)S(1)} %get-tuple-element.45), channel_id=1, source_target_pairs={{0,256},{64,320},{128,384},{192,448},{256,0},{320,64},{384,128},{4... | collective-permute-start | bytes 786440 | tf_op jit(solution)/shard_map/ppermute | solution.py:200

commit v12 on v8

--- a/solution.py
+++ b/solution.py
@@ -109,12 +109,13 @@
     back_ref[...] = product(split(pair.T), split(first))
 
 
-def near_kernel(sym_ref, across_ref, first_ref, *refs):
-    *first_grp_refs, near_ref = refs
-    first_grp = jnp.concatenate([ref[...] for ref in first_grp_refs], axis=0)
-    near_ref[...] = product(split(sym_ref[...]), split(first_ref[...])) + product(
-        split(across_ref[...]), split(first_grp)
-    )
+def near_kernel(role, sym_ref, across_ref, own_ref, own_grp_ref, other_ref, *refs):
+    *other_grp_refs, near_ref = refs
+    owner = role[0, 0] > 0
+    other_grp = jnp.concatenate([ref[...] for ref in other_grp_refs], axis=0)
+    first = jnp.where(owner, own_ref[...], other_ref[...])
+    first_grp = jnp.where(owner, own_grp_ref[...], other_grp)
+    near_ref[...] = product(split(sym_ref[...]), split(first)) + product(split(across_ref[...]), split(first_grp))
 
 
 def far_kernel(pair_ref, base_in_ref, back_ref, far_ref):
@@ -146,6 +147,15 @@
     to_owner = [(i, i ^ half) for i in range(n_slab) if not owns(i, half)]
     from_owner = [(i, i ^ half) for i in range(n_slab) if owns(i, half)]
     grp_pairs = [(i, i ^ (n_grp // 2)) for i in range(n_grp)]
+
+    def role_pairs(role):
+        return [
+            (g * n_slab + i, (g ^ (n_grp // 2)) * n_slab + i)
+            for g in range(n_grp)
+            for i in range(n_slab)
+            if owns(i, half) == role
+        ]
+
     f32 = jnp.float32
     square = jax.ShapeDtypeStruct((rows, rows), f32)
     block = jax.ShapeDtypeStruct(vectors.shape, f32)
@@ -201,9 +211,12 @@
     back2_in = lax.ppermute(back2, "slab", from_owner)
 
     far = local_call(far_kernel, (pair, base_in, back), block)
-    first = jnp.where(owner, first_own, (base + back_in) / HALF_SPAN)
-    first_grp = [lax.ppermute(x, "grp", grp_pairs) for x in jnp.split(first, 2, axis=0)]
-    near = local_call(near_kernel, (sym, across, first, *first_grp), block)
+    own_grp = lax.ppermute(first_own, ("grp", "slab"), role_pairs(True))
+    far = local_call(far_kernel, (pair, base_in, back), block)
+    first = (base + back_in) / HALF_SPAN
+    first_grp = [lax.ppermute(x, ("grp", "slab"), role_pairs(False)) for x in jnp.split(first, 2, axis=0)]
+    role = owner.astype(jnp.int32).reshape(1, 1)
+    near = local_call(near_kernel, (role, sym, across, first_own, own_grp, first, *first_grp), block)
     total = near + jnp.where(owner, far, back2_in)
     return 2.0 * total / HALF_SPAN - vectors
 

time: 155 us -> 160 us (1.032)
  the two profiles are of different devices: /device:TPU:49 before, /device:TPU:35 now
where the time goes in v12:
time: 160 us
  waiting for transfers between devices  76.5 us (48%)
  starting transfers between devices  51.4 us (32%)
  Pallas kernels  16.4 us (10%)
  local copies, waits for them, and re-layouts  10.6 us (7%)
  other arithmetic  3.72 us (2%)
    ppermute x1, waiting for transfers between devices, body(): back_in = lax.ppermute(back, 'slab', from_owner)  45.9 us
    pallas_call x7, Pallas kernels, local_call(): pl.pallas_call(kernel, out_shape=out_shape, in_specs=spaces, out_specs=(v...  16.4 us
    ppermute x1, starting transfers between devices, body(): bulk_in = lax.ppermute(bulk, 'slab', to_owner)  14.7 us
    ppermute x1, starting transfers between devices, body(): base_in = lax.ppermute(base, 'slab', to_owner)  14 us
    ppermute x2, waiting for transfers between devices, body(): grp_in = [lax.ppermute(x, 'grp', grp_pairs) for x in grp_blocks]  10.1 us
    unnamed x32, local copies, waits for them, and re-layouts  8.99 us
    ppermute x1, waiting for transfers between devices, body(): bulk_in = lax.ppermute(bulk, 'slab', to_owner)  8.13 us
    ppermute x2, starting transfers between devices, body(): grp_in = [lax.ppermute(x, 'grp', grp_pairs) for x in grp_blocks]  6.78 us
  transfers between devices with their start and end apart: 11, of which 7 were waited for; matrix products, arithmetic and copies ran while one was open for 2% of the time, Pallas kernels for 9%

profile of v12, /device:TPU:35, one launch (start us, length us, event | category | flops | bytes accessed | tf_op | source)
XLA Modules:
  0.0 159.5 jit_solution(8289645988116014771)
XLA Ops:
  1.9 1.8 %shard_map.66 = (f32[1544,128]{1,0:T(8,128)}, f32[4,128,128]{2,1,0:T(8,128)}) custom-call(s32[4,4]{1,0:T(4,128)S(1)} %copy-done.13, f32[512,512]{1,0:T(8,128)S(1)} %copy-done.1), custom_call_target="tpu_custom_call" | custom-call | flops 1000 | bytes 1000 | tf_op jit(solution)/shard_map/pallas_call | solution.py:130
  3.7 14.7 %collective-permute-start.4 = (f32[1544,128]{1,0:T(8,128)}, f32[1544,128]{1,0:T(8,128)S(1)}, u32[]{:S(2)}, u32[]{:S(2)}) collective-permute-start(f32[1544,128]{1,0:T(8,128)} %get-tuple-element.29), channel_id=1, source_target_pairs={{1,33},{3,35},{5,37},{7,39},{9,41},{11,43},{13,45},{15,47},{17,49}... | collective-permute-start | bytes 2371592 | tf_op jit(solution)/shard_map/ppermute | solution.py:174
  18.5 1.5 shard_map.64
  19.9 3.7 %collective-permute-start.2 = (f32[256,512]{1,0:T(8,128)S(1)}, f32[256,512]{1,0:T(8,128)}, u32[]{:S(2)}, u32[]{:S(2)}) collective-permute-start(f32[256,512]{1,0:T(8,128)S(1)} %get-tuple-element.24.refs_0_), channel_id=1, source_target_pairs={{0,256},{64,320},{128,384},{192,448},{256,0},{320,64},{384,128},{4... | collective-permute-start | bytes 1572872 | tf_op jit(solution)/shard_map/ppermute | solution.py:180
  23.7 3.0 %collective-permute-start.3 = (f32[256,512]{1,0:T(8,128)}, f32[256,512]{1,0:T(8,128)}, u32[]{:S(2)}, u32[]{:S(2)}) collective-permute-start(f32[256,512]{1,0:T(8,128)} %get-tuple-element.25.refs_1_), channel_id=1, source_target_pairs={{0,256},{64,320},{128,384},{192,448},{256,0},{320,64},{384,128},{4... | collective-permute-start | bytes 1572872 | tf_op jit(solution)/shard_map/ppermute | solution.py:180
  26.7 3.7 %collective-permute-start.1 = (f32[512,256]{1,0:T(8,128)S(1)}, f32[512,256]{1,0:T(8,128)}, u32[]{:S(2)}, u32[]{:S(2)}) collective-permute-start(f32[512,256]{1,0:T(8,128)S(1)} %copy-done), channel_id=1, source_target_pairs={{0,256},{64,320},{128,384},{192,448},{256,0},{320,64},{384,128},{4... | collective-permute-start | bytes 1572872 | tf_op jit(solution)/shard_map/ppermute | solution.py:163
  30.5 1.3 collective-permute-start.5
  31.8 4.5 %collective-permute-done.2.refs_2_ = f32[256,512]{1,0:T(8,128)} collective-permute-done((f32[256,512]{1,0:T(8,128)S(1)}, f32[256,512]{1,0:T(8,128)}, u32[]{:S(2)}, u32[]{:S(2)}) %collective-permute-start.2) | collective-permute-done | bytes 524320 | tf_op jit(solution)/shard_map/ppermute | solution.py:180
  36.3 5.6 %collective-permute-done.3.refs_3_ = f32[256,512]{1,0:T(8,128)} collective-permute-done((f32[256,512]{1,0:T(8,128)}, f32[256,512]{1,0:T(8,128)}, u32[]{:S(2)}, u32[]{:S(2)}) %collective-permute-start.3) | collective-permute-done | bytes 524320 | tf_op jit(solution)/shard_map/ppermute | solution.py:180
  41.9 5.6 %collective-permute-done.1.vec_grp_ref = f32[512,256]{1,0:T(8,128)} collective-permute-done((f32[512,256]{1,0:T(8,128)S(1)}, f32[512,256]{1,0:T(8,128)}, u32[]{:S(2)}, u32[]{:S(2)}) %collective-permute-start.1) | collective-permute-done | bytes 524320 | tf_op jit(solution)/shard_map/ppermute | solution.py:163
  48.8 3.6 %shard_map.65 = (f32[512,256]{1,0:T(8,128)}, f32[512,512]{1,0:T(8,128)S(1)}, f32[512,512]{1,0:T(8,128)S(1)}) custom-call(f32[512,256]{1,0:T(8,128)S(1)} %copy-done, f32[512,512]{1,0:T(8,128)S(1)} %copy-done.8, f32[512,256]{1,0:T(8,128)} %collective-permute-done.1.vec_grp_ref, f32[256,512]{1,0:T(8,128)S(1)} %get-tuple-element.24.refs_0_, ...), custom_call_target="tpu_custom_call" | custom-call | flops 1000 | bytes 1000 | tf_op jit(solution)/shard_map/pallas_call | solution.py:130
  54.3 8.1 %collective-permute-done.4.bulk_ref = f32[1544,128]{1,0:T(8,128)S(1)} collective-permute-done((f32[1544,128]{1,0:T(8,128)}, f32[1544,128]{1,0:T(8,128)S(1)}, u32[]{:S(2)}, u32[]{:S(2)}) %collective-permute-start.4) | collective-permute-done | bytes 790560 | tf_op jit(solution)/shard_map/ppermute | solution.py:174
  67.2 1.9 %shard_map.67 = (f32[512,512]{1,0:T(8,128)S(1)}, f32[512,256]{1,0:T(8,128)S(1)}) custom-call(s32[4,4]{1,0:T(4,128)S(1)} %copy-done.14, s32[4,4]{1,0:T(4,128)S(1)} %slice_convert_fusion.in_mask, f32[512,512]{1,0:T(8,128)S(1)} %copy-done.2, f32[1544,128]{1,0:T(8,128)S(1)} %copy-done.10, f32[4,128,128]{2,1,0:T(8,128)} %get-tuple-element.41.extra_ref, ...), custom_call_target="tpu_custom_call" | custom-call | flops 1000 | bytes 1000 | tf_op jit(solution)/shard_map/pallas_call | solution.py:130
  70.5 14.0 %collective-permute-start.10 = (f32[512,256]{1,0:T(8,128)}, f32[512,256]{1,0:T(8,128)}, u32[]{:S(2)}, u32[]{:S(2)}) collective-permute-start(f32[512,256]{1,0:T(8,128)} %get-tuple-element.30.base_ref), channel_id=1, source_target_pairs={{1,33},{3,35},{5,37},{7,39},{9,41},{11,43},{13,45},{15,47},{17,49}... | collective-permute-start | bytes 1572872 | tf_op jit(solution)/shard_map/ppermute | solution.py:185
  84.5 3.7 %shard_map.68 = (f32[512,256]{1,0:T(8,128)}, f32[512,256]{1,0:T(8,128)}) custom-call(f32[512,256]{1,0:T(8,128)} %get-tuple-element.30.base_ref, f32[512,512]{1,0:T(8,128)S(1)} %get-tuple-element.33.pair_ref, f32[512,256]{1,0:T(8,128)S(1)} %collective-permute-done.5.vec_in_ref), custom_call_target="tpu_custom_call" | custom-call | flops 1000 | bytes 1000 | tf_op jit(solution)/shard_map/pallas_call | solution.py:130
  88.2 1.5 collective-permute-start.6
  89.6 45.9 %collective-permute-done.7 = f32[512,256]{1,0:T(8,128)S(1)} collective-permute-done((f32[512,256]{1,0:T(8,128)S(1)}, f32[512,256]{1,0:T(8,128)S(1)}, u32[]{:S(2)}, u32[]{:S(2)}) %collective-permute-start.7) | collective-permute-done | bytes 524320 | tf_op jit(solution)/shard_map/ppermute | solution.py:208
  138.8 1.9 %collective-permute-start.8 = (f32[256,256]{1,0:T(8,128)}, f32[256,256]{1,0:T(8,128)S(1)}, u32[]{:S(2)}, u32[]{:S(2)}) collective-permute-start(f32[256,256]{1,0:T(8,128)} %get-tuple-element.40), channel_id=1, source_target_pairs={{1,257},{3,259},{5,261},{7,263},{9,265},{11,267},{13,269},{15,271}... | collective-permute-start | bytes 786440 | tf_op jit(solution)/shard_map/ppermute | solution.py:217
  140.7 4.9 %collective-permute-start.9 = (f32[256,256]{1,0:T(8,128)}, f32[256,256]{1,0:T(8,128)}, u32[]{:S(2)}, u32[]{:S(2)}) collective-permute-start(f32[256,256]{1,0:T(8,128)} %get-tuple-element.39), channel_id=1, source_target_pairs={{1,257},{3,259},{5,261},{7,263},{9,265},{11,267},{13,269},{15,271}... | collective-permute-start | bytes 786440 | tf_op jit(solution)/shard_map/ppermute | solution.py:217
  146.8 1.7 %shard_map.70 = f32[512,256]{1,0:T(8,128)S(1)} custom-call(f32[512,512]{1,0:T(8,128)S(1)} %get-tuple-element.33.pair_ref, f32[512,256]{1,0:T(8,128)} %collective-permute-done.10.base_in_ref, f32[512,256]{1,0:T(8,128)S(1)} %copy-done.12), custom_call_target="tpu_custom_call" | custom-call | flops 1000 | bytes 1000 | tf_op jit(solution)/shard_map/pallas_call | solution.py:130
  148.5 2.0 %collective-permute-done.9.refs_1_ = f32[256,256]{1,0:T(8,128)} collective-permute-done((f32[256,256]{1,0:T(8,128)}, f32[256,256]{1,0:T(8,128)}, u32[]{:S(2)}, u32[]{:S(2)}) %collective-permute-start.9) | collective-permute-done | bytes 262176 | tf_op jit(solution)/shard_map/ppermute | solution.py:217
  150.5 2.3 %shard_map.69 = f32[512,256]{1,0:T(8,128)S(1)} custom-call(s32[1,1]{1,0:T(1,128)} %bitcast.role, f32[512,512]{1,0:T(8,128)S(1)} %copy-done.4, f32[512,512]{1,0:T(8,128)S(1)} %copy-done.6, f32[512,256]{1,0:T(8,128)} %get-tuple-element.34.own_ref, f32[512,256]{1,0:T(8,128)} %collective-permute-done.6.own_grp_ref, f32[512,256]{1,0:T(8,128)S(1)} %add_multiply_fusion.other_ref, ...), custom_call_target="tpu_custom_call" | custom-call | flops 1000 | bytes 1000 | tf_op jit(solution)/shard_map/pallas_call | solution.py:130
  152.8 4.7 %collective-permute-done.11 = f32[512,256]{1,0:T(8,128)} collective-permute-done((f32[512,256]{1,0:T(8,128)}, f32[512,256]{1,0:T(8,128)}, u32[]{:S(2)}, u32[]{:S(2)}) %collective-permute-start.11) | collective-permute-done | bytes 524320 | tf_op jit(solution)/shard_map/ppermute | solution.py:211
  157.5 2.0 %multiply_subtract_fusion = f32[512,256]{1,0:T(8,128)} fusion(f32[512,256]{1,0:T(8,128)S(1)} %copy-done, f32[512,256]{1,0:T(8,128)S(1)} %shard_map.69, f32[512,256]{1,0:T(8,128)S(1)} %shard_map.70, f32[512,256]{1,0:T(8,128)} %collective-permute-done.11, pred[]{:T(512)S(6)} %eq.9), kind=kLoop, calls=%fused_computation | loop fusion | flops 524288 | bytes 2621441 | tf_op jit(solution)/shard_map/sub | solution.py:221
  (44 shorter events, 15.6 us)
Async XLA Ops:
  0.0 1.2 copy-start.1
  1.9 16.5 %copy-start.7 = (f32[512,512]{1,0:T(8,128)S(1)}, f32[512,512]{1,0:T(8,128)}, u32[]{:S(2)}) copy-start(f32[512,512]{1,0:T(8,128)} %tiles_ref.1) | copy-start | bytes 3145732
  1.9 16.5 %copy-start.15 = (s32[4,4]{1,0:T(4,128)S(1)}, s32[4,4]{1,0:T(4,128)}, u32[]{:S(2)}) copy-start(s32[4,4]{1,0:T(4,128)} %mask.1) | copy-start | bytes 196
  3.7 23.0 %copy-start = (f32[512,256]{1,0:T(8,128)S(1)}, f32[512,256]{1,0:T(8,128)}, u32[]{:S(2)}) copy-start(f32[512,256]{1,0:T(8,128)} %vec_ref.3) | copy-start | bytes 1572868
  3.7 58.7 %collective-permute-start.4 = (f32[1544,128]{1,0:T(8,128)}, f32[1544,128]{1,0:T(8,128)S(1)}, u32[]{:S(2)}, u32[]{:S(2)}) collective-permute-start(f32[1544,128]{1,0:T(8,128)} %get-tuple-element.29), channel_id=1, source_target_pairs={{1,33},{3,35},{5,37},{7,39},{9,41},{11,43},{13,45},{15,47},{17,49}... | collective-permute-start | bytes 2371592 | tf_op jit(solution)/shard_map/ppermute | solution.py:174
  19.9 16.4 %collective-permute-start.2 = (f32[256,512]{1,0:T(8,128)S(1)}, f32[256,512]{1,0:T(8,128)}, u32[]{:S(2)}, u32[]{:S(2)}) collective-permute-start(f32[256,512]{1,0:T(8,128)S(1)} %get-tuple-element.24.refs_0_), channel_id=1, source_target_pairs={{0,256},{64,320},{128,384},{192,448},{256,0},{320,64},{384,128},{4... | collective-permute-start | bytes 1572872 | tf_op jit(solution)/shard_map/ppermute | solution.py:180
  23.7 18.3 %collective-permute-start.3 = (f32[256,512]{1,0:T(8,128)}, f32[256,512]{1,0:T(8,128)}, u32[]{:S(2)}, u32[]{:S(2)}) collective-permute-start(f32[256,512]{1,0:T(8,128)} %get-tuple-element.25.refs_1_), channel_id=1, source_target_pairs={{0,256},{64,320},{128,384},{192,448},{256,0},{320,64},{384,128},{4... | collective-permute-start | bytes 1572872 | tf_op jit(solution)/shard_map/ppermute | solution.py:180
  26.7 20.8 %collective-permute-start.1 = (f32[512,256]{1,0:T(8,128)S(1)}, f32[512,256]{1,0:T(8,128)}, u32[]{:S(2)}, u32[]{:S(2)}) collective-permute-start(f32[512,256]{1,0:T(8,128)S(1)} %copy-done), channel_id=1, source_target_pairs={{0,256},{64,320},{128,384},{192,448},{256,0},{320,64},{384,128},{4... | collective-permute-start | bytes 1572872 | tf_op jit(solution)/shard_map/ppermute | solution.py:163
  30.5 54.0 %collective-permute-start.5 = (f32[512,256]{1,0:T(8,128)S(1)}, f32[512,256]{1,0:T(8,128)S(1)}, u32[]{:S(2)}, u32[]{:S(2)}) collective-permute-start(f32[512,256]{1,0:T(8,128)S(1)} %copy-done), channel_id=1, source_target_pairs={{1,33},{3,35},{5,37},{7,39},{9,41},{11,43},{13,45},{15,47},{17,49}... | collective-permute-start | bytes 1572872 | tf_op jit(solution)/shard_map/ppermute | solution.py:164
  31.8 34.2 %copy-start.2 = (f32[512,512]{1,0:T(8,128)S(1)}, f32[512,512]{1,0:T(8,128)}, u32[]{:S(2)}) copy-start(f32[512,512]{1,0:T(8,128)} %own_ref.1) | copy-start | bytes 3145732
  47.6 1.2 copy-start.8
  52.4 1.0 copy-start.3
  53.4 1.0 copy-start.5
  66.1 1.1 copy-start.10
  69.1 19.0 %copy-start.11 = (f32[512,256]{1,0:T(8,128)}, f32[512,256]{1,0:T(8,128)S(1)}, u32[]{:S(2)}) copy-start(f32[512,256]{1,0:T(8,128)S(1)} %get-tuple-element.36.back_ref) | copy-start | bytes 1572868
  69.2 66.4 %collective-permute-start.7 = (f32[512,256]{1,0:T(8,128)S(1)}, f32[512,256]{1,0:T(8,128)S(1)}, u32[]{:S(2)}, u32[]{:S(2)}) collective-permute-start(f32[512,256]{1,0:T(8,128)S(1)} %get-tuple-element.36.back_ref), channel_id=1, source_target_pairs={{0,32},{2,34},{4,36},{6,38},{8,40},{10,42},{12,44},{14,46},{16,48}... | collective-permute-start | bytes 1572872 | tf_op jit(solution)/shard_map/ppermute | solution.py:208
  70.5 75.2 %collective-permute-start.10 = (f32[512,256]{1,0:T(8,128)}, f32[512,256]{1,0:T(8,128)}, u32[]{:S(2)}, u32[]{:S(2)}) collective-permute-start(f32[512,256]{1,0:T(8,128)} %get-tuple-element.30.base_ref), channel_id=1, source_target_pairs={{1,33},{3,35},{5,37},{7,39},{9,41},{11,43},{13,45},{15,47},{17,49}... | collective-permute-start | bytes 1572872 | tf_op jit(solution)/shard_map/ppermute | solution.py:185
  88.2 60.3 %collective-permute-start.6 = (f32[512,256]{1,0:T(8,128)}, f32[512,256]{1,0:T(8,128)}, u32[]{:S(2)}, u32[]{:S(2)}) collective-permute-start(f32[512,256]{1,0:T(8,128)} %get-tuple-element.34.own_ref), channel_id=1, source_target_pairs={{0,256},{2,258},{4,260},{6,262},{8,264},{10,266},{12,268},{14,270}... | collective-permute-start | bytes 1572872 | tf_op jit(solution)/shard_map/ppermute | solution.py:214
  135.5 22.0 %collective-permute-start.11 = (f32[512,256]{1,0:T(8,128)}, f32[512,256]{1,0:T(8,128)}, u32[]{:S(2)}, u32[]{:S(2)}) collective-permute-start(f32[512,256]{1,0:T(8,128)} %get-tuple-element.38), channel_id=1, source_target_pairs={{0,32},{2,34},{4,36},{6,38},{8,40},{10,42},{12,44},{14,46},{16,48}... | collective-permute-start | bytes 1572872 | tf_op jit(solution)/shard_map/ppermute | solution.py:211
  138.8 9.7 %collective-permute-start.8 = (f32[256,256]{1,0:T(8,128)}, f32[256,256]{1,0:T(8,128)S(1)}, u32[]{:S(2)}, u32[]{:S(2)}) collective-permute-start(f32[256,256]{1,0:T(8,128)} %get-tuple-element.40), channel_id=1, source_target_pairs={{1,257},{3,259},{5,261},{7,263},{9,265},{11,267},{13,269},{15,271}... | collective-permute-start | bytes 786440 | tf_op jit(solution)/shard_map/ppermute | solution.py:217
  140.7 9.8 %collective-permute-start.9 = (f32[256,256]{1,0:T(8,128)}, f32[256,256]{1,0:T(8,128)}, u32[]{:S(2)}, u32[]{:S(2)}) collective-permute-start(f32[256,256]{1,0:T(8,128)} %get-tuple-element.39), channel_id=1, source_target_pairs={{1,257},{3,259},{5,261},{7,263},{9,265},{11,267},{13,269},{15,271}... | collective-permute-start | bytes 786440 | tf_op jit(solution)/shard_map/ppermute | solution.py:217
  145.6 4.9 %copy-start.4 = (f32[512,512]{1,0:T(8,128)S(1)}, f32[512,512]{1,0:T(8,128)}, u32[]{:S(2)}) copy-start(f32[512,512]{1,0:T(8,128)} %copy-done.3) | copy-start | bytes 3145732
  145.6 4.9 %copy-start.6 = (f32[512,512]{1,0:T(8,128)S(1)}, f32[512,512]{1,0:T(8,128)}, u32[]{:S(2)}) copy-start(f32[512,512]{1,0:T(8,128)} %copy-done.5) | copy-start | bytes 3145732
  145.6 1.2 copy-start.12
  (3 other events, 2.3 us)

commit v13 on v6

--- a/solution.py
+++ b/solution.py
@@ -89,7 +89,7 @@
 
 
 def base_kernel(vec_ref, diag_ref, vec_grp_ref, *refs):
-    *grp_refs, base_ref, sym_ref, across_ref = refs
+    *grp_refs, low_ref, high_ref, sym_ref, across_ref = refs
     half = len(grp_refs) // 2
     grp, grp_in = (jnp.concatenate([ref[...] for ref in part], axis=0) for part in (grp_refs[:half], grp_refs[half:]))
     raw = diag_ref[...]
@@ -99,26 +99,29 @@
     across = grp + grp_in.T
     sym_ref[...] = sym
     across_ref[...] = across
-    base_ref[...] = product(split(sym), split(vec_ref[...])) + product(split(across), split(vec_grp_ref[...]))
-
-
-def first_kernel(base_ref, pair_ref, vec_in_ref, first_ref, back_ref):
+    base = product(split(sym), split(vec_ref[...])) + product(split(across), split(vec_grp_ref[...]))
+    low_ref[...], high_ref[...] = base[: low_ref.shape[0]], base[low_ref.shape[0] :]
+
+
+def joined(refs):
+    return jnp.concatenate([ref[...] for ref in refs], axis=0)
+
+
+def first_kernel(low_ref, high_ref, pair_ref, vec_in_ref, first_low_ref, first_high_ref, back_ref):
     pair = pair_ref[...]
-    first = (base_ref[...] + product(split(pair), split(vec_in_ref[...]))) / HALF_SPAN
-    first_ref[...] = first
+    first = (joined((low_ref, high_ref)) + product(split(pair), split(vec_in_ref[...]))) / HALF_SPAN
+    first_low_ref[...], first_high_ref[...] = first[: low_ref.shape[0]], first[low_ref.shape[0] :]
     back_ref[...] = product(split(pair.T), split(first))
 
 
-def near_kernel(sym_ref, across_ref, first_ref, *refs):
-    *first_grp_refs, near_ref = refs
-    first_grp = jnp.concatenate([ref[...] for ref in first_grp_refs], axis=0)
-    near_ref[...] = product(split(sym_ref[...]), split(first_ref[...])) + product(
-        split(across_ref[...]), split(first_grp)
-    )
-
-
-def far_kernel(pair_ref, base_in_ref, back_ref, far_ref):
-    first = (base_in_ref[...] + back_ref[...]) / HALF_SPAN
+def near_kernel(sym_ref, across_ref, low_ref, high_ref, grp_low_ref, grp_high_ref, near_ref):
+    near_ref[...] = product(split(sym_ref[...]), split(joined((low_ref, high_ref)))) + product(
+        split(across_ref[...]), split(joined((grp_low_ref, grp_high_ref)))
+    )
+
+
+def far_kernel(pair_ref, low_ref, high_ref, back_ref, far_ref):
+    first = (joined((low_ref, high_ref)) + back_ref[...]) / HALF_SPAN
     far_ref[...] = product(split(pair_ref[...]), split(first))
 
 
@@ -169,12 +172,15 @@
     )
     grp_in = [lax.ppermute(x, "grp", grp_pairs) for x in grp_blocks]
 
-    base, sym, across = local_call(
-        base_kernel, (vectors, diag_block, vecs_grp, *grp_blocks, *grp_in), (block, square, square)
-    )
-    base_in = lax.ppermute(base, "slab", to_owner)
-
-    base, bulk_in = lax.optimization_barrier((base, bulk_in))
+    half_block = jax.ShapeDtypeStruct((rows // 2, vectors.shape[1]), f32)
+    *base, sym, across = local_call(
+        base_kernel,
+        (vectors, diag_block, vecs_grp, *grp_blocks, *grp_in),
+        (half_block, half_block, square, square),
+    )
+    base_in = [lax.ppermute(x, "slab", to_owner) for x in base]
+
+    base[0], bulk_in = lax.optimization_barrier((base[0], bulk_in))
     mask_in = bulk_in[FIXED * tile : FIXED * tile + n_tile, :n_tile].astype(jnp.int32)
     sizes = (0, slots - FIXED)
 
@@ -196,13 +202,17 @@
         (square, block),
     )
     back_in = lax.ppermute(back, "slab", from_owner)
-    first_own, back2 = local_call(first_kernel, (base, pair, vecs_in), (block, block))
+    *first_own, back2 = local_call(first_kernel, (*base, pair, vecs_in), (half_block, half_block, block))
+    back2, base_in[0] = lax.optimization_barrier((back2, base_in[0]))
     back2_in = lax.ppermute(back2, "slab", from_owner)
 
-    far = local_call(far_kernel, (pair, base_in, back), block)
-    first = jnp.where(owner, first_own, (base + back_in) / HALF_SPAN)
-    first_grp = [lax.ppermute(x, "grp", grp_pairs) for x in jnp.split(first, 2, axis=0)]
-    near = local_call(near_kernel, (sym, across, first, *first_grp), block)
+    far = local_call(far_kernel, (pair, *base_in, back), block)
+    first = [
+        jnp.where(owner, own, (part + got) / HALF_SPAN)
+        for own, part, got in zip(first_own, base, jnp.split(back_in, 2), strict=True)
+    ]
+    first_grp = [lax.ppermute(x, "grp", grp_pairs) for x in first]
+    near = local_call(near_kernel, (sym, across, *first, *first_grp), block)
     total = near + jnp.where(owner, far, back2_in)
     return 2.0 * total / HALF_SPAN - vectors
 

time: 160 us -> 159 us (level)
  the two profiles are of different devices: /device:TPU:57 before, /device:TPU:199 now
where the time goes in v13:
time: 159 us; the launch traced here: 158 us
  waiting for transfers between devices  85.1 us (54%)
  starting transfers between devices  46.1 us (29%)
  local copies, waits for them, and re-layouts  11.6 us (7%)
  Pallas kernels  11.6 us (7%)
  other arithmetic  3.04 us (2%)
    ppermute x2, waiting for transfers between devices, body(): base_in = [lax.ppermute(x, 'slab', to_owner) for x in base]  34.1 us
    ppermute x1, waiting for transfers between devices, body(): back_in = lax.ppermute(back, 'slab', from_owner)  17.6 us
    ppermute x2, starting transfers between devices, body(): base_in = [lax.ppermute(x, 'slab', to_owner) for x in base]  15 us
    ppermute x2, waiting for transfers between devices, body(): grp_in = [lax.ppermute(x, 'grp', grp_pairs) for x in grp_blocks]  14.3 us
    pallas_call x7, Pallas kernels, local_call(): pl.pallas_call(kernel, out_shape=out_shape, in_specs=spaces, out_specs=(v...  11.6 us
    unnamed x32, local copies, waits for them, and re-layouts  10.9 us
    ppermute x1, waiting for transfers between devices, body(): bulk_in = lax.ppermute(bulk, 'slab', to_owner)  10.3 us
    ppermute x1, starting transfers between devices, body(): bulk_in = lax.ppermute(bulk, 'slab', to_owner)  9.73 us
  transfers between devices with their start and end apart: 11, of which 8 were waited for; matrix products, arithmetic and copies ran while one was open for 2% of the time, Pallas kernels for 6%

profile of v13, /device:TPU:199, one launch (start us, length us, event | category | flops | bytes accessed | tf_op | source)
XLA Modules:
  0.0 158.3 jit_solution(8948332019847645374)
XLA Ops:
  0.0 1.3 copy-done.1
  2.0 1.7 %shard_map.66 = (f32[1544,128]{1,0:T(8,128)}, f32[4,128,128]{2,1,0:T(8,128)S(1)}) custom-call(s32[4,4]{1,0:T(4,128)S(1)} %copy-done.13, f32[512,512]{1,0:T(8,128)S(1)} %copy-done.1), custom_call_target="tpu_custom_call" | custom-call | flops 1000 | bytes 1000 | tf_op jit(solution)/shard_map/pallas_call | solution.py:132
  3.7 9.7 %collective-permute-start.4 = (f32[1544,128]{1,0:T(8,128)}, f32[1544,128]{1,0:T(8,128)}, u32[]{:S(2)}, u32[]{:S(2)}) collective-permute-start(f32[1544,128]{1,0:T(8,128)} %get-tuple-element.31), channel_id=1, source_target_pairs={{1,33},{3,35},{5,37},{7,39},{9,41},{11,43},{13,45},{15,47},{17,49}... | collective-permute-start | bytes 2371592 | tf_op jit(solution)/shard_map/ppermute | solution.py:167
  13.4 3.0 %collective-permute-start.1 = (f32[512,256]{1,0:T(8,128)S(1)}, f32[512,256]{1,0:T(8,128)S(1)}, u32[]{:S(2)}, u32[]{:S(2)}) collective-permute-start(f32[512,256]{1,0:T(8,128)S(1)} %copy-done), channel_id=1, source_target_pairs={{0,256},{64,320},{128,384},{192,448},{256,0},{320,64},{384,128},{4... | collective-permute-start | bytes 1572872 | tf_op jit(solution)/shard_map/ppermute | solution.py:156
  18.4 3.8 %collective-permute-start.2 = (f32[256,512]{1,0:T(8,128)S(1)}, f32[256,512]{1,0:T(8,128)}, u32[]{:S(2)}, u32[]{:S(2)}) collective-permute-start(f32[256,512]{1,0:T(8,128)S(1)} %get-tuple-element.26.refs_0_), channel_id=1, source_target_pairs={{0,256},{64,320},{128,384},{192,448},{256,0},{320,64},{384,128},{4... | collective-permute-start | bytes 1572872 | tf_op jit(solution)/shard_map/ppermute | solution.py:173
  22.9 3.0 %collective-permute-start.3 = (f32[256,512]{1,0:T(8,128)S(1)}, f32[256,512]{1,0:T(8,128)}, u32[]{:S(2)}, u32[]{:S(2)}) collective-permute-start(f32[256,512]{1,0:T(8,128)S(1)} %get-tuple-element.27.refs_1_), channel_id=1, source_target_pairs={{0,256},{64,320},{128,384},{192,448},{256,0},{320,64},{384,128},{4... | collective-permute-start | bytes 1572872 | tf_op jit(solution)/shard_map/ppermute | solution.py:173
  26.8 2.1 %collective-permute-start.5 = (f32[512,256]{1,0:T(8,128)S(1)}, f32[512,256]{1,0:T(8,128)}, u32[]{:S(2)}, u32[]{:S(2)}) collective-permute-start(f32[512,256]{1,0:T(8,128)S(1)} %copy-done), channel_id=1, source_target_pairs={{1,33},{3,35},{5,37},{7,39},{9,41},{11,43},{13,45},{15,47},{17,49}... | collective-permute-start | bytes 1572872 | tf_op jit(solution)/shard_map/ppermute | solution.py:157
  28.8 2.1 %collective-permute-done.1.vec_grp_ref = f32[512,256]{1,0:T(8,128)S(1)} collective-permute-done((f32[512,256]{1,0:T(8,128)S(1)}, f32[512,256]{1,0:T(8,128)S(1)}, u32[]{:S(2)}, u32[]{:S(2)}) %collective-permute-start.1) | collective-permute-done | bytes 524320 | tf_op jit(solution)/shard_map/ppermute | solution.py:156
  31.7 8.7 %collective-permute-done.2.refs_2_ = f32[256,512]{1,0:T(8,128)} collective-permute-done((f32[256,512]{1,0:T(8,128)S(1)}, f32[256,512]{1,0:T(8,128)}, u32[]{:S(2)}, u32[]{:S(2)}) %collective-permute-start.2) | collective-permute-done | bytes 524320 | tf_op jit(solution)/shard_map/ppermute | solution.py:173
  40.4 5.6 %collective-permute-done.3.refs_3_ = f32[256,512]{1,0:T(8,128)} collective-permute-done((f32[256,512]{1,0:T(8,128)S(1)}, f32[256,512]{1,0:T(8,128)}, u32[]{:S(2)}, u32[]{:S(2)}) %collective-permute-start.3) | collective-permute-done | bytes 524320 | tf_op jit(solution)/shard_map/ppermute | solution.py:173
  50.4 2.5 %shard_map.65 = (f32[256,256]{1,0:T(8,128)S(1)}, f32[256,256]{1,0:T(8,128)S(1)}, f32[512,512]{1,0:T(8,128)S(1)}, f32[512,512]{1,0:T(8,128)S(1)}) custom-call(f32[512,256]{1,0:T(8,128)S(1)} %copy-done, f32[512,512]{1,0:T(8,128)S(1)} %copy-done.6, f32[512,256]{1,0:T(8,128)S(1)} %copy-done.8, f32[256,512]{1,0:T(8,128)S(1)} %copy-done.10, ...), custom_call_target="tpu_custom_call" | custom-call | flops 1000 | bytes 1000 | tf_op jit(solution)/shard_map/pallas_call | solution.py:132
  53.9 10.3 %collective-permute-done.4.bulk_ref = f32[1544,128]{1,0:T(8,128)} collective-permute-done((f32[1544,128]{1,0:T(8,128)}, f32[1544,128]{1,0:T(8,128)}, u32[]{:S(2)}, u32[]{:S(2)}) %collective-permute-start.4) | collective-permute-done | bytes 790560 | tf_op jit(solution)/shard_map/ppermute | solution.py:167
  64.9 1.3 select_reduce_fusion
  67.6 2.2 %shard_map.67 = (f32[512,512]{1,0:T(8,128)S(1)}, f32[512,256]{1,0:T(8,128)S(1)}) custom-call(s32[4,4]{1,0:T(4,128)S(1)} %copy-done.14, s32[4,4]{1,0:T(4,128)S(1)} %slice_convert_fusion.in_mask, f32[512,512]{1,0:T(8,128)S(1)} %copy-done.2, f32[1544,128]{1,0:T(8,128)} %collective-permute-done.4.bulk_ref, f32[4,128,128]{2,1,0:T(8,128)} %get-tuple-element.45.extra_ref, ...), custom_call_target="tpu_custom_call" | custom-call | flops 1000 | bytes 1000 | tf_op jit(solution)/shard_map/pallas_call | solution.py:132
  69.8 1.3 collective-permute-start.6
  71.1 13.7 %collective-permute-start.9 = (f32[256,256]{1,0:T(8,128)S(1)}, f32[256,256]{1,0:T(8,128)S(1)}, u32[]{:S(2)}, u32[]{:S(2)}) collective-permute-start(f32[256,256]{1,0:T(8,128)S(1)} %get-tuple-element.32.low_ref), channel_id=1, source_target_pairs={{1,33},{3,35},{5,37},{7,39},{9,41},{11,43},{13,45},{15,47},{17,49}... | collective-permute-start | bytes 786440 | tf_op jit(solution)/shard_map/ppermute | solution.py:181
  84.8 1.3 collective-permute-start.10
  86.1 2.9 %shard_map.68 = (f32[256,256]{1,0:T(8,128)S(1)}, f32[256,256]{1,0:T(8,128)S(1)}, f32[512,256]{1,0:T(8,128)S(1)}) custom-call(f32[256,256]{1,0:T(8,128)S(1)} %get-tuple-element.32.low_ref, f32[256,256]{1,0:T(8,128)S(1)} %get-tuple-element.33.high_ref, f32[512,512]{1,0:T(8,128)S(1)} %get-tuple-element.36.pair_ref, f32[512,256]{1,0:T(8,128)} %collective-permute-done.5.vec_in_ref), custom_call_target="tpu_custom_call" | custom-call | flops 1000 | bytes 1000 | tf_op jit(solution)/shard_map/pallas_call | solution.py:132
  89.0 34.1 %collective-permute-done.9.low_ref = f32[256,256]{1,0:T(8,128)S(1)} collective-permute-done((f32[256,256]{1,0:T(8,128)S(1)}, f32[256,256]{1,0:T(8,128)S(1)}, u32[]{:S(2)}, u32[]{:S(2)}) %collective-permute-start.9) | collective-permute-done | bytes 262176 | tf_op jit(solution)/shard_map/ppermute | solution.py:181
  124.4 17.6 %collective-permute-done.6 = f32[512,256]{1,0:T(8,128)S(1)} collective-permute-done((f32[512,256]{1,0:T(8,128)S(1)}, f32[512,256]{1,0:T(8,128)S(1)}, u32[]{:S(2)}, u32[]{:S(2)}) %collective-permute-start.6) | collective-permute-done | bytes 524320 | tf_op jit(solution)/shard_map/ppermute | solution.py:204
  142.1 3.0 %collective-permute-start.7 = (f32[256,256]{1,0:T(8,128)S(1)}, f32[256,256]{1,0:T(8,128)S(1)}, u32[]{:S(2)}, u32[]{:S(2)}) collective-permute-start(f32[256,256]{1,0:T(8,128)S(1)} %get-tuple-element.44.low_ref), channel_id=1, source_target_pairs={{0,256},{64,320},{128,384},{192,448},{256,0},{320,64},{384,128},{4... | collective-permute-start | bytes 786440 | tf_op jit(solution)/shard_map/ppermute | solution.py:214
  145.2 3.9 %collective-permute-start.8 = (f32[256,256]{1,0:T(8,128)S(1)}, f32[256,256]{1,0:T(8,128)S(1)}, u32[]{:S(2)}, u32[]{:S(2)}) collective-permute-start(f32[256,256]{1,0:T(8,128)S(1)} %get-tuple-element.43.high_ref), channel_id=1, source_target_pairs={{0,256},{64,320},{128,384},{192,448},{256,0},{320,64},{384,128},{4... | collective-permute-start | bytes 786440 | tf_op jit(solution)/shard_map/ppermute | solution.py:214
  149.7 3.7 %collective-permute-done.7.grp_low_ref = f32[256,256]{1,0:T(8,128)S(1)} collective-permute-done((f32[256,256]{1,0:T(8,128)S(1)}, f32[256,256]{1,0:T(8,128)S(1)}, u32[]{:S(2)}, u32[]{:S(2)}) %collective-permute-start.7) | collective-permute-done | bytes 262176 | tf_op jit(solution)/shard_map/ppermute | solution.py:214
  153.5 2.9 %collective-permute-done.8.grp_high_ref = f32[256,256]{1,0:T(8,128)S(1)} collective-permute-done((f32[256,256]{1,0:T(8,128)S(1)}, f32[256,256]{1,0:T(8,128)S(1)}, u32[]{:S(2)}, u32[]{:S(2)}) %collective-permute-start.8) | collective-permute-done | bytes 262176 | tf_op jit(solution)/shard_map/ppermute | solution.py:214
  (43 shorter events, 16.4 us)
Async XLA Ops:
  0.0 13.4 %copy-start = (f32[512,256]{1,0:T(8,128)S(1)}, f32[512,256]{1,0:T(8,128)}, u32[]{:S(2)}) copy-start(f32[512,256]{1,0:T(8,128)} %vec_ref.3) | copy-start | bytes 1572868
  0.0 1.3 copy-start.1
  2.0 14.5 %copy-start.15 = (s32[4,4]{1,0:T(4,128)S(1)}, s32[4,4]{1,0:T(4,128)}, u32[]{:S(2)}) copy-start(s32[4,4]{1,0:T(4,128)} %mask.1) | copy-start | bytes 196
  3.7 60.5 %collective-permute-start.4 = (f32[1544,128]{1,0:T(8,128)}, f32[1544,128]{1,0:T(8,128)}, u32[]{:S(2)}, u32[]{:S(2)}) collective-permute-start(f32[1544,128]{1,0:T(8,128)} %get-tuple-element.31), channel_id=1, source_target_pairs={{1,33},{3,35},{5,37},{7,39},{9,41},{11,43},{13,45},{15,47},{17,49}... | collective-permute-start | bytes 2371592 | tf_op jit(solution)/shard_map/ppermute | solution.py:167
  13.4 17.5 %collective-permute-start.1 = (f32[512,256]{1,0:T(8,128)S(1)}, f32[512,256]{1,0:T(8,128)S(1)}, u32[]{:S(2)}, u32[]{:S(2)}) collective-permute-start(f32[512,256]{1,0:T(8,128)S(1)} %copy-done), channel_id=1, source_target_pairs={{0,256},{64,320},{128,384},{192,448},{256,0},{320,64},{384,128},{4... | collective-permute-start | bytes 1572872 | tf_op jit(solution)/shard_map/ppermute | solution.py:156
  16.5 1.2 copy-start.5
  18.4 22.0 %collective-permute-start.2 = (f32[256,512]{1,0:T(8,128)S(1)}, f32[256,512]{1,0:T(8,128)}, u32[]{:S(2)}, u32[]{:S(2)}) collective-permute-start(f32[256,512]{1,0:T(8,128)S(1)} %get-tuple-element.26.refs_0_), channel_id=1, source_target_pairs={{0,256},{64,320},{128,384},{192,448},{256,0},{320,64},{384,128},{4... | collective-permute-start | bytes 1572872 | tf_op jit(solution)/shard_map/ppermute | solution.py:173
  22.1 0.8 copy-start.9
  22.9 23.1 %collective-permute-start.3 = (f32[256,512]{1,0:T(8,128)S(1)}, f32[256,512]{1,0:T(8,128)}, u32[]{:S(2)}, u32[]{:S(2)}) collective-permute-start(f32[256,512]{1,0:T(8,128)S(1)} %get-tuple-element.27.refs_1_), channel_id=1, source_target_pairs={{0,256},{64,320},{128,384},{192,448},{256,0},{320,64},{384,128},{4... | collective-permute-start | bytes 1572872 | tf_op jit(solution)/shard_map/ppermute | solution.py:173
  26.8 59.4 %collective-permute-start.5 = (f32[512,256]{1,0:T(8,128)S(1)}, f32[512,256]{1,0:T(8,128)}, u32[]{:S(2)}, u32[]{:S(2)}) collective-permute-start(f32[512,256]{1,0:T(8,128)S(1)} %copy-done), channel_id=1, source_target_pairs={{1,33},{3,35},{5,37},{7,39},{9,41},{11,43},{13,45},{15,47},{17,49}... | collective-permute-start | bytes 1572872 | tf_op jit(solution)/shard_map/ppermute | solution.py:157
  28.8 38.8 %copy-start.2 = (f32[512,512]{1,0:T(8,128)S(1)}, f32[512,512]{1,0:T(8,128)}, u32[]{:S(2)}) copy-start(f32[512,512]{1,0:T(8,128)} %own_ref.1) | copy-start | bytes 3145732
  30.9 0.8 copy-start.7
  46.0 1.2 copy-start.6
  47.3 1.0 copy-start.8
  48.3 1.0 copy-start.10
  49.3 1.0 copy-start.12
  52.9 1.0 copy-start.3
  69.8 72.2 %collective-permute-start.6 = (f32[512,256]{1,0:T(8,128)S(1)}, f32[512,256]{1,0:T(8,128)S(1)}, u32[]{:S(2)}, u32[]{:S(2)}) collective-permute-start(f32[512,256]{1,0:T(8,128)S(1)} %get-tuple-element.38.back_ref), channel_id=1, source_target_pairs={{0,32},{2,34},{4,36},{6,38},{8,40},{10,42},{12,44},{14,46},{16,48}... | collective-permute-start | bytes 1572872 | tf_op jit(solution)/shard_map/ppermute | solution.py:204
  71.1 52.0 %collective-permute-start.9 = (f32[256,256]{1,0:T(8,128)S(1)}, f32[256,256]{1,0:T(8,128)S(1)}, u32[]{:S(2)}, u32[]{:S(2)}) collective-permute-start(f32[256,256]{1,0:T(8,128)S(1)} %get-tuple-element.32.low_ref), channel_id=1, source_target_pairs={{1,33},{3,35},{5,37},{7,39},{9,41},{11,43},{13,45},{15,47},{17,49}... | collective-permute-start | bytes 786440 | tf_op jit(solution)/shard_map/ppermute | solution.py:181
  84.8 64.3 %collective-permute-start.10 = (f32[256,256]{1,0:T(8,128)S(1)}, f32[256,256]{1,0:T(8,128)S(1)}, u32[]{:S(2)}, u32[]{:S(2)}) collective-permute-start(f32[256,256]{1,0:T(8,128)S(1)} %get-tuple-element.33.high_ref), channel_id=1, source_target_pairs={{1,33},{3,35},{5,37},{7,39},{9,41},{11,43},{13,45},{15,47},{17,49}... | collective-permute-start | bytes 786440 | tf_op jit(solution)/shard_map/ppermute | solution.py:181
  123.1 34.3 %collective-permute-start.11 = (f32[512,256]{1,0:T(8,128)S(1)}, f32[512,256]{1,0:T(8,128)S(1)}, u32[]{:S(2)}, u32[]{:S(2)}) collective-permute-start(f32[512,256]{1,0:T(8,128)S(1)} %get-tuple-element.42), channel_id=1, source_target_pairs={{0,32},{2,34},{4,36},{6,38},{8,40},{10,42},{12,44},{14,46},{16,48}... | collective-permute-start | bytes 1572872 | tf_op jit(solution)/shard_map/ppermute | solution.py:207
  142.1 11.3 %collective-permute-start.7 = (f32[256,256]{1,0:T(8,128)S(1)}, f32[256,256]{1,0:T(8,128)S(1)}, u32[]{:S(2)}, u32[]{:S(2)}) collective-permute-start(f32[256,256]{1,0:T(8,128)S(1)} %get-tuple-element.44.low_ref), channel_id=1, source_target_pairs={{0,256},{64,320},{128,384},{192,448},{256,0},{320,64},{384,128},{4... | collective-permute-start | bytes 786440 | tf_op jit(solution)/shard_map/ppermute | solution.py:214
  145.2 11.2 %copy-start.4 = (f32[512,512]{1,0:T(8,128)S(1)}, f32[512,512]{1,0:T(8,128)}, u32[]{:S(2)}) copy-start(f32[512,512]{1,0:T(8,128)} %copy-done.3) | copy-start | bytes 3145732
  145.2 11.2 %collective-permute-start.8 = (f32[256,256]{1,0:T(8,128)S(1)}, f32[256,256]{1,0:T(8,128)S(1)}, u32[]{:S(2)}, u32[]{:S(2)}) collective-permute-start(f32[256,256]{1,0:T(8,128)S(1)} %get-tuple-element.43.high_ref), channel_id=1, source_target_pairs={{0,256},{64,320},{128,384},{192,448},{256,0},{320,64},{384,128},{4... | collective-permute-start | bytes 786440 | tf_op jit(solution)/shard_map/ppermute | solution.py:214
  (3 other events, 2.2 us)

commit v14 on v6

--- a/solution.py
+++ b/solution.py
@@ -172,8 +172,6 @@
     base, sym, across = local_call(
         base_kernel, (vectors, diag_block, vecs_grp, *grp_blocks, *grp_in), (block, square, square)
     )
-    base_in = lax.ppermute(base, "slab", to_owner)
-
     base, bulk_in = lax.optimization_barrier((base, bulk_in))
     mask_in = bulk_in[FIXED * tile : FIXED * tile + n_tile, :n_tile].astype(jnp.int32)
     sizes = (0, slots - FIXED)
@@ -198,6 +196,8 @@
     back_in = lax.ppermute(back, "slab", from_owner)
     first_own, back2 = local_call(first_kernel, (base, pair, vecs_in), (block, block))
     back2_in = lax.ppermute(back2, "slab", from_owner)
+    later, back_in = lax.optimization_barrier((base, back_in))
+    base_in = lax.ppermute(later, "slab", to_owner)
 
     far = local_call(far_kernel, (pair, base_in, back), block)
     first = jnp.where(owner, first_own, (base + back_in) / HALF_SPAN)

time: 160 us -> 156 us (0.975)
  starting transfers between devices: 52 us -> 39.9 us
  waiting for transfers between devices: 79.7 us -> 88.6 us
    ppermute x1, starting transfers between devices: 13.5 us -> 1.49 us  [body(): base_in = lax.ppermute(later, 'slab', to_owner)]
    ppermute x1, waiting for transfers between devices: 56.2 us -> 61 us  [body(): back_in = lax.ppermute(back, 'slab', from_owner)]
    ppermute x1, waiting for transfers between devices: 0.01 us -> 4.6 us  [body(): vecs_in = lax.ppermute(vectors, 'slab', to_owner)]
  transfers between devices with their start and end apart: 10 -> 10, of which waited for: 6 -> 7; matrix products, arithmetic and copies ran while one was open for 2% -> 2% of each run, Pallas kernels for 6% -> 6%
where the time goes in v14:
time: 156 us
  waiting for transfers between devices  88.6 us (57%)
  starting transfers between devices  39.9 us (26%)
  local copies, waits for them, and re-layouts  11.7 us (8%)
  Pallas kernels  11.5 us (7%)
  other arithmetic  3.05 us (2%)
    ppermute x1, waiting for transfers between devices, body(): back_in = lax.ppermute(back, 'slab', from_owner)  61 us
    ppermute x1, starting transfers between devices, body(): bulk_in = lax.ppermute(bulk, 'slab', to_owner)  15.4 us
    pallas_call x7, Pallas kernels, local_call(): pl.pallas_call(kernel, out_shape=out_shape, in_specs=spaces, out_specs=(v...  11.5 us
    unnamed x32, local copies, waits for them, and re-layouts  10.9 us
    ppermute x2, waiting for transfers between devices, body(): grp_in = [lax.ppermute(x, 'grp', grp_pairs) for x in grp_blocks]  10.3 us
    ppermute x2, waiting for transfers between devices, body(): lax.ppermute(x, 'grp', grp_pairs)  7.44 us
    ppermute x2, starting transfers between devices, body(): lax.ppermute(x, 'grp', grp_pairs)  6.92 us
    ppermute x2, starting transfers between devices, body(): grp_in = [lax.ppermute(x, 'grp', grp_pairs) for x in grp_blocks]  6.78 us
  transfers between devices with their start and end apart: 10, of which 7 were waited for; matrix products, arithmetic and copies ran while one was open for 2% of the time, Pallas kernels for 6%

profile of v14, /device:TPU:57, one launch (start us, length us, event | category | flops | bytes accessed | tf_op | source)
XLA Modules:
  0.0 155.7 jit_solution(2733080375860051777)
XLA Ops:
  0.0 1.3 copy-done.1
  2.0 1.7 %shard_map.66 = (f32[1544,128]{1,0:T(8,128)}, f32[4,128,128]{2,1,0:T(8,128)S(1)}) custom-call(s32[4,4]{1,0:T(4,128)S(1)} %copy-done.13, f32[512,512]{1,0:T(8,128)S(1)} %copy-done.1), custom_call_target="tpu_custom_call" | custom-call | flops 1000 | bytes 1000 | tf_op jit(solution)/shard_map/pallas_call | solution.py:129
  3.7 15.4 %collective-permute-start.4 = (f32[1544,128]{1,0:T(8,128)}, f32[1544,128]{1,0:T(8,128)}, u32[]{:S(2)}, u32[]{:S(2)}) collective-permute-start(f32[1544,128]{1,0:T(8,128)} %get-tuple-element.29), channel_id=1, source_target_pairs={{1,33},{3,35},{5,37},{7,39},{9,41},{11,43},{13,45},{15,47},{17,49}... | collective-permute-start | bytes 2371592 | tf_op jit(solution)/shard_map/ppermute | solution.py:164
  19.1 4.6 %collective-permute-start.1 = (f32[512,256]{1,0:T(8,128)S(1)}, f32[512,256]{1,0:T(8,128)S(1)}, u32[]{:S(2)}, u32[]{:S(2)}) collective-permute-start(f32[512,256]{1,0:T(8,128)S(1)} %copy-done), channel_id=1, source_target_pairs={{0,256},{64,320},{128,384},{192,448},{256,0},{320,64},{384,128},{4... | collective-permute-start | bytes 1572872 | tf_op jit(solution)/shard_map/ppermute | solution.py:153
  25.7 2.1 %collective-permute-start.2 = (f32[256,512]{1,0:T(8,128)S(1)}, f32[256,512]{1,0:T(8,128)}, u32[]{:S(2)}, u32[]{:S(2)}) collective-permute-start(f32[256,512]{1,0:T(8,128)S(1)} %get-tuple-element.24.refs_0_), channel_id=1, source_target_pairs={{0,256},{64,320},{128,384},{192,448},{256,0},{320,64},{384,128},{4... | collective-permute-start | bytes 1572872 | tf_op jit(solution)/shard_map/ppermute | solution.py:170
  28.6 4.7 %collective-permute-start.3 = (f32[256,512]{1,0:T(8,128)S(1)}, f32[256,512]{1,0:T(8,128)}, u32[]{:S(2)}, u32[]{:S(2)}) collective-permute-start(f32[256,512]{1,0:T(8,128)S(1)} %get-tuple-element.25.refs_1_), channel_id=1, source_target_pairs={{0,256},{64,320},{128,384},{192,448},{256,0},{320,64},{384,128},{4... | collective-permute-start | bytes 1572872 | tf_op jit(solution)/shard_map/ppermute | solution.py:170
  34.1 2.1 %collective-permute-start.5 = (f32[512,256]{1,0:T(8,128)S(1)}, f32[512,256]{1,0:T(8,128)}, u32[]{:S(2)}, u32[]{:S(2)}) collective-permute-start(f32[512,256]{1,0:T(8,128)S(1)} %copy-done), channel_id=1, source_target_pairs={{1,33},{3,35},{5,37},{7,39},{9,41},{11,43},{13,45},{15,47},{17,49}... | collective-permute-start | bytes 1572872 | tf_op jit(solution)/shard_map/ppermute | solution.py:154
  37.0 4.7 %collective-permute-done.2.refs_2_ = f32[256,512]{1,0:T(8,128)} collective-permute-done((f32[256,512]{1,0:T(8,128)S(1)}, f32[256,512]{1,0:T(8,128)}, u32[]{:S(2)}, u32[]{:S(2)}) %collective-permute-start.2) | collective-permute-done | bytes 524320 | tf_op jit(solution)/shard_map/ppermute | solution.py:170
  41.7 5.6 %collective-permute-done.3.refs_3_ = f32[256,512]{1,0:T(8,128)} collective-permute-done((f32[256,512]{1,0:T(8,128)S(1)}, f32[256,512]{1,0:T(8,128)}, u32[]{:S(2)}, u32[]{:S(2)}) %collective-permute-start.3) | collective-permute-done | bytes 524320 | tf_op jit(solution)/shard_map/ppermute | solution.py:170
  47.3 1.2 copy-done.6
  51.6 2.5 %shard_map.65 = (f32[512,256]{1,0:T(8,128)S(1)}, f32[512,512]{1,0:T(8,128)S(1)}, f32[512,512]{1,0:T(8,128)S(1)}) custom-call(f32[512,256]{1,0:T(8,128)S(1)} %copy-done, f32[512,512]{1,0:T(8,128)S(1)} %copy-done.6, f32[512,256]{1,0:T(8,128)S(1)} %copy-done.8, f32[256,512]{1,0:T(8,128)S(1)} %copy-done.10, f32[256,512]{1,0:T(8,128)S(1)} %copy-done.12, ...), custom_call_target="tpu_custom_call" | custom-call | flops 1000 | bytes 1000 | tf_op jit(solution)/shard_map/pallas_call | solution.py:129
  55.1 5.2 %collective-permute-done.4.bulk_ref = f32[1544,128]{1,0:T(8,128)} collective-permute-done((f32[1544,128]{1,0:T(8,128)}, f32[1544,128]{1,0:T(8,128)}, u32[]{:S(2)}, u32[]{:S(2)}) %collective-permute-start.4) | collective-permute-done | bytes 790560 | tf_op jit(solution)/shard_map/ppermute | solution.py:164
  61.0 1.3 select_reduce_fusion
  63.8 2.2 %shard_map.67 = (f32[512,512]{1,0:T(8,128)S(1)}, f32[512,256]{1,0:T(8,128)S(1)}) custom-call(s32[4,4]{1,0:T(4,128)S(1)} %copy-done.14, s32[4,4]{1,0:T(4,128)S(1)} %slice_convert_fusion.in_mask, f32[512,512]{1,0:T(8,128)S(1)} %copy-done.2, f32[1544,128]{1,0:T(8,128)} %collective-permute-done.4.bulk_ref, f32[4,128,128]{2,1,0:T(8,128)} %get-tuple-element.41.extra_ref, ...), custom_call_target="tpu_custom_call" | custom-call | flops 1000 | bytes 1000 | tf_op jit(solution)/shard_map/pallas_call | solution.py:129
  66.0 1.3 collective-permute-start.6
  67.3 4.6 %collective-permute-done.5.vec_in_ref = f32[512,256]{1,0:T(8,128)} collective-permute-done((f32[512,256]{1,0:T(8,128)S(1)}, f32[512,256]{1,0:T(8,128)}, u32[]{:S(2)}, u32[]{:S(2)}) %collective-permute-start.5) | collective-permute-done | bytes 524320 | tf_op jit(solution)/shard_map/ppermute | solution.py:154
  71.9 2.9 %shard_map.68 = (f32[512,256]{1,0:T(8,128)S(1)}, f32[512,256]{1,0:T(8,128)S(1)}) custom-call(f32[512,256]{1,0:T(8,128)S(1)} %get-tuple-element.37.base_ref, f32[512,512]{1,0:T(8,128)S(1)} %get-tuple-element.33.pair_ref, f32[512,256]{1,0:T(8,128)} %collective-permute-done.5.vec_in_ref), custom_call_target="tpu_custom_call" | custom-call | flops 1000 | bytes 1000 | tf_op jit(solution)/shard_map/pallas_call | solution.py:129
  74.7 1.3 collective-permute-start.10
  76.0 61.0 %collective-permute-done.6 = f32[512,256]{1,0:T(8,128)S(1)} collective-permute-done((f32[512,256]{1,0:T(8,128)S(1)}, f32[512,256]{1,0:T(8,128)S(1)}, u32[]{:S(2)}, u32[]{:S(2)}) %collective-permute-start.6) | collective-permute-done | bytes 524320 | tf_op jit(solution)/shard_map/ppermute | solution.py:196
  137.1 1.5 collective-permute-start.9
  138.7 4.9 %collective-permute-start.8 = (f32[256,256]{1,0:T(8,128)S(1)}, f32[256,256]{1,0:T(8,128)S(1)}, u32[]{:S(2)}, u32[]{:S(2)}) collective-permute-start(f32[256,256]{1,0:T(8,128)S(1)} %get-tuple-element.39), channel_id=1, source_target_pairs={{0,256},{64,320},{128,384},{192,448},{256,0},{320,64},{384,128},{4... | collective-permute-start | bytes 786440 | tf_op jit(solution)/shard_map/ppermute | solution.py:204
  143.7 2.0 %collective-permute-start.7 = (f32[256,256]{1,0:T(8,128)S(1)}, f32[256,256]{1,0:T(8,128)S(1)}, u32[]{:S(2)}, u32[]{:S(2)}) collective-permute-start(f32[256,256]{1,0:T(8,128)S(1)} %get-tuple-element.40), channel_id=1, source_target_pairs={{0,256},{64,320},{128,384},{192,448},{256,0},{320,64},{384,128},{4... | collective-permute-start | bytes 786440 | tf_op jit(solution)/shard_map/ppermute | solution.py:204
  145.7 4.7 %collective-permute-done.8.refs_1_ = f32[256,256]{1,0:T(8,128)S(1)} collective-permute-done((f32[256,256]{1,0:T(8,128)S(1)}, f32[256,256]{1,0:T(8,128)S(1)}, u32[]{:S(2)}, u32[]{:S(2)}) %collective-permute-start.8) | collective-permute-done | bytes 262176 | tf_op jit(solution)/shard_map/ppermute | solution.py:204
  150.3 2.8 %collective-permute-done.7.refs_0_ = f32[256,256]{1,0:T(8,128)S(1)} collective-permute-done((f32[256,256]{1,0:T(8,128)S(1)}, f32[256,256]{1,0:T(8,128)S(1)}, u32[]{:S(2)}, u32[]{:S(2)}) %collective-permute-start.7) | collective-permute-done | bytes 262176 | tf_op jit(solution)/shard_map/ppermute | solution.py:204
  (42 shorter events, 13.9 us)
Async XLA Ops:
  0.0 19.1 %copy-start = (f32[512,256]{1,0:T(8,128)S(1)}, f32[512,256]{1,0:T(8,128)}, u32[]{:S(2)}) copy-start(f32[512,256]{1,0:T(8,128)} %vec_ref.3) | copy-start | bytes 1572868
  0.0 1.3 copy-start.1
  2.0 21.8 %copy-start.15 = (s32[4,4]{1,0:T(4,128)S(1)}, s32[4,4]{1,0:T(4,128)}, u32[]{:S(2)}) copy-start(s32[4,4]{1,0:T(4,128)} %mask.1) | copy-start | bytes 196
  3.7 56.6 %collective-permute-start.4 = (f32[1544,128]{1,0:T(8,128)}, f32[1544,128]{1,0:T(8,128)}, u32[]{:S(2)}, u32[]{:S(2)}) collective-permute-start(f32[1544,128]{1,0:T(8,128)} %get-tuple-element.29), channel_id=1, source_target_pairs={{1,33},{3,35},{5,37},{7,39},{9,41},{11,43},{13,45},{15,47},{17,49}... | collective-permute-start | bytes 2371592 | tf_op jit(solution)/shard_map/ppermute | solution.py:164
  19.1 17.0 %collective-permute-start.1 = (f32[512,256]{1,0:T(8,128)S(1)}, f32[512,256]{1,0:T(8,128)S(1)}, u32[]{:S(2)}, u32[]{:S(2)}) collective-permute-start(f32[512,256]{1,0:T(8,128)S(1)} %copy-done), channel_id=1, source_target_pairs={{0,256},{64,320},{128,384},{192,448},{256,0},{320,64},{384,128},{4... | collective-permute-start | bytes 1572872 | tf_op jit(solution)/shard_map/ppermute | solution.py:153
  23.8 1.2 copy-start.5
  25.7 16.0 %collective-permute-start.2 = (f32[256,512]{1,0:T(8,128)S(1)}, f32[256,512]{1,0:T(8,128)}, u32[]{:S(2)}, u32[]{:S(2)}) collective-permute-start(f32[256,512]{1,0:T(8,128)S(1)} %get-tuple-element.24.refs_0_), channel_id=1, source_target_pairs={{0,256},{64,320},{128,384},{192,448},{256,0},{320,64},{384,128},{4... | collective-permute-start | bytes 1572872 | tf_op jit(solution)/shard_map/ppermute | solution.py:170
  27.8 0.8 copy-start.9
  28.6 18.6 %collective-permute-start.3 = (f32[256,512]{1,0:T(8,128)S(1)}, f32[256,512]{1,0:T(8,128)}, u32[]{:S(2)}, u32[]{:S(2)}) collective-permute-start(f32[256,512]{1,0:T(8,128)S(1)} %get-tuple-element.25.refs_1_), channel_id=1, source_target_pairs={{0,256},{64,320},{128,384},{192,448},{256,0},{320,64},{384,128},{4... | collective-permute-start | bytes 1572872 | tf_op jit(solution)/shard_map/ppermute | solution.py:170
  33.3 0.8 copy-start.11
  34.1 37.8 %collective-permute-start.5 = (f32[512,256]{1,0:T(8,128)S(1)}, f32[512,256]{1,0:T(8,128)}, u32[]{:S(2)}, u32[]{:S(2)}) collective-permute-start(f32[512,256]{1,0:T(8,128)S(1)} %copy-done), channel_id=1, source_target_pairs={{1,33},{3,35},{5,37},{7,39},{9,41},{11,43},{13,45},{15,47},{17,49}... | collective-permute-start | bytes 1572872 | tf_op jit(solution)/shard_map/ppermute | solution.py:154
  36.2 27.6 %copy-start.2 = (f32[512,512]{1,0:T(8,128)S(1)}, f32[512,512]{1,0:T(8,128)}, u32[]{:S(2)}) copy-start(f32[512,512]{1,0:T(8,128)} %own_ref.1) | copy-start | bytes 3145732
  36.2 0.8 copy-start.7
  47.3 1.2 copy-start.6
  48.5 1.0 copy-start.8
  49.5 1.0 copy-start.10
  50.6 1.0 copy-start.12
  54.1 1.0 copy-start.3
  66.0 71.1 %collective-permute-start.6 = (f32[512,256]{1,0:T(8,128)S(1)}, f32[512,256]{1,0:T(8,128)S(1)}, u32[]{:S(2)}, u32[]{:S(2)}) collective-permute-start(f32[512,256]{1,0:T(8,128)S(1)} %get-tuple-element.35.back_ref), channel_id=1, source_target_pairs={{0,32},{2,34},{4,36},{6,38},{8,40},{10,42},{12,44},{14,46},{16,48}... | collective-permute-start | bytes 1572872 | tf_op jit(solution)/shard_map/ppermute | solution.py:196
  74.7 80.0 %collective-permute-start.10 = (f32[512,256]{1,0:T(8,128)S(1)}, f32[512,256]{1,0:T(8,128)S(1)}, u32[]{:S(2)}, u32[]{:S(2)}) collective-permute-start(f32[512,256]{1,0:T(8,128)S(1)} %get-tuple-element.38), channel_id=1, source_target_pairs={{0,32},{2,34},{4,36},{6,38},{8,40},{10,42},{12,44},{14,46},{16,48}... | collective-permute-start | bytes 1572872 | tf_op jit(solution)/shard_map/ppermute | solution.py:198
  137.1 17.0 %collective-permute-start.9 = (f32[512,256]{1,0:T(8,128)S(1)}, f32[512,256]{1,0:T(8,128)S(1)}, u32[]{:S(2)}, u32[]{:S(2)}) collective-permute-start(f32[512,256]{1,0:T(8,128)S(1)} %get-tuple-element.37.base_ref), channel_id=1, source_target_pairs={{1,33},{3,35},{5,37},{7,39},{9,41},{11,43},{13,45},{15,47},{17,49}... | collective-permute-start | bytes 1572872 | tf_op jit(solution)/shard_map/ppermute | solution.py:200
  138.7 14.4 %copy-start.4 = (f32[512,512]{1,0:T(8,128)S(1)}, f32[512,512]{1,0:T(8,128)}, u32[]{:S(2)}) copy-start(f32[512,512]{1,0:T(8,128)} %copy-done.3) | copy-start | bytes 3145732
  138.7 11.6 %collective-permute-start.8 = (f32[256,256]{1,0:T(8,128)S(1)}, f32[256,256]{1,0:T(8,128)S(1)}, u32[]{:S(2)}, u32[]{:S(2)}) collective-permute-start(f32[256,256]{1,0:T(8,128)S(1)} %get-tuple-element.39), channel_id=1, source_target_pairs={{0,256},{64,320},{128,384},{192,448},{256,0},{320,64},{384,128},{4... | collective-permute-start | bytes 786440 | tf_op jit(solution)/shard_map/ppermute | solution.py:204
  143.7 9.4 %collective-permute-start.7 = (f32[256,256]{1,0:T(8,128)S(1)}, f32[256,256]{1,0:T(8,128)S(1)}, u32[]{:S(2)}, u32[]{:S(2)}) collective-permute-start(f32[256,256]{1,0:T(8,128)S(1)} %get-tuple-element.40), channel_id=1, source_target_pairs={{0,256},{64,320},{128,384},{192,448},{256,0},{320,64},{384,128},{4... | collective-permute-start | bytes 786440 | tf_op jit(solution)/shard_map/ppermute | solution.py:204
  (2 other events, 1.4 us)

commit v15 on v9

--- a/solution.py
+++ b/solution.py
@@ -184,8 +184,6 @@
     base, sym, across = local_call(
         base_kernel, (vectors, diag_block, vecs_grp, *grp_blocks, *grp_in), (block, square, square)
     )
-    base_in = lax.ppermute(base, "slab", to_owner)
-
     base, bulk_in = lax.optimization_barrier((base, bulk_in))
     mask_in = bulk_in[FIXED * tile : FIXED * tile + n_tile, :n_tile].astype(jnp.int32)
     sizes = (0, slots - FIXED)
@@ -210,8 +208,9 @@
     )
     back_in = [lax.ppermute(x, "slab", from_owner) for x in back]
     first_own, back2 = local_call(first_kernel, (base, pair, vecs_in), (block, block))
-    back2, back_in[0] = lax.optimization_barrier((back2, back_in[0]))
     back2_in = lax.ppermute(back2, "slab", from_owner)
+    later, back_in[-1] = lax.optimization_barrier((base, back_in[-1]))
+    base_in = lax.ppermute(later, "slab", to_owner)
 
     far = local_call(far_kernel, (pair, base_in, *back), block)
     role = owner.astype(jnp.int32).reshape(1, 1)

time: 164 us -> 156 us (0.951)
  the two profiles are of different devices: /device:TPU:40 before, /device:TPU:35 now
where the time goes in v15:
time: 156 us; the launch traced here: 155 us
  waiting for transfers between devices  87.2 us (56%)
  starting transfers between devices  40.2 us (26%)
  Pallas kernels  14.4 us (9%)
  local copies, waits for them, and re-layouts  9.65 us (6%)
  other arithmetic  2.61 us (2%)
    ppermute x2, waiting for transfers between devices, body(): back_in = [lax.ppermute(x, 'slab', from_owner) for x in back]  39.7 us
    ppermute x1, starting transfers between devices, body(): bulk_in = lax.ppermute(bulk, 'slab', to_owner)  14.7 us
    pallas_call x9, Pallas kernels, local_call(): pl.pallas_call(kernel, out_shape=out_shape, in_specs=spaces, out_specs=(v...  14.4 us
    ppermute x1, waiting for transfers between devices, body(): back2_in = lax.ppermute(back2, 'slab', from_owner)  10.5 us
    unnamed x36, local copies, waits for them, and re-layouts  8.94 us
    ppermute x1, waiting for transfers between devices, body(): base_in = lax.ppermute(later, 'slab', to_owner)  8.71 us
    ppermute x2, waiting for transfers between devices, body(): grp_in = [lax.ppermute(x, 'grp', grp_pairs) for x in grp_blocks]  8.58 us
    ppermute x1, waiting for transfers between devices, body(): bulk_in = lax.ppermute(bulk, 'slab', to_owner)  7.13 us
  transfers between devices with their start and end apart: 11, of which 10 were waited for; matrix products, arithmetic and copies ran while one was open for 1% of the time, Pallas kernels for 8%

profile of v15, /device:TPU:35, one launch (start us, length us, event | category | flops | bytes accessed | tf_op | source)
XLA Modules:
  0.0 155.0 jit_solution(13509052544723391376)
XLA Ops:
  1.9 1.8 %shard_map.66 = (f32[1544,128]{1,0:T(8,128)}, f32[4,128,128]{2,1,0:T(8,128)}) custom-call(s32[4,4]{1,0:T(4,128)S(1)} %copy-done.15, f32[512,512]{1,0:T(8,128)S(1)} %copy-done.1), custom_call_target="tpu_custom_call" | custom-call | flops 1000 | bytes 1000 | tf_op jit(solution)/shard_map/pallas_call | solution.py:141
  3.7 14.7 %collective-permute-start.4 = (f32[1544,128]{1,0:T(8,128)}, f32[1544,128]{1,0:T(8,128)S(1)}, u32[]{:S(2)}, u32[]{:S(2)}) collective-permute-start(f32[1544,128]{1,0:T(8,128)} %get-tuple-element.30), channel_id=1, source_target_pairs={{1,33},{3,35},{5,37},{7,39},{9,41},{11,43},{13,45},{15,47},{17,49}... | collective-permute-start | bytes 2371592 | tf_op jit(solution)/shard_map/ppermute | solution.py:176
  19.1 3.8 %collective-permute-start.2 = (f32[256,512]{1,0:T(8,128)S(1)}, f32[256,512]{1,0:T(8,128)}, u32[]{:S(2)}, u32[]{:S(2)}) collective-permute-start(f32[256,512]{1,0:T(8,128)S(1)} %get-tuple-element.25.refs_0_), channel_id=1, source_target_pairs={{0,256},{64,320},{128,384},{192,448},{256,0},{320,64},{384,128},{4... | collective-permute-start | bytes 1572872 | tf_op jit(solution)/shard_map/ppermute | solution.py:182
  22.9 3.0 %collective-permute-start.3 = (f32[256,512]{1,0:T(8,128)S(1)}, f32[256,512]{1,0:T(8,128)}, u32[]{:S(2)}, u32[]{:S(2)}) collective-permute-start(f32[256,512]{1,0:T(8,128)S(1)} %get-tuple-element.26.refs_1_), channel_id=1, source_target_pairs={{0,256},{64,320},{128,384},{192,448},{256,0},{320,64},{384,128},{4... | collective-permute-start | bytes 1572872 | tf_op jit(solution)/shard_map/ppermute | solution.py:182
  26.7 3.8 %collective-permute-start.1 = (f32[512,256]{1,0:T(8,128)S(1)}, f32[512,256]{1,0:T(8,128)}, u32[]{:S(2)}, u32[]{:S(2)}) collective-permute-start(f32[512,256]{1,0:T(8,128)S(1)} %copy-done), channel_id=1, source_target_pairs={{0,256},{64,320},{128,384},{192,448},{256,0},{320,64},{384,128},{4... | collective-permute-start | bytes 1572872 | tf_op jit(solution)/shard_map/ppermute | solution.py:165
  30.5 2.1 %collective-permute-start.5 = (f32[512,256]{1,0:T(8,128)S(1)}, f32[512,256]{1,0:T(8,128)}, u32[]{:S(2)}, u32[]{:S(2)}) collective-permute-start(f32[512,256]{1,0:T(8,128)S(1)} %copy-done), channel_id=1, source_target_pairs={{1,33},{3,35},{5,37},{7,39},{9,41},{11,43},{13,45},{15,47},{17,49}... | collective-permute-start | bytes 1572872 | tf_op jit(solution)/shard_map/ppermute | solution.py:166
  32.6 3.0 %collective-permute-done.2.refs_2_ = f32[256,512]{1,0:T(8,128)} collective-permute-done((f32[256,512]{1,0:T(8,128)S(1)}, f32[256,512]{1,0:T(8,128)}, u32[]{:S(2)}, u32[]{:S(2)}) %collective-permute-start.2) | collective-permute-done | bytes 524320 | tf_op jit(solution)/shard_map/ppermute | solution.py:182
  35.6 5.6 %collective-permute-done.3.refs_3_ = f32[256,512]{1,0:T(8,128)} collective-permute-done((f32[256,512]{1,0:T(8,128)S(1)}, f32[256,512]{1,0:T(8,128)}, u32[]{:S(2)}, u32[]{:S(2)}) %collective-permute-start.3) | collective-permute-done | bytes 524320 | tf_op jit(solution)/shard_map/ppermute | solution.py:182
  41.2 5.6 %collective-permute-done.1.vec_grp_ref = f32[512,256]{1,0:T(8,128)} collective-permute-done((f32[512,256]{1,0:T(8,128)S(1)}, f32[512,256]{1,0:T(8,128)}, u32[]{:S(2)}, u32[]{:S(2)}) %collective-permute-start.1) | collective-permute-done | bytes 524320 | tf_op jit(solution)/shard_map/ppermute | solution.py:165
  49.1 2.7 %shard_map.65 = (f32[512,256]{1,0:T(8,128)S(1)}, f32[512,512]{1,0:T(8,128)S(1)}, f32[512,512]{1,0:T(8,128)S(1)}) custom-call(f32[512,256]{1,0:T(8,128)S(1)} %copy-done, f32[512,512]{1,0:T(8,128)S(1)} %copy-done.8, f32[512,256]{1,0:T(8,128)} %collective-permute-done.1.vec_grp_ref, f32[256,512]{1,0:T(8,128)S(1)} %get-tuple-element.25.refs_0_, ...), custom_call_target="tpu_custom_call" | custom-call | flops 1000 | bytes 1000 | tf_op jit(solution)/shard_map/pallas_call | solution.py:141
  53.7 7.1 %collective-permute-done.4.bulk_ref = f32[1544,128]{1,0:T(8,128)S(1)} collective-permute-done((f32[1544,128]{1,0:T(8,128)}, f32[1544,128]{1,0:T(8,128)S(1)}, u32[]{:S(2)}, u32[]{:S(2)}) %collective-permute-start.4) | collective-permute-done | bytes 790560 | tf_op jit(solution)/shard_map/ppermute | solution.py:176
  64.8 1.9 %shard_map.67 = (f32[512,512]{1,0:T(8,128)S(1)}, f32[256,256]{1,0:T(8,128)S(1)}, f32[256,256]{1,0:T(8,128)S(1)}) custom-call(s32[4,4]{1,0:T(4,128)S(1)} %copy-done.16, s32[4,4]{1,0:T(4,128)S(1)} %slice_convert_fusion.in_mask, f32[512,512]{1,0:T(8,128)S(1)} %copy-done.2, f32[1544,128]{1,0:T(8,128)S(1)} %copy-done.10, ...), custom_call_target="tpu_custom_call" | custom-call | flops 1000 | bytes 1000 | tf_op jit(solution)/shard_map/pallas_call | solution.py:141
  66.8 1.3 collective-permute-start.7
  69.4 2.9 %collective-permute-done.5.vec_in_ref = f32[512,256]{1,0:T(8,128)} collective-permute-done((f32[512,256]{1,0:T(8,128)S(1)}, f32[512,256]{1,0:T(8,128)}, u32[]{:S(2)}, u32[]{:S(2)}) %collective-permute-start.5) | collective-permute-done | bytes 524320 | tf_op jit(solution)/shard_map/ppermute | solution.py:166
  72.3 3.7 %shard_map.68 = (f32[512,256]{1,0:T(8,128)S(1)}, f32[512,256]{1,0:T(8,128)}) custom-call(f32[512,256]{1,0:T(8,128)S(1)} %get-tuple-element.39.base_ref, f32[512,512]{1,0:T(8,128)S(1)} %get-tuple-element.34.pair_ref, f32[512,256]{1,0:T(8,128)} %collective-permute-done.5.vec_in_ref), custom_call_target="tpu_custom_call" | custom-call | flops 1000 | bytes 1000 | tf_op jit(solution)/shard_map/pallas_call | solution.py:141
  76.0 39.7 %collective-permute-done.7.back_ref = f32[256,256]{1,0:T(8,128)S(1)} collective-permute-done((f32[256,256]{1,0:T(8,128)S(1)}, f32[256,256]{1,0:T(8,128)S(1)}, u32[]{:S(2)}, u32[]{:S(2)}) %collective-permute-start.7) | collective-permute-done | bytes 262176 | tf_op jit(solution)/shard_map/ppermute | solution.py:209
  115.7 2.1 %collective-permute-start.10 = (f32[512,256]{1,0:T(8,128)S(1)}, f32[512,256]{1,0:T(8,128)}, u32[]{:S(2)}, u32[]{:S(2)}) collective-permute-start(f32[512,256]{1,0:T(8,128)S(1)} %get-tuple-element.39.base_ref), channel_id=1, source_target_pairs={{1,33},{3,35},{5,37},{7,39},{9,41},{11,43},{13,45},{15,47},{17,49}... | collective-permute-start | bytes 1572872 | tf_op jit(solution)/shard_map/ppermute | solution.py:213
  119.1 2.1 %collective-permute-start.9 = (f32[256,256]{1,0:T(8,128)S(1)}, f32[256,256]{1,0:T(8,128)S(1)}, u32[]{:S(2)}, u32[]{:S(2)}) collective-permute-start(f32[256,256]{1,0:T(8,128)S(1)} %shard_map.70.refs_1_), channel_id=1, source_target_pairs={{0,256},{64,320},{128,384},{192,448},{256,0},{320,64},{384,128},{4... | collective-permute-start | bytes 786440 | tf_op jit(solution)/shard_map/ppermute | solution.py:223
  122.2 4.9 %collective-permute-start.8 = (f32[256,256]{1,0:T(8,128)S(1)}, f32[256,256]{1,0:T(8,128)S(1)}, u32[]{:S(2)}, u32[]{:S(2)}) collective-permute-start(f32[256,256]{1,0:T(8,128)S(1)} %shard_map.69.refs_0_), channel_id=1, source_target_pairs={{0,256},{64,320},{128,384},{192,448},{256,0},{320,64},{384,128},{4... | collective-permute-start | bytes 786440 | tf_op jit(solution)/shard_map/ppermute | solution.py:223
  128.3 2.9 %collective-permute-done.8.refs_2_ = f32[256,256]{1,0:T(8,128)S(1)} collective-permute-done((f32[256,256]{1,0:T(8,128)S(1)}, f32[256,256]{1,0:T(8,128)S(1)}, u32[]{:S(2)}, u32[]{:S(2)}) %collective-permute-start.8) | collective-permute-done | bytes 262176 | tf_op jit(solution)/shard_map/ppermute | solution.py:223
  132.2 8.7 %collective-permute-done.10.base_in_ref = f32[512,256]{1,0:T(8,128)} collective-permute-done((f32[512,256]{1,0:T(8,128)S(1)}, f32[512,256]{1,0:T(8,128)}, u32[]{:S(2)}, u32[]{:S(2)}) %collective-permute-start.10) | collective-permute-done | bytes 524320 | tf_op jit(solution)/shard_map/ppermute | solution.py:213
  140.9 1.7 %shard_map.72 = f32[512,256]{1,0:T(8,128)S(1)} custom-call(f32[512,512]{1,0:T(8,128)S(1)} %get-tuple-element.34.pair_ref, f32[512,256]{1,0:T(8,128)} %collective-permute-done.10.base_in_ref, f32[256,256]{1,0:T(8,128)S(1)} %get-tuple-element.36.refs_0_, f32[256,256]{1,0:T(8,128)S(1)} %copy-done.14), custom_call_target="tpu_custom_call" | custom-call | flops 1000 | bytes 1000 | tf_op jit(solution)/shard_map/pallas_call | solution.py:141
  142.6 10.5 %collective-permute-done.11 = f32[512,256]{1,0:T(8,128)} collective-permute-done((f32[512,256]{1,0:T(8,128)}, f32[512,256]{1,0:T(8,128)}, u32[]{:S(2)}, u32[]{:S(2)}) %collective-permute-start.11) | collective-permute-done | bytes 524320 | tf_op jit(solution)/shard_map/ppermute | solution.py:211
  153.1 2.0 %multiply_subtract_fusion = f32[512,256]{1,0:T(8,128)} fusion(f32[512,256]{1,0:T(8,128)S(1)} %copy-done, f32[512,256]{1,0:T(8,128)S(1)} %shard_map.71, f32[512,256]{1,0:T(8,128)S(1)} %shard_map.72, f32[512,256]{1,0:T(8,128)} %collective-permute-done.11, pred[]{:T(512)S(6)} %eq.9), kind=kLoop, calls=%fused_computation | loop fusion | flops 524288 | bytes 2621441 | tf_op jit(solution)/shard_map/sub | solution.py:226
  (48 shorter events, 17.5 us)
Async XLA Ops:
  0.0 1.2 copy-start.1
  1.9 16.5 %copy-start.7 = (f32[512,512]{1,0:T(8,128)S(1)}, f32[512,512]{1,0:T(8,128)}, u32[]{:S(2)}) copy-start(f32[512,512]{1,0:T(8,128)} %tiles_ref.1) | copy-start | bytes 3145732
  1.9 16.5 %copy-start.17 = (s32[4,4]{1,0:T(4,128)S(1)}, s32[4,4]{1,0:T(4,128)}, u32[]{:S(2)}) copy-start(s32[4,4]{1,0:T(4,128)} %mask.1) | copy-start | bytes 196
  3.7 23.0 %copy-start = (f32[512,256]{1,0:T(8,128)S(1)}, f32[512,256]{1,0:T(8,128)}, u32[]{:S(2)}) copy-start(f32[512,256]{1,0:T(8,128)} %vec_ref.3) | copy-start | bytes 1572868
  3.7 57.1 %collective-permute-start.4 = (f32[1544,128]{1,0:T(8,128)}, f32[1544,128]{1,0:T(8,128)S(1)}, u32[]{:S(2)}, u32[]{:S(2)}) collective-permute-start(f32[1544,128]{1,0:T(8,128)} %get-tuple-element.30), channel_id=1, source_target_pairs={{1,33},{3,35},{5,37},{7,39},{9,41},{11,43},{13,45},{15,47},{17,49}... | collective-permute-start | bytes 2371592 | tf_op jit(solution)/shard_map/ppermute | solution.py:176
  19.1 16.4 %collective-permute-start.2 = (f32[256,512]{1,0:T(8,128)S(1)}, f32[256,512]{1,0:T(8,128)}, u32[]{:S(2)}, u32[]{:S(2)}) collective-permute-start(f32[256,512]{1,0:T(8,128)S(1)} %get-tuple-element.25.refs_0_), channel_id=1, source_target_pairs={{0,256},{64,320},{128,384},{192,448},{256,0},{320,64},{384,128},{4... | collective-permute-start | bytes 1572872 | tf_op jit(solution)/shard_map/ppermute | solution.py:182
  22.9 18.3 %collective-permute-start.3 = (f32[256,512]{1,0:T(8,128)S(1)}, f32[256,512]{1,0:T(8,128)}, u32[]{:S(2)}, u32[]{:S(2)}) collective-permute-start(f32[256,512]{1,0:T(8,128)S(1)} %get-tuple-element.26.refs_1_), channel_id=1, source_target_pairs={{0,256},{64,320},{128,384},{192,448},{256,0},{320,64},{384,128},{4... | collective-permute-start | bytes 1572872 | tf_op jit(solution)/shard_map/ppermute | solution.py:182
  26.7 20.1 %collective-permute-start.1 = (f32[512,256]{1,0:T(8,128)S(1)}, f32[512,256]{1,0:T(8,128)}, u32[]{:S(2)}, u32[]{:S(2)}) collective-permute-start(f32[512,256]{1,0:T(8,128)S(1)} %copy-done), channel_id=1, source_target_pairs={{0,256},{64,320},{128,384},{192,448},{256,0},{320,64},{384,128},{4... | collective-permute-start | bytes 1572872 | tf_op jit(solution)/shard_map/ppermute | solution.py:165
  30.5 41.8 %collective-permute-start.5 = (f32[512,256]{1,0:T(8,128)S(1)}, f32[512,256]{1,0:T(8,128)}, u32[]{:S(2)}, u32[]{:S(2)}) collective-permute-start(f32[512,256]{1,0:T(8,128)S(1)} %copy-done), channel_id=1, source_target_pairs={{1,33},{3,35},{5,37},{7,39},{9,41},{11,43},{13,45},{15,47},{17,49}... | collective-permute-start | bytes 1572872 | tf_op jit(solution)/shard_map/ppermute | solution.py:166
  32.6 31.1 %copy-start.2 = (f32[512,512]{1,0:T(8,128)S(1)}, f32[512,512]{1,0:T(8,128)}, u32[]{:S(2)}) copy-start(f32[512,512]{1,0:T(8,128)} %own_ref.1) | copy-start | bytes 3145732
  46.8 1.2 copy-start.8
  48.0 1.0 copy-start.12
  49.1 11.7 %copy-start.16 = (s32[4,4]{1,0:T(4,128)S(1)}, s32[4,4]{1,0:T(4,128)}, u32[]{:S(2)}) copy-start(s32[4,4]{1,0:T(4,128)} %own_mask.1) | copy-start | bytes 196
  63.7 1.1 copy-start.10
  66.8 9.2 %copy-start.13 = (f32[256,256]{1,0:T(8,128)}, f32[256,256]{1,0:T(8,128)S(1)}, u32[]{:S(2)}) copy-start(f32[256,256]{1,0:T(8,128)S(1)} %get-tuple-element.37.refs_1_) | copy-start | bytes 786436
  66.8 48.9 %collective-permute-start.7 = (f32[256,256]{1,0:T(8,128)S(1)}, f32[256,256]{1,0:T(8,128)S(1)}, u32[]{:S(2)}, u32[]{:S(2)}) collective-permute-start(f32[256,256]{1,0:T(8,128)S(1)} %get-tuple-element.37.refs_1_), channel_id=1, source_target_pairs={{0,32},{2,34},{4,36},{6,38},{8,40},{10,42},{12,44},{14,46},{16,48}... | collective-permute-start | bytes 786440 | tf_op jit(solution)/shard_map/ppermute | solution.py:209
  68.1 53.1 %collective-permute-start.6 = (f32[256,256]{1,0:T(8,128)S(1)}, f32[256,256]{1,0:T(8,128)}, u32[]{:S(2)}, u32[]{:S(2)}) collective-permute-start(f32[256,256]{1,0:T(8,128)S(1)} %get-tuple-element.36.refs_0_), channel_id=1, source_target_pairs={{0,32},{2,34},{4,36},{6,38},{8,40},{10,42},{12,44},{14,46},{16,48}... | collective-permute-start | bytes 786440 | tf_op jit(solution)/shard_map/ppermute | solution.py:209
  115.7 25.3 %collective-permute-start.10 = (f32[512,256]{1,0:T(8,128)S(1)}, f32[512,256]{1,0:T(8,128)}, u32[]{:S(2)}, u32[]{:S(2)}) collective-permute-start(f32[512,256]{1,0:T(8,128)S(1)} %get-tuple-element.39.base_ref), channel_id=1, source_target_pairs={{1,33},{3,35},{5,37},{7,39},{9,41},{11,43},{13,45},{15,47},{17,49}... | collective-permute-start | bytes 1572872 | tf_op jit(solution)/shard_map/ppermute | solution.py:213
  117.8 35.3 %collective-permute-start.11 = (f32[512,256]{1,0:T(8,128)}, f32[512,256]{1,0:T(8,128)}, u32[]{:S(2)}, u32[]{:S(2)}) collective-permute-start(f32[512,256]{1,0:T(8,128)} %get-tuple-element.40), channel_id=1, source_target_pairs={{0,32},{2,34},{4,36},{6,38},{8,40},{10,42},{12,44},{14,46},{16,48}... | collective-permute-start | bytes 1572872 | tf_op jit(solution)/shard_map/ppermute | solution.py:211
  119.1 12.2 %copy-start.6 = (f32[512,512]{1,0:T(8,128)S(1)}, f32[512,512]{1,0:T(8,128)}, u32[]{:S(2)}) copy-start(f32[512,512]{1,0:T(8,128)} %copy-done.5) | copy-start | bytes 3145732
  119.1 12.1 %copy-start.4 = (f32[512,512]{1,0:T(8,128)S(1)}, f32[512,512]{1,0:T(8,128)}, u32[]{:S(2)}) copy-start(f32[512,512]{1,0:T(8,128)} %copy-done.3) | copy-start | bytes 3145732
  119.1 9.2 %collective-permute-start.9 = (f32[256,256]{1,0:T(8,128)S(1)}, f32[256,256]{1,0:T(8,128)S(1)}, u32[]{:S(2)}, u32[]{:S(2)}) collective-permute-start(f32[256,256]{1,0:T(8,128)S(1)} %shard_map.70.refs_1_), channel_id=1, source_target_pairs={{0,256},{64,320},{128,384},{192,448},{256,0},{320,64},{384,128},{4... | collective-permute-start | bytes 786440 | tf_op jit(solution)/shard_map/ppermute | solution.py:223
  122.2 9.0 %collective-permute-start.8 = (f32[256,256]{1,0:T(8,128)S(1)}, f32[256,256]{1,0:T(8,128)S(1)}, u32[]{:S(2)}, u32[]{:S(2)}) collective-permute-start(f32[256,256]{1,0:T(8,128)S(1)} %shard_map.69.refs_0_), channel_id=1, source_target_pairs={{0,256},{64,320},{128,384},{192,448},{256,0},{320,64},{384,128},{4... | collective-permute-start | bytes 786440 | tf_op jit(solution)/shard_map/ppermute | solution.py:223
  131.2 9.7 %copy-start.14 = (f32[256,256]{1,0:T(8,128)S(1)}, f32[256,256]{1,0:T(8,128)}, u32[]{:S(2)}) copy-start(f32[256,256]{1,0:T(8,128)} %copy-done.13) | copy-start | bytes 786436
  (5 other events, 4.3 us)

commit v16 on v15

--- a/solution.py
+++ b/solution.py
@@ -119,13 +119,14 @@
     out_ref[...] = jnp.where(owner[0, 0] > 0, own_ref[rows], stepped)
 
 
-def near_kernel(sym_ref, across_ref, *refs):
+def near_kernel(owner, sym_ref, across_ref, back_ref, *refs):
     *first_refs, near_ref = refs
     half = len(first_refs) // 2
     first, first_grp = (
         jnp.concatenate([ref[...] for ref in part], axis=0) for part in (first_refs[:half], first_refs[half:])
     )
-    near_ref[...] = product(split(sym_ref[...]), split(first)) + product(split(across_ref[...]), split(first_grp))
+    near = product(split(sym_ref[...]), split(first)) + product(split(across_ref[...]), split(first_grp))
+    near_ref[...] = near + jnp.where(owner[0, 0] > 0, jnp.float32(0), back_ref[...])
 
 
 def far_kernel(pair_ref, base_in_ref, *refs):
@@ -221,8 +222,8 @@
         for at, got in enumerate(back_in)
     ]
     first_grp = [lax.ppermute(x, "grp", grp_pairs) for x in first]
-    near = local_call(near_kernel, (sym, across, *first, *first_grp), block)
-    total = near + jnp.where(owner, far, back2_in)
+    near = local_call(near_kernel, (role, sym, across, back2_in, *first, *first_grp), block)
+    total = near + jnp.where(owner, far, 0.0)
     return 2.0 * total / HALF_SPAN - vectors
 
 

time: 156 us -> 156 us (level)
  the two profiles are of different devices: /device:TPU:35 before, /device:TPU:193 now
where the time goes in v16:
time: 156 us; the launch traced here: 155 us
  waiting for transfers between devices  90 us (58%)
  starting transfers between devices  36.6 us (23%)
  Pallas kernels  14.5 us (9%)
  local copies, waits for them, and re-layouts  11.3 us (7%)
    ppermute x2, waiting for transfers between devices, body(): back_in = [lax.ppermute(x, 'slab', from_owner) for x in back]  53.7 us
    pallas_call x9, Pallas kernels, local_call(): pl.pallas_call(kernel, out_shape=out_shape, in_specs=spaces, out_specs=(v...  14.5 us
    ppermute x2, waiting for transfers between devices, body(): grp_in = [lax.ppermute(x, 'grp', grp_pairs) for x in grp_blocks]  13.4 us
    unnamed x40, local copies, waits for them, and re-layouts  10.6 us
    ppermute x1, waiting for transfers between devices, body(): bulk_in = lax.ppermute(bulk, 'slab', to_owner)  10.6 us
    ppermute x1, starting transfers between devices, body(): bulk_in = lax.ppermute(bulk, 'slab', to_owner)  8.98 us
    ppermute x2, starting transfers between devices, body(): first_grp = [lax.ppermute(x, 'grp', grp_pairs) for x in first]  8.73 us
    ppermute x2, starting transfers between devices, body(): grp_in = [lax.ppermute(x, 'grp', grp_pairs) for x in grp_blocks]  6.79 us
  transfers between devices with their start and end apart: 11, of which 7 were waited for; matrix products, arithmetic and copies ran while one was open for 1% of the time, Pallas kernels for 8%

profile of v16, /device:TPU:193, one launch (start us, length us, event | category | flops | bytes accessed | tf_op | source)
XLA Modules:
  0.0 154.8 jit_solution(7191652640895171828)
XLA Ops:
  1.9 1.8 %shard_map.66 = (f32[1544,128]{1,0:T(8,128)}, f32[4,128,128]{2,1,0:T(8,128)}) custom-call(s32[4,4]{1,0:T(4,128)S(1)} %copy-done.17, f32[512,512]{1,0:T(8,128)S(1)} %copy-done.1), custom_call_target="tpu_custom_call" | custom-call | flops 1000 | bytes 1000 | tf_op jit(solution)/shard_map/pallas_call | solution.py:142
  3.7 9.0 %collective-permute-start.4 = (f32[1544,128]{1,0:T(8,128)}, f32[1544,128]{1,0:T(8,128)S(1)}, u32[]{:S(2)}, u32[]{:S(2)}) collective-permute-start(f32[1544,128]{1,0:T(8,128)} %get-tuple-element.30), channel_id=1, source_target_pairs={{1,33},{3,35},{5,37},{7,39},{9,41},{11,43},{13,45},{15,47},{17,49}... | collective-permute-start | bytes 2371592 | tf_op jit(solution)/shard_map/ppermute | solution.py:177
  13.4 4.7 %collective-permute-start.2 = (f32[256,512]{1,0:T(8,128)S(1)}, f32[256,512]{1,0:T(8,128)}, u32[]{:S(2)}, u32[]{:S(2)}) collective-permute-start(f32[256,512]{1,0:T(8,128)S(1)} %get-tuple-element.25.refs_0_), channel_id=1, source_target_pairs={{0,256},{64,320},{128,384},{192,448},{256,0},{320,64},{384,128},{4... | collective-permute-start | bytes 1572872 | tf_op jit(solution)/shard_map/ppermute | solution.py:183
  18.1 2.1 %collective-permute-start.3 = (f32[256,512]{1,0:T(8,128)S(1)}, f32[256,512]{1,0:T(8,128)}, u32[]{:S(2)}, u32[]{:S(2)}) collective-permute-start(f32[256,512]{1,0:T(8,128)S(1)} %get-tuple-element.26.refs_1_), channel_id=1, source_target_pairs={{0,256},{64,320},{128,384},{192,448},{256,0},{320,64},{384,128},{4... | collective-permute-start | bytes 1572872 | tf_op jit(solution)/shard_map/ppermute | solution.py:183
  21.0 4.7 %collective-permute-start.1 = (f32[512,256]{1,0:T(8,128)S(1)}, f32[512,256]{1,0:T(8,128)}, u32[]{:S(2)}, u32[]{:S(2)}) collective-permute-start(f32[512,256]{1,0:T(8,128)S(1)} %copy-done), channel_id=1, source_target_pairs={{0,256},{64,320},{128,384},{192,448},{256,0},{320,64},{384,128},{4... | collective-permute-start | bytes 1572872 | tf_op jit(solution)/shard_map/ppermute | solution.py:166
  25.7 2.1 %collective-permute-start.5 = (f32[512,256]{1,0:T(8,128)S(1)}, f32[512,256]{1,0:T(8,128)}, u32[]{:S(2)}, u32[]{:S(2)}) collective-permute-start(f32[512,256]{1,0:T(8,128)S(1)} %copy-done), channel_id=1, source_target_pairs={{1,33},{3,35},{5,37},{7,39},{9,41},{11,43},{13,45},{15,47},{17,49}... | collective-permute-start | bytes 1572872 | tf_op jit(solution)/shard_map/ppermute | solution.py:167
  27.8 3.2 %collective-permute-done.2.refs_2_ = f32[256,512]{1,0:T(8,128)} collective-permute-done((f32[256,512]{1,0:T(8,128)S(1)}, f32[256,512]{1,0:T(8,128)}, u32[]{:S(2)}, u32[]{:S(2)}) %collective-permute-start.2) | collective-permute-done | bytes 524320 | tf_op jit(solution)/shard_map/ppermute | solution.py:183
  30.9 10.2 %collective-permute-done.3.refs_3_ = f32[256,512]{1,0:T(8,128)} collective-permute-done((f32[256,512]{1,0:T(8,128)S(1)}, f32[256,512]{1,0:T(8,128)}, u32[]{:S(2)}, u32[]{:S(2)}) %collective-permute-start.3) | collective-permute-done | bytes 524320 | tf_op jit(solution)/shard_map/ppermute | solution.py:183
  41.2 5.6 %collective-permute-done.1.vec_grp_ref = f32[512,256]{1,0:T(8,128)} collective-permute-done((f32[512,256]{1,0:T(8,128)S(1)}, f32[512,256]{1,0:T(8,128)}, u32[]{:S(2)}, u32[]{:S(2)}) %collective-permute-start.1) | collective-permute-done | bytes 524320 | tf_op jit(solution)/shard_map/ppermute | solution.py:166
  46.8 1.2 copy-done.8
  49.0 2.7 %shard_map.65 = (f32[512,256]{1,0:T(8,128)S(1)}, f32[512,512]{1,0:T(8,128)S(1)}, f32[512,512]{1,0:T(8,128)S(1)}) custom-call(f32[512,256]{1,0:T(8,128)S(1)} %copy-done, f32[512,512]{1,0:T(8,128)S(1)} %copy-done.8, f32[512,256]{1,0:T(8,128)} %collective-permute-done.1.vec_grp_ref, f32[256,512]{1,0:T(8,128)S(1)} %get-tuple-element.25.refs_0_, ...), custom_call_target="tpu_custom_call" | custom-call | flops 1000 | bytes 1000 | tf_op jit(solution)/shard_map/pallas_call | solution.py:142
  53.7 10.6 %collective-permute-done.4.bulk_ref = f32[1544,128]{1,0:T(8,128)S(1)} collective-permute-done((f32[1544,128]{1,0:T(8,128)}, f32[1544,128]{1,0:T(8,128)S(1)}, u32[]{:S(2)}, u32[]{:S(2)}) %collective-permute-start.4) | collective-permute-done | bytes 790560 | tf_op jit(solution)/shard_map/ppermute | solution.py:177
  68.3 1.9 %shard_map.67 = (f32[512,512]{1,0:T(8,128)S(1)}, f32[256,256]{1,0:T(8,128)S(1)}, f32[256,256]{1,0:T(8,128)S(1)}) custom-call(s32[4,4]{1,0:T(4,128)S(1)} %copy-done.18, s32[4,4]{1,0:T(4,128)S(1)} %slice_convert_fusion.in_mask, f32[512,512]{1,0:T(8,128)S(1)} %copy-done.2, f32[1544,128]{1,0:T(8,128)S(1)} %copy-done.10, ...), custom_call_target="tpu_custom_call" | custom-call | flops 1000 | bytes 1000 | tf_op jit(solution)/shard_map/pallas_call | solution.py:142
  70.2 1.3 collective-permute-start.8
  71.5 1.3 collective-permute-start.7
  72.8 3.7 %shard_map.68 = (f32[512,256]{1,0:T(8,128)S(1)}, f32[512,256]{1,0:T(8,128)}) custom-call(f32[512,256]{1,0:T(8,128)S(1)} %get-tuple-element.40.base_ref, f32[512,512]{1,0:T(8,128)S(1)} %get-tuple-element.34.pair_ref, f32[512,256]{1,0:T(8,128)} %collective-permute-done.5.vec_in_ref), custom_call_target="tpu_custom_call" | custom-call | flops 1000 | bytes 1000 | tf_op jit(solution)/shard_map/pallas_call | solution.py:142
  76.5 1.3 collective-permute-start.6
  77.8 53.7 %collective-permute-done.8.back_ref = f32[256,256]{1,0:T(8,128)S(1)} collective-permute-done((f32[256,256]{1,0:T(8,128)S(1)}, f32[256,256]{1,0:T(8,128)S(1)}, u32[]{:S(2)}, u32[]{:S(2)}) %collective-permute-start.8) | collective-permute-done | bytes 262176 | tf_op jit(solution)/shard_map/ppermute | solution.py:210
  132.2 1.5 collective-permute-start.11
  134.7 6.8 %collective-permute-start.10 = (f32[256,256]{1,0:T(8,128)S(1)}, f32[256,256]{1,0:T(8,128)S(1)}, u32[]{:S(2)}, u32[]{:S(2)}) collective-permute-start(f32[256,256]{1,0:T(8,128)S(1)} %shard_map.70.refs_1_), channel_id=1, source_target_pairs={{0,256},{64,320},{128,384},{192,448},{256,0},{320,64},{384,128},{4... | collective-permute-start | bytes 786440 | tf_op jit(solution)/shard_map/ppermute | solution.py:224
  142.5 1.9 %collective-permute-start.9 = (f32[256,256]{1,0:T(8,128)S(1)}, f32[256,256]{1,0:T(8,128)S(1)}, u32[]{:S(2)}, u32[]{:S(2)}) collective-permute-start(f32[256,256]{1,0:T(8,128)S(1)} %shard_map.69.refs_0_), channel_id=1, source_target_pairs={{0,256},{64,320},{128,384},{192,448},{256,0},{320,64},{384,128},{4... | collective-permute-start | bytes 786440 | tf_op jit(solution)/shard_map/ppermute | solution.py:224
  144.5 3.2 %collective-permute-done.10.refs_3_ = f32[256,256]{1,0:T(8,128)S(1)} collective-permute-done((f32[256,256]{1,0:T(8,128)S(1)}, f32[256,256]{1,0:T(8,128)S(1)}, u32[]{:S(2)}, u32[]{:S(2)}) %collective-permute-start.10) | collective-permute-done | bytes 262176 | tf_op jit(solution)/shard_map/ppermute | solution.py:224
  147.6 3.5 %collective-permute-done.9.refs_2_ = f32[256,256]{1,0:T(8,128)S(1)} collective-permute-done((f32[256,256]{1,0:T(8,128)S(1)}, f32[256,256]{1,0:T(8,128)S(1)}, u32[]{:S(2)}, u32[]{:S(2)}) %collective-permute-start.9) | collective-permute-done | bytes 262176 | tf_op jit(solution)/shard_map/ppermute | solution.py:224
  151.2 2.1 %shard_map.71 = f32[512,256]{1,0:T(8,128)S(1)} custom-call(s32[1,1]{1,0:T(1,128)} %bitcast.owner, f32[512,512]{1,0:T(8,128)S(1)} %copy-done.4, f32[512,512]{1,0:T(8,128)S(1)} %copy-done.6, f32[512,256]{1,0:T(8,128)} %collective-permute-done.6.back_ref, f32[256,256]{1,0:T(8,128)S(1)} %shard_map.69.refs_0_, f32[256,256]{1,0:T(8,128)S(1)} %shard_map.70.refs_1_, ...), custom_call_target="tpu_custom_call" | custom-call | flops 1000 | bytes 1000 | tf_op jit(solution)/shard_map/pallas_call | solution.py:142
  (52 shorter events, 14.7 us)
Async XLA Ops:
  0.0 1.2 copy-start.1
  1.9 10.8 %copy-start.7 = (f32[512,512]{1,0:T(8,128)S(1)}, f32[512,512]{1,0:T(8,128)}, u32[]{:S(2)}) copy-start(f32[512,512]{1,0:T(8,128)} %tiles_ref.1) | copy-start | bytes 3145732
  1.9 10.8 %copy-start.19 = (s32[4,4]{1,0:T(4,128)S(1)}, s32[4,4]{1,0:T(4,128)}, u32[]{:S(2)}) copy-start(s32[4,4]{1,0:T(4,128)} %mask.1) | copy-start | bytes 196
  3.7 17.3 %copy-start = (f32[512,256]{1,0:T(8,128)S(1)}, f32[512,256]{1,0:T(8,128)}, u32[]{:S(2)}) copy-start(f32[512,256]{1,0:T(8,128)} %vec_ref.3) | copy-start | bytes 1572868
  3.7 60.5 %collective-permute-start.4 = (f32[1544,128]{1,0:T(8,128)}, f32[1544,128]{1,0:T(8,128)S(1)}, u32[]{:S(2)}, u32[]{:S(2)}) collective-permute-start(f32[1544,128]{1,0:T(8,128)} %get-tuple-element.30), channel_id=1, source_target_pairs={{1,33},{3,35},{5,37},{7,39},{9,41},{11,43},{13,45},{15,47},{17,49}... | collective-permute-start | bytes 2371592 | tf_op jit(solution)/shard_map/ppermute | solution.py:177
  13.4 17.5 %collective-permute-start.2 = (f32[256,512]{1,0:T(8,128)S(1)}, f32[256,512]{1,0:T(8,128)}, u32[]{:S(2)}, u32[]{:S(2)}) collective-permute-start(f32[256,512]{1,0:T(8,128)S(1)} %get-tuple-element.25.refs_0_), channel_id=1, source_target_pairs={{0,256},{64,320},{128,384},{192,448},{256,0},{320,64},{384,128},{4... | collective-permute-start | bytes 1572872 | tf_op jit(solution)/shard_map/ppermute | solution.py:183
  18.1 23.1 %collective-permute-start.3 = (f32[256,512]{1,0:T(8,128)S(1)}, f32[256,512]{1,0:T(8,128)}, u32[]{:S(2)}, u32[]{:S(2)}) collective-permute-start(f32[256,512]{1,0:T(8,128)S(1)} %get-tuple-element.26.refs_1_), channel_id=1, source_target_pairs={{0,256},{64,320},{128,384},{192,448},{256,0},{320,64},{384,128},{4... | collective-permute-start | bytes 1572872 | tf_op jit(solution)/shard_map/ppermute | solution.py:183
  21.0 25.8 %collective-permute-start.1 = (f32[512,256]{1,0:T(8,128)S(1)}, f32[512,256]{1,0:T(8,128)}, u32[]{:S(2)}, u32[]{:S(2)}) collective-permute-start(f32[512,256]{1,0:T(8,128)S(1)} %copy-done), channel_id=1, source_target_pairs={{0,256},{64,320},{128,384},{192,448},{256,0},{320,64},{384,128},{4... | collective-permute-start | bytes 1572872 | tf_op jit(solution)/shard_map/ppermute | solution.py:166
  25.7 47.2 %collective-permute-start.5 = (f32[512,256]{1,0:T(8,128)S(1)}, f32[512,256]{1,0:T(8,128)}, u32[]{:S(2)}, u32[]{:S(2)}) collective-permute-start(f32[512,256]{1,0:T(8,128)S(1)} %copy-done), channel_id=1, source_target_pairs={{1,33},{3,35},{5,37},{7,39},{9,41},{11,43},{13,45},{15,47},{17,49}... | collective-permute-start | bytes 1572872 | tf_op jit(solution)/shard_map/ppermute | solution.py:167
  27.8 39.4 %copy-start.2 = (f32[512,512]{1,0:T(8,128)S(1)}, f32[512,512]{1,0:T(8,128)}, u32[]{:S(2)}) copy-start(f32[512,512]{1,0:T(8,128)} %own_ref.1) | copy-start | bytes 3145732
  46.8 1.2 copy-start.8
  48.0 1.0 copy-start.12
  49.0 15.2 %copy-start.18 = (s32[4,4]{1,0:T(4,128)S(1)}, s32[4,4]{1,0:T(4,128)}, u32[]{:S(2)}) copy-start(s32[4,4]{1,0:T(4,128)} %own_mask.1) | copy-start | bytes 196
  67.1 1.1 copy-start.10
  70.2 6.3 %copy-start.13 = (f32[256,256]{1,0:T(8,128)}, f32[256,256]{1,0:T(8,128)S(1)}, u32[]{:S(2)}) copy-start(f32[256,256]{1,0:T(8,128)S(1)} %get-tuple-element.38.refs_1_) | copy-start | bytes 786436
  70.2 61.3 %collective-permute-start.8 = (f32[256,256]{1,0:T(8,128)S(1)}, f32[256,256]{1,0:T(8,128)S(1)}, u32[]{:S(2)}, u32[]{:S(2)}) collective-permute-start(f32[256,256]{1,0:T(8,128)S(1)} %get-tuple-element.38.refs_1_), channel_id=1, source_target_pairs={{0,32},{2,34},{4,36},{6,38},{8,40},{10,42},{12,44},{14,46},{16,48}... | collective-permute-start | bytes 786440 | tf_op jit(solution)/shard_map/ppermute | solution.py:210
  71.5 70.0 %collective-permute-start.7 = (f32[256,256]{1,0:T(8,128)S(1)}, f32[256,256]{1,0:T(8,128)}, u32[]{:S(2)}, u32[]{:S(2)}) collective-permute-start(f32[256,256]{1,0:T(8,128)S(1)} %get-tuple-element.37.refs_0_), channel_id=1, source_target_pairs={{0,32},{2,34},{4,36},{6,38},{8,40},{10,42},{12,44},{14,46},{16,48}... | collective-permute-start | bytes 786440 | tf_op jit(solution)/shard_map/ppermute | solution.py:210
  76.5 67.9 %collective-permute-start.6 = (f32[512,256]{1,0:T(8,128)}, f32[512,256]{1,0:T(8,128)}, u32[]{:S(2)}, u32[]{:S(2)}) collective-permute-start(f32[512,256]{1,0:T(8,128)} %get-tuple-element.35), channel_id=1, source_target_pairs={{0,32},{2,34},{4,36},{6,38},{8,40},{10,42},{12,44},{14,46},{16,48}... | collective-permute-start | bytes 1572872 | tf_op jit(solution)/shard_map/ppermute | solution.py:212
  132.2 21.0 %collective-permute-start.11 = (f32[512,256]{1,0:T(8,128)S(1)}, f32[512,256]{1,0:T(8,128)S(1)}, u32[]{:S(2)}, u32[]{:S(2)}) collective-permute-start(f32[512,256]{1,0:T(8,128)S(1)} %get-tuple-element.40.base_ref), channel_id=1, source_target_pairs={{1,33},{3,35},{5,37},{7,39},{9,41},{11,43},{13,45},{15,47},{17,49}... | collective-permute-start | bytes 1572872 | tf_op jit(solution)/shard_map/ppermute | solution.py:214
  134.6 16.5 %copy-start.6 = (f32[512,512]{1,0:T(8,128)S(1)}, f32[512,512]{1,0:T(8,128)}, u32[]{:S(2)}) copy-start(f32[512,512]{1,0:T(8,128)} %copy-done.5) | copy-start | bytes 3145732
  134.7 16.5 %copy-start.4 = (f32[512,512]{1,0:T(8,128)S(1)}, f32[512,512]{1,0:T(8,128)}, u32[]{:S(2)}) copy-start(f32[512,512]{1,0:T(8,128)} %copy-done.3) | copy-start | bytes 3145732
  134.7 12.9 %collective-permute-start.10 = (f32[256,256]{1,0:T(8,128)S(1)}, f32[256,256]{1,0:T(8,128)S(1)}, u32[]{:S(2)}, u32[]{:S(2)}) collective-permute-start(f32[256,256]{1,0:T(8,128)S(1)} %shard_map.70.refs_1_), channel_id=1, source_target_pairs={{0,256},{64,320},{128,384},{192,448},{256,0},{320,64},{384,128},{4... | collective-permute-start | bytes 786440 | tf_op jit(solution)/shard_map/ppermute | solution.py:224
  142.5 8.6 %collective-permute-start.9 = (f32[256,256]{1,0:T(8,128)S(1)}, f32[256,256]{1,0:T(8,128)S(1)}, u32[]{:S(2)}, u32[]{:S(2)}) collective-permute-start(f32[256,256]{1,0:T(8,128)S(1)} %shard_map.69.refs_0_), channel_id=1, source_target_pairs={{0,256},{64,320},{128,384},{192,448},{256,0},{320,64},{384,128},{4... | collective-permute-start | bytes 786440 | tf_op jit(solution)/shard_map/ppermute | solution.py:224
  151.2 2.1 %copy-start.14 = (f32[256,256]{1,0:T(8,128)S(1)}, f32[256,256]{1,0:T(8,128)}, u32[]{:S(2)}) copy-start(f32[256,256]{1,0:T(8,128)} %copy-done.13) | copy-start | bytes 786436
  (7 other events, 6.0 us)

commit v17 on v16

--- a/solution.py
+++ b/solution.py
@@ -65,7 +65,8 @@
             out_ref[top : top + tile, cols] = tiles_ref[i * tile : (i + 1) * tile, cols] * mask[i, j].astype(jnp.float32)
 
 
-def pair_kernel(tile, own_mask, in_mask, own_ref, bulk_ref, extra_ref, vec_ref, out_ref, *back_refs):
+def pair_kernel(tile, extras, own_mask, in_mask, own_ref, bulk_ref, vec_ref, *refs):
+    extra_ref, out_ref, *back_refs = refs if extras else (None, *refs)
     n = own_ref.shape[0] // tile
     for i in range(n):
         for j in range(n):
@@ -81,9 +82,11 @@
             def _():
                 out_ref[to] += bulk_ref[pl.ds(pl.multiple_of(slot * tile, tile), tile), :].T
 
-            @pl.when(jnp.logical_and(stored, slot >= FIXED))
-            def _():
-                out_ref[to] += extra_ref[slot - FIXED].T
+            if extras:
+
+                @pl.when(jnp.logical_and(stored, slot >= FIXED))
+                def _():
+                    out_ref[to] += extra_ref[slot - FIXED].T
 
             slot = slot + stored.astype(jnp.int32)
     back, top = product(split(out_ref[...].T), split(vec_ref[...])), 0
@@ -187,26 +190,19 @@
     )
     base, bulk_in = lax.optimization_barrier((base, bulk_in))
     mask_in = bulk_in[FIXED * tile : FIXED * tile + n_tile, :n_tile].astype(jnp.int32)
-    sizes = (0, slots - FIXED)
-
-    def send(k):
-        def branch(tiles):
-            if k == 0:
-                return jnp.zeros_like(tiles)
-            return lax.ppermute(tiles, "slab", to_owner)
-
-        return branch
-
-    over = jnp.sum(jnp.where(owner, mask_in, slab_mask)) - FIXED
-    which = sum((over > k).astype(jnp.int32) for k in sizes[:-1])
-    extra_in = lax.switch(which, [send(k) for k in sizes], extra)
-
     half_block = jax.ShapeDtypeStruct((rows // CUTS, vectors.shape[1]), f32)
-    pair, *back = local_call(
-        functools.partial(pair_kernel, tile),
-        (slab_mask, mask_in, slab_tiles, bulk_in, extra_in, vectors),
-        (square,) + (half_block,) * CUTS,
-    )
+
+    def whole(extras, *ins):
+        return local_call(functools.partial(pair_kernel, tile, extras), ins, (square,) + (half_block,) * CUTS)
+
+    def plain(own_mask, in_mask, own, got, vecs, tiles):
+        return whole(False, own_mask, in_mask, own, got, vecs)
+
+    def more(own_mask, in_mask, own, got, vecs, tiles):
+        return whole(True, own_mask, in_mask, own, got, vecs, lax.ppermute(tiles, "slab", to_owner))
+
+    over = jnp.sum(jnp.where(owner, mask_in, slab_mask)) > FIXED
+    pair, *back = lax.cond(over, more, plain, slab_mask, mask_in, slab_tiles, bulk_in, vectors, extra)
     back_in = [lax.ppermute(x, "slab", from_owner) for x in back]
     first_own, back2 = local_call(first_kernel, (base, pair, vecs_in), (block, block))
     back2_in = lax.ppermute(back2, "slab", from_owner)

time: 156 us -> 156 us (level)
  the two profiles are of different devices: /device:TPU:193 before, /device:TPU:217 now
where the time goes in v17:
time: 156 us; the launch traced here: 155 us
  waiting for transfers between devices  84.7 us (54%)
  starting transfers between devices  35.5 us (23%)
  Pallas kernels  16.6 us (11%)
  local copies, waits for them, and re-layouts  13.9 us (9%)
  other arithmetic  3.93 us (3%)
    ppermute x2, waiting for transfers between devices, body(): back_in = [lax.ppermute(x, 'slab', from_owner) for x in back]  53.7 us
    pallas_call x9, Pallas kernels, local_call(): pl.pallas_call(kernel, out_shape=out_shape, in_specs=spaces, out_specs=(v...  16.6 us
    unnamed x40, local copies, waits for them, and re-layouts  13.9 us
    ppermute x2, waiting for transfers between devices, body(): grp_in = [lax.ppermute(x, 'grp', grp_pairs) for x in grp_blocks]  11.9 us
    ppermute x1, starting transfers between devices, body(): bulk_in = lax.ppermute(bulk, 'slab', to_owner)  9.74 us
    ppermute x1, waiting for transfers between devices, body(): bulk_in = lax.ppermute(bulk, 'slab', to_owner)  7.75 us
    ppermute x2, starting transfers between devices, body(): first_grp = [lax.ppermute(x, 'grp', grp_pairs) for x in first]  6.79 us
    ppermute x2, starting transfers between devices, body(): grp_in = [lax.ppermute(x, 'grp', grp_pairs) for x in grp_blocks]  6.77 us
  transfers between devices with their start and end apart: 11, of which 7 were waited for; matrix products, arithmetic and copies ran while one was open for 1% of the time, Pallas kernels for 8%

profile of v17, /device:TPU:217, one launch (start us, length us, event | category | flops | bytes accessed | tf_op | source)
XLA Modules:
  0.0 155.4 jit_solution(17798797309147063665)
XLA Ops:
  0.0 2.5 %shard_map.66 = (f32[1544,128]{1,0:T(8,128)}, f32[4,128,128]{2,1,0:T(8,128)S(1)}) custom-call(s32[4,4]{1,0:T(4,128)} %slab_mask.1, f32[512,512]{1,0:T(8,128)} %slab_ref.1), custom_call_target="tpu_custom_call" | custom-call | flops 1000 | bytes 1000 | tf_op jit(solution)/shard_map/pallas_call | solution.py:145
  2.5 9.7 %collective-permute-start.4 = (f32[1544,128]{1,0:T(8,128)}, f32[1544,128]{1,0:T(8,128)}, u32[]{:S(2)}, u32[]{:S(2)}) collective-permute-start(f32[1544,128]{1,0:T(8,128)} %get-tuple-element.59), channel_id=1, source_target_pairs={{1,33},{3,35},{5,37},{7,39},{9,41},{11,43},{13,45},{15,47},{17,49}... | collective-permute-start | bytes 2371592 | tf_op jit(solution)/shard_map/ppermute | solution.py:180
  12.9 4.7 %collective-permute-start.2 = (f32[256,512]{1,0:T(8,128)S(1)}, f32[256,512]{1,0:T(8,128)S(1)}, u32[]{:S(2)}, u32[]{:S(2)}) collective-permute-start(f32[256,512]{1,0:T(8,128)S(1)} %get-tuple-element.54.refs_0_), channel_id=1, source_target_pairs={{0,256},{64,320},{128,384},{192,448},{256,0},{320,64},{384,128},{4... | collective-permute-start | bytes 1572872 | tf_op jit(solution)/shard_map/ppermute | solution.py:186
  18.3 2.1 %collective-permute-start.3 = (f32[256,512]{1,0:T(8,128)S(1)}, f32[256,512]{1,0:T(8,128)S(1)}, u32[]{:S(2)}, u32[]{:S(2)}) collective-permute-start(f32[256,512]{1,0:T(8,128)S(1)} %get-tuple-element.55.refs_1_), channel_id=1, source_target_pairs={{0,256},{64,320},{128,384},{192,448},{256,0},{320,64},{384,128},{4... | collective-permute-start | bytes 1572872 | tf_op jit(solution)/shard_map/ppermute | solution.py:186
  21.3 4.6 %collective-permute-start.1 = (f32[512,256]{1,0:T(8,128)}, f32[512,256]{1,0:T(8,128)S(1)}, u32[]{:S(2)}, u32[]{:S(2)}) collective-permute-start(f32[512,256]{1,0:T(8,128)} %vec_ref.1), channel_id=1, source_target_pairs={{0,256},{64,320},{128,384},{192,448},{256,0},{320,64},{384,128},{4... | collective-permute-start | bytes 1572872 | tf_op jit(solution)/shard_map/ppermute | solution.py:169
  25.9 1.3 collective-permute-start.5
  27.3 3.1 %collective-permute-done.2.refs_2_ = f32[256,512]{1,0:T(8,128)S(1)} collective-permute-done((f32[256,512]{1,0:T(8,128)S(1)}, f32[256,512]{1,0:T(8,128)S(1)}, u32[]{:S(2)}, u32[]{:S(2)}) %collective-permute-start.2) | collective-permute-done | bytes 524320 | tf_op jit(solution)/shard_map/ppermute | solution.py:186
  31.2 8.8 %collective-permute-done.3.refs_3_ = f32[256,512]{1,0:T(8,128)S(1)} collective-permute-done((f32[256,512]{1,0:T(8,128)S(1)}, f32[256,512]{1,0:T(8,128)S(1)}, u32[]{:S(2)}, u32[]{:S(2)}) %collective-permute-start.3) | collective-permute-done | bytes 524320 | tf_op jit(solution)/shard_map/ppermute | solution.py:186
  40.8 4.8 %collective-permute-done.1.vec_grp_ref = f32[512,256]{1,0:T(8,128)S(1)} collective-permute-done((f32[512,256]{1,0:T(8,128)}, f32[512,256]{1,0:T(8,128)S(1)}, u32[]{:S(2)}, u32[]{:S(2)}) %collective-permute-start.1) | collective-permute-done | bytes 524320 | tf_op jit(solution)/shard_map/ppermute | solution.py:169
  52.8 2.3 %shard_map.65 = (f32[512,256]{1,0:T(8,128)S(1)}, f32[512,512]{1,0:T(8,128)S(1)}, f32[512,512]{1,0:T(8,128)S(1)}) custom-call(f32[512,256]{1,0:T(8,128)} %vec_ref.1, f32[512,512]{1,0:T(8,128)S(1)} %copy-done.1, f32[512,256]{1,0:T(8,128)S(1)} %copy-done.13, f32[256,512]{1,0:T(8,128)S(1)} %copy-done.5, f32[256,512]{1,0:T(8,128)S(1)} %copy-done.7, ...), custom_call_target="tpu_custom_call" | custom-call | flops 1000 | bytes 1000 | tf_op jit(solution)/shard_map/pallas_call | solution.py:145
  55.2 7.8 %collective-permute-done.4 = f32[1544,128]{1,0:T(8,128)} collective-permute-done((f32[1544,128]{1,0:T(8,128)}, f32[1544,128]{1,0:T(8,128)}, u32[]{:S(2)}, u32[]{:S(2)}) %collective-permute-start.4) | collective-permute-done | bytes 790560 | tf_op jit(solution)/shard_map/ppermute | solution.py:180
  62.9 1.3 select_reduce_fusion
  65.6 3.3 %conditional.1 = ((f32[512,512]{1,0:T(8,128)}, f32[256,256]{1,0:T(8,128)}, f32[256,256]{1,0:T(8,128)})) conditional(s32[]{:T(128)} %convert_element_type.8, (s32[4,4]{1,0:T(4,128)S(1)}, s32[4,4]{1,0:T(4,128)S(1)}, f32[512,512]{1,0:T(8,128)}, f32[1544,128]{1,0:T(8,128)}, f32[512,256]{1,0:T(8,128)}) %tuple.21, (f32[4,128,128]{2,1,0:T(8,128)S(1)}, ...), branch_computations={%region_1.2_spmd, %region_2.3_spmd} | conditional | flops 1000 | bytes 1049624 | solution.py:205
  65.6 3.3 %branch_0_fun.1 = (f32[512,512]{1,0:T(8,128)}, f32[256,256]{1,0:T(8,128)}, f32[256,256]{1,0:T(8,128)}) custom-call(s32[4,4]{1,0:T(4,128)S(1)} %get-tuple-element.27.own_mask, s32[4,4]{1,0:T(4,128)S(1)} %get-tuple-element.28.in_mask, f32[512,512]{1,0:T(8,128)} %get-tuple-element.29.own_ref, f32[1544,128]{1,0:T(8,128)} %get-tuple-element.30.bulk_ref, ...), custom_call_target="tpu_custom_call" | custom-call | flops 1000 | bytes 1000 | tf_op jit(solution)/shard_map/cond/branch_0_fun/pallas_call | solution.py:145
  73.3 3.8 %shard_map.67 = (f32[512,256]{1,0:T(8,128)S(1)}, f32[512,256]{1,0:T(8,128)}) custom-call(f32[512,256]{1,0:T(8,128)S(1)} %get-tuple-element.69.base_ref, f32[512,512]{1,0:T(8,128)} %get-tuple-element.63.pair_ref, f32[512,256]{1,0:T(8,128)S(1)} %copy-done.3), custom_call_target="tpu_custom_call" | custom-call | flops 1000 | bytes 1000 | tf_op jit(solution)/shard_map/pallas_call | solution.py:145
  78.4 53.7 %collective-permute-done.8.back_ref = f32[256,256]{1,0:T(8,128)S(1)} collective-permute-done((f32[256,256]{1,0:T(8,128)}, f32[256,256]{1,0:T(8,128)S(1)}, u32[]{:S(2)}, u32[]{:S(2)}) %collective-permute-start.8) | collective-permute-done | bytes 262176 | tf_op jit(solution)/shard_map/ppermute | solution.py:206
  132.9 2.4 %collective-permute-start.11 = (f32[512,256]{1,0:T(8,128)S(1)}, f32[512,256]{1,0:T(8,128)}, u32[]{:S(2)}, u32[]{:S(2)}) collective-permute-start(f32[512,256]{1,0:T(8,128)S(1)} %get-tuple-element.69.base_ref), channel_id=1, source_target_pairs={{1,33},{3,35},{5,37},{7,39},{9,41},{11,43},{13,45},{15,47},{17,49}... | collective-permute-start | bytes 1572872 | tf_op jit(solution)/shard_map/ppermute | solution.py:210
  136.2 4.6 %collective-permute-start.10 = (f32[256,256]{1,0:T(8,128)S(1)}, f32[256,256]{1,0:T(8,128)S(1)}, u32[]{:S(2)}, u32[]{:S(2)}) collective-permute-start(f32[256,256]{1,0:T(8,128)S(1)} %shard_map.69.refs_1_), channel_id=1, source_target_pairs={{0,256},{64,320},{128,384},{192,448},{256,0},{320,64},{384,128},{4... | collective-permute-start | bytes 786440 | tf_op jit(solution)/shard_map/ppermute | solution.py:220
  140.9 2.2 %collective-permute-start.9 = (f32[256,256]{1,0:T(8,128)S(1)}, f32[256,256]{1,0:T(8,128)S(1)}, u32[]{:S(2)}, u32[]{:S(2)}) collective-permute-start(f32[256,256]{1,0:T(8,128)S(1)} %shard_map.68.refs_0_), channel_id=1, source_target_pairs={{0,256},{64,320},{128,384},{192,448},{256,0},{320,64},{384,128},{4... | collective-permute-start | bytes 786440 | tf_op jit(solution)/shard_map/ppermute | solution.py:220
  143.1 2.6 %collective-permute-done.10.refs_3_ = f32[256,256]{1,0:T(8,128)S(1)} collective-permute-done((f32[256,256]{1,0:T(8,128)S(1)}, f32[256,256]{1,0:T(8,128)S(1)}, u32[]{:S(2)}, u32[]{:S(2)}) %collective-permute-start.10) | collective-permute-done | bytes 262176 | tf_op jit(solution)/shard_map/ppermute | solution.py:220
  145.7 3.9 %collective-permute-done.9.refs_2_ = f32[256,256]{1,0:T(8,128)S(1)} collective-permute-done((f32[256,256]{1,0:T(8,128)S(1)}, f32[256,256]{1,0:T(8,128)S(1)}, u32[]{:S(2)}, u32[]{:S(2)}) %collective-permute-start.9) | collective-permute-done | bytes 262176 | tf_op jit(solution)/shard_map/ppermute | solution.py:220
  149.5 2.1 %shard_map.70 = f32[512,256]{1,0:T(8,128)S(1)} custom-call(s32[1,1]{1,0:T(1,128)} %bitcast.owner, f32[512,512]{1,0:T(8,128)S(1)} %get-tuple-element.56.sym_ref, f32[512,512]{1,0:T(8,128)S(1)} %get-tuple-element.57.across_ref, f32[512,256]{1,0:T(8,128)} %collective-permute-done.6.back_ref, f32[256,256]{1,0:T(8,128)S(1)} %shard_map.68.refs_0_, ...), custom_call_target="tpu_custom_call" | custom-call | flops 1000 | bytes 1000 | tf_op jit(solution)/shard_map/pallas_call | solution.py:145
  151.7 1.7 %shard_map.71 = f32[512,256]{1,0:T(8,128)S(1)} custom-call(f32[512,512]{1,0:T(8,128)S(1)} %copy-done.17, f32[512,256]{1,0:T(8,128)} %collective-permute-done.11.base_in_ref, f32[256,256]{1,0:T(8,128)S(1)} %copy-done.18, f32[256,256]{1,0:T(8,128)} %get-tuple-element.67.refs_1_), custom_call_target="tpu_custom_call" | custom-call | flops 1000 | bytes 1000 | tf_op jit(solution)/shard_map/pallas_call | solution.py:145
  153.5 1.9 %multiply_subtract_fusion = f32[512,256]{1,0:T(8,128)} fusion(f32[512,256]{1,0:T(8,128)} %vec_ref.1, f32[512,256]{1,0:T(8,128)S(1)} %shard_map.70, f32[512,256]{1,0:T(8,128)S(1)} %shard_map.71, pred[]{:T(512)S(6)} %eq.9), kind=kLoop, calls=%fused_computation | loop fusion | flops 524288 | bytes 2097153 | tf_op jit(solution)/shard_map/sub | solution.py:223
  (51 shorter events, 19.2 us)
Async XLA Ops:
  0.0 12.2 %copy-start = (f32[512,512]{1,0:T(8,128)S(1)}, f32[512,512]{1,0:T(8,128)}, u32[]{:S(2)}) copy-start(f32[512,512]{1,0:T(8,128)} %tiles_ref.1) | copy-start | bytes 3145732
  0.0 12.2 %copy-start.16 = (s32[4,4]{1,0:T(4,128)S(1)}, s32[4,4]{1,0:T(4,128)}, u32[]{:S(2)}) copy-start(s32[4,4]{1,0:T(4,128)} %mask.1) | copy-start | bytes 196
  2.5 60.5 %collective-permute-start.4 = (f32[1544,128]{1,0:T(8,128)}, f32[1544,128]{1,0:T(8,128)}, u32[]{:S(2)}, u32[]{:S(2)}) collective-permute-start(f32[1544,128]{1,0:T(8,128)} %get-tuple-element.59), channel_id=1, source_target_pairs={{1,33},{3,35},{5,37},{7,39},{9,41},{11,43},{13,45},{15,47},{17,49}... | collective-permute-start | bytes 2371592 | tf_op jit(solution)/shard_map/ppermute | solution.py:180
  12.9 17.5 %collective-permute-start.2 = (f32[256,512]{1,0:T(8,128)S(1)}, f32[256,512]{1,0:T(8,128)S(1)}, u32[]{:S(2)}, u32[]{:S(2)}) collective-permute-start(f32[256,512]{1,0:T(8,128)S(1)} %get-tuple-element.54.refs_0_), channel_id=1, source_target_pairs={{0,256},{64,320},{128,384},{192,448},{256,0},{320,64},{384,128},{4... | collective-permute-start | bytes 1572872 | tf_op jit(solution)/shard_map/ppermute | solution.py:186
  18.3 21.6 %collective-permute-start.3 = (f32[256,512]{1,0:T(8,128)S(1)}, f32[256,512]{1,0:T(8,128)S(1)}, u32[]{:S(2)}, u32[]{:S(2)}) collective-permute-start(f32[256,512]{1,0:T(8,128)S(1)} %get-tuple-element.55.refs_1_), channel_id=1, source_target_pairs={{0,256},{64,320},{128,384},{192,448},{256,0},{320,64},{384,128},{4... | collective-permute-start | bytes 1572872 | tf_op jit(solution)/shard_map/ppermute | solution.py:186
  21.3 24.3 %collective-permute-start.1 = (f32[512,256]{1,0:T(8,128)}, f32[512,256]{1,0:T(8,128)S(1)}, u32[]{:S(2)}, u32[]{:S(2)}) collective-permute-start(f32[512,256]{1,0:T(8,128)} %vec_ref.1), channel_id=1, source_target_pairs={{0,256},{64,320},{128,384},{192,448},{256,0},{320,64},{384,128},{4... | collective-permute-start | bytes 1572872 | tf_op jit(solution)/shard_map/ppermute | solution.py:169
  25.9 45.6 %collective-permute-start.5 = (f32[512,256]{1,0:T(8,128)}, f32[512,256]{1,0:T(8,128)S(1)}, u32[]{:S(2)}, u32[]{:S(2)}) collective-permute-start(f32[512,256]{1,0:T(8,128)} %vec_ref.1), channel_id=1, source_target_pairs={{1,33},{3,35},{5,37},{7,39},{9,41},{11,43},{13,45},{15,47},{17,49}... | collective-permute-start | bytes 1572872 | tf_op jit(solution)/shard_map/ppermute | solution.py:170
  46.4 1.2 copy-start.1
  47.6 1.0 copy-start.5
  48.7 1.0 copy-start.7
  49.7 1.0 copy-start.9
  50.7 1.0 copy-start.11
  51.8 1.0 copy-start.13
  52.8 10.1 %copy-start.19 = (s32[4,4]{1,0:T(4,128)S(1)}, s32[4,4]{1,0:T(4,128)}, u32[]{:S(2)}) copy-start(s32[4,4]{1,0:T(4,128)} %slab_mask.1) | copy-start | bytes 196
  68.9 63.3 %collective-permute-start.8 = (f32[256,256]{1,0:T(8,128)}, f32[256,256]{1,0:T(8,128)S(1)}, u32[]{:S(2)}, u32[]{:S(2)}) collective-permute-start(f32[256,256]{1,0:T(8,128)} %get-tuple-element.67.refs_1_), channel_id=1, source_target_pairs={{0,32},{2,34},{4,36},{6,38},{8,40},{10,42},{12,44},{14,46},{16,48}... | collective-permute-start | bytes 786440 | tf_op jit(solution)/shard_map/ppermute | solution.py:206
  70.2 70.7 %collective-permute-start.7 = (f32[256,256]{1,0:T(8,128)}, f32[256,256]{1,0:T(8,128)S(1)}, u32[]{:S(2)}, u32[]{:S(2)}) collective-permute-start(f32[256,256]{1,0:T(8,128)} %get-tuple-element.66.refs_0_), channel_id=1, source_target_pairs={{0,32},{2,34},{4,36},{6,38},{8,40},{10,42},{12,44},{14,46},{16,48}... | collective-permute-start | bytes 786440 | tf_op jit(solution)/shard_map/ppermute | solution.py:206
  72.3 1.0 copy-start.3
  77.2 66.0 %collective-permute-start.6 = (f32[512,256]{1,0:T(8,128)}, f32[512,256]{1,0:T(8,128)}, u32[]{:S(2)}, u32[]{:S(2)}) collective-permute-start(f32[512,256]{1,0:T(8,128)} %get-tuple-element.64), channel_id=1, source_target_pairs={{0,32},{2,34},{4,36},{6,38},{8,40},{10,42},{12,44},{14,46},{16,48}... | collective-permute-start | bytes 1572872 | tf_op jit(solution)/shard_map/ppermute | solution.py:208
  132.9 18.8 %collective-permute-start.11 = (f32[512,256]{1,0:T(8,128)S(1)}, f32[512,256]{1,0:T(8,128)}, u32[]{:S(2)}, u32[]{:S(2)}) collective-permute-start(f32[512,256]{1,0:T(8,128)S(1)} %get-tuple-element.69.base_ref), channel_id=1, source_target_pairs={{1,33},{3,35},{5,37},{7,39},{9,41},{11,43},{13,45},{15,47},{17,49}... | collective-permute-start | bytes 1572872 | tf_op jit(solution)/shard_map/ppermute | solution.py:210
  135.2 0.9 copy-start.15
  136.2 9.4 %collective-permute-start.10 = (f32[256,256]{1,0:T(8,128)S(1)}, f32[256,256]{1,0:T(8,128)S(1)}, u32[]{:S(2)}, u32[]{:S(2)}) collective-permute-start(f32[256,256]{1,0:T(8,128)S(1)} %shard_map.69.refs_1_), channel_id=1, source_target_pairs={{0,256},{64,320},{128,384},{192,448},{256,0},{320,64},{384,128},{4... | collective-permute-start | bytes 786440 | tf_op jit(solution)/shard_map/ppermute | solution.py:220
  140.9 8.6 %collective-permute-start.9 = (f32[256,256]{1,0:T(8,128)S(1)}, f32[256,256]{1,0:T(8,128)S(1)}, u32[]{:S(2)}, u32[]{:S(2)}) collective-permute-start(f32[256,256]{1,0:T(8,128)S(1)} %shard_map.68.refs_0_), channel_id=1, source_target_pairs={{0,256},{64,320},{128,384},{192,448},{256,0},{320,64},{384,128},{4... | collective-permute-start | bytes 786440 | tf_op jit(solution)/shard_map/ppermute | solution.py:220
  149.5 2.2 %copy-start.17 = (f32[512,512]{1,0:T(8,128)S(1)}, f32[512,512]{1,0:T(8,128)}, u32[]{:S(2)}) copy-start(f32[512,512]{1,0:T(8,128)} %get-tuple-element.63.pair_ref) | copy-start | bytes 3145732
  149.5 2.2 %copy-start.18 = (f32[256,256]{1,0:T(8,128)S(1)}, f32[256,256]{1,0:T(8,128)}, u32[]{:S(2)}) copy-start(f32[256,256]{1,0:T(8,128)} %get-tuple-element.66.refs_0_) | copy-start | bytes 786436
  (7 other events, 5.5 us)

commit v18 on v16

--- a/solution.py
+++ b/solution.py
@@ -210,7 +210,7 @@
     back_in = [lax.ppermute(x, "slab", from_owner) for x in back]
     first_own, back2 = local_call(first_kernel, (base, pair, vecs_in), (block, block))
     back2_in = lax.ppermute(back2, "slab", from_owner)
-    later, back_in[-1] = lax.optimization_barrier((base, back_in[-1]))
+    later, *_ = lax.optimization_barrier((base, *back_in))
     base_in = lax.ppermute(later, "slab", to_owner)
 
     far = local_call(far_kernel, (pair, base_in, *back), block)

time: 156 us -> 159 us (1.019)
  the two profiles are of different devices: /device:TPU:193 before, /device:TPU:35 now
where the time goes in v18:
time: 159 us; the launch traced here: 157 us
  waiting for transfers between devices  80.5 us (51%)
  starting transfers between devices  48.7 us (31%)
  Pallas kernels  13.5 us (8%)
  local copies, waits for them, and re-layouts  12 us (8%)
    ppermute x2, waiting for transfers between devices, body(): back_in = [lax.ppermute(x, 'slab', from_owner) for x in back]  49.1 us
    ppermute x2, starting transfers between devices, body(): first_grp = [lax.ppermute(x, 'grp', grp_pairs) for x in first]  16.1 us
    ppermute x1, starting transfers between devices, body(): bulk_in = lax.ppermute(bulk, 'slab', to_owner)  14.7 us
    pallas_call x9, Pallas kernels, local_call(): pl.pallas_call(kernel, out_shape=out_shape, in_specs=spaces, out_specs=(v...  13.5 us
    unnamed x44, local copies, waits for them, and re-layouts  11.3 us
    ppermute x2, waiting for transfers between devices, body(): grp_in = [lax.ppermute(x, 'grp', grp_pairs) for x in grp_blocks]  8.59 us
    ppermute x2, waiting for transfers between devices, body(): first_grp = [lax.ppermute(x, 'grp', grp_pairs) for x in first]  7.36 us
    ppermute x1, waiting for transfers between devices, body(): bulk_in = lax.ppermute(bulk, 'slab', to_owner)  6.92 us
  transfers between devices with their start and end apart: 11, of which 9 were waited for; matrix products, arithmetic and copies ran while one was open for 1% of the time, Pallas kernels for 7%

profile of v18, /device:TPU:35, one launch (start us, length us, event | category | flops | bytes accessed | tf_op | source)
XLA Modules:
  0.0 157.1 jit_solution(13292848009775038931)
XLA Ops:
  1.9 1.8 %shard_map.66 = (f32[1544,128]{1,0:T(8,128)}, f32[4,128,128]{2,1,0:T(8,128)}) custom-call(s32[4,4]{1,0:T(4,128)S(1)} %copy-done.19, f32[512,512]{1,0:T(8,128)S(1)} %copy-done.1), custom_call_target="tpu_custom_call" | custom-call | flops 1000 | bytes 1000 | tf_op jit(solution)/shard_map/pallas_call | solution.py:142
  3.7 14.7 %collective-permute-start.4 = (f32[1544,128]{1,0:T(8,128)}, f32[1544,128]{1,0:T(8,128)S(1)}, u32[]{:S(2)}, u32[]{:S(2)}) collective-permute-start(f32[1544,128]{1,0:T(8,128)} %get-tuple-element.29), channel_id=1, source_target_pairs={{1,33},{3,35},{5,37},{7,39},{9,41},{11,43},{13,45},{15,47},{17,49}... | collective-permute-start | bytes 2371592 | tf_op jit(solution)/shard_map/ppermute | solution.py:177
  19.1 3.8 %collective-permute-start.2 = (f32[256,512]{1,0:T(8,128)S(1)}, f32[256,512]{1,0:T(8,128)}, u32[]{:S(2)}, u32[]{:S(2)}) collective-permute-start(f32[256,512]{1,0:T(8,128)S(1)} %get-tuple-element.24.refs_0_), channel_id=1, source_target_pairs={{0,256},{64,320},{128,384},{192,448},{256,0},{320,64},{384,128},{4... | collective-permute-start | bytes 1572872 | tf_op jit(solution)/shard_map/ppermute | solution.py:183
  22.9 3.0 %collective-permute-start.3 = (f32[256,512]{1,0:T(8,128)S(1)}, f32[256,512]{1,0:T(8,128)}, u32[]{:S(2)}, u32[]{:S(2)}) collective-permute-start(f32[256,512]{1,0:T(8,128)S(1)} %get-tuple-element.25.refs_1_), channel_id=1, source_target_pairs={{0,256},{64,320},{128,384},{192,448},{256,0},{320,64},{384,128},{4... | collective-permute-start | bytes 1572872 | tf_op jit(solution)/shard_map/ppermute | solution.py:183
  26.7 3.7 %collective-permute-start.1 = (f32[512,256]{1,0:T(8,128)S(1)}, f32[512,256]{1,0:T(8,128)}, u32[]{:S(2)}, u32[]{:S(2)}) collective-permute-start(f32[512,256]{1,0:T(8,128)S(1)} %copy-done), channel_id=1, source_target_pairs={{0,256},{64,320},{128,384},{192,448},{256,0},{320,64},{384,128},{4... | collective-permute-start | bytes 1572872 | tf_op jit(solution)/shard_map/ppermute | solution.py:166
  30.5 2.1 %collective-permute-start.5 = (f32[512,256]{1,0:T(8,128)S(1)}, f32[512,256]{1,0:T(8,128)}, u32[]{:S(2)}, u32[]{:S(2)}) collective-permute-start(f32[512,256]{1,0:T(8,128)S(1)} %copy-done), channel_id=1, source_target_pairs={{1,33},{3,35},{5,37},{7,39},{9,41},{11,43},{13,45},{15,47},{17,49}... | collective-permute-start | bytes 1572872 | tf_op jit(solution)/shard_map/ppermute | solution.py:167
  32.6 3.0 %collective-permute-done.2.refs_2_ = f32[256,512]{1,0:T(8,128)} collective-permute-done((f32[256,512]{1,0:T(8,128)S(1)}, f32[256,512]{1,0:T(8,128)}, u32[]{:S(2)}, u32[]{:S(2)}) %collective-permute-start.2) | collective-permute-done | bytes 524320 | tf_op jit(solution)/shard_map/ppermute | solution.py:183
  35.5 5.6 %collective-permute-done.3.refs_3_ = f32[256,512]{1,0:T(8,128)} collective-permute-done((f32[256,512]{1,0:T(8,128)S(1)}, f32[256,512]{1,0:T(8,128)}, u32[]{:S(2)}, u32[]{:S(2)}) %collective-permute-start.3) | collective-permute-done | bytes 524320 | tf_op jit(solution)/shard_map/ppermute | solution.py:183
  41.2 5.6 %collective-permute-done.1.vec_grp_ref = f32[512,256]{1,0:T(8,128)} collective-permute-done((f32[512,256]{1,0:T(8,128)S(1)}, f32[512,256]{1,0:T(8,128)}, u32[]{:S(2)}, u32[]{:S(2)}) %collective-permute-start.1) | collective-permute-done | bytes 524320 | tf_op jit(solution)/shard_map/ppermute | solution.py:166
  49.0 2.7 %shard_map.65 = (f32[512,256]{1,0:T(8,128)S(1)}, f32[512,512]{1,0:T(8,128)S(1)}, f32[512,512]{1,0:T(8,128)S(1)}) custom-call(f32[512,256]{1,0:T(8,128)S(1)} %copy-done, f32[512,512]{1,0:T(8,128)S(1)} %copy-done.8, f32[512,256]{1,0:T(8,128)} %collective-permute-done.1.vec_grp_ref, f32[256,512]{1,0:T(8,128)S(1)} %get-tuple-element.24.refs_0_, ...), custom_call_target="tpu_custom_call" | custom-call | flops 1000 | bytes 1000 | tf_op jit(solution)/shard_map/pallas_call | solution.py:142
  53.6 6.9 %collective-permute-done.4.bulk_ref = f32[1544,128]{1,0:T(8,128)S(1)} collective-permute-done((f32[1544,128]{1,0:T(8,128)}, f32[1544,128]{1,0:T(8,128)S(1)}, u32[]{:S(2)}, u32[]{:S(2)}) %collective-permute-start.4) | collective-permute-done | bytes 790560 | tf_op jit(solution)/shard_map/ppermute | solution.py:177
  64.6 1.9 %shard_map.67 = (f32[512,512]{1,0:T(8,128)S(1)}, f32[256,256]{1,0:T(8,128)S(1)}, f32[256,256]{1,0:T(8,128)S(1)}) custom-call(s32[4,4]{1,0:T(4,128)S(1)} %copy-done.20, s32[4,4]{1,0:T(4,128)S(1)} %slice_convert_fusion.in_mask, f32[512,512]{1,0:T(8,128)S(1)} %copy-done.2, f32[1544,128]{1,0:T(8,128)S(1)} %copy-done.10, ...), custom_call_target="tpu_custom_call" | custom-call | flops 1000 | bytes 1000 | tf_op jit(solution)/shard_map/pallas_call | solution.py:142
  66.6 1.3 collective-permute-start.7
  67.9 1.3 collective-permute-start.8
  69.2 2.9 %collective-permute-done.5.vec_in_ref = f32[512,256]{1,0:T(8,128)} collective-permute-done((f32[512,256]{1,0:T(8,128)S(1)}, f32[512,256]{1,0:T(8,128)}, u32[]{:S(2)}, u32[]{:S(2)}) %collective-permute-start.5) | collective-permute-done | bytes 524320 | tf_op jit(solution)/shard_map/ppermute | solution.py:167
  72.1 3.7 %shard_map.68 = (f32[512,256]{1,0:T(8,128)S(1)}, f32[512,256]{1,0:T(8,128)}) custom-call(f32[512,256]{1,0:T(8,128)S(1)} %get-tuple-element.38.base_ref, f32[512,512]{1,0:T(8,128)S(1)} %get-tuple-element.33.pair_ref, f32[512,256]{1,0:T(8,128)} %collective-permute-done.5.vec_in_ref), custom_call_target="tpu_custom_call" | custom-call | flops 1000 | bytes 1000 | tf_op jit(solution)/shard_map/pallas_call | solution.py:142
  77.0 46.8 %collective-permute-done.7.back_ref = f32[256,256]{1,0:T(8,128)S(1)} collective-permute-done((f32[256,256]{1,0:T(8,128)S(1)}, f32[256,256]{1,0:T(8,128)S(1)}, u32[]{:S(2)}, u32[]{:S(2)}) %collective-permute-start.7) | collective-permute-done | bytes 262176 | tf_op jit(solution)/shard_map/ppermute | solution.py:210
  124.6 2.3 %collective-permute-done.8.back_ref = f32[256,256]{1,0:T(8,128)S(1)} collective-permute-done((f32[256,256]{1,0:T(8,128)S(1)}, f32[256,256]{1,0:T(8,128)S(1)}, u32[]{:S(2)}, u32[]{:S(2)}) %collective-permute-start.8) | collective-permute-done | bytes 262176 | tf_op jit(solution)/shard_map/ppermute | solution.py:210
  127.5 1.4 collective-permute-start.11
  130.0 14.2 %collective-permute-start.10 = (f32[256,256]{1,0:T(8,128)S(1)}, f32[256,256]{1,0:T(8,128)S(1)}, u32[]{:S(2)}, u32[]{:S(2)}) collective-permute-start(f32[256,256]{1,0:T(8,128)S(1)} %shard_map.70.refs_1_), channel_id=1, source_target_pairs={{0,256},{64,320},{128,384},{192,448},{256,0},{320,64},{384,128},{4... | collective-permute-start | bytes 786440 | tf_op jit(solution)/shard_map/ppermute | solution.py:224
  144.2 1.9 %collective-permute-start.9 = (f32[256,256]{1,0:T(8,128)S(1)}, f32[256,256]{1,0:T(8,128)S(1)}, u32[]{:S(2)}, u32[]{:S(2)}) collective-permute-start(f32[256,256]{1,0:T(8,128)S(1)} %shard_map.69.refs_0_), channel_id=1, source_target_pairs={{0,256},{64,320},{128,384},{192,448},{256,0},{320,64},{384,128},{4... | collective-permute-start | bytes 786440 | tf_op jit(solution)/shard_map/ppermute | solution.py:224
  146.1 4.3 %collective-permute-done.10.refs_3_ = f32[256,256]{1,0:T(8,128)S(1)} collective-permute-done((f32[256,256]{1,0:T(8,128)S(1)}, f32[256,256]{1,0:T(8,128)S(1)}, u32[]{:S(2)}, u32[]{:S(2)}) %collective-permute-start.10) | collective-permute-done | bytes 262176 | tf_op jit(solution)/shard_map/ppermute | solution.py:224
  150.4 3.1 %collective-permute-done.9.refs_2_ = f32[256,256]{1,0:T(8,128)S(1)} collective-permute-done((f32[256,256]{1,0:T(8,128)S(1)}, f32[256,256]{1,0:T(8,128)S(1)}, u32[]{:S(2)}, u32[]{:S(2)}) %collective-permute-start.9) | collective-permute-done | bytes 262176 | tf_op jit(solution)/shard_map/ppermute | solution.py:224
  153.5 2.1 %shard_map.71 = f32[512,256]{1,0:T(8,128)S(1)} custom-call(s32[1,1]{1,0:T(1,128)} %bitcast.owner, f32[512,512]{1,0:T(8,128)S(1)} %copy-done.4, f32[512,512]{1,0:T(8,128)S(1)} %copy-done.6, f32[512,256]{1,0:T(8,128)} %collective-permute-done.6.back_ref, f32[256,256]{1,0:T(8,128)S(1)} %shard_map.69.refs_0_, f32[256,256]{1,0:T(8,128)S(1)} %shard_map.70.refs_1_, ...), custom_call_target="tpu_custom_call" | custom-call | flops 1000 | bytes 1000 | tf_op jit(solution)/shard_map/pallas_call | solution.py:142
  (56 shorter events, 16.9 us)
Async XLA Ops:
  0.0 1.2 copy-start.1
  1.9 16.5 %copy-start.7 = (f32[512,512]{1,0:T(8,128)S(1)}, f32[512,512]{1,0:T(8,128)}, u32[]{:S(2)}) copy-start(f32[512,512]{1,0:T(8,128)} %tiles_ref.1) | copy-start | bytes 3145732
  1.9 16.5 %copy-start.21 = (s32[4,4]{1,0:T(4,128)S(1)}, s32[4,4]{1,0:T(4,128)}, u32[]{:S(2)}) copy-start(s32[4,4]{1,0:T(4,128)} %mask.1) | copy-start | bytes 196
  3.7 23.0 %copy-start = (f32[512,256]{1,0:T(8,128)S(1)}, f32[512,256]{1,0:T(8,128)}, u32[]{:S(2)}) copy-start(f32[512,256]{1,0:T(8,128)} %vec_ref.3) | copy-start | bytes 1572868
  3.7 56.8 %collective-permute-start.4 = (f32[1544,128]{1,0:T(8,128)}, f32[1544,128]{1,0:T(8,128)S(1)}, u32[]{:S(2)}, u32[]{:S(2)}) collective-permute-start(f32[1544,128]{1,0:T(8,128)} %get-tuple-element.29), channel_id=1, source_target_pairs={{1,33},{3,35},{5,37},{7,39},{9,41},{11,43},{13,45},{15,47},{17,49}... | collective-permute-start | bytes 2371592 | tf_op jit(solution)/shard_map/ppermute | solution.py:177
  19.1 16.4 %collective-permute-start.2 = (f32[256,512]{1,0:T(8,128)S(1)}, f32[256,512]{1,0:T(8,128)}, u32[]{:S(2)}, u32[]{:S(2)}) collective-permute-start(f32[256,512]{1,0:T(8,128)S(1)} %get-tuple-element.24.refs_0_), channel_id=1, source_target_pairs={{0,256},{64,320},{128,384},{192,448},{256,0},{320,64},{384,128},{4... | collective-permute-start | bytes 1572872 | tf_op jit(solution)/shard_map/ppermute | solution.py:183
  22.9 18.3 %collective-permute-start.3 = (f32[256,512]{1,0:T(8,128)S(1)}, f32[256,512]{1,0:T(8,128)}, u32[]{:S(2)}, u32[]{:S(2)}) collective-permute-start(f32[256,512]{1,0:T(8,128)S(1)} %get-tuple-element.25.refs_1_), channel_id=1, source_target_pairs={{0,256},{64,320},{128,384},{192,448},{256,0},{320,64},{384,128},{4... | collective-permute-start | bytes 1572872 | tf_op jit(solution)/shard_map/ppermute | solution.py:183
  26.7 20.0 %collective-permute-start.1 = (f32[512,256]{1,0:T(8,128)S(1)}, f32[512,256]{1,0:T(8,128)}, u32[]{:S(2)}, u32[]{:S(2)}) collective-permute-start(f32[512,256]{1,0:T(8,128)S(1)} %copy-done), channel_id=1, source_target_pairs={{0,256},{64,320},{128,384},{192,448},{256,0},{320,64},{384,128},{4... | collective-permute-start | bytes 1572872 | tf_op jit(solution)/shard_map/ppermute | solution.py:166
  30.5 41.6 %collective-permute-start.5 = (f32[512,256]{1,0:T(8,128)S(1)}, f32[512,256]{1,0:T(8,128)}, u32[]{:S(2)}, u32[]{:S(2)}) collective-permute-start(f32[512,256]{1,0:T(8,128)S(1)} %copy-done), channel_id=1, source_target_pairs={{1,33},{3,35},{5,37},{7,39},{9,41},{11,43},{13,45},{15,47},{17,49}... | collective-permute-start | bytes 1572872 | tf_op jit(solution)/shard_map/ppermute | solution.py:167
  32.6 30.9 %copy-start.2 = (f32[512,512]{1,0:T(8,128)S(1)}, f32[512,512]{1,0:T(8,128)}, u32[]{:S(2)}) copy-start(f32[512,512]{1,0:T(8,128)} %own_ref.1) | copy-start | bytes 3145732
  46.8 1.2 copy-start.8
  49.0 11.5 %copy-start.20 = (s32[4,4]{1,0:T(4,128)S(1)}, s32[4,4]{1,0:T(4,128)}, u32[]{:S(2)}) copy-start(s32[4,4]{1,0:T(4,128)} %own_mask.1) | copy-start | bytes 196
  63.5 1.1 copy-start.10
  66.6 9.2 %copy-start.13 = (f32[256,256]{1,0:T(8,128)}, f32[256,256]{1,0:T(8,128)S(1)}, u32[]{:S(2)}) copy-start(f32[256,256]{1,0:T(8,128)S(1)} %get-tuple-element.37.refs_1_) | copy-start | bytes 786436
  66.6 57.3 %collective-permute-start.7 = (f32[256,256]{1,0:T(8,128)S(1)}, f32[256,256]{1,0:T(8,128)S(1)}, u32[]{:S(2)}, u32[]{:S(2)}) collective-permute-start(f32[256,256]{1,0:T(8,128)S(1)} %get-tuple-element.36.refs_0_), channel_id=1, source_target_pairs={{0,32},{2,34},{4,36},{6,38},{8,40},{10,42},{12,44},{14,46},{16,48}... | collective-permute-start | bytes 786440 | tf_op jit(solution)/shard_map/ppermute | solution.py:210
  67.9 59.0 %collective-permute-start.8 = (f32[256,256]{1,0:T(8,128)S(1)}, f32[256,256]{1,0:T(8,128)S(1)}, u32[]{:S(2)}, u32[]{:S(2)}) collective-permute-start(f32[256,256]{1,0:T(8,128)S(1)} %get-tuple-element.37.refs_1_), channel_id=1, source_target_pairs={{0,32},{2,34},{4,36},{6,38},{8,40},{10,42},{12,44},{14,46},{16,48}... | collective-permute-start | bytes 786440 | tf_op jit(solution)/shard_map/ppermute | solution.py:210
  75.7 70.4 %collective-permute-start.6 = (f32[512,256]{1,0:T(8,128)}, f32[512,256]{1,0:T(8,128)}, u32[]{:S(2)}, u32[]{:S(2)}) collective-permute-start(f32[512,256]{1,0:T(8,128)} %get-tuple-element.34), channel_id=1, source_target_pairs={{0,32},{2,34},{4,36},{6,38},{8,40},{10,42},{12,44},{14,46},{16,48}... | collective-permute-start | bytes 1572872 | tf_op jit(solution)/shard_map/ppermute | solution.py:212
  127.5 28.0 %collective-permute-start.11 = (f32[512,256]{1,0:T(8,128)S(1)}, f32[512,256]{1,0:T(8,128)S(1)}, u32[]{:S(2)}, u32[]{:S(2)}) collective-permute-start(f32[512,256]{1,0:T(8,128)S(1)} %get-tuple-element.38.base_ref), channel_id=1, source_target_pairs={{1,33},{3,35},{5,37},{7,39},{9,41},{11,43},{13,45},{15,47},{17,49}... | collective-permute-start | bytes 1572872 | tf_op jit(solution)/shard_map/ppermute | solution.py:214
  129.9 14.2 %copy-start.16 = (f32[256,256]{1,0:T(8,128)S(1)}, f32[256,256]{1,0:T(8,128)}, u32[]{:S(2)}) copy-start(f32[256,256]{1,0:T(8,128)} %copy-done.15) | copy-start | bytes 786436
  129.9 23.6 %copy-start.6 = (f32[512,512]{1,0:T(8,128)S(1)}, f32[512,512]{1,0:T(8,128)}, u32[]{:S(2)}) copy-start(f32[512,512]{1,0:T(8,128)} %copy-done.5) | copy-start | bytes 3145732
  129.9 23.6 %copy-start.4 = (f32[512,512]{1,0:T(8,128)S(1)}, f32[512,512]{1,0:T(8,128)}, u32[]{:S(2)}) copy-start(f32[512,512]{1,0:T(8,128)} %copy-done.3) | copy-start | bytes 3145732
  130.0 20.5 %collective-permute-start.10 = (f32[256,256]{1,0:T(8,128)S(1)}, f32[256,256]{1,0:T(8,128)S(1)}, u32[]{:S(2)}, u32[]{:S(2)}) collective-permute-start(f32[256,256]{1,0:T(8,128)S(1)} %shard_map.70.refs_1_), channel_id=1, source_target_pairs={{0,256},{64,320},{128,384},{192,448},{256,0},{320,64},{384,128},{4... | collective-permute-start | bytes 786440 | tf_op jit(solution)/shard_map/ppermute | solution.py:224
  144.2 9.3 %collective-permute-start.9 = (f32[256,256]{1,0:T(8,128)S(1)}, f32[256,256]{1,0:T(8,128)S(1)}, u32[]{:S(2)}, u32[]{:S(2)}) collective-permute-start(f32[256,256]{1,0:T(8,128)S(1)} %shard_map.69.refs_0_), channel_id=1, source_target_pairs={{0,256},{64,320},{128,384},{192,448},{256,0},{320,64},{384,128},{4... | collective-permute-start | bytes 786440 | tf_op jit(solution)/shard_map/ppermute | solution.py:224
  153.5 2.1 %copy-start.14 = (f32[256,256]{1,0:T(8,128)S(1)}, f32[256,256]{1,0:T(8,128)}, u32[]{:S(2)}) copy-start(f32[256,256]{1,0:T(8,128)} %copy-done.13) | copy-start | bytes 786436
  (9 other events, 7.7 us)
